TPU v7x, 512 devices: a whole 4x8x8 slice. The times are simulated.
512 devices in a mesh: row: 16 (over y, core), col: 32 (over z, x).
Axes of the slice: x: 4, y: 8, z: 8, core: 2. Of those that a mesh axis runs over, the one named last changes fastest.
Arguments:
- inside: float32 [2, 16, 1, 32, 256, 256], P(None, 'row', None, 'col'), may hold values from -0.375 to 0.375
- outer: float32 [2, 16, 1, 32, 256, 256], P(None, 'row', None, 'col'), may hold values from -6 to 6
- sequence: int32 [8192], replicated, may hold values from 0 to 3
Outputs:
- window: float32 [3, 2, 16, 256, 256], P(None, None, 'row', 'col')
Inputs may be any that keep to these rules, and one draw needn't show every extreme that they name: `sequence`: codes 0 A, 1 C, 2 G, 3 U.
All inputs are finite; a program needn't handle non-finite values.
Results may differ from a plain program's by a relative error of at most 0.0001.
Values sent between devices are 32-bit elements; how exact they have to be, the bound alone decides.
No kernel may reach another device: no remote copies, remote signals or barrier semaphores. Data moves between devices by JAX's collectives and lax.ppermute only.
A program may use at most 64 MiB of HBM per device.

v0:
```python
import math

import jax
import jax.numpy as jnp
from jax import lax
from jax.sharding import PartitionSpec as P

TOP = 4
WIN = 3


def passed_along(x, axis, by):
    length = lax.axis_size(axis)
    return lax.ppermute(x, axis, [(i, (i + by) % length) for i in range(length)])


def on_device(inside, outer, sequence):
    rows_count = lax.axis_size("row")
    cols_count = lax.axis_size("col")
    row_index = lax.axis_index("row")
    col_index = lax.axis_index("col")
    inner = inside[:, 0, :, 0]
    outer_local = outer[:, 0, :, 0]
    row_tiles = inner.shape[0]
    col_tiles = inner.shape[1]
    tile_size = inner.shape[2]
    tile_count = col_tiles * cols_count
    piece_rows = tile_size // cols_count
    factor = 1.0 / math.sqrt(tile_count)
    codes = sequence.reshape(tile_count, tile_size)
    row_ids = jnp.arange(row_tiles, dtype=jnp.int32) * rows_count + row_index
    col_ids = jnp.arange(col_tiles, dtype=jnp.int32) * cols_count + col_index
    tile_gap = col_ids[None, :] - row_ids[:, None]
    offsets = jnp.arange(tile_size, dtype=jnp.int32)
    col_pos = col_ids[:, None] * tile_size + offsets[None, :]
    col_codes = jnp.take(codes, col_ids, axis=0)
    earlier = []
    pieces = []
    for window_step in range(WIN):
        diagonal = TOP - window_step
        amount = -diagonal % rows_count
        received = passed_along(inner, "row", amount)
        wrapped = (row_index + diagonal % rows_count >= rows_count).astype(jnp.int32)
        extra = diagonal // rows_count + 1
        padded = jnp.concatenate(
            [received, jnp.zeros((extra, col_tiles, tile_size, tile_size), inner.dtype)], 0
        )
        shifted = lax.dynamic_slice_in_dim(padded, diagonal // rows_count + wrapped, row_tiles, 0)
        inner_rows = row_ids + diagonal
        row_codes = jnp.take(codes, jnp.minimum(inner_rows, tile_count - 1), axis=0)
        row_pos = inner_rows[:, None] * tile_size + offsets[None, :]
        code_sum = row_codes[:, None, :, None] + col_codes[None, :, None, :]
        allowed = ((code_sum == 3) | (code_sum == 5)) & (
            col_pos[None, :, None, :] - row_pos[:, None, :, None] > 3
        )
        masked = jnp.where(allowed, shifted, 0.0)
        left = jnp.where((tile_gap > TOP)[:, :, None, None], outer_local, 0.0)
        for prior_diag, prior_full in earlier:
            left = left + jnp.where(
                (tile_gap == prior_diag)[:, :, None, None], prior_full[:, None], 0.0
            )
        diag_term = jnp.sum(
            jnp.where((tile_gap == diagonal)[:, :, None, None], outer_local, 0.0), axis=1
        )
        products = jnp.einsum("abuv,abwv->auw", left, masked, precision=lax.Precision.HIGHEST)
        partial_sum = diag_term + factor * products
        whole_tiles = lax.psum(partial_sum, "col")
        piece = lax.dynamic_slice_in_dim(whole_tiles, col_index * piece_rows, piece_rows, 1)
        earlier.append((diagonal, whole_tiles))
        pieces.append(piece)
    return jnp.stack(pieces)[:, :, None]


def solution(mesh):
    placed = (P(None, "row", None, "col", None, None), P(None, "row", None, "col", None, None), P())
    return jax.shard_map(
        on_device,
        mesh=mesh,
        in_specs=placed,
        out_specs=P(None, None, "row", "col", None),
        check_vma=False,
    )
```

profile of v0, /device:TPU:6, one launch (start us, length us, event | category | flops | bytes accessed | tf_op | source)
XLA Modules:
  0.0 526.7 jit_solution(15176504899722476431)
XLA Ops:
  6.5 0.0 copy-start
  6.5 0.0 all-reduce.7.cloned.1.call-start
  6.5 6.3 %collective-permute-start = (f32[2,1,256,256]{3,2,0,1:T(8,128)}, f32[2,1,256,256]{3,2,0,1:T(8,128)S(1)}, u32[]{:S(2)}, u32[]{:S(2)}) collective-permute-start(f32[2,1,256,256]{3,2,0,1:T(8,128)} %bitcast.43), channel_id=1, source_target_pairs={{0,384},{32,416},{64,448},{96,480},{128,0},{160,32},{192,64},{224,... | collective-permute-start | bytes 1572872 | tf_op jit(solution)/shard_map/ppermute | solution.py:14
  12.8 3.2 collective-permute-start.1
  16.0 2.4 collective-permute-start.2
  18.5 0.0 copy-done
  18.6 0.6 gather_fusion
  19.2 0.6 gather_fusion.1
  19.7 0.6 gather_fusion.2
  20.3 0.1 iota_add_fusion.2
  20.4 15.7 %collective-permute-done = f32[2,1,256,256]{3,2,0,1:T(8,128)S(1)} collective-permute-done((f32[2,1,256,256]{3,2,0,1:T(8,128)}, f32[2,1,256,256]{3,2,0,1:T(8,128)S(1)}, u32[]{:S(2)}, u32[]{:S(2)}) %collective-permute-start) | collective-permute-done | bytes 524320 | tf_op jit(solution)/shard_map/ppermute | solution.py:14
  36.1 2.9 fusion.2
  39.0 0.0 copy-start.2
  39.0 0.0 all-reduce.7.cloned.1.call-update
  39.0 0.0 all-reduce.9.cloned.1.call-start
  39.1 0.1 iota_add_fusion.1
  39.2 0.1 broadcast_select_fusion.1
  39.2 12.9 %collective-permute-done.1 = f32[2,1,256,256]{3,2,0,1:T(8,128)S(1)} collective-permute-done((f32[2,1,256,256]{3,2,0,1:T(8,128)}, f32[2,1,256,256]{3,2,0,1:T(8,128)S(1)}, u32[]{:S(2)}, u32[]{:S(2)}) %collective-permute-start.1) | collective-permute-done | bytes 524320 | tf_op jit(solution)/shard_map/ppermute | solution.py:14
  52.1 148.2 %all-reduce.7.cloned.1.call-done = f32[2,256,256]{2,1,0:T(8,128)} async-done(((f32[2,256,256]{2,1,0:T(8,128)}), f32[2,256,256]{2,1,0:T(8,128)}) %all-reduce.7.cloned.1.call-update) | async-done | bytes 524304 | tf_op jit(solution)/shard_map/psum | solution.py:67
  200.3 0.0 copy-done.2
  200.3 2.8 fusion.1
  203.1 0.0 copy-start.1
  203.1 0.0 all-reduce.9.cloned.1.call-update
  203.1 0.0 all-reduce.11.cloned.1.call-start
  203.2 0.1 iota_add_fusion
  203.3 0.1 broadcast_select_fusion
  203.3 0.0 collective-permute-done.2
  203.3 156.4 %all-reduce.9.cloned.1.call-done = f32[2,256,256]{2,1,0:T(8,128)} async-done(((f32[2,256,256]{2,1,0:T(8,128)}), f32[2,256,256]{2,1,0:T(8,128)}) %all-reduce.9.cloned.1.call-update) | async-done | bytes 524304 | tf_op jit(solution)/shard_map/psum | solution.py:67
  359.7 0.0 copy-done.1
  359.7 2.9 fusion
  362.6 0.0 all-reduce.11.cloned.1.call-update
  362.6 0.7 dynamic-slice_bitcast_fusion.1
  363.4 155.5 %all-reduce.11.cloned.1.call-done = f32[2,256,256]{2,1,0:T(8,128)} async-done(((f32[2,256,256]{2,1,0:T(8,128)}), f32[2,256,256]{2,1,0:T(8,128)}) %all-reduce.11.cloned.1.call-update) | async-done | bytes 524304 | tf_op jit(solution)/shard_map/psum | solution.py:67
  518.8 0.7 dynamic-slice_bitcast_fusion
  519.6 0.6 maximum_bitcast_fusion
  (17 shorter events, 0.1 us)
Async XLA Ops:
  6.5 12.0 %copy-start = (s32[8192]{0:T(1024)S(1)}, s32[8192]{0:T(1024)}, u32[]{:S(2)}) copy-start(s32[8192]{0:T(1024)} %param.7) | copy-start | bytes 98308
  6.5 193.8 %all-reduce.7.cloned.1.call-start = ((), (), s32[]{:S(2)}) async-start(), calls=%async_computation | async-start | bytes 1048576 | tf_op jit(solution)/shard_map/psum | solution.py:67
  6.5 29.6 %collective-permute-start = (f32[2,1,256,256]{3,2,0,1:T(8,128)}, f32[2,1,256,256]{3,2,0,1:T(8,128)S(1)}, u32[]{:S(2)}, u32[]{:S(2)}) collective-permute-start(f32[2,1,256,256]{3,2,0,1:T(8,128)} %bitcast.43), channel_id=1, source_target_pairs={{0,384},{32,416},{64,448},{96,480},{128,0},{160,32},{192,64},{224,... | collective-permute-start | bytes 1572872 | tf_op jit(solution)/shard_map/ppermute | solution.py:14
  12.8 39.3 %collective-permute-start.1 = (f32[2,1,256,256]{3,2,0,1:T(8,128)}, f32[2,1,256,256]{3,2,0,1:T(8,128)S(1)}, u32[]{:S(2)}, u32[]{:S(2)}) collective-permute-start(f32[2,1,256,256]{3,2,0,1:T(8,128)} %bitcast.44), channel_id=1, source_target_pairs={{0,416},{32,448},{64,480},{96,0},{128,32},{160,64},{192,96},{224,1... | collective-permute-start | bytes 1572872 | tf_op jit(solution)/shard_map/ppermute | solution.py:14
  16.0 187.3 %collective-permute-start.2 = (f32[2,1,256,256]{3,2,0,1:T(8,128)}, f32[2,1,256,256]{3,2,0,1:T(8,128)S(1)}, u32[]{:S(2)}, u32[]{:S(2)}) collective-permute-start(f32[2,1,256,256]{3,2,0,1:T(8,128)} %bitcast.45), channel_id=1, source_target_pairs={{0,448},{32,480},{64,0},{96,32},{128,64},{160,96},{192,128},{224,1... | collective-permute-start | bytes 1572872 | tf_op jit(solution)/shard_map/ppermute | solution.py:14
  39.0 161.3 %copy-start.2 = (f32[2,1,1,1,256,256]{5,4,3,2,1,0:T(8,128)S(1)}, f32[2,1,1,1,256,256]{5,4,3,2,1,0:T(8,128)}, u32[]{:S(2)}) copy-start(f32[2,1,1,1,256,256]{5,4,3,2,1,0:T(8,128)} %param.6) | copy-start | bytes 1572868
  39.0 320.7 %all-reduce.9.cloned.1.call-start = ((), (), s32[]{:S(2)}) async-start(), calls=%async_computation.1 | async-start | bytes 1048576 | tf_op jit(solution)/shard_map/psum | solution.py:67
  203.1 156.6 %copy-start.1 = (f32[2,256,256]{2,1,0:T(8,128)S(1)}, f32[2,256,256]{2,1,0:T(8,128)}, u32[]{:S(2)}) copy-start(f32[2,256,256]{2,1,0:T(8,128)} %all-reduce.7.cloned.1.call-done) | copy-start | bytes 1572868
  203.1 315.7 %all-reduce.11.cloned.1.call-start = ((), (), s32[]{:S(2)}) async-start(), calls=%async_computation.2 | async-start | bytes 1048576 | tf_op jit(solution)/shard_map/psum | solution.py:67
Sparse Core Ops, SparseCore 0:
  39.2 161.0 all-reduce.6
  204.1 155.6 all-reduce.8
  363.1 155.6 all-reduce.10
where the time goes:
time: 528 us; the launch traced here: 527 us
  waiting for transfers between devices  489 us (93%)
  between operations  13.3 us (3%)
  starting transfers between devices  11.9 us (2%)
  matrix products  8.54 us (2%)
    psum x3, waiting for transfers between devices, on_device(): whole_tiles = lax.psum(partial_sum, 'col')  460 us
    ppermute x3, waiting for transfers between devices, passed_along(): lax.ppermute(x, axis, [(i, (i + by) % length) for i in range(length)])  28.6 us
    ppermute x3, starting transfers between devices, passed_along(): lax.ppermute(x, axis, [(i, (i + by) % length) for i in range(length)])  11.8 us
  transfers between devices with their start and end apart: 6, of which 5 were waited for; matrix products, arithmetic and copies ran while one was open for 2% of the time, Pallas kernels for 0%

commit v1 on v0

v1 whole, which is shorter than its diff:
```python
import math

import jax
import jax.numpy as jnp
import numpy as np
from jax import lax
from jax.sharding import Mesh, PartitionSpec as P

TOP = 4
WIN = 3
AXES = ("y", "core", "zh", "zl", "x")


def pairs_of(sizes, target):
    pairs = []
    for number in range(math.prod(sizes)):
        there = target(*np.unravel_index(number, sizes))
        pairs.append((number, int(np.ravel_multi_index(there, sizes))))
    return pairs


def on_device(sizes, inside, outer, sequence):
    rows_count = sizes[0] * sizes[1]
    cols_count = sizes[2] * sizes[3] * sizes[4]
    size = inside.shape[-1]
    slots = inside.shape[0]
    tile_count = slots * rows_count
    part = slots * size // cols_count
    factor = 1.0 / math.sqrt(tile_count)
    core = lax.axis_index("core")
    row = lax.axis_index("y") * sizes[1] + core
    half = lax.axis_index("zh")
    col = lax.axis_index(AXES[2:])
    home = inside[:, 0, 0, 0]
    out_tiles = outer[:, 0, 0, 0]

    def row_shift(x, by):
        n = sizes[0]
        return lax.ppermute(x, "y", [(i, (i + by) % n) for i in range(n)])

    left = row_shift(out_tiles, 1)
    ahead = row_shift(home, -1)
    left = jnp.where(row < 2, jnp.stack([jnp.zeros_like(left[0]), left[0]]), left)
    ahead = jnp.where(row >= rows_count - 2, jnp.stack([ahead[1], ahead[0]]), ahead)
    beside = lax.ppermute(jnp.where(core == 1, home, ahead), "core", [(0, 1), (1, 0)])

    slot = jnp.arange(slots, dtype=jnp.int32)
    tile_row = slot * rows_count + row - 2
    codes = sequence.reshape(tile_count, size)
    offsets = jnp.arange(size, dtype=jnp.int32)
    col_codes = lax.dynamic_index_in_dim(codes, col, 0, False)
    col_pos = col * size + offsets

    def masked(tiles, rows):
        row_codes = jnp.take(codes, jnp.clip(rows, 0, tile_count - 1), axis=0)
        total = row_codes[:, :, None] + col_codes[None, None, :]
        far = col_pos[None, None, :] - (rows[:, None] * size + offsets)[:, :, None] > 3
        return jnp.where(((total == 3) | (total == 5)) & far, tiles, 0.0)

    gap = col - row
    near = masked(home, slot * rows_count + row)
    mine = jnp.where((gap == 1) | (gap == 2), near[0], near[1])
    mine = mine.reshape(1, size // part, part, size)
    spread = jnp.broadcast_to(mine, (slots,) + mine.shape[1:]).reshape(cols_count, part, size)
    spread = lax.all_to_all(spread, AXES[2:], 0, 0)
    first = jnp.minimum(row + half * rows_count + 1, cols_count - 1)
    second = jnp.minimum(row + half * rows_count + 2, cols_count - 1)
    near1 = lax.dynamic_index_in_dim(spread, first, 0, False)
    near2 = lax.dynamic_index_in_dim(spread, second, 0, False)

    def previous_row(y, c, zh, zl, x):
        r = y * sizes[1] + c
        zh = zh if r > 0 else (zh + 1) % sizes[2]
        r = (r - 1) % rows_count
        return r // sizes[1], r % sizes[1], zh, zl, x

    next1 = lax.ppermute(near1, AXES, pairs_of(sizes, previous_row))
    bits = jnp.stack([near1, near2, next1])
    bits = lax.all_to_all(jnp.broadcast_to(bits, (sizes[3],) + bits.shape), "zl", 0, 0)
    bits = lax.all_to_all(jnp.broadcast_to(bits, (sizes[4],) + bits.shape), "x", 0, 0)
    whole = jnp.transpose(bits, (2, 1, 0, 3, 4)).reshape(3, size, size)

    def summed(tiles, e):
        right = masked(tiles, tile_row + e)
        product = jnp.einsum("auv,awv->auw", left, right, precision=lax.Precision.HIGH)
        real = (tile_row >= 0)[:, None, None]
        inner = (col > tile_row + TOP)[:, None, None]
        own = (col == tile_row + e)[:, None, None]
        part_sum = jnp.where(real & inner, factor * product, jnp.where(real & own, left, 0.0))
        got = lax.all_to_all(part_sum.reshape(cols_count, part, size), AXES[2:], 0, 0)
        return jnp.sum(got, axis=0)

    sum2 = summed(home, 2)
    sum4 = summed(ahead, 4)
    sum3 = summed(beside, 3)

    def times(a, b):
        return factor * jnp.einsum("ru,ku->rk", a, b, precision=lax.Precision.HIGH)

    w4 = sum4
    w3 = sum3 + times(w4, whole[2])
    w2 = sum2 + times(w4, whole[1]) + times(w3, whole[0])
    result = jnp.stack([w4, w3, w2])

    def sent_to(flip):
        def target(y, c, zh, zl, x):
            r = (y * sizes[1] + c - 2) % rows_count
            pick = zh if flip == 0 else 1 - zh
            n = 2 * (zl * sizes[4] + x) + pick
            zl2 = n // sizes[4] % sizes[3]
            return r // sizes[1], r % sizes[1], n // (sizes[3] * sizes[4]), zl2, n % sizes[4]
        return target

    piece = part // slots
    split = result.reshape(WIN, slots, piece, size)
    got = []
    for flip in range(2):
        which = half if flip == 0 else 1 - half
        mine = lax.dynamic_index_in_dim(split, which, 1, False)
        got.append(lax.ppermute(mine, AXES, pairs_of(sizes, sent_to(flip))))
    swap = (col % 2 == 1) ^ (row >= rows_count - 2)
    low = jnp.where(swap, got[1], got[0])
    high = jnp.where(swap, got[0], got[1])
    return jnp.stack([low, high], 1)[:, :, None]


def solution(mesh):
    sizes = (mesh.shape["row"] // 2, 2, 2, mesh.shape["col"] // 8, 4)
    fine = Mesh(mesh.devices.reshape(sizes), AXES)
    rows, cols = AXES[:2], AXES[2:]
    placed = (P(None, rows, None, cols, None, None), P(None, rows, None, cols, None, None), P())
    return jax.shard_map(
        lambda *args: on_device(sizes, *args),
        mesh=fine,
        in_specs=placed,
        out_specs=P(None, None, rows, cols, None),
        check_vma=False,
    )
```

time: 528 us -> 166 us (0.31)
  waiting for transfers between devices: 489 us -> 76 us
  starting transfers between devices: 11.9 us -> 75.5 us
  between operations: 13.3 us -> 0.38 us
    psum x3 -> x0, waiting for transfers between devices: 460 us -> none  [on_device(): whole_tiles = lax.psum(partial_sum, 'col')]
    all_to_all x0 -> x6, waiting for transfers between devices: none -> 53.6 us  [the longest x3 28.1 us: summed(): lax.all_to_all(part_sum.reshape(cols_count, part, size), AXES[2:], 0, 0)]
    all_to_all x0 -> x6, starting transfers between devices: none -> 39.8 us  [the longest x3 25.6 us: summed(): lax.all_to_all(part_sum.reshape(cols_count, part, size), AXES[2:], 0, 0)]
    ppermute x3 -> x6, starting transfers between devices: 11.8 us -> 35.7 us  [the longest x2 15.9 us: on_device(): got.append(lax.ppermute(mine, AXES, pairs_of(sizes, sent_to(flip))))]
    ppermute x3 -> x6, waiting for transfers between devices: 28.6 us -> 22.5 us  [the longest x2 11 us: on_device(): got.append(lax.ppermute(mine, AXES, pairs_of(sizes, sent_to(flip))))]
  transfers between devices with their start and end apart: 6 -> 12, of which waited for: 5 -> 10; matrix products, arithmetic and copies ran while one was open for 2% -> 5% of each run, Pallas kernels for 0% -> 0%
where the time goes in v1:
time: 166 us; the launch traced here: 165 us
  waiting for transfers between devices  76 us (46%)
  starting transfers between devices  75.5 us (45%)
  matrix products  5.76 us (3%)
  local copies, waits for them, and re-layouts  5.02 us (3%)
  other arithmetic  2.43 us (1%)
    all_to_all x3, waiting for transfers between devices, summed(): lax.all_to_all(part_sum.reshape(cols_count, part, size), AXES[2:], 0, 0)  28.1 us
    all_to_all x3, starting transfers between devices, summed(): lax.all_to_all(part_sum.reshape(cols_count, part, size), AXES[2:], 0, 0)  25.6 us
    ppermute x2, starting transfers between devices, on_device(): got.append(lax.ppermute(mine, AXES, pairs_of(sizes, sent_to(flip))))  15.9 us
    all_to_all x1, waiting for transfers between devices, on_device(): spread = lax.all_to_all(spread, AXES[2:], 0, 0)  14.4 us
    ppermute x2, waiting for transfers between devices, on_device(): got.append(lax.ppermute(mine, AXES, pairs_of(sizes, sent_to(flip))))  11 us
    ppermute x1, starting transfers between devices, on_device(): next1 = lax.ppermute(near1, AXES, pairs_of(sizes, previous_row))  10.6 us
    ppermute x2, waiting for transfers between devices, row_shift(): return lax.ppermute(x, 'y', [(i, (i + by) % n) for i in range(n)])  10.1 us
    ppermute x2, starting transfers between devices, row_shift(): return lax.ppermute(x, 'y', [(i, (i + by) % n) for i in range(n)])  7.29 us
  transfers between devices with their start and end apart: 12, of which 10 were waited for; matrix products, arithmetic and copies ran while one was open for 5% of the time, Pallas kernels for 0%

profile of v1, /device:TPU:6, one launch (start us, length us, event | category | flops | bytes accessed | tf_op | source)
XLA Modules:
  0.0 165.1 jit_solution(16328133517572406795)
XLA Ops:
  0.0 3.5 %collective-permute-start = (f32[2,256,256]{2,1,0:T(8,128)}, f32[2,256,256]{2,1,0:T(8,128)S(1)}, u32[]{:S(2)}, u32[]{:S(2)}) collective-permute-start(f32[2,256,256]{2,1,0:T(8,128)} %bitcast.54), channel_id=1, source_target_pairs={{0,64},{64,128},{128,192},{192,256},{256,320},{320,384},{384,448},... | collective-permute-start | bytes 1572872 | tf_op jit(solution)/shard_map/ppermute | solution.py:39
  3.5 3.8 %collective-permute-start.1 = (f32[2,256,256]{2,1,0:T(8,128)}, f32[2,256,256]{2,1,0:T(8,128)S(1)}, u32[]{:S(2)}, u32[]{:S(2)}) collective-permute-start(f32[2,256,256]{2,1,0:T(8,128)} %bitcast.46), channel_id=1, source_target_pairs={{0,448},{64,0},{128,64},{192,128},{256,192},{320,256},{384,320},{4... | collective-permute-start | bytes 1572872 | tf_op jit(solution)/shard_map/ppermute | solution.py:39
  7.5 0.6 copy-done.2
  8.1 0.6 gather_fusion
  8.7 0.1 iota_add_fusion.2
  8.7 0.1 broadcast_select_fusion.3
  8.8 8.7 %collective-permute-done = f32[2,256,256]{2,1,0:T(8,128)S(1)} collective-permute-done((f32[2,256,256]{2,1,0:T(8,128)}, f32[2,256,256]{2,1,0:T(8,128)S(1)}, u32[]{:S(2)}, u32[]{:S(2)}) %collective-permute-start) | collective-permute-done | bytes 524320 | tf_op jit(solution)/shard_map/ppermute | solution.py:39
  17.5 1.5 collective-permute-done.1
  19.0 1.4 fusion.2
  20.4 13.5 %all-to-all-start = ((f32[32,16,256]{2,1,0:T(8,128)}), f32[32,16,256]{2,1,0:T(8,128)S(1)}, u32[]{:S(2)}, u32[]{:S(2)}) async-start(f32[32,16,256]{2,1,0:T(8,128)} %bitcast.3), calls=%async_computation | async-start | bytes 1048576 | tf_op jit(solution)/shard_map/all_to_all | solution.py:90
  34.0 0.6 gather_fusion.2
  34.5 0.1 iota_add_fusion
  34.6 0.1 broadcast_select_fusion.1
  34.7 1.0 broadcast_select_fusion
  35.7 14.0 %all-to-all-done = f32[32,16,256]{2,1,0:T(8,128)S(1)} async-done(((f32[32,16,256]{2,1,0:T(8,128)}), f32[32,16,256]{2,1,0:T(8,128)S(1)}, u32[]{:S(2)}, u32[]{:S(2)}) %all-to-all-start) | async-done | bytes 524320 | tf_op jit(solution)/shard_map/all_to_all | solution.py:90
  49.7 0.9 broadcast_in_dim.103
  50.6 5.6 %all-to-all-start.2 = ((f32[32,16,256]{2,1,0:T(8,128)}), f32[32,16,256]{2,1,0:T(8,128)S(1)}, u32[]{:S(2)}, u32[]{:S(2)}) async-start(f32[32,16,256]{2,1,0:T(8,128)} %bitcast.7), calls=%async_computation.2 | async-start | bytes 1048576 | tf_op jit(solution)/shard_map/all_to_all | solution.py:65
  56.2 1.2 fusion
  57.4 14.4 %all-to-all-done.2 = f32[32,16,256]{2,1,0:T(8,128)S(1)} async-done(((f32[32,16,256]{2,1,0:T(8,128)}), f32[32,16,256]{2,1,0:T(8,128)S(1)}, u32[]{:S(2)}, u32[]{:S(2)}) %all-to-all-start.2) | async-done | bytes 524320 | tf_op jit(solution)/shard_map/all_to_all | solution.py:65
  71.8 5.7 %all-to-all-start.5 = ((f32[32,16,256]{2,1,0:T(8,128)}), f32[32,16,256]{2,1,0:T(8,128)S(1)}, u32[]{:S(2)}, u32[]{:S(2)}) async-start(f32[32,16,256]{2,1,0:T(8,128)} %bitcast.13), calls=%async_computation.5 | async-start | bytes 1048576 | tf_op jit(solution)/shard_map/all_to_all | solution.py:90
  77.6 0.6 gather_fusion.1
  78.1 0.1 broadcast_select_fusion.2
  78.2 1.9 %collective-permute-start.2 = (f32[2,256,256]{2,1,0:T(8,128)S(1)}, f32[2,256,256]{2,1,0:T(8,128)}, u32[]{:S(2)}, u32[]{:S(2)}) collective-permute-start(f32[2,256,256]{2,1,0:T(8,128)S(1)} %copy-done.1), channel_id=1, source_target_pairs={{0,32},{32,0},{1,33},{33,1},{2,34},{34,2},{3,35},{35,3},{4,36},{36... | collective-permute-start | bytes 1572872 | tf_op jit(solution)/shard_map/ppermute | solution.py:45
  80.1 10.6 %collective-permute-start.3 = (f32[16,256]{1,0:T(8,128)S(1)}, f32[16,256]{1,0:T(8,128)S(1)}, u32[]{:S(2)}, u32[]{:S(2)}) collective-permute-start(f32[16,256]{1,0:T(8,128)S(1)} %bitcast.49), channel_id=1, source_target_pairs={{0,496},{1,497},{2,498},{3,499},{4,500},{5,501},{6,502},{7,503},{8... | collective-permute-start | bytes 49160 | tf_op jit(solution)/shard_map/ppermute | solution.py:77
  90.8 0.1 iota_add_fusion.1
  90.8 1.4 collective-permute-done.3
  92.2 0.8 all-to-all-done.5
  93.0 0.7 broadcast_in_dim.104
  93.7 3.4 %all-to-all-start.3 = ((f32[4,3,16,256]{3,2,1,0:T(8,128)}), f32[4,3,16,256]{3,2,1,0:T(8,128)S(1)}, u32[]{:S(2)}, u32[]{:S(2)}) async-start(f32[4,3,16,256]{3,2,1,0:T(8,128)} %broadcast_in_dim.104), calls=%async_computation.3 | async-start | bytes 393216 | tf_op jit(solution)/shard_map/all_to_all | solution.py:79
  97.1 0.0 collective-permute-done.2
  97.1 2.4 %fusion.1 = f32[2,256,256]{2,1,0:T(8,128)} fusion(f32[2,256,256]{2,1,0:T(8,128)} %collective-permute-done.2, s32[2,256]{1,0:T(2,128)S(1)} %iota_add_fusion.1, s32[2,256]{1,0:T(2,128)S(1)} %broadcast_select_fusion.2, s32[256]{0:T(256)S(1)} %iota_add_fusion.3, s32[256]{0:T(256)S(1)} %bitcast.53, pred[2]{0:T(512)(128)(4,1)S(1)} %compare_and_fusion.4, ...), kind=kOutput, calls=%fused_computation.6 | convolution fusion | flops 203030528 | bytes 1841157 | tf_op jit(solution)/shard_map/auv,awv->auw/dot_general | solution.py:85
  99.5 3.8 %all-to-all-done.3 = f32[4,3,16,256]{3,2,1,0:T(8,128)S(1)} async-done(((f32[4,3,16,256]{3,2,1,0:T(8,128)}), f32[4,3,16,256]{3,2,1,0:T(8,128)S(1)}, u32[]{:S(2)}, u32[]{:S(2)}) %all-to-all-start.3) | async-done | bytes 196640 | tf_op jit(solution)/shard_map/all_to_all | solution.py:79
  103.3 6.4 %all-to-all-start.1 = ((f32[32,16,256]{2,1,0:T(8,128)}), f32[32,16,256]{2,1,0:T(8,128)S(1)}, u32[]{:S(2)}, u32[]{:S(2)}) async-start(f32[32,16,256]{2,1,0:T(8,128)} %bitcast.5), calls=%async_computation.1 | async-start | bytes 1048576 | tf_op jit(solution)/shard_map/all_to_all | solution.py:90
  109.7 13.3 %all-to-all-done.1 = f32[32,16,256]{2,1,0:T(8,128)S(1)} async-done(((f32[32,16,256]{2,1,0:T(8,128)}), f32[32,16,256]{2,1,0:T(8,128)S(1)}, u32[]{:S(2)}, u32[]{:S(2)}) %all-to-all-start.1) | async-done | bytes 524320 | tf_op jit(solution)/shard_map/all_to_all | solution.py:90
  123.0 1.0 broadcast_in_dim.105
  124.0 5.3 %all-to-all-start.4 = ((f32[4,4,3,16,256]{4,3,1,2,0:T(8,128)}), f32[4,4,3,16,256]{4,3,1,2,0:T(8,128)S(1)}, u32[]{:S(2)}, u32[]{:S(2)}) async-start(f32[4,4,3,16,256]{4,3,1,2,0:T(8,128)} %broadcast_in_dim.105), calls=%async_computation.4 | async-start | bytes 1572864 | tf_op jit(solution)/shard_map/all_to_all | solution.py:80
  129.4 7.3 %all-to-all-done.4 = f32[4,4,3,16,256]{4,3,1,2,0:T(8,128)S(1)} async-done(((f32[4,4,3,16,256]{4,3,1,2,0:T(8,128)}), f32[4,4,3,16,256]{4,3,1,2,0:T(8,128)S(1)}, u32[]{:S(2)}, u32[]{:S(2)}) %all-to-all-start.4) | async-done | bytes 786464 | tf_op jit(solution)/shard_map/all_to_all | solution.py:80
  136.6 0.1 copy.10
  136.7 0.1 fusion.42
  136.8 0.2 fusion.6
  137.0 0.3 fusion.5
  137.2 0.3 fusion.4
  137.5 0.1 pad_maximum_fusion.1
  137.6 14.0 %collective-permute-start.4 = (f32[3,8,256]{2,1,0:T(8,128)S(1)}, f32[3,8,256]{2,1,0:T(8,128)S(1)}, u32[]{:S(2)}, u32[]{:S(2)}) collective-permute-start(f32[3,8,256]{2,1,0:T(8,128)S(1)} %get-tuple-element.17), channel_id=1, source_target_pairs={{0,449},{1,451},{2,453},{3,455},{4,457},{5,459},{6,461},{7,463},{8... | collective-permute-start | bytes 73736 | tf_op jit(solution)/shard_map/ppermute | solution.py:120
  151.5 1.9 %collective-permute-start.5 = (f32[3,8,256]{2,1,0:T(8,128)S(1)}, f32[3,8,256]{2,1,0:T(8,128)S(1)}, u32[]{:S(2)}, u32[]{:S(2)}) collective-permute-start(f32[3,8,256]{2,1,0:T(8,128)S(1)} %get-tuple-element.18), channel_id=1, source_target_pairs={{0,448},{1,450},{2,452},{3,454},{4,456},{5,458},{6,460},{7,462},{8... | collective-permute-start | bytes 73736 | tf_op jit(solution)/shard_map/ppermute | solution.py:120
  153.5 0.0 collective-permute-done.4
  153.5 11.0 %collective-permute-done.5 = f32[3,8,256]{2,1,0:T(8,128)S(1)} collective-permute-done((f32[3,8,256]{2,1,0:T(8,128)S(1)}, f32[3,8,256]{2,1,0:T(8,128)S(1)}, u32[]{:S(2)}, u32[]{:S(2)}) %collective-permute-start.5) | collective-permute-done | bytes 24608 | tf_op jit(solution)/shard_map/ppermute | solution.py:120
  164.5 0.6 maximum_bitcast_fusion
  (32 shorter events, 0.4 us)
Async XLA Ops:
  0.0 17.5 %collective-permute-start = (f32[2,256,256]{2,1,0:T(8,128)}, f32[2,256,256]{2,1,0:T(8,128)S(1)}, u32[]{:S(2)}, u32[]{:S(2)}) collective-permute-start(f32[2,256,256]{2,1,0:T(8,128)} %bitcast.54), channel_id=1, source_target_pairs={{0,64},{64,128},{128,192},{192,256},{256,320},{320,384},{384,448},... | collective-permute-start | bytes 1572872 | tf_op jit(solution)/shard_map/ppermute | solution.py:39
  3.5 15.5 %collective-permute-start.1 = (f32[2,256,256]{2,1,0:T(8,128)}, f32[2,256,256]{2,1,0:T(8,128)S(1)}, u32[]{:S(2)}, u32[]{:S(2)}) collective-permute-start(f32[2,256,256]{2,1,0:T(8,128)} %bitcast.46), channel_id=1, source_target_pairs={{0,448},{64,0},{128,64},{192,128},{256,192},{320,256},{384,320},{4... | collective-permute-start | bytes 1572872 | tf_op jit(solution)/shard_map/ppermute | solution.py:39
  7.3 0.8 copy-start.2
  20.4 14.3 %copy-start = (f32[2,1,1,1,256,256]{5,4,3,2,1,0:T(8,128)S(1)}, f32[2,1,1,1,256,256]{5,4,3,2,1,0:T(8,128)}, u32[]{:S(2)}) copy-start(f32[2,1,1,1,256,256]{5,4,3,2,1,0:T(8,128)} %param.5) | copy-start | bytes 1572868
  20.4 29.3 %all-to-all-start = ((f32[32,16,256]{2,1,0:T(8,128)}), f32[32,16,256]{2,1,0:T(8,128)S(1)}, u32[]{:S(2)}, u32[]{:S(2)}) async-start(f32[32,16,256]{2,1,0:T(8,128)} %bitcast.3), calls=%async_computation | async-start | bytes 1048576 | tf_op jit(solution)/shard_map/all_to_all | solution.py:90
  50.6 21.2 %all-to-all-start.2 = ((f32[32,16,256]{2,1,0:T(8,128)}), f32[32,16,256]{2,1,0:T(8,128)S(1)}, u32[]{:S(2)}, u32[]{:S(2)}) async-start(f32[32,16,256]{2,1,0:T(8,128)} %bitcast.7), calls=%async_computation.2 | async-start | bytes 1048576 | tf_op jit(solution)/shard_map/all_to_all | solution.py:65
  71.8 6.4 %copy-start.1 = (f32[2,256,256]{2,1,0:T(8,128)S(1)}, f32[2,256,256]{2,1,0:T(8,128)}, u32[]{:S(2)}) copy-start(f32[2,256,256]{2,1,0:T(8,128)} %get-tuple-element.9) | copy-start | bytes 1572868
  71.8 21.1 %all-to-all-start.5 = ((f32[32,16,256]{2,1,0:T(8,128)}), f32[32,16,256]{2,1,0:T(8,128)S(1)}, u32[]{:S(2)}, u32[]{:S(2)}) async-start(f32[32,16,256]{2,1,0:T(8,128)} %bitcast.13), calls=%async_computation.5 | async-start | bytes 1048576 | tf_op jit(solution)/shard_map/all_to_all | solution.py:90
  78.2 18.9 %collective-permute-start.2 = (f32[2,256,256]{2,1,0:T(8,128)S(1)}, f32[2,256,256]{2,1,0:T(8,128)}, u32[]{:S(2)}, u32[]{:S(2)}) collective-permute-start(f32[2,256,256]{2,1,0:T(8,128)S(1)} %copy-done.1), channel_id=1, source_target_pairs={{0,32},{32,0},{1,33},{33,1},{2,34},{34,2},{3,35},{35,3},{4,36},{36... | collective-permute-start | bytes 1572872 | tf_op jit(solution)/shard_map/ppermute | solution.py:45
  80.1 12.1 %collective-permute-start.3 = (f32[16,256]{1,0:T(8,128)S(1)}, f32[16,256]{1,0:T(8,128)S(1)}, u32[]{:S(2)}, u32[]{:S(2)}) collective-permute-start(f32[16,256]{1,0:T(8,128)S(1)} %bitcast.49), channel_id=1, source_target_pairs={{0,496},{1,497},{2,498},{3,499},{4,500},{5,501},{6,502},{7,503},{8... | collective-permute-start | bytes 49160 | tf_op jit(solution)/shard_map/ppermute | solution.py:77
  93.7 9.6 %all-to-all-start.3 = ((f32[4,3,16,256]{3,2,1,0:T(8,128)}), f32[4,3,16,256]{3,2,1,0:T(8,128)S(1)}, u32[]{:S(2)}, u32[]{:S(2)}) async-start(f32[4,3,16,256]{3,2,1,0:T(8,128)} %broadcast_in_dim.104), calls=%async_computation.3 | async-start | bytes 393216 | tf_op jit(solution)/shard_map/all_to_all | solution.py:79
  103.3 19.7 %all-to-all-start.1 = ((f32[32,16,256]{2,1,0:T(8,128)}), f32[32,16,256]{2,1,0:T(8,128)S(1)}, u32[]{:S(2)}, u32[]{:S(2)}) async-start(f32[32,16,256]{2,1,0:T(8,128)} %bitcast.5), calls=%async_computation.1 | async-start | bytes 1048576 | tf_op jit(solution)/shard_map/all_to_all | solution.py:90
  124.0 12.7 %all-to-all-start.4 = ((f32[4,4,3,16,256]{4,3,1,2,0:T(8,128)}), f32[4,4,3,16,256]{4,3,1,2,0:T(8,128)S(1)}, u32[]{:S(2)}, u32[]{:S(2)}) async-start(f32[4,4,3,16,256]{4,3,1,2,0:T(8,128)} %broadcast_in_dim.105), calls=%async_computation.4 | async-start | bytes 1572864 | tf_op jit(solution)/shard_map/all_to_all | solution.py:80
  137.6 15.9 %collective-permute-start.4 = (f32[3,8,256]{2,1,0:T(8,128)S(1)}, f32[3,8,256]{2,1,0:T(8,128)S(1)}, u32[]{:S(2)}, u32[]{:S(2)}) collective-permute-start(f32[3,8,256]{2,1,0:T(8,128)S(1)} %get-tuple-element.17), channel_id=1, source_target_pairs={{0,449},{1,451},{2,453},{3,455},{4,457},{5,459},{6,461},{7,463},{8... | collective-permute-start | bytes 73736 | tf_op jit(solution)/shard_map/ppermute | solution.py:120
  151.5 12.9 %collective-permute-start.5 = (f32[3,8,256]{2,1,0:T(8,128)S(1)}, f32[3,8,256]{2,1,0:T(8,128)S(1)}, u32[]{:S(2)}, u32[]{:S(2)}) collective-permute-start(f32[3,8,256]{2,1,0:T(8,128)S(1)} %get-tuple-element.18), channel_id=1, source_target_pairs={{0,448},{1,450},{2,452},{3,454},{4,456},{5,458},{6,460},{7,462},{8... | collective-permute-start | bytes 73736 | tf_op jit(solution)/shard_map/ppermute | solution.py:120

commit v2 on v1

v2 whole, which is shorter than its diff:
```python
import functools
import math

import jax
import jax.numpy as jnp
import numpy as np
from jax import lax
from jax.experimental import pallas as pl
from jax.experimental.pallas import tpu as pltpu
from jax.sharding import Mesh, PartitionSpec as P

TOP = 4
WIN = 3
AXES = ("y", "core", "zh", "zl", "x")
F32 = jnp.float32


def pairs_of(sizes, target):
    pairs = []
    for number in range(math.prod(sizes)):
        there = target(*(int(i) for i in np.unravel_index(number, sizes)))
        if there is not None:
            pairs.append((number, int(np.ravel_multi_index(there, sizes))))
    return pairs


def halves(x):
    high = x.astype(jnp.bfloat16)
    return high, (x - high.astype(F32)).astype(jnp.bfloat16)


def times(a, b):
    dims = (((1,), (1,)), ((), ()))
    dot = functools.partial(lax.dot_general, dimension_numbers=dims, preferred_element_type=F32)
    return dot(a[0], b[0]) + (dot(a[0], b[1]) + dot(a[1], b[0]))


def product_kernel(steps, tile_count, factor, place, left_ref, *refs):
    pick_count = len(steps)
    right_refs, (row_codes, col_codes), rest = refs[:pick_count], refs[pick_count:pick_count + 2], refs[pick_count + 2:]
    outs, full = rest[:-1], rest[-1]
    row, col, x = place[0], place[1], place[4]
    slots, size = left_ref.shape[0], left_ref.shape[1]
    rows_count = tile_count // slots
    block = size // len(outs)
    gap = lax.broadcasted_iota(jnp.int32, (size, size), 1) - lax.broadcasted_iota(jnp.int32, (size, size), 0)
    for slot in range(slots):
        tile_row = slot * rows_count + row - 2
        left = left_ref[jnp.where(row < 2, 0, slot)]
        left_halves = halves(left)
        live = (tile_row >= 0) & (col > tile_row + TOP)
        scale = jnp.where(live, factor, 0.0).astype(F32)
        for number, (e, tile_of) in enumerate(steps):
            tile = tile_of(right_refs[number], slot, row)
            total = row_codes[number, slot] + col_codes[...]
            allowed = ((total == 3) | (total == 5)) & (gap + (col - tile_row - e) * size > 3)
            right = halves(jnp.where(allowed, tile, 0.0))
            own = jnp.where((tile_row >= 0) & (col == tile_row + e), 1.0, 0.0).astype(F32)
            full[...] = scale * times(left_halves, right) + own * left
            for j, out in enumerate(outs):
                out[number, slot] = full[pl.ds(pl.multiple_of((x ^ j) * block, block), block), :]


def add_kernel(counts, *refs):
    out = refs[-1]
    parts = [refs[:counts], refs[counts:2 * counts]]
    slots, rows = parts[0][0].shape[1:3]
    deep = out.shape[0] // slots
    piece = rows // deep
    for group, number, place in ((0, 1, 0), (1, 0, 1), (0, 0, 2)):
        for slot in range(slots):
            total = parts[group][0][number, slot]
            for ref in parts[group][1:]:
                total = total + ref[number, slot]
            for z in range(deep):
                out[slot * deep + z, place] = total[z * piece:(z + 1) * piece]


def finish_kernel(factor, place, got, whole, out_a, out_b, rows):
    half = place[2]
    sums = []
    for w in range(WIN):
        total = got[0, w]
        for k in range(1, got.shape[0]):
            total = total + got[k, w]
        sums.append(total)
    tiles = [halves(whole[k]) for k in range(3)]
    w4 = sums[0]
    w4_halves = halves(w4)
    w3 = sums[1] + factor * times(w4_halves, tiles[2])
    w2 = sums[2] + factor * (times(w4_halves, tiles[1]) + times(halves(w3), tiles[0]))
    piece = out_a.shape[1]
    for w, value in enumerate((w4, w3, w2)):
        rows[w] = value
        out_a[w] = rows[w, pl.ds(pl.multiple_of(half * piece, piece), piece), :]
        out_b[w] = rows[w, pl.ds(pl.multiple_of((1 - half) * piece, piece), piece), :]


def call(kernel, in_count, outs, scratch, flops, *args):
    spec = pl.BlockSpec(memory_space=pltpu.VMEM)
    moved = sum(math.prod(a.shape) * 4 for a in args) + sum(math.prod(s) * 4 for s in outs)
    return pl.pallas_call(
        kernel,
        out_shape=[jax.ShapeDtypeStruct(s, F32) for s in outs],
        in_specs=[pl.BlockSpec(memory_space=pltpu.SMEM)] * in_count + [spec] * (len(args) - in_count),
        out_specs=[spec] * len(outs),
        scratch_shapes=scratch,
        cost_estimate=pl.CostEstimate(flops=flops, bytes_accessed=moved, transcendentals=0),
        compiler_params=pltpu.CompilerParams(vmem_limit_bytes=24 * 1024 * 1024),
    )(*args)


def on_device(sizes, inside, outer, sequence):
    rows_count = sizes[0] * sizes[1]
    cols_count = sizes[2] * sizes[3] * sizes[4]
    size = inside.shape[-1]
    slots = inside.shape[0]
    tile_count = slots * rows_count
    part = slots * size // cols_count
    factor = 1.0 / math.sqrt(tile_count)
    core = lax.axis_index("core")
    row = lax.axis_index("y") * sizes[1] + core
    half = lax.axis_index("zh")
    col = lax.axis_index(AXES[2:])
    place = jnp.stack([row, col, half, core, lax.axis_index("x")]).astype(jnp.int32)
    home = inside[:, 0, 0, 0]
    out_tiles = outer[:, 0, 0, 0]

    def row_shift(v, by):
        n = sizes[0]
        return lax.ppermute(v, "y", [(i, (i + by) % n) for i in range(n)])

    left = row_shift(out_tiles, 1)
    ahead = row_shift(home, -1)
    beside0 = lax.ppermute(home, "core", [(1, 0)])
    beside1 = lax.ppermute(ahead, "core", [(0, 1)])

    slot = jnp.arange(slots, dtype=jnp.int32)
    codes = sequence.reshape(tile_count, size)
    offsets = jnp.arange(size, dtype=jnp.int32)
    col_codes = lax.dynamic_index_in_dim(codes, col, 0, True)
    col_pos = col * size + offsets
    wanted = slot[None, :] * rows_count + row + jnp.arange(WIN, dtype=jnp.int32)[:, None]
    row_codes = jnp.take(codes, jnp.clip(wanted, 0, tile_count - 1), axis=0)

    gap = col - row
    early = (gap == 1) | (gap == 2)
    near_row = jnp.where(early, row, rows_count + row)
    near_codes = jnp.where(early, row_codes[0, 0], row_codes[0, 1])
    total = near_codes[:, None] + col_codes
    far = col_pos[None, :] - (near_row * size + offsets)[:, None] > 3
    near = jnp.where(((total == 3) | (total == 5)) & far, jnp.where(early, home[0], home[1]), 0.0)
    near = near.reshape(1, size // part, part, size)
    spread = jnp.broadcast_to(near, (slots,) + near.shape[1:]).reshape(cols_count, part, size)
    spread = lax.all_to_all(spread, AXES[2:], 0, 0)
    first = jnp.minimum(row + half * rows_count + 1, cols_count - 1)
    second = jnp.minimum(row + half * rows_count + 2, cols_count - 1)
    near1 = lax.dynamic_index_in_dim(spread, first, 0, False)
    near2 = lax.dynamic_index_in_dim(spread, second, 0, False)

    def previous_row(y, c, zh, zl, x):
        r = y * sizes[1] + c
        zh = zh if r > 0 else (zh + 1) % sizes[2]
        r = (r - 1) % rows_count
        return r // sizes[1], r % sizes[1], zh, zl, x

    next1 = lax.ppermute(near1, AXES, pairs_of(sizes, previous_row))
    bits = jnp.stack([near1, near2, next1])
    bits = lax.all_to_all(jnp.broadcast_to(bits, (sizes[3],) + bits.shape), "zl", 0, 0)
    bits = lax.all_to_all(jnp.broadcast_to(bits, (sizes[4],) + bits.shape), "x", 0, 0)
    whole = jnp.transpose(bits, (2, 1, 0, 3, 4)).reshape(WIN, size, size)

    def own_tile(ref, s, r):
        return ref[s]

    def ahead_tile(ref, s, r):
        return ref[jnp.where(r >= rows_count - 2, slots - 1 - s, s)]

    def beside_tile(ref, s, r):
        return ref[jnp.where(r >= rows_count - 1, slots - 1 - s, s)]

    def summed_parts(steps, rights, chosen):
        blocks = [(len(steps), slots, size // sizes[4], size)] * sizes[4]
        return call(
            functools.partial(product_kernel, steps, tile_count, factor),
            1, blocks, [pltpu.VMEM((size, size), F32)], len(steps) * slots * 6 * size**3,
            place, left, *rights, row_codes[chosen][..., None], col_codes,
        )

    def exchanged(parts):
        n = sizes[4]
        return [parts[0]] + [lax.ppermute(parts[j], "x", [(i, i ^ j) for i in range(n)]) for j in range(1, n)]

    parts24 = summed_parts([(2, own_tile), (4, ahead_tile)], [home, ahead], np.array([0, 2]))
    parts24 = exchanged(parts24)
    beside = beside0 + beside1
    parts3 = exchanged(summed_parts([(3, beside_tile)], [beside], np.array([1])))
    (ready,) = call(
        functools.partial(add_kernel, sizes[4]),
        0, [(slots * sizes[3], WIN, part, size)], [], 10**6, *parts24, *parts3,
    )
    got = lax.all_to_all(ready, ("zh", "zl"), 0, 0)
    piece = part // slots
    sent = call(
        functools.partial(finish_kernel, factor),
        1, [(WIN, piece, size)] * 2, [pltpu.VMEM((WIN, part, size), F32)], 3 * 6 * part * size**2,
        place, got, whole,
    )

    def sent_to(flip):
        def target(y, c, zh, zl, x):
            r = (y * sizes[1] + c - 2) % rows_count
            pick = zh if flip == 0 else 1 - zh
            n = 2 * (x * sizes[3] + zl) + pick
            return r // sizes[1], r % sizes[1], n // (sizes[3] * sizes[4]), n // sizes[4] % sizes[3], n % sizes[4]
        return target

    back = [lax.ppermute(sent[flip], AXES, pairs_of(sizes, sent_to(flip))) for flip in range(2)]
    swap = (col % 2 == 1) ^ (row >= rows_count - 2)
    low = jnp.where(swap, back[1], back[0])
    high = jnp.where(swap, back[0], back[1])
    return jnp.stack([low, high], 1)[:, :, None]


def solution(mesh):
    sizes = (mesh.shape["row"] // 2, 2, 2, mesh.shape["col"] // 8, 4)
    fine = Mesh(mesh.devices.reshape(sizes), AXES)
    rows, cols = AXES[:2], AXES[2:]
    placed = (P(None, rows, None, cols, None, None), P(None, rows, None, cols, None, None), P())
    return jax.shard_map(
        lambda *args: on_device(sizes, *args),
        mesh=fine,
        in_specs=placed,
        out_specs=P(None, None, rows, cols, None),
        check_vma=False,
    )
```

time: 166 us -> 130 us (0.78)
  waiting for transfers between devices: 76 us -> 35.5 us
  matrix products: 5.76 us -> 0 us
  Pallas kernels: 0 us -> 5.41 us
  starting transfers between devices: 75.5 us -> 78.1 us
  local copies, waits for them, and re-layouts: 5.02 us -> 6.93 us
    ppermute x5 -> x12, starting transfers between devices: 25.1 us -> 46.2 us  [the longest x6 20.8 us: exchanged(): lax.ppermute(parts[j], 'x', [(i, i ^ j) for i in range(n)])]
    all_to_all x3 -> x1, starting transfers between devices: 25.6 us -> 4.53 us  [on_device(): got = lax.all_to_all(ready, ('zh', 'zl'), 0, 0)]
    all_to_all x3 -> x1, waiting for transfers between devices: 28.1 us -> 11.5 us  [on_device(): got = lax.all_to_all(ready, ('zh', 'zl'), 0, 0)]
    ppermute x5 -> x12, waiting for transfers between devices: 21.1 us -> 12 us  [the longest x2 9.09 us: on_device(): lax.ppermute(sent[flip], AXES, pairs_of(sizes, sent_to(flip)))]
    all_to_all x1, starting transfers between devices: 5.57 us -> 13.5 us  [on_device(): spread = lax.all_to_all(spread, AXES[2:], 0, 0)]
    all_to_all x1, waiting for transfers between devices: 7.27 us -> 0.01 us  [on_device(): lax.all_to_all(jnp.broadcast_to(bits, (sizes[4],) + bits.shape), 'x', 0, 0)]
    ppermute x1, starting transfers between devices: 10.6 us -> 3.93 us  [on_device(): next1 = lax.ppermute(near1, AXES, pairs_of(sizes, previous_row))]
    dot_general x6 -> x0, matrix products: 5.76 us -> none  [the longest x3 5.06 us: summed(): jnp.einsum('auv,awv->auw', left, right, precision=lax.Precision.HIGH)]
  transfers between devices with their start and end apart: 12 -> 17, of which waited for: 10 -> 5; matrix products, arithmetic and copies ran while one was open for 5% -> 4% of each run, Pallas kernels for 0% -> 3%
where the time goes in v2:
time: 130 us; the launch traced here: 129 us
  starting transfers between devices  78.1 us (60%)
  waiting for transfers between devices  35.5 us (27%)
  local copies, waits for them, and re-layouts  6.93 us (5%)
  Pallas kernels  5.41 us (4%)
  other arithmetic  2.65 us (2%)
    ppermute x6, starting transfers between devices, exchanged(): lax.ppermute(parts[j], 'x', [(i, i ^ j) for i in range(n)])  20.8 us
    all_to_all x1, starting transfers between devices, on_device(): spread = lax.all_to_all(spread, AXES[2:], 0, 0)  13.5 us
    ppermute x2, starting transfers between devices, on_device(): lax.ppermute(sent[flip], AXES, pairs_of(sizes, sent_to(flip)))  12.2 us
    all_to_all x1, waiting for transfers between devices, on_device(): got = lax.all_to_all(ready, ('zh', 'zl'), 0, 0)  11.5 us
    all_to_all x1, waiting for transfers between devices, on_device(): spread = lax.all_to_all(spread, AXES[2:], 0, 0)  11.4 us
    ppermute x2, waiting for transfers between devices, on_device(): lax.ppermute(sent[flip], AXES, pairs_of(sizes, sent_to(flip)))  9.09 us
    ppermute x2, starting transfers between devices, row_shift(): return lax.ppermute(v, 'y', [(i, (i + by) % n) for i in range(n)])  7.3 us
    all_to_all x1, starting transfers between devices, on_device(): lax.all_to_all(jnp.broadcast_to(bits, (sizes[4],) + bits.shape), 'x', 0, 0)  5.5 us
  transfers between devices with their start and end apart: 17, of which 5 were waited for; matrix products, arithmetic and copies ran while one was open for 4% of the time, Pallas kernels for 3%

profile of v2, /device:TPU:6, one launch (start us, length us, event | category | flops | bytes accessed | tf_op | source)
XLA Modules:
  0.0 129.0 jit_solution(11088180289178704294)
XLA Ops:
  0.1 0.7 copy-done.1
  0.8 0.1 reshape.166
  0.9 0.6 gather_fusion
  1.5 0.1 broadcast_select_fusion
  1.6 0.1 select_n.107
  1.6 1.1 slice_select_fusion
  2.7 0.1 fusion.1
  2.9 0.9 broadcast_in_dim.52
  3.7 13.5 %all-to-all-start.1 = ((f32[32,16,256]{2,1,0:T(8,128)}), f32[32,16,256]{2,1,0:T(8,128)S(1)}, u32[]{:S(2)}, u32[]{:S(2)}) async-start(f32[32,16,256]{2,1,0:T(8,128)} %bitcast.11), calls=%async_computation.1 | async-start | bytes 1048576 | tf_op jit(solution)/shard_map/all_to_all | solution.py:155
  17.3 5.4 %collective-permute-start.1 = (f32[2,256,256]{2,1,0:T(8,128)S(1)}, f32[2,256,256]{2,1,0:T(8,128)S(1)}, u32[]{:S(2)}, u32[]{:S(2)}) collective-permute-start(f32[2,256,256]{2,1,0:T(8,128)S(1)} %bitcast.26), channel_id=1, source_target_pairs={{0,448},{64,0},{128,64},{192,128},{256,192},{320,256},{384,320},{4... | collective-permute-start | bytes 1572872 | tf_op jit(solution)/shard_map/ppermute | solution.py:131
  22.7 11.4 %all-to-all-done.1 = f32[32,16,256]{2,1,0:T(8,128)S(1)} async-done(((f32[32,16,256]{2,1,0:T(8,128)}), f32[32,16,256]{2,1,0:T(8,128)S(1)}, u32[]{:S(2)}, u32[]{:S(2)}) %all-to-all-start.1) | async-done | bytes 524320 | tf_op jit(solution)/shard_map/all_to_all | solution.py:155
  34.1 3.9 %collective-permute-start.10 = (f32[16,256]{1,0:T(8,128)S(1)}, f32[16,256]{1,0:T(8,128)S(1)}, u32[]{:S(2)}, u32[]{:S(2)}) collective-permute-start(f32[16,256]{1,0:T(8,128)S(1)} %bitcast.31), channel_id=1, source_target_pairs={{0,496},{1,497},{2,498},{3,499},{4,500},{5,501},{6,502},{7,503},{8... | collective-permute-start | bytes 49160 | tf_op jit(solution)/shard_map/ppermute | solution.py:167
  38.1 1.9 %collective-permute-start = (f32[2,256,256]{2,1,0:T(8,128)S(1)}, f32[2,256,256]{2,1,0:T(8,128)S(1)}, u32[]{:S(2)}, u32[]{:S(2)}) collective-permute-start(f32[2,256,256]{2,1,0:T(8,128)S(1)} %bitcast.34), channel_id=1, source_target_pairs={{0,64},{64,128},{128,192},{192,256},{256,320},{320,384},{384,448},... | collective-permute-start | bytes 1572872 | tf_op jit(solution)/shard_map/ppermute | solution.py:131
  40.0 0.0 collective-permute-done.10
  40.0 0.7 broadcast_in_dim.53
  40.7 4.4 %all-to-all-start.2 = ((f32[4,3,16,256]{3,2,1,0:T(8,128)}), f32[4,3,16,256]{3,2,1,0:T(8,128)S(1)}, u32[]{:S(2)}, u32[]{:S(2)}) async-start(f32[4,3,16,256]{3,2,1,0:T(8,128)} %broadcast_in_dim.53), calls=%async_computation.2 | async-start | bytes 393216 | tf_op jit(solution)/shard_map/all_to_all | solution.py:169
  45.1 1.3 collective-permute-start.5
  46.4 0.0 collective-permute-done.1.refs_1_
  46.4 4.6 %collective-permute-start.6 = (f32[2,256,256]{2,1,0:T(8,128)S(1)}, f32[2,256,256]{2,1,0:T(8,128)}, u32[]{:S(2)}, u32[]{:S(2)}) collective-permute-start(f32[2,256,256]{2,1,0:T(8,128)S(1)} %collective-permute-done.1.refs_1_), channel_id=1, source_target_pairs={{0,32},{1,33},{2,34},{3,35},{4,36},{5,37},{6,38},{7,39},{8,40},{9,... | collective-permute-start | bytes 1572872 | tf_op jit(solution)/shard_map/ppermute | solution.py:136
  51.0 0.6 all-to-all-done.2
  51.6 1.0 broadcast_in_dim.54
  52.6 5.5 %all-to-all-start.3 = ((f32[4,4,3,16,256]{4,3,1,2,0:T(8,128)}), f32[4,4,3,16,256]{4,3,1,2,0:T(8,128)}, u32[]{:S(2)}, u32[]{:S(2)}) async-start(f32[4,4,3,16,256]{4,3,1,2,0:T(8,128)} %broadcast_in_dim.54), calls=%async_computation.3 | async-start | bytes 1572864 | tf_op jit(solution)/shard_map/all_to_all | solution.py:170
  58.2 0.6 gather_fusion.1
  58.7 0.2 copy.15.refs_2_
  59.0 0.1 stack.40.place
  59.0 2.3 %shard_map.73 = (f32[2,2,64,256]{3,2,1,0:T(8,128)S(1)}, f32[2,2,64,256]{3,2,1,0:T(8,128)}, f32[2,2,64,256]{3,2,1,0:T(8,128)S(1)}, f32[2,2,64,256]{3,2,1,0:T(8,128)S(1)}) custom-call(s32[5]{0:T(128)S(1)} %stack.40.place, f32[2,256,256]{2,1,0:T(8,128)S(1)} %collective-permute-done.left_ref, f32[2,256,256]{2,1,0:T(8,128)S(1)} %bitcast.28, ...), custom_call_target="tpu_custom_call" | custom-call | flops 402653184 | bytes 2626580 | tf_op jit(solution)/shard_map/pallas_call | solution.py:102
  61.3 2.7 %collective-permute-start.2 = (f32[2,2,64,256]{3,2,1,0:T(8,128)}, f32[2,2,64,256]{3,2,1,0:T(8,128)S(1)}, u32[]{:S(2)}, u32[]{:S(2)}) collective-permute-start(f32[2,2,64,256]{3,2,1,0:T(8,128)} %get-tuple-element.16), channel_id=1, source_target_pairs={{0,1},{1,0},{2,3},{3,2},{4,5},{5,4},{6,7},{7,6},{8,9},{9,8},{10,11... | collective-permute-start | bytes 786440 | tf_op jit(solution)/shard_map/ppermute | solution.py:192
  64.1 2.6 %collective-permute-start.3 = (f32[2,2,64,256]{3,2,1,0:T(8,128)S(1)}, f32[2,2,64,256]{3,2,1,0:T(8,128)S(1)}, u32[]{:S(2)}, u32[]{:S(2)}) collective-permute-start(f32[2,2,64,256]{3,2,1,0:T(8,128)S(1)} %get-tuple-element.17), channel_id=1, source_target_pairs={{0,2},{1,3},{2,0},{3,1},{4,6},{5,7},{6,4},{7,5},{8,10},{9,11},{10,... | collective-permute-start | bytes 786440 | tf_op jit(solution)/shard_map/ppermute | solution.py:192
  66.6 5.1 %collective-permute-start.4 = (f32[2,2,64,256]{3,2,1,0:T(8,128)S(1)}, f32[2,2,64,256]{3,2,1,0:T(8,128)S(1)}, u32[]{:S(2)}, u32[]{:S(2)}) collective-permute-start(f32[2,2,64,256]{3,2,1,0:T(8,128)S(1)} %get-tuple-element.18), channel_id=1, source_target_pairs={{0,3},{1,2},{2,1},{3,0},{4,7},{5,6},{6,5},{7,4},{8,11},{9,10},{10,... | collective-permute-start | bytes 786440 | tf_op jit(solution)/shard_map/ppermute | solution.py:192
  71.8 0.1 copy.16.refs_1_
  71.9 0.0 collective-permute-done.5
  71.9 1.3 add.156.refs_0_
  73.2 1.2 shard_map.74
  74.4 1.9 %collective-permute-start.7 = (f32[1,2,64,256]{3,2,1,0:T(8,128)S(1)}, f32[1,2,64,256]{3,2,1,0:T(8,128)S(1)}, u32[]{:S(2)}, u32[]{:S(2)}) collective-permute-start(f32[1,2,64,256]{3,2,1,0:T(8,128)S(1)} %get-tuple-element.20), channel_id=1, source_target_pairs={{0,1},{1,0},{2,3},{3,2},{4,5},{5,4},{6,7},{7,6},{8,9},{9,8},{10,11... | collective-permute-start | bytes 393224 | tf_op jit(solution)/shard_map/ppermute | solution.py:192
  76.3 3.4 %collective-permute-start.8 = (f32[1,2,64,256]{3,2,1,0:T(8,128)S(1)}, f32[1,2,64,256]{3,2,1,0:T(8,128)S(1)}, u32[]{:S(2)}, u32[]{:S(2)}) collective-permute-start(f32[1,2,64,256]{3,2,1,0:T(8,128)S(1)} %get-tuple-element.21), channel_id=1, source_target_pairs={{0,2},{1,3},{2,0},{3,1},{4,6},{5,7},{6,4},{7,5},{8,10},{9,11},{10,... | collective-permute-start | bytes 393224 | tf_op jit(solution)/shard_map/ppermute | solution.py:192
  79.8 5.1 %collective-permute-start.9 = (f32[1,2,64,256]{3,2,1,0:T(8,128)S(1)}, f32[1,2,64,256]{3,2,1,0:T(8,128)S(1)}, u32[]{:S(2)}, u32[]{:S(2)}) collective-permute-start(f32[1,2,64,256]{3,2,1,0:T(8,128)S(1)} %get-tuple-element.22), channel_id=1, source_target_pairs={{0,3},{1,2},{2,1},{3,0},{4,7},{5,6},{6,5},{7,4},{8,11},{9,10},{10,... | collective-permute-start | bytes 393224 | tf_op jit(solution)/shard_map/ppermute | solution.py:192
  84.9 0.0 collective-permute-done.4.refs_3_
  84.9 2.9 %collective-permute-done.9.refs_7_ = f32[1,2,64,256]{3,2,1,0:T(8,128)S(1)} collective-permute-done((f32[1,2,64,256]{3,2,1,0:T(8,128)S(1)}, f32[1,2,64,256]{3,2,1,0:T(8,128)S(1)}, u32[]{:S(2)}, u32[]{:S(2)}) %collective-permute-start.9) | collective-permute-done | bytes 131104 | tf_op jit(solution)/shard_map/ppermute | solution.py:192
  87.8 0.8 shard_map.75
  88.7 4.5 %all-to-all-start = ((f32[8,3,16,256]{3,2,1,0:T(8,128)}), f32[8,3,16,256]{3,2,1,0:T(8,128)S(1)}, u32[]{:S(2)}, u32[]{:S(2)}) async-start(f32[8,3,16,256]{3,2,1,0:T(8,128)} %shard_map.75), calls=%async_computation | async-start | bytes 786432 | tf_op jit(solution)/shard_map/all_to_all | solution.py:202
  93.2 1.2 copy.18
  94.4 11.5 %all-to-all-done.got = f32[8,3,16,256]{3,2,1,0:T(8,128)S(1)} async-done(((f32[8,3,16,256]{3,2,1,0:T(8,128)}), f32[8,3,16,256]{3,2,1,0:T(8,128)S(1)}, u32[]{:S(2)}, u32[]{:S(2)}) %all-to-all-start) | async-done | bytes 393248 | tf_op jit(solution)/shard_map/all_to_all | solution.py:202
  105.9 1.1 shard_map.76
  107.0 9.6 %collective-permute-start.11 = (f32[3,8,256]{2,1,0:T(8,128)S(1)}, f32[3,8,256]{2,1,0:T(8,128)S(1)}, u32[]{:S(2)}, u32[]{:S(2)}) collective-permute-start(f32[3,8,256]{2,1,0:T(8,128)S(1)} %get-tuple-element.23), channel_id=1, source_target_pairs={{0,449},{1,457},{2,465},{3,473},{4,451},{5,459},{6,467},{7,475},{8... | collective-permute-start | bytes 73736 | tf_op jit(solution)/shard_map/ppermute | solution.py:218
  116.6 2.6 %collective-permute-start.12 = (f32[3,8,256]{2,1,0:T(8,128)S(1)}, f32[3,8,256]{2,1,0:T(8,128)S(1)}, u32[]{:S(2)}, u32[]{:S(2)}) collective-permute-start(f32[3,8,256]{2,1,0:T(8,128)S(1)} %get-tuple-element.24), channel_id=1, source_target_pairs={{0,448},{1,456},{2,464},{3,472},{4,450},{5,458},{6,466},{7,474},{8... | collective-permute-start | bytes 73736 | tf_op jit(solution)/shard_map/ppermute | solution.py:218
  119.2 0.0 collective-permute-done.11
  119.3 9.1 %collective-permute-done.12 = f32[3,8,256]{2,1,0:T(8,128)S(1)} collective-permute-done((f32[3,8,256]{2,1,0:T(8,128)S(1)}, f32[3,8,256]{2,1,0:T(8,128)S(1)}, u32[]{:S(2)}, u32[]{:S(2)}) %collective-permute-start.12) | collective-permute-done | bytes 24608 | tf_op jit(solution)/shard_map/ppermute | solution.py:218
  128.4 0.6 copy.19
  (30 shorter events, 0.2 us)
Async XLA Ops:
  0.0 0.8 copy-start.1
  3.7 13.6 %copy-start = (f32[2,1,1,1,256,256]{5,4,3,2,1,0:T(8,128)S(1)}, f32[2,1,1,1,256,256]{5,4,3,2,1,0:T(8,128)}, u32[]{:S(2)}) copy-start(f32[2,1,1,1,256,256]{5,4,3,2,1,0:T(8,128)} %param.7) | copy-start | bytes 1572868
  3.7 34.3 %copy-start.2 = (f32[2,1,1,1,256,256]{5,4,3,2,1,0:T(8,128)S(1)}, f32[2,1,1,1,256,256]{5,4,3,2,1,0:T(8,128)}, u32[]{:S(2)}) copy-start(f32[2,1,1,1,256,256]{5,4,3,2,1,0:T(8,128)} %param.8) | copy-start | bytes 1572868
  3.7 30.4 %all-to-all-start.1 = ((f32[32,16,256]{2,1,0:T(8,128)}), f32[32,16,256]{2,1,0:T(8,128)S(1)}, u32[]{:S(2)}, u32[]{:S(2)}) async-start(f32[32,16,256]{2,1,0:T(8,128)} %bitcast.11), calls=%async_computation.1 | async-start | bytes 1048576 | tf_op jit(solution)/shard_map/all_to_all | solution.py:155
  17.3 29.1 %collective-permute-start.1 = (f32[2,256,256]{2,1,0:T(8,128)S(1)}, f32[2,256,256]{2,1,0:T(8,128)S(1)}, u32[]{:S(2)}, u32[]{:S(2)}) collective-permute-start(f32[2,256,256]{2,1,0:T(8,128)S(1)} %bitcast.26), channel_id=1, source_target_pairs={{0,448},{64,0},{128,64},{192,128},{256,192},{320,256},{384,320},{4... | collective-permute-start | bytes 1572872 | tf_op jit(solution)/shard_map/ppermute | solution.py:131
  34.1 5.9 %collective-permute-start.10 = (f32[16,256]{1,0:T(8,128)S(1)}, f32[16,256]{1,0:T(8,128)S(1)}, u32[]{:S(2)}, u32[]{:S(2)}) collective-permute-start(f32[16,256]{1,0:T(8,128)S(1)} %bitcast.31), channel_id=1, source_target_pairs={{0,496},{1,497},{2,498},{3,499},{4,500},{5,501},{6,502},{7,503},{8... | collective-permute-start | bytes 49160 | tf_op jit(solution)/shard_map/ppermute | solution.py:167
  38.1 21.0 %collective-permute-start = (f32[2,256,256]{2,1,0:T(8,128)S(1)}, f32[2,256,256]{2,1,0:T(8,128)S(1)}, u32[]{:S(2)}, u32[]{:S(2)}) collective-permute-start(f32[2,256,256]{2,1,0:T(8,128)S(1)} %bitcast.34), channel_id=1, source_target_pairs={{0,64},{64,128},{128,192},{192,256},{256,320},{320,384},{384,448},... | collective-permute-start | bytes 1572872 | tf_op jit(solution)/shard_map/ppermute | solution.py:131
  40.7 10.9 %all-to-all-start.2 = ((f32[4,3,16,256]{3,2,1,0:T(8,128)}), f32[4,3,16,256]{3,2,1,0:T(8,128)S(1)}, u32[]{:S(2)}, u32[]{:S(2)}) async-start(f32[4,3,16,256]{3,2,1,0:T(8,128)} %broadcast_in_dim.53), calls=%async_computation.2 | async-start | bytes 393216 | tf_op jit(solution)/shard_map/all_to_all | solution.py:169
  45.1 26.8 %collective-permute-start.5 = (f32[2,256,256]{2,1,0:T(8,128)S(1)}, f32[2,256,256]{2,1,0:T(8,128)}, u32[]{:S(2)}, u32[]{:S(2)}) collective-permute-start(f32[2,256,256]{2,1,0:T(8,128)S(1)} %bitcast.27), channel_id=1, source_target_pairs={{32,0},{33,1},{34,2},{35,3},{36,4},{37,5},{38,6},{39,7},{40,8},{41... | collective-permute-start | bytes 1572872 | tf_op jit(solution)/shard_map/ppermute | solution.py:135
  46.4 25.5 %collective-permute-start.6 = (f32[2,256,256]{2,1,0:T(8,128)S(1)}, f32[2,256,256]{2,1,0:T(8,128)}, u32[]{:S(2)}, u32[]{:S(2)}) collective-permute-start(f32[2,256,256]{2,1,0:T(8,128)S(1)} %collective-permute-done.1.refs_1_), channel_id=1, source_target_pairs={{0,32},{1,33},{2,34},{3,35},{4,36},{5,37},{6,38},{7,39},{8,40},{9,... | collective-permute-start | bytes 1572872 | tf_op jit(solution)/shard_map/ppermute | solution.py:136
  52.6 36.0 %all-to-all-start.3 = ((f32[4,4,3,16,256]{4,3,1,2,0:T(8,128)}), f32[4,4,3,16,256]{4,3,1,2,0:T(8,128)}, u32[]{:S(2)}, u32[]{:S(2)}) async-start(f32[4,4,3,16,256]{4,3,1,2,0:T(8,128)} %broadcast_in_dim.54), calls=%async_computation.3 | async-start | bytes 1572864 | tf_op jit(solution)/shard_map/all_to_all | solution.py:170
  61.3 18.4 %collective-permute-start.2 = (f32[2,2,64,256]{3,2,1,0:T(8,128)}, f32[2,2,64,256]{3,2,1,0:T(8,128)S(1)}, u32[]{:S(2)}, u32[]{:S(2)}) collective-permute-start(f32[2,2,64,256]{3,2,1,0:T(8,128)} %get-tuple-element.16), channel_id=1, source_target_pairs={{0,1},{1,0},{2,3},{3,2},{4,5},{5,4},{6,7},{7,6},{8,9},{9,8},{10,11... | collective-permute-start | bytes 786440 | tf_op jit(solution)/shard_map/ppermute | solution.py:192
  64.1 20.8 %collective-permute-start.3 = (f32[2,2,64,256]{3,2,1,0:T(8,128)S(1)}, f32[2,2,64,256]{3,2,1,0:T(8,128)S(1)}, u32[]{:S(2)}, u32[]{:S(2)}) collective-permute-start(f32[2,2,64,256]{3,2,1,0:T(8,128)S(1)} %get-tuple-element.17), channel_id=1, source_target_pairs={{0,2},{1,3},{2,0},{3,1},{4,6},{5,7},{6,4},{7,5},{8,10},{9,11},{10,... | collective-permute-start | bytes 786440 | tf_op jit(solution)/shard_map/ppermute | solution.py:192
  66.6 18.2 %collective-permute-start.4 = (f32[2,2,64,256]{3,2,1,0:T(8,128)S(1)}, f32[2,2,64,256]{3,2,1,0:T(8,128)S(1)}, u32[]{:S(2)}, u32[]{:S(2)}) collective-permute-start(f32[2,2,64,256]{3,2,1,0:T(8,128)S(1)} %get-tuple-element.18), channel_id=1, source_target_pairs={{0,3},{1,2},{2,1},{3,0},{4,7},{5,6},{6,5},{7,4},{8,11},{9,10},{10,... | collective-permute-start | bytes 786440 | tf_op jit(solution)/shard_map/ppermute | solution.py:192
  74.4 10.5 %collective-permute-start.7 = (f32[1,2,64,256]{3,2,1,0:T(8,128)S(1)}, f32[1,2,64,256]{3,2,1,0:T(8,128)S(1)}, u32[]{:S(2)}, u32[]{:S(2)}) collective-permute-start(f32[1,2,64,256]{3,2,1,0:T(8,128)S(1)} %get-tuple-element.20), channel_id=1, source_target_pairs={{0,1},{1,0},{2,3},{3,2},{4,5},{5,4},{6,7},{7,6},{8,9},{9,8},{10,11... | collective-permute-start | bytes 393224 | tf_op jit(solution)/shard_map/ppermute | solution.py:192
  76.3 8.6 %collective-permute-start.8 = (f32[1,2,64,256]{3,2,1,0:T(8,128)S(1)}, f32[1,2,64,256]{3,2,1,0:T(8,128)S(1)}, u32[]{:S(2)}, u32[]{:S(2)}) collective-permute-start(f32[1,2,64,256]{3,2,1,0:T(8,128)S(1)} %get-tuple-element.21), channel_id=1, source_target_pairs={{0,2},{1,3},{2,0},{3,1},{4,6},{5,7},{6,4},{7,5},{8,10},{9,11},{10,... | collective-permute-start | bytes 393224 | tf_op jit(solution)/shard_map/ppermute | solution.py:192
  79.8 8.1 %collective-permute-start.9 = (f32[1,2,64,256]{3,2,1,0:T(8,128)S(1)}, f32[1,2,64,256]{3,2,1,0:T(8,128)S(1)}, u32[]{:S(2)}, u32[]{:S(2)}) collective-permute-start(f32[1,2,64,256]{3,2,1,0:T(8,128)S(1)} %get-tuple-element.22), channel_id=1, source_target_pairs={{0,3},{1,2},{2,1},{3,0},{4,7},{5,6},{6,5},{7,4},{8,11},{9,10},{10,... | collective-permute-start | bytes 393224 | tf_op jit(solution)/shard_map/ppermute | solution.py:192
  88.7 17.2 %all-to-all-start = ((f32[8,3,16,256]{3,2,1,0:T(8,128)}), f32[8,3,16,256]{3,2,1,0:T(8,128)S(1)}, u32[]{:S(2)}, u32[]{:S(2)}) async-start(f32[8,3,16,256]{3,2,1,0:T(8,128)} %shard_map.75), calls=%async_computation | async-start | bytes 786432 | tf_op jit(solution)/shard_map/all_to_all | solution.py:202
  107.0 12.3 %collective-permute-start.11 = (f32[3,8,256]{2,1,0:T(8,128)S(1)}, f32[3,8,256]{2,1,0:T(8,128)S(1)}, u32[]{:S(2)}, u32[]{:S(2)}) collective-permute-start(f32[3,8,256]{2,1,0:T(8,128)S(1)} %get-tuple-element.23), channel_id=1, source_target_pairs={{0,449},{1,457},{2,465},{3,473},{4,451},{5,459},{6,467},{7,475},{8... | collective-permute-start | bytes 73736 | tf_op jit(solution)/shard_map/ppermute | solution.py:218
  116.6 11.7 %collective-permute-start.12 = (f32[3,8,256]{2,1,0:T(8,128)S(1)}, f32[3,8,256]{2,1,0:T(8,128)S(1)}, u32[]{:S(2)}, u32[]{:S(2)}) collective-permute-start(f32[3,8,256]{2,1,0:T(8,128)S(1)} %get-tuple-element.24), channel_id=1, source_target_pairs={{0,448},{1,456},{2,464},{3,472},{4,450},{5,458},{6,466},{7,474},{8... | collective-permute-start | bytes 73736 | tf_op jit(solution)/shard_map/ppermute | solution.py:218

commit v3 on v2

--- a/solution.py
+++ b/solution.py
@@ -35,60 +35,69 @@
     return dot(a[0], b[0]) + (dot(a[0], b[1]) + dot(a[1], b[0]))
 
 
-def product_kernel(steps, tile_count, factor, place, left_ref, *refs):
-    pick_count = len(steps)
-    right_refs, (row_codes, col_codes), rest = refs[:pick_count], refs[pick_count:pick_count + 2], refs[pick_count + 2:]
-    outs, full = rest[:-1], rest[-1]
-    row, col, x = place[0], place[1], place[4]
+def product_kernel(tile_count, factor, place, left_ref, home_ref, ahead_ref, beside0_ref, beside1_ref, row_codes, col_codes, out):
+    row, col, core = place[0], place[1], place[3]
     slots, size = left_ref.shape[0], left_ref.shape[1]
     rows_count = tile_count // slots
-    block = size // len(outs)
+    block = size // out.shape[0]
     gap = lax.broadcasted_iota(jnp.int32, (size, size), 1) - lax.broadcasted_iota(jnp.int32, (size, size), 0)
     for slot in range(slots):
+        other = slots - 1 - slot
         tile_row = slot * rows_count + row - 2
         left = left_ref[jnp.where(row < 2, 0, slot)]
         left_halves = halves(left)
         live = (tile_row >= 0) & (col > tile_row + TOP)
         scale = jnp.where(live, factor, 0.0).astype(F32)
-        for number, (e, tile_of) in enumerate(steps):
-            tile = tile_of(right_refs[number], slot, row)
+        for number in range(WIN):
+            e = TOP - number
+            if e == 4:
+                tile = ahead_ref[jnp.where(row >= rows_count - 2, other, slot)]
+            elif e == 3:
+                after = beside1_ref[jnp.where(row >= rows_count - 1, other, slot)]
+                tile = jnp.where(core == 0, beside0_ref[slot], after)
+            else:
+                tile = home_ref[slot]
             total = row_codes[number, slot] + col_codes[...]
             allowed = ((total == 3) | (total == 5)) & (gap + (col - tile_row - e) * size > 3)
             right = halves(jnp.where(allowed, tile, 0.0))
             own = jnp.where((tile_row >= 0) & (col == tile_row + e), 1.0, 0.0).astype(F32)
-            full[...] = scale * times(left_halves, right) + own * left
-            for j, out in enumerate(outs):
-                out[number, slot] = full[pl.ds(pl.multiple_of((x ^ j) * block, block), block), :]
-
-
-def add_kernel(counts, *refs):
-    out = refs[-1]
-    parts = [refs[:counts], refs[counts:2 * counts]]
-    slots, rows = parts[0][0].shape[1:3]
+            full = scale * times(left_halves, right) + own * left
+            for x in range(out.shape[0]):
+                out[x, number, slot] = full[x * block:(x + 1) * block]
+
+
+def add_kernel(got, out):
+    slots, rows = got.shape[2:4]
     deep = out.shape[0] // slots
     piece = rows // deep
-    for group, number, place in ((0, 1, 0), (1, 0, 1), (0, 0, 2)):
+    for number in range(WIN):
         for slot in range(slots):
-            total = parts[group][0][number, slot]
-            for ref in parts[group][1:]:
-                total = total + ref[number, slot]
+            total = got[0, number, slot]
+            for k in range(1, got.shape[0]):
+                total = total + got[k, number, slot]
             for z in range(deep):
-                out[slot * deep + z, place] = total[z * piece:(z + 1) * piece]
-
-
-def finish_kernel(factor, place, got, whole, out_a, out_b, rows):
-    half = place[2]
+                out[slot * deep + z, number] = total[z * piece:(z + 1) * piece]
+
+
+def finish_kernel(factor, place, got, *refs):
+    packs, out_a, out_b, whole, rows = refs[:-4], refs[-4], refs[-3], refs[-2], refs[-1]
+    half, x, zl = place[2], place[4], place[5]
+    deep, _, part, _ = packs[0].shape
+    for j, pack in enumerate(packs):
+        for i in range(deep):
+            start = pl.multiple_of(((zl ^ i) * len(packs) + (x ^ j)) * part, part)
+            for k in range(3):
+                whole[k, pl.ds(start, part), :] = pack[i, k]
     sums = []
     for w in range(WIN):
         total = got[0, w]
         for k in range(1, got.shape[0]):
             total = total + got[k, w]
         sums.append(total)
-    tiles = [halves(whole[k]) for k in range(3)]
     w4 = sums[0]
     w4_halves = halves(w4)
-    w3 = sums[1] + factor * times(w4_halves, tiles[2])
-    w2 = sums[2] + factor * (times(w4_halves, tiles[1]) + times(halves(w3), tiles[0]))
+    w3 = sums[1] + factor * times(w4_halves, halves(whole[2]))
+    w2 = sums[2] + factor * (times(w4_halves, halves(whole[1])) + times(halves(w3), halves(whole[0])))
     piece = out_a.shape[1]
     for w, value in enumerate((w4, w3, w2)):
         rows[w] = value
@@ -122,7 +131,7 @@
     row = lax.axis_index("y") * sizes[1] + core
     half = lax.axis_index("zh")
     col = lax.axis_index(AXES[2:])
-    place = jnp.stack([row, col, half, core, lax.axis_index("x")]).astype(jnp.int32)
+    place = jnp.stack([row, col, half, core, lax.axis_index("x"), lax.axis_index("zl")]).astype(jnp.int32)
     home = inside[:, 0, 0, 0]
     out_tiles = outer[:, 0, 0, 0]
 
@@ -140,13 +149,13 @@
     offsets = jnp.arange(size, dtype=jnp.int32)
     col_codes = lax.dynamic_index_in_dim(codes, col, 0, True)
     col_pos = col * size + offsets
-    wanted = slot[None, :] * rows_count + row + jnp.arange(WIN, dtype=jnp.int32)[:, None]
+    wanted = slot[None, :] * rows_count + row + (WIN - 1) - jnp.arange(WIN, dtype=jnp.int32)[:, None]
     row_codes = jnp.take(codes, jnp.clip(wanted, 0, tile_count - 1), axis=0)
 
     gap = col - row
     early = (gap == 1) | (gap == 2)
     near_row = jnp.where(early, row, rows_count + row)
-    near_codes = jnp.where(early, row_codes[0, 0], row_codes[0, 1])
+    near_codes = jnp.where(early, row_codes[WIN - 1, 0], row_codes[WIN - 1, 1])
     total = near_codes[:, None] + col_codes
     far = col_pos[None, :] - (near_row * size + offsets)[:, None] > 3
     near = jnp.where(((total == 3) | (total == 5)) & far, jnp.where(early, home[0], home[1]), 0.0)
@@ -157,6 +166,7 @@
     second = jnp.minimum(row + half * rows_count + 2, cols_count - 1)
     near1 = lax.dynamic_index_in_dim(spread, first, 0, False)
     near2 = lax.dynamic_index_in_dim(spread, second, 0, False)
+    near1, near2, left, ahead = lax.optimization_barrier((near1, near2, left, ahead))
 
     def previous_row(y, c, zh, zl, x):
         r = y * sizes[1] + c
@@ -166,45 +176,26 @@
 
     next1 = lax.ppermute(near1, AXES, pairs_of(sizes, previous_row))
     bits = jnp.stack([near1, near2, next1])
-    bits = lax.all_to_all(jnp.broadcast_to(bits, (sizes[3],) + bits.shape), "zl", 0, 0)
-    bits = lax.all_to_all(jnp.broadcast_to(bits, (sizes[4],) + bits.shape), "x", 0, 0)
-    whole = jnp.transpose(bits, (2, 1, 0, 3, 4)).reshape(WIN, size, size)
-
-    def own_tile(ref, s, r):
-        return ref[s]
-
-    def ahead_tile(ref, s, r):
-        return ref[jnp.where(r >= rows_count - 2, slots - 1 - s, s)]
-
-    def beside_tile(ref, s, r):
-        return ref[jnp.where(r >= rows_count - 1, slots - 1 - s, s)]
-
-    def summed_parts(steps, rights, chosen):
-        blocks = [(len(steps), slots, size // sizes[4], size)] * sizes[4]
-        return call(
-            functools.partial(product_kernel, steps, tile_count, factor),
-            1, blocks, [pltpu.VMEM((size, size), F32)], len(steps) * slots * 6 * size**3,
-            place, left, *rights, row_codes[chosen][..., None], col_codes,
-        )
-
-    def exchanged(parts):
-        n = sizes[4]
-        return [parts[0]] + [lax.ppermute(parts[j], "x", [(i, i ^ j) for i in range(n)]) for j in range(1, n)]
-
-    parts24 = summed_parts([(2, own_tile), (4, ahead_tile)], [home, ahead], np.array([0, 2]))
-    parts24 = exchanged(parts24)
-    beside = beside0 + beside1
-    parts3 = exchanged(summed_parts([(3, beside_tile)], [beside], np.array([1])))
-    (ready,) = call(
-        functools.partial(add_kernel, sizes[4]),
-        0, [(slots * sizes[3], WIN, part, size)], [], 10**6, *parts24, *parts3,
+
+    def partners(v, axis, n):
+        return [v] + [lax.ppermute(v, axis, [(i, i ^ j) for i in range(n)]) for j in range(1, n)]
+
+    packs = partners(jnp.stack(partners(bits, "zl", sizes[3])), "x", sizes[4])
+
+    wide = (sizes[4], WIN, slots, size // sizes[4], size)
+    (parts,) = call(
+        functools.partial(product_kernel, tile_count, factor),
+        1, [wide], [], WIN * slots * 6 * size**3,
+        place, left, home, ahead, beside0, beside1, row_codes[..., None], col_codes,
     )
+    parts = lax.all_to_all(parts, "x", 0, 0)
+    (ready,) = call(add_kernel, 0, [(slots * sizes[3], WIN, part, size)], [], 10**6, parts)
     got = lax.all_to_all(ready, ("zh", "zl"), 0, 0)
     piece = part // slots
     sent = call(
         functools.partial(finish_kernel, factor),
-        1, [(WIN, piece, size)] * 2, [pltpu.VMEM((WIN, part, size), F32)], 3 * 6 * part * size**2,
-        place, got, whole,
+        1, [(WIN, piece, size)] * 2, [pltpu.VMEM((3, size, size), F32), pltpu.VMEM((WIN, part, size), F32)],
+        3 * 6 * part * size**2, place, got, *packs,
     )
 
     def sent_to(flip):

time: 130 us -> 129 us (level)
  blocking collectives: 0 us -> 21.5 us
  starting transfers between devices: 78.1 us -> 68.2 us
  waiting for transfers between devices: 35.5 us -> 26.7 us
  local copies, waits for them, and re-layouts: 6.93 us -> 5.33 us
  Pallas kernels: 5.41 us -> 3.91 us
    all_to_all x0 -> x1, blocking collectives: none -> 21.5 us  [on_device(): parts = lax.all_to_all(parts, 'x', 0, 0)]
    all_to_all x1, waiting for transfers between devices: 11.5 us -> 0.01 us  [on_device(): got = lax.all_to_all(ready, ('zh', 'zl'), 0, 0)]
    all_to_all x1, waiting for transfers between devices: 11.4 us -> 0.01 us  [on_device(): spread = lax.all_to_all(spread, AXES[2:], 0, 0)]
    all_to_all x2 -> x0, starting transfers between devices: 9.86 us -> none  [the longest x1 5.5 us: on_device(): lax.all_to_all(jnp.broadcast_to(bits, (sizes[4],) + bits.shape), 'x', 0, 0)]
    ppermute x2, waiting for transfers between devices: 0.01 us -> 7.97 us  [row_shift(): return lax.ppermute(v, 'y', [(i, (i + by) % n) for i in range(n)])]
    ppermute x6, waiting for transfers between devices: 2.94 us -> 7.72 us  [partners(): lax.ppermute(v, axis, [(i, i ^ j) for i in range(n)])]
    ppermute x1, starting transfers between devices: 4.62 us -> 1.31 us  [on_device(): beside1 = lax.ppermute(ahead, 'core', [(0, 1)])]
    ppermute x1, starting transfers between devices: 3.93 us -> 6.83 us  [on_device(): next1 = lax.ppermute(near1, AXES, pairs_of(sizes, previous_row))]
  transfers between devices with their start and end apart: 17 -> 15, of which waited for: 5 -> 7; matrix products, arithmetic and copies ran while one was open for 4% -> 3% of each run, Pallas kernels for 3% -> 0%
where the time goes in v3:
time: 129 us
  starting transfers between devices  68.2 us (53%)
  waiting for transfers between devices  26.7 us (21%)
  blocking collectives  21.5 us (17%)
  local copies, waits for them, and re-layouts  5.33 us (4%)
  Pallas kernels  3.91 us (3%)
  other arithmetic  2.7 us (2%)
    all_to_all x1, blocking collectives, on_device(): parts = lax.all_to_all(parts, 'x', 0, 0)  21.5 us
    ppermute x6, starting transfers between devices, partners(): lax.ppermute(v, axis, [(i, i ^ j) for i in range(n)])  20.5 us
    all_to_all x1, starting transfers between devices, on_device(): spread = lax.all_to_all(spread, AXES[2:], 0, 0)  13.5 us
    ppermute x2, starting transfers between devices, on_device(): lax.ppermute(sent[flip], AXES, pairs_of(sizes, sent_to(flip)))  10.9 us
    ppermute x2, waiting for transfers between devices, on_device(): lax.ppermute(sent[flip], AXES, pairs_of(sizes, sent_to(flip)))  9.61 us
    ppermute x2, waiting for transfers between devices, row_shift(): return lax.ppermute(v, 'y', [(i, (i + by) % n) for i in range(n)])  7.97 us
    ppermute x6, waiting for transfers between devices, partners(): lax.ppermute(v, axis, [(i, i ^ j) for i in range(n)])  7.72 us
    ppermute x2, starting transfers between devices, row_shift(): return lax.ppermute(v, 'y', [(i, (i + by) % n) for i in range(n)])  7.3 us
  transfers between devices with their start and end apart: 15, of which 7 were waited for; matrix products, arithmetic and copies ran while one was open for 3% of the time, Pallas kernels for 0%

profile of v3, /device:TPU:6, one launch (start us, length us, event | category | flops | bytes accessed | tf_op | source)
XLA Modules:
  0.0 128.7 jit_solution(3547881331435898045)
XLA Ops:
  0.0 0.0 copy-start
  0.1 1.1 slice_select_fusion
  1.2 0.8 reshape.146
  2.0 0.1 reshape.150
  2.1 0.6 gather_fusion
  2.7 0.1 broadcast_select_fusion.1
  2.8 0.1 select_n.107
  2.8 0.1 fusion.1
  3.0 0.9 broadcast_in_dim.35
  3.8 13.5 %all-to-all-start = ((f32[32,16,256]{2,1,0:T(8,128)}), f32[32,16,256]{2,1,0:T(8,128)}, u32[]{:S(2)}, u32[]{:S(2)}) async-start(f32[32,16,256]{2,1,0:T(8,128)} %bitcast.8), calls=%async_computation | async-start | bytes 1048576 | tf_op jit(solution)/shard_map/all_to_all | solution.py:164
  17.3 5.4 %collective-permute-start.1 = (f32[2,256,256]{2,1,0:T(8,128)S(1)}, f32[2,256,256]{2,1,0:T(8,128)S(1)}, u32[]{:S(2)}, u32[]{:S(2)}) collective-permute-start(f32[2,256,256]{2,1,0:T(8,128)S(1)} %bitcast.31), channel_id=1, source_target_pairs={{0,448},{64,0},{128,64},{192,128},{256,192},{320,256},{384,320},{4... | collective-permute-start | bytes 1572872 | tf_op jit(solution)/shard_map/ppermute | solution.py:140
  22.7 1.9 %collective-permute-start = (f32[2,256,256]{2,1,0:T(8,128)}, f32[2,256,256]{2,1,0:T(8,128)S(1)}, u32[]{:S(2)}, u32[]{:S(2)}) collective-permute-start(f32[2,256,256]{2,1,0:T(8,128)} %bitcast.11), channel_id=1, source_target_pairs={{0,64},{64,128},{128,192},{192,256},{256,320},{320,384},{384,448},... | collective-permute-start | bytes 1572872 | tf_op jit(solution)/shard_map/ppermute | solution.py:140
  24.6 1.3 %collective-permute-start.2 = (f32[2,256,256]{2,1,0:T(8,128)S(1)}, f32[2,256,256]{2,1,0:T(8,128)S(1)}, u32[]{:S(2)}, u32[]{:S(2)}) collective-permute-start(f32[2,256,256]{2,1,0:T(8,128)S(1)} %bitcast.32), channel_id=1, source_target_pairs={{32,0},{33,1},{34,2},{35,3},{36,4},{37,5},{38,6},{39,7},{40,8},{41... | collective-permute-start | bytes 1572872 | tf_op jit(solution)/shard_map/ppermute | solution.py:144
  25.9 7.4 %collective-permute-done.1.ahead_ref = f32[2,256,256]{2,1,0:T(8,128)S(1)} collective-permute-done((f32[2,256,256]{2,1,0:T(8,128)S(1)}, f32[2,256,256]{2,1,0:T(8,128)S(1)}, u32[]{:S(2)}, u32[]{:S(2)}) %collective-permute-start.1) | collective-permute-done | bytes 524320 | tf_op jit(solution)/shard_map/ppermute | solution.py:140
  33.3 1.3 %collective-permute-start.3 = (f32[2,256,256]{2,1,0:T(8,128)S(1)}, f32[2,256,256]{2,1,0:T(8,128)S(1)}, u32[]{:S(2)}, u32[]{:S(2)}) collective-permute-start(f32[2,256,256]{2,1,0:T(8,128)S(1)} %collective-permute-done.1.ahead_ref), channel_id=1, source_target_pairs={{0,32},{1,33},{2,34},{3,35},{4,36},{5,37},{6,38},{7,39},{8,40},{9,... | collective-permute-start | bytes 1572872 | tf_op jit(solution)/shard_map/ppermute | solution.py:145
  34.6 1.5 %gather.10 = s32[3,2,256,1]{3,2,1,0:T(8,128)} reshape(s32[6,256]{1,0:T(8,128)S(1)} %gather_fusion) | data formatting | bytes 12288 | tf_op jit(solution)/shard_map/jit(_take)/gather | solution.py:153
  36.2 0.1 stack.63.place
  36.2 1.3 broadcast_select_fusion.row_codes
  37.5 0.0 all-to-all-done
  37.5 0.7 dynamic-slice_bitcast_fusion
  38.2 0.6 collective-permute-done.left_ref
  38.9 0.0 collective-permute-done.2.beside0_ref
  38.9 0.0 collective-permute-done.3.beside1_ref
  38.9 1.9 %shard_map.37 = f32[4,3,2,64,256]{4,3,2,1,0:T(8,128)S(1)} custom-call(s32[6]{0:T(128)S(1)} %stack.63.place, f32[2,256,256]{2,1,0:T(8,128)S(1)} %collective-permute-done.left_ref, f32[2,256,256]{2,1,0:T(8,128)S(1)} %bitcast.33, f32[2,256,256]{2,1,0:T(8,128)S(1)} %collective-permute-done.1.ahead_ref, f32[2,256,256]{2,1,0:T(8,128)S(1)} %collective-permute-done.2.beside0_ref, ...), custom_call_target="tpu_custom_call" | custom-call | flops 603979776 | bytes 4201496 | tf_op jit(solution)/shard_map/pallas_call | solution.py:111
  40.8 21.5 %all_to_all.15.got = f32[4,3,2,64,256]{4,3,2,1,0:T(8,128)S(1)} all-to-all(f32[4,3,2,64,256]{4,3,2,1,0:T(8,128)S(1)} %shard_map.37), channel_id=1, replica_groups=mesh['y'=8,'core'=2,'zh'=2,'zl'=4,'x'=4] {'x'}, dimensions={0} | all-to-all | bytes 3145728 | tf_op jit(solution)/shard_map/all_to_all | solution.py:191
  62.3 0.8 shard_map.38
  63.1 6.7 %all-to-all-start.2 = ((f32[8,3,16,256]{3,2,1,0:T(8,128)}), f32[8,3,16,256]{3,2,1,0:T(8,128)S(1)}, u32[]{:S(2)}, u32[]{:S(2)}) async-start(f32[8,3,16,256]{3,2,1,0:T(8,128)} %shard_map.38), calls=%async_computation.2 | async-start | bytes 786432 | tf_op jit(solution)/shard_map/all_to_all | solution.py:193
  69.7 6.8 %collective-permute-start.4 = (f32[16,256]{1,0:T(8,128)S(1)}, f32[16,256]{1,0:T(8,128)S(1)}, u32[]{:S(2)}, u32[]{:S(2)}) collective-permute-start(f32[16,256]{1,0:T(8,128)S(1)} %get-tuple-element.13), channel_id=1, source_target_pairs={{0,496},{1,497},{2,498},{3,499},{4,500},{5,501},{6,502},{7,503},{8... | collective-permute-start | bytes 49160 | tf_op jit(solution)/shard_map/ppermute | solution.py:177
  76.6 1.4 %collective-permute-done.4 = f32[16,256]{1,0:T(8,128)S(1)} collective-permute-done((f32[16,256]{1,0:T(8,128)S(1)}, f32[16,256]{1,0:T(8,128)S(1)}, u32[]{:S(2)}, u32[]{:S(2)}) %collective-permute-start.4) | collective-permute-done | bytes 16416 | tf_op jit(solution)/shard_map/ppermute | solution.py:177
  78.0 2.5 %collective-permute-start.7 = (f32[3,16,256]{2,1,0:T(8,128)S(1)}, f32[3,16,256]{2,1,0:T(8,128)S(1)}, u32[]{:S(2)}, u32[]{:S(2)}) collective-permute-start(f32[3,16,256]{2,1,0:T(8,128)S(1)} %get-tuple-element.22), channel_id=1, source_target_pairs={{0,12},{4,8},{8,4},{12,0},{1,13},{5,9},{9,5},{13,1},{2,14},{6,10},... | collective-permute-start | bytes 147464 | tf_op jit(solution)/shard_map/ppermute | solution.py:181
  80.5 3.4 %collective-permute-start.6 = (f32[3,16,256]{2,1,0:T(8,128)S(1)}, f32[3,16,256]{2,1,0:T(8,128)S(1)}, u32[]{:S(2)}, u32[]{:S(2)}) collective-permute-start(f32[3,16,256]{2,1,0:T(8,128)S(1)} %get-tuple-element.22), channel_id=1, source_target_pairs={{0,8},{4,12},{8,0},{12,4},{1,9},{5,13},{9,1},{13,5},{2,10},{6,14},... | collective-permute-start | bytes 147464 | tf_op jit(solution)/shard_map/ppermute | solution.py:181
  83.9 4.3 %collective-permute-start.5 = (f32[3,16,256]{2,1,0:T(8,128)S(1)}, f32[3,16,256]{2,1,0:T(8,128)S(1)}, u32[]{:S(2)}, u32[]{:S(2)}) collective-permute-start(f32[3,16,256]{2,1,0:T(8,128)S(1)} %get-tuple-element.22), channel_id=1, source_target_pairs={{0,4},{4,0},{8,12},{12,8},{1,5},{5,1},{9,13},{13,9},{2,6},{6,2},{1... | collective-permute-start | bytes 147464 | tf_op jit(solution)/shard_map/ppermute | solution.py:181
  88.1 0.0 collective-permute-done.7
  88.1 0.0 collective-permute-done.6
  88.2 2.0 %collective-permute-done.5 = f32[3,16,256]{2,1,0:T(8,128)S(1)} collective-permute-done((f32[3,16,256]{2,1,0:T(8,128)S(1)}, f32[3,16,256]{2,1,0:T(8,128)S(1)}, u32[]{:S(2)}, u32[]{:S(2)}) %collective-permute-start.5) | collective-permute-done | bytes 49184 | tf_op jit(solution)/shard_map/ppermute | solution.py:181
  90.2 1.9 %collective-permute-start.8 = (f32[4,3,16,256]{3,2,1,0:T(8,128)S(1)}, f32[4,3,16,256]{3,2,1,0:T(8,128)S(1)}, u32[]{:S(2)}, u32[]{:S(2)}) collective-permute-start(f32[4,3,16,256]{3,2,1,0:T(8,128)S(1)} %pad_maximum_fusion.refs_0_), channel_id=1, source_target_pairs={{0,1},{1,0},{2,3},{3,2},{4,5},{5,4},{6,7},{7,6},{8,9},{9,8},{10,11... | collective-permute-start | bytes 589832 | tf_op jit(solution)/shard_map/ppermute | solution.py:181
  92.1 5.4 %collective-permute-start.9 = (f32[4,3,16,256]{3,2,1,0:T(8,128)S(1)}, f32[4,3,16,256]{3,2,1,0:T(8,128)S(1)}, u32[]{:S(2)}, u32[]{:S(2)}) collective-permute-start(f32[4,3,16,256]{3,2,1,0:T(8,128)S(1)} %pad_maximum_fusion.refs_0_), channel_id=1, source_target_pairs={{0,2},{1,3},{2,0},{3,1},{4,6},{5,7},{6,4},{7,5},{8,10},{9,11},{10,... | collective-permute-start | bytes 589832 | tf_op jit(solution)/shard_map/ppermute | solution.py:181
  97.6 3.1 %collective-permute-start.10 = (f32[4,3,16,256]{3,2,1,0:T(8,128)S(1)}, f32[4,3,16,256]{3,2,1,0:T(8,128)S(1)}, u32[]{:S(2)}, u32[]{:S(2)}) collective-permute-start(f32[4,3,16,256]{3,2,1,0:T(8,128)S(1)} %pad_maximum_fusion.refs_0_), channel_id=1, source_target_pairs={{0,3},{1,2},{2,1},{3,0},{4,7},{5,6},{6,5},{7,4},{8,11},{9,10},{10,... | collective-permute-start | bytes 589832 | tf_op jit(solution)/shard_map/ppermute | solution.py:181
  100.7 0.0 collective-permute-done.8.refs_1_
  100.7 0.8 collective-permute-done.9.refs_2_
  101.5 4.9 %collective-permute-done.10.refs_3_ = f32[4,3,16,256]{3,2,1,0:T(8,128)S(1)} collective-permute-done((f32[4,3,16,256]{3,2,1,0:T(8,128)S(1)}, f32[4,3,16,256]{3,2,1,0:T(8,128)S(1)}, u32[]{:S(2)}, u32[]{:S(2)}) %collective-permute-start.10) | collective-permute-done | bytes 196640 | tf_op jit(solution)/shard_map/ppermute | solution.py:181
  106.3 0.0 all-to-all-done.2.got
  106.3 1.2 shard_map.39
  107.5 8.8 %collective-permute-start.11 = (f32[3,8,256]{2,1,0:T(8,128)S(1)}, f32[3,8,256]{2,1,0:T(8,128)S(1)}, u32[]{:S(2)}, u32[]{:S(2)}) collective-permute-start(f32[3,8,256]{2,1,0:T(8,128)S(1)} %get-tuple-element.15), channel_id=1, source_target_pairs={{0,449},{1,457},{2,465},{3,473},{4,451},{5,459},{6,467},{7,475},{8... | collective-permute-start | bytes 73736 | tf_op jit(solution)/shard_map/ppermute | solution.py:209
  116.3 2.1 %collective-permute-start.12 = (f32[3,8,256]{2,1,0:T(8,128)S(1)}, f32[3,8,256]{2,1,0:T(8,128)S(1)}, u32[]{:S(2)}, u32[]{:S(2)}) collective-permute-start(f32[3,8,256]{2,1,0:T(8,128)S(1)} %get-tuple-element.16), channel_id=1, source_target_pairs={{0,448},{1,456},{2,464},{3,472},{4,450},{5,458},{6,466},{7,474},{8... | collective-permute-start | bytes 73736 | tf_op jit(solution)/shard_map/ppermute | solution.py:209
  118.4 0.0 collective-permute-done.11
  118.4 9.6 %collective-permute-done.12 = f32[3,8,256]{2,1,0:T(8,128)S(1)} collective-permute-done((f32[3,8,256]{2,1,0:T(8,128)S(1)}, f32[3,8,256]{2,1,0:T(8,128)S(1)}, u32[]{:S(2)}, u32[]{:S(2)}) %collective-permute-start.12) | collective-permute-done | bytes 24608 | tf_op jit(solution)/shard_map/ppermute | solution.py:209
  128.0 0.6 copy.6
  (14 shorter events, 0.1 us)
Async XLA Ops:
  0.0 17.3 %copy-start = (f32[2,1,1,1,256,256]{5,4,3,2,1,0:T(8,128)S(1)}, f32[2,1,1,1,256,256]{5,4,3,2,1,0:T(8,128)}, u32[]{:S(2)}) copy-start(f32[2,1,1,1,256,256]{5,4,3,2,1,0:T(8,128)} %param.3) | copy-start | bytes 1572868
  3.8 33.6 %all-to-all-start = ((f32[32,16,256]{2,1,0:T(8,128)}), f32[32,16,256]{2,1,0:T(8,128)}, u32[]{:S(2)}, u32[]{:S(2)}) async-start(f32[32,16,256]{2,1,0:T(8,128)} %bitcast.8), calls=%async_computation | async-start | bytes 1048576 | tf_op jit(solution)/shard_map/all_to_all | solution.py:164
  17.3 16.0 %collective-permute-start.1 = (f32[2,256,256]{2,1,0:T(8,128)S(1)}, f32[2,256,256]{2,1,0:T(8,128)S(1)}, u32[]{:S(2)}, u32[]{:S(2)}) collective-permute-start(f32[2,256,256]{2,1,0:T(8,128)S(1)} %bitcast.31), channel_id=1, source_target_pairs={{0,448},{64,0},{128,64},{192,128},{256,192},{320,256},{384,320},{4... | collective-permute-start | bytes 1572872 | tf_op jit(solution)/shard_map/ppermute | solution.py:140
  22.7 16.1 %collective-permute-start = (f32[2,256,256]{2,1,0:T(8,128)}, f32[2,256,256]{2,1,0:T(8,128)S(1)}, u32[]{:S(2)}, u32[]{:S(2)}) collective-permute-start(f32[2,256,256]{2,1,0:T(8,128)} %bitcast.11), channel_id=1, source_target_pairs={{0,64},{64,128},{128,192},{192,256},{256,320},{320,384},{384,448},... | collective-permute-start | bytes 1572872 | tf_op jit(solution)/shard_map/ppermute | solution.py:140
  24.6 14.2 %collective-permute-start.2 = (f32[2,256,256]{2,1,0:T(8,128)S(1)}, f32[2,256,256]{2,1,0:T(8,128)S(1)}, u32[]{:S(2)}, u32[]{:S(2)}) collective-permute-start(f32[2,256,256]{2,1,0:T(8,128)S(1)} %bitcast.32), channel_id=1, source_target_pairs={{32,0},{33,1},{34,2},{35,3},{36,4},{37,5},{38,6},{39,7},{40,8},{41... | collective-permute-start | bytes 1572872 | tf_op jit(solution)/shard_map/ppermute | solution.py:144
  33.3 5.5 %collective-permute-start.3 = (f32[2,256,256]{2,1,0:T(8,128)S(1)}, f32[2,256,256]{2,1,0:T(8,128)S(1)}, u32[]{:S(2)}, u32[]{:S(2)}) collective-permute-start(f32[2,256,256]{2,1,0:T(8,128)S(1)} %collective-permute-done.1.ahead_ref), channel_id=1, source_target_pairs={{0,32},{1,33},{2,34},{3,35},{4,36},{5,37},{6,38},{7,39},{8,40},{9,... | collective-permute-start | bytes 1572872 | tf_op jit(solution)/shard_map/ppermute | solution.py:145
  63.1 43.3 %all-to-all-start.2 = ((f32[8,3,16,256]{3,2,1,0:T(8,128)}), f32[8,3,16,256]{3,2,1,0:T(8,128)S(1)}, u32[]{:S(2)}, u32[]{:S(2)}) async-start(f32[8,3,16,256]{3,2,1,0:T(8,128)} %shard_map.38), calls=%async_computation.2 | async-start | bytes 786432 | tf_op jit(solution)/shard_map/all_to_all | solution.py:193
  69.7 8.3 %collective-permute-start.4 = (f32[16,256]{1,0:T(8,128)S(1)}, f32[16,256]{1,0:T(8,128)S(1)}, u32[]{:S(2)}, u32[]{:S(2)}) collective-permute-start(f32[16,256]{1,0:T(8,128)S(1)} %get-tuple-element.13), channel_id=1, source_target_pairs={{0,496},{1,497},{2,498},{3,499},{4,500},{5,501},{6,502},{7,503},{8... | collective-permute-start | bytes 49160 | tf_op jit(solution)/shard_map/ppermute | solution.py:177
  78.0 10.1 %collective-permute-start.7 = (f32[3,16,256]{2,1,0:T(8,128)S(1)}, f32[3,16,256]{2,1,0:T(8,128)S(1)}, u32[]{:S(2)}, u32[]{:S(2)}) collective-permute-start(f32[3,16,256]{2,1,0:T(8,128)S(1)} %get-tuple-element.22), channel_id=1, source_target_pairs={{0,12},{4,8},{8,4},{12,0},{1,13},{5,9},{9,5},{13,1},{2,14},{6,10},... | collective-permute-start | bytes 147464 | tf_op jit(solution)/shard_map/ppermute | solution.py:181
  80.5 7.7 %collective-permute-start.6 = (f32[3,16,256]{2,1,0:T(8,128)S(1)}, f32[3,16,256]{2,1,0:T(8,128)S(1)}, u32[]{:S(2)}, u32[]{:S(2)}) collective-permute-start(f32[3,16,256]{2,1,0:T(8,128)S(1)} %get-tuple-element.22), channel_id=1, source_target_pairs={{0,8},{4,12},{8,0},{12,4},{1,9},{5,13},{9,1},{13,5},{2,10},{6,14},... | collective-permute-start | bytes 147464 | tf_op jit(solution)/shard_map/ppermute | solution.py:181
  83.9 6.3 %collective-permute-start.5 = (f32[3,16,256]{2,1,0:T(8,128)S(1)}, f32[3,16,256]{2,1,0:T(8,128)S(1)}, u32[]{:S(2)}, u32[]{:S(2)}) collective-permute-start(f32[3,16,256]{2,1,0:T(8,128)S(1)} %get-tuple-element.22), channel_id=1, source_target_pairs={{0,4},{4,0},{8,12},{12,8},{1,5},{5,1},{9,13},{13,9},{2,6},{6,2},{1... | collective-permute-start | bytes 147464 | tf_op jit(solution)/shard_map/ppermute | solution.py:181
  90.2 10.5 %collective-permute-start.8 = (f32[4,3,16,256]{3,2,1,0:T(8,128)S(1)}, f32[4,3,16,256]{3,2,1,0:T(8,128)S(1)}, u32[]{:S(2)}, u32[]{:S(2)}) collective-permute-start(f32[4,3,16,256]{3,2,1,0:T(8,128)S(1)} %pad_maximum_fusion.refs_0_), channel_id=1, source_target_pairs={{0,1},{1,0},{2,3},{3,2},{4,5},{5,4},{6,7},{7,6},{8,9},{9,8},{10,11... | collective-permute-start | bytes 589832 | tf_op jit(solution)/shard_map/ppermute | solution.py:181
  92.1 9.4 %collective-permute-start.9 = (f32[4,3,16,256]{3,2,1,0:T(8,128)S(1)}, f32[4,3,16,256]{3,2,1,0:T(8,128)S(1)}, u32[]{:S(2)}, u32[]{:S(2)}) collective-permute-start(f32[4,3,16,256]{3,2,1,0:T(8,128)S(1)} %pad_maximum_fusion.refs_0_), channel_id=1, source_target_pairs={{0,2},{1,3},{2,0},{3,1},{4,6},{5,7},{6,4},{7,5},{8,10},{9,11},{10,... | collective-permute-start | bytes 589832 | tf_op jit(solution)/shard_map/ppermute | solution.py:181
  97.6 8.8 %collective-permute-start.10 = (f32[4,3,16,256]{3,2,1,0:T(8,128)S(1)}, f32[4,3,16,256]{3,2,1,0:T(8,128)S(1)}, u32[]{:S(2)}, u32[]{:S(2)}) collective-permute-start(f32[4,3,16,256]{3,2,1,0:T(8,128)S(1)} %pad_maximum_fusion.refs_0_), channel_id=1, source_target_pairs={{0,3},{1,2},{2,1},{3,0},{4,7},{5,6},{6,5},{7,4},{8,11},{9,10},{10,... | collective-permute-start | bytes 589832 | tf_op jit(solution)/shard_map/ppermute | solution.py:181
  107.5 10.9 %collective-permute-start.11 = (f32[3,8,256]{2,1,0:T(8,128)S(1)}, f32[3,8,256]{2,1,0:T(8,128)S(1)}, u32[]{:S(2)}, u32[]{:S(2)}) collective-permute-start(f32[3,8,256]{2,1,0:T(8,128)S(1)} %get-tuple-element.15), channel_id=1, source_target_pairs={{0,449},{1,457},{2,465},{3,473},{4,451},{5,459},{6,467},{7,475},{8... | collective-permute-start | bytes 73736 | tf_op jit(solution)/shard_map/ppermute | solution.py:209
  116.3 11.7 %collective-permute-start.12 = (f32[3,8,256]{2,1,0:T(8,128)S(1)}, f32[3,8,256]{2,1,0:T(8,128)S(1)}, u32[]{:S(2)}, u32[]{:S(2)}) collective-permute-start(f32[3,8,256]{2,1,0:T(8,128)S(1)} %get-tuple-element.16), channel_id=1, source_target_pairs={{0,448},{1,456},{2,464},{3,472},{4,450},{5,458},{6,466},{7,474},{8... | collective-permute-start | bytes 73736 | tf_op jit(solution)/shard_map/ppermute | solution.py:209

commit v4 on v3

--- a/solution.py
+++ b/solution.py
@@ -35,11 +35,25 @@
     return dot(a[0], b[0]) + (dot(a[0], b[1]) + dot(a[1], b[0]))
 
 
-def product_kernel(tile_count, factor, place, left_ref, home_ref, ahead_ref, beside0_ref, beside1_ref, row_codes, col_codes, out):
+def codes_of(codes, tile):
+    return codes[pl.ds(jnp.clip(tile, 0, codes.shape[0] - 1), 1), :].astype(F32)
+
+
+def down(values):
+    size = values.shape[1]
+    return jnp.broadcast_to(values, (size, size)).T
+
+
+def masked(tile, total, gap):
+    return jnp.where(((total == 3.0) | (total == 5.0)) & (gap > 3), tile, 0.0)
+
+
+def product_kernel(factor, place, left_ref, home_ref, ahead_ref, beside0_ref, beside1_ref, codes, out):
     row, col, core = place[0], place[1], place[3]
     slots, size = left_ref.shape[0], left_ref.shape[1]
-    rows_count = tile_count // slots
+    rows_count = codes.shape[0] // slots
     block = size // out.shape[0]
+    col_codes = codes_of(codes, col)
     gap = lax.broadcasted_iota(jnp.int32, (size, size), 1) - lax.broadcasted_iota(jnp.int32, (size, size), 0)
     for slot in range(slots):
         other = slots - 1 - slot
@@ -57,9 +71,8 @@
                 tile = jnp.where(core == 0, beside0_ref[slot], after)
             else:
                 tile = home_ref[slot]
-            total = row_codes[number, slot] + col_codes[...]
-            allowed = ((total == 3) | (total == 5)) & (gap + (col - tile_row - e) * size > 3)
-            right = halves(jnp.where(allowed, tile, 0.0))
+            total = down(codes_of(codes, tile_row + e)) + col_codes
+            right = halves(masked(tile, total, gap + (col - tile_row - e) * size))
             own = jnp.where((tile_row >= 0) & (col == tile_row + e), 1.0, 0.0).astype(F32)
             full = scale * times(left_halves, right) + own * left
             for x in range(out.shape[0]):
@@ -77,6 +90,21 @@
                 total = total + got[k, number, slot]
             for z in range(deep):
                 out[slot * deep + z, number] = total[z * piece:(z + 1) * piece]
+
+
+def pack_kernel(wide, place, codes, *refs):
+    bits, out, columns = refs[:-2], refs[-2], refs[-1]
+    row, half, x, zl = place[0], place[2], place[4], place[5]
+    part, size = out.shape[2:]
+    first = row + half * (codes.shape[0] // 2)
+    for k, (at, beyond) in enumerate(((0, 1), (0, 2), (1, 1))):
+        columns[...] = down(codes_of(codes, first + at))
+        lanes = codes_of(codes, first + at + beyond)
+        for i, ref in enumerate(bits):
+            start = pl.multiple_of(((zl ^ i) * wide + x) * part, part)
+            total = columns[pl.ds(start, part), :] + lanes
+            steps = lax.broadcasted_iota(jnp.int32, (part, size), 1) - lax.broadcasted_iota(jnp.int32, (part, size), 0)
+            out[i, k] = masked(ref[k], total, steps - start + beyond * size)
 
 
 def finish_kernel(factor, place, got, *refs):
@@ -144,29 +172,14 @@
     beside0 = lax.ppermute(home, "core", [(1, 0)])
     beside1 = lax.ppermute(ahead, "core", [(0, 1)])
 
-    slot = jnp.arange(slots, dtype=jnp.int32)
     codes = sequence.reshape(tile_count, size)
-    offsets = jnp.arange(size, dtype=jnp.int32)
-    col_codes = lax.dynamic_index_in_dim(codes, col, 0, True)
-    col_pos = col * size + offsets
-    wanted = slot[None, :] * rows_count + row + (WIN - 1) - jnp.arange(WIN, dtype=jnp.int32)[:, None]
-    row_codes = jnp.take(codes, jnp.clip(wanted, 0, tile_count - 1), axis=0)
-
-    gap = col - row
-    early = (gap == 1) | (gap == 2)
-    near_row = jnp.where(early, row, rows_count + row)
-    near_codes = jnp.where(early, row_codes[WIN - 1, 0], row_codes[WIN - 1, 1])
-    total = near_codes[:, None] + col_codes
-    far = col_pos[None, :] - (near_row * size + offsets)[:, None] > 3
-    near = jnp.where(((total == 3) | (total == 5)) & far, jnp.where(early, home[0], home[1]), 0.0)
-    near = near.reshape(1, size // part, part, size)
-    spread = jnp.broadcast_to(near, (slots,) + near.shape[1:]).reshape(cols_count, part, size)
+
+    spread, beside0 = lax.optimization_barrier((home.reshape(cols_count, part, size), beside0))
     spread = lax.all_to_all(spread, AXES[2:], 0, 0)
     first = jnp.minimum(row + half * rows_count + 1, cols_count - 1)
     second = jnp.minimum(row + half * rows_count + 2, cols_count - 1)
     near1 = lax.dynamic_index_in_dim(spread, first, 0, False)
     near2 = lax.dynamic_index_in_dim(spread, second, 0, False)
-    near1, near2, left, ahead = lax.optimization_barrier((near1, near2, left, ahead))
 
     def previous_row(y, c, zh, zl, x):
         r = y * sizes[1] + c
@@ -180,15 +193,21 @@
     def partners(v, axis, n):
         return [v] + [lax.ppermute(v, axis, [(i, i ^ j) for i in range(n)]) for j in range(1, n)]
 
-    packs = partners(jnp.stack(partners(bits, "zl", sizes[3])), "x", sizes[4])
+    (pack,) = call(
+        functools.partial(pack_kernel, sizes[4]),
+        1, [(sizes[3], 3, part, size)], [pltpu.VMEM((size, size), F32)], 10**6,
+        place, codes, *partners(bits, "zl", sizes[3]),
+    )
 
     wide = (sizes[4], WIN, slots, size // sizes[4], size)
     (parts,) = call(
-        functools.partial(product_kernel, tile_count, factor),
+        functools.partial(product_kernel, factor),
         1, [wide], [], WIN * slots * 6 * size**3,
-        place, left, home, ahead, beside0, beside1, row_codes[..., None], col_codes,
+        place, left, home, ahead, beside0, beside1, codes,
     )
     parts = lax.all_to_all(parts, "x", 0, 0)
+    parts, pack = lax.optimization_barrier((parts, pack))
+    packs = partners(pack, "x", sizes[4])
     (ready,) = call(add_kernel, 0, [(slots * sizes[3], WIN, part, size)], [], 10**6, parts)
     got = lax.all_to_all(ready, ("zh", "zl"), 0, 0)
     piece = part // slots

time: 129 us -> 112 us (0.87)
  blocking collectives: 21.5 us -> 0 us
  waiting for transfers between devices: 26.7 us -> 32.4 us
  local copies, waits for them, and re-layouts: 5.33 us -> 2.53 us
  other arithmetic: 2.7 us -> 0.02 us
  starting transfers between devices: 68.2 us -> 70.6 us
  Pallas kernels: 3.91 us -> 5.76 us
    all_to_all x1 -> x0, blocking collectives: 21.5 us -> none  [on_device(): parts = lax.all_to_all(parts, 'x', 0, 0)]
    all_to_all x0 -> x1, starting transfers between devices: none -> 4.8 us  [on_device(): parts = lax.all_to_all(parts, 'x', 0, 0)]
    ppermute x2, waiting for transfers between devices: 7.97 us -> 12.4 us  [row_shift(): return lax.ppermute(v, 'y', [(i, (i + by) % n) for i in range(n)])]
    select_n x6 -> x0, other arithmetic: 2.62 us -> none  [the longest x3 1.34 us: on_device(): row_codes = jnp.take(codes, jnp.clip(wanted, 0, tile_count - 1), axis=0)]
    all_to_all x1, starting transfers between devices: 6.65 us -> 4.57 us  [on_device(): got = lax.all_to_all(ready, ('zh', 'zl'), 0, 0)]
    gather x3 -> x0, local copies, waits for them, and re-layouts: 2.08 us -> none  [on_device(): row_codes = jnp.take(codes, jnp.clip(wanted, 0, tile_count - 1), axis=0)]
    pallas_call x3 -> x4, Pallas kernels: 3.91 us -> 5.76 us  [call(): pl.pallas_call(kernel, out_shape=[jax.ShapeDtypeStruct(s, F32) for s in o...]
    ppermute x1, starting transfers between devices: 6.83 us -> 5.4 us  [on_device(): next1 = lax.ppermute(near1, AXES, pairs_of(sizes, previous_row))]
  transfers between devices with their start and end apart: 15 -> 16, of which waited for: 7 -> 6; matrix products, arithmetic and copies ran while one was open for 3% -> 1% of each run, Pallas kernels for 0% -> 3%
where the time goes in v4:
time: 112 us
  starting transfers between devices  70.6 us (63%)
  waiting for transfers between devices  32.4 us (29%)
  Pallas kernels  5.76 us (5%)
  local copies, waits for them, and re-layouts  2.53 us (2%)
    ppermute x6, starting transfers between devices, partners(): lax.ppermute(v, axis, [(i, i ^ j) for i in range(n)])  20.5 us
    all_to_all x1, starting transfers between devices, on_device(): spread = lax.all_to_all(spread, AXES[2:], 0, 0)  13.4 us
    ppermute x2, waiting for transfers between devices, row_shift(): return lax.ppermute(v, 'y', [(i, (i + by) % n) for i in range(n)])  12.4 us
    ppermute x2, starting transfers between devices, on_device(): lax.ppermute(sent[flip], AXES, pairs_of(sizes, sent_to(flip)))  11.1 us
    ppermute x2, waiting for transfers between devices, on_device(): lax.ppermute(sent[flip], AXES, pairs_of(sizes, sent_to(flip)))  9.78 us
    ppermute x6, waiting for transfers between devices, partners(): lax.ppermute(v, axis, [(i, i ^ j) for i in range(n)])  8.86 us
    ppermute x2, starting transfers between devices, row_shift(): return lax.ppermute(v, 'y', [(i, (i + by) % n) for i in range(n)])  7.3 us
    pallas_call x4, Pallas kernels, call(): pl.pallas_call(kernel, out_shape=[jax.ShapeDtypeStruct(s, F32) for s in o...  5.76 us
  transfers between devices with their start and end apart: 16, of which 6 were waited for; matrix products, arithmetic and copies ran while one was open for 1% of the time, Pallas kernels for 3%

profile of v4, /device:TPU:6, one launch (start us, length us, event | category | flops | bytes accessed | tf_op | source)
XLA Modules:
  0.0 111.6 jit_solution(1906363762903190012)
XLA Ops:
  0.0 1.3 %collective-permute-start.2 = (f32[2,256,256]{2,1,0:T(8,128)}, f32[2,256,256]{2,1,0:T(8,128)S(1)}, u32[]{:S(2)}, u32[]{:S(2)}) collective-permute-start(f32[2,256,256]{2,1,0:T(8,128)} %bitcast.17), channel_id=1, source_target_pairs={{32,0},{33,1},{34,2},{35,3},{36,4},{37,5},{38,6},{39,7},{40,8},{41... | collective-permute-start | bytes 1572872 | tf_op jit(solution)/shard_map/ppermute | solution.py:172
  1.3 5.4 %collective-permute-start.1 = (f32[2,256,256]{2,1,0:T(8,128)}, f32[2,256,256]{2,1,0:T(8,128)S(1)}, u32[]{:S(2)}, u32[]{:S(2)}) collective-permute-start(f32[2,256,256]{2,1,0:T(8,128)} %bitcast.18), channel_id=1, source_target_pairs={{0,448},{64,0},{128,64},{192,128},{256,192},{320,256},{384,320},{4... | collective-permute-start | bytes 1572872 | tf_op jit(solution)/shard_map/ppermute | solution.py:168
  6.7 0.0 collective-permute-done.2.beside0_ref
  6.7 13.4 %all-to-all-start.1 = ((f32[32,16,256]{2,1,0:T(8,128)}), f32[32,16,256]{2,1,0:T(8,128)S(1)}, u32[]{:S(2)}, u32[]{:S(2)}) async-start(f32[32,16,256]{2,1,0:T(8,128)} %bitcast.19), calls=%async_computation.1 | async-start | bytes 1048576 | tf_op jit(solution)/shard_map/all_to_all | solution.py:178
  20.1 1.9 %collective-permute-start = (f32[2,256,256]{2,1,0:T(8,128)}, f32[2,256,256]{2,1,0:T(8,128)S(1)}, u32[]{:S(2)}, u32[]{:S(2)}) collective-permute-start(f32[2,256,256]{2,1,0:T(8,128)} %bitcast.23), channel_id=1, source_target_pairs={{0,64},{64,128},{128,192},{192,256},{256,320},{320,384},{384,448},... | collective-permute-start | bytes 1572872 | tf_op jit(solution)/shard_map/ppermute | solution.py:168
  22.0 0.0 collective-permute-done.1.ahead_ref
  22.1 2.3 %collective-permute-start.3 = (f32[2,256,256]{2,1,0:T(8,128)S(1)}, f32[2,256,256]{2,1,0:T(8,128)S(1)}, u32[]{:S(2)}, u32[]{:S(2)}) collective-permute-start(f32[2,256,256]{2,1,0:T(8,128)S(1)} %collective-permute-done.1.ahead_ref), channel_id=1, source_target_pairs={{0,32},{1,33},{2,34},{3,35},{4,36},{5,37},{6,38},{7,39},{8,40},{9,... | collective-permute-start | bytes 1572872 | tf_op jit(solution)/shard_map/ppermute | solution.py:173
  24.3 0.8 reshape.3.codes
  25.1 0.1 stack.44.place
  25.2 12.4 %collective-permute-done.left_ref = f32[2,256,256]{2,1,0:T(8,128)S(1)} collective-permute-done((f32[2,256,256]{2,1,0:T(8,128)}, f32[2,256,256]{2,1,0:T(8,128)S(1)}, u32[]{:S(2)}, u32[]{:S(2)}) %collective-permute-start) | collective-permute-done | bytes 524320 | tf_op jit(solution)/shard_map/ppermute | solution.py:168
  37.6 0.0 collective-permute-done.3.beside1_ref
  37.6 0.0 copy-start
  37.6 1.0 copy-done
  38.6 3.0 %shard_map.37 = f32[4,3,2,64,256]{4,3,2,1,0:T(8,128)} custom-call(s32[6]{0:T(128)S(1)} %stack.44.place, f32[2,256,256]{2,1,0:T(8,128)S(1)} %collective-permute-done.left_ref, f32[2,256,256]{2,1,0:T(8,128)S(1)} %bitcast.20, f32[2,256,256]{2,1,0:T(8,128)S(1)} %collective-permute-done.1.ahead_ref, f32[2,256,256]{2,1,0:T(8,128)S(1)} %collective-permute-done.2.beside0_ref, ...), custom_call_target="tpu_custom_call" | custom-call | flops 603979776 | bytes 4227096 | tf_op jit(solution)/shard_map/pallas_call | solution.py:139
  41.7 0.0 all-to-all-done.1
  41.7 4.8 %all-to-all-start = ((f32[4,3,2,64,256]{4,3,2,1,0:T(8,128)}), f32[4,3,2,64,256]{4,3,2,1,0:T(8,128)S(1)}, u32[]{:S(2)}, u32[]{:S(2)}) async-start(f32[4,3,2,64,256]{4,3,2,1,0:T(8,128)} %shard_map.37), calls=%async_computation | async-start | bytes 3145728 | tf_op jit(solution)/shard_map/all_to_all | solution.py:208
  46.5 5.4 %collective-permute-start.4 = (f32[16,256]{1,0:T(8,128)S(1)}, f32[16,256]{1,0:T(8,128)S(1)}, u32[]{:S(2)}, u32[]{:S(2)}) collective-permute-start(f32[16,256]{1,0:T(8,128)S(1)} %bitcast.21), channel_id=1, source_target_pairs={{0,496},{1,497},{2,498},{3,499},{4,500},{5,501},{6,502},{7,503},{8... | collective-permute-start | bytes 49160 | tf_op jit(solution)/shard_map/ppermute | solution.py:190
  51.9 1.4 %collective-permute-done.4 = f32[16,256]{1,0:T(8,128)S(1)} collective-permute-done((f32[16,256]{1,0:T(8,128)S(1)}, f32[16,256]{1,0:T(8,128)S(1)}, u32[]{:S(2)}, u32[]{:S(2)}) %collective-permute-start.4) | collective-permute-done | bytes 16416 | tf_op jit(solution)/shard_map/ppermute | solution.py:190
  53.3 2.5 %collective-permute-start.5 = (f32[3,16,256]{2,1,0:T(8,128)S(1)}, f32[3,16,256]{2,1,0:T(8,128)S(1)}, u32[]{:S(2)}, u32[]{:S(2)}) collective-permute-start(f32[3,16,256]{2,1,0:T(8,128)S(1)} %pad_maximum_fusion.refs_0_), channel_id=1, source_target_pairs={{0,4},{4,0},{8,12},{12,8},{1,5},{5,1},{9,13},{13,9},{2,6},{6,2},{1... | collective-permute-start | bytes 147464 | tf_op jit(solution)/shard_map/ppermute | solution.py:194
  55.8 2.5 %collective-permute-start.6 = (f32[3,16,256]{2,1,0:T(8,128)S(1)}, f32[3,16,256]{2,1,0:T(8,128)S(1)}, u32[]{:S(2)}, u32[]{:S(2)}) collective-permute-start(f32[3,16,256]{2,1,0:T(8,128)S(1)} %pad_maximum_fusion.refs_0_), channel_id=1, source_target_pairs={{0,8},{4,12},{8,0},{12,4},{1,9},{5,13},{9,1},{13,5},{2,10},{6,14},... | collective-permute-start | bytes 147464 | tf_op jit(solution)/shard_map/ppermute | solution.py:194
  58.3 5.1 %collective-permute-start.7 = (f32[3,16,256]{2,1,0:T(8,128)S(1)}, f32[3,16,256]{2,1,0:T(8,128)S(1)}, u32[]{:S(2)}, u32[]{:S(2)}) collective-permute-start(f32[3,16,256]{2,1,0:T(8,128)S(1)} %pad_maximum_fusion.refs_0_), channel_id=1, source_target_pairs={{0,12},{4,8},{8,4},{12,0},{1,13},{5,9},{9,5},{13,1},{2,14},{6,10},... | collective-permute-start | bytes 147464 | tf_op jit(solution)/shard_map/ppermute | solution.py:194
  63.4 0.0 collective-permute-done.5.refs_1_
  63.4 0.0 collective-permute-done.6.refs_2_
  63.4 2.7 %collective-permute-done.7.refs_3_ = f32[3,16,256]{2,1,0:T(8,128)S(1)} collective-permute-done((f32[3,16,256]{2,1,0:T(8,128)S(1)}, f32[3,16,256]{2,1,0:T(8,128)S(1)}, u32[]{:S(2)}, u32[]{:S(2)}) %collective-permute-start.7) | collective-permute-done | bytes 49184 | tf_op jit(solution)/shard_map/ppermute | solution.py:194
  66.1 0.7 shard_map.38.refs_0_
  66.9 0.0 all-to-all-done.got
  66.9 0.8 shard_map.39
  67.7 4.6 %all-to-all-start.2 = ((f32[8,3,16,256]{3,2,1,0:T(8,128)}), f32[8,3,16,256]{3,2,1,0:T(8,128)S(1)}, u32[]{:S(2)}, u32[]{:S(2)}) async-start(f32[8,3,16,256]{3,2,1,0:T(8,128)} %shard_map.39), calls=%async_computation.2 | async-start | bytes 786432 | tf_op jit(solution)/shard_map/all_to_all | solution.py:212
  72.3 2.6 %collective-permute-start.8 = (f32[4,3,16,256]{3,2,1,0:T(8,128)S(1)}, f32[4,3,16,256]{3,2,1,0:T(8,128)S(1)}, u32[]{:S(2)}, u32[]{:S(2)}) collective-permute-start(f32[4,3,16,256]{3,2,1,0:T(8,128)S(1)} %shard_map.38.refs_0_), channel_id=1, source_target_pairs={{0,1},{1,0},{2,3},{3,2},{4,5},{5,4},{6,7},{7,6},{8,9},{9,8},{10,11... | collective-permute-start | bytes 589832 | tf_op jit(solution)/shard_map/ppermute | solution.py:194
  74.9 4.7 %collective-permute-start.9 = (f32[4,3,16,256]{3,2,1,0:T(8,128)S(1)}, f32[4,3,16,256]{3,2,1,0:T(8,128)S(1)}, u32[]{:S(2)}, u32[]{:S(2)}) collective-permute-start(f32[4,3,16,256]{3,2,1,0:T(8,128)S(1)} %shard_map.38.refs_0_), channel_id=1, source_target_pairs={{0,2},{1,3},{2,0},{3,1},{4,6},{5,7},{6,4},{7,5},{8,10},{9,11},{10,... | collective-permute-start | bytes 589832 | tf_op jit(solution)/shard_map/ppermute | solution.py:194
  79.6 3.1 %collective-permute-start.10 = (f32[4,3,16,256]{3,2,1,0:T(8,128)S(1)}, f32[4,3,16,256]{3,2,1,0:T(8,128)S(1)}, u32[]{:S(2)}, u32[]{:S(2)}) collective-permute-start(f32[4,3,16,256]{3,2,1,0:T(8,128)S(1)} %shard_map.38.refs_0_), channel_id=1, source_target_pairs={{0,3},{1,2},{2,1},{3,0},{4,7},{5,6},{6,5},{7,4},{8,11},{9,10},{10,... | collective-permute-start | bytes 589832 | tf_op jit(solution)/shard_map/ppermute | solution.py:194
  82.7 0.0 collective-permute-done.8.refs_1_
  82.7 2.1 %collective-permute-done.9.refs_2_ = f32[4,3,16,256]{3,2,1,0:T(8,128)S(1)} collective-permute-done((f32[4,3,16,256]{3,2,1,0:T(8,128)S(1)}, f32[4,3,16,256]{3,2,1,0:T(8,128)S(1)}, u32[]{:S(2)}, u32[]{:S(2)}) %collective-permute-start.9) | collective-permute-done | bytes 196640 | tf_op jit(solution)/shard_map/ppermute | solution.py:194
  84.8 4.1 %collective-permute-done.10.refs_3_ = f32[4,3,16,256]{3,2,1,0:T(8,128)S(1)} collective-permute-done((f32[4,3,16,256]{3,2,1,0:T(8,128)S(1)}, f32[4,3,16,256]{3,2,1,0:T(8,128)S(1)}, u32[]{:S(2)}, u32[]{:S(2)}) %collective-permute-start.10) | collective-permute-done | bytes 196640 | tf_op jit(solution)/shard_map/ppermute | solution.py:194
  88.9 0.0 all-to-all-done.2.got
  88.9 1.2 %shard_map.40 = (f32[3,8,256]{2,1,0:T(8,128)S(1)}, f32[3,8,256]{2,1,0:T(8,128)S(1)}) custom-call(s32[6]{0:T(128)S(1)} %stack.44.place, f32[8,3,16,256]{3,2,1,0:T(8,128)S(1)} %all-to-all-done.2.got, f32[4,3,16,256]{3,2,1,0:T(8,128)S(1)} %shard_map.38.refs_0_, f32[4,3,16,256]{3,2,1,0:T(8,128)S(1)} %collective-permute-done.8.refs_1_, ...), custom_call_target="tpu_custom_call" | custom-call | flops 18874368 | bytes 1228824 | tf_op jit(solution)/shard_map/pallas_call | solution.py:139
  90.1 9.1 %collective-permute-start.11 = (f32[3,8,256]{2,1,0:T(8,128)S(1)}, f32[3,8,256]{2,1,0:T(8,128)S(1)}, u32[]{:S(2)}, u32[]{:S(2)}) collective-permute-start(f32[3,8,256]{2,1,0:T(8,128)S(1)} %get-tuple-element.15), channel_id=1, source_target_pairs={{0,449},{1,457},{2,465},{3,473},{4,451},{5,459},{6,467},{7,475},{8... | collective-permute-start | bytes 73736 | tf_op jit(solution)/shard_map/ppermute | solution.py:228
  99.2 1.9 %collective-permute-start.12 = (f32[3,8,256]{2,1,0:T(8,128)S(1)}, f32[3,8,256]{2,1,0:T(8,128)S(1)}, u32[]{:S(2)}, u32[]{:S(2)}) collective-permute-start(f32[3,8,256]{2,1,0:T(8,128)S(1)} %get-tuple-element.16), channel_id=1, source_target_pairs={{0,448},{1,456},{2,464},{3,472},{4,450},{5,458},{6,466},{7,474},{8... | collective-permute-start | bytes 73736 | tf_op jit(solution)/shard_map/ppermute | solution.py:228
  101.2 0.0 collective-permute-done.11
  101.2 9.8 %collective-permute-done.12 = f32[3,8,256]{2,1,0:T(8,128)S(1)} collective-permute-done((f32[3,8,256]{2,1,0:T(8,128)S(1)}, f32[3,8,256]{2,1,0:T(8,128)S(1)}, u32[]{:S(2)}, u32[]{:S(2)}) %collective-permute-start.12) | collective-permute-done | bytes 24608 | tf_op jit(solution)/shard_map/ppermute | solution.py:228
  111.0 0.6 copy.4
  (4 shorter events, 0.0 us)
Async XLA Ops:
  0.0 6.7 %collective-permute-start.2 = (f32[2,256,256]{2,1,0:T(8,128)}, f32[2,256,256]{2,1,0:T(8,128)S(1)}, u32[]{:S(2)}, u32[]{:S(2)}) collective-permute-start(f32[2,256,256]{2,1,0:T(8,128)} %bitcast.17), channel_id=1, source_target_pairs={{32,0},{33,1},{34,2},{35,3},{36,4},{37,5},{38,6},{39,7},{40,8},{41... | collective-permute-start | bytes 1572872 | tf_op jit(solution)/shard_map/ppermute | solution.py:172
  1.3 20.8 %collective-permute-start.1 = (f32[2,256,256]{2,1,0:T(8,128)}, f32[2,256,256]{2,1,0:T(8,128)S(1)}, u32[]{:S(2)}, u32[]{:S(2)}) collective-permute-start(f32[2,256,256]{2,1,0:T(8,128)} %bitcast.18), channel_id=1, source_target_pairs={{0,448},{64,0},{128,64},{192,128},{256,192},{320,256},{384,320},{4... | collective-permute-start | bytes 1572872 | tf_op jit(solution)/shard_map/ppermute | solution.py:168
  6.7 35.0 %all-to-all-start.1 = ((f32[32,16,256]{2,1,0:T(8,128)}), f32[32,16,256]{2,1,0:T(8,128)S(1)}, u32[]{:S(2)}, u32[]{:S(2)}) async-start(f32[32,16,256]{2,1,0:T(8,128)} %bitcast.19), calls=%async_computation.1 | async-start | bytes 1048576 | tf_op jit(solution)/shard_map/all_to_all | solution.py:178
  20.1 17.5 %collective-permute-start = (f32[2,256,256]{2,1,0:T(8,128)}, f32[2,256,256]{2,1,0:T(8,128)S(1)}, u32[]{:S(2)}, u32[]{:S(2)}) collective-permute-start(f32[2,256,256]{2,1,0:T(8,128)} %bitcast.23), channel_id=1, source_target_pairs={{0,64},{64,128},{128,192},{192,256},{256,320},{320,384},{384,448},... | collective-permute-start | bytes 1572872 | tf_op jit(solution)/shard_map/ppermute | solution.py:168
  22.1 15.5 %collective-permute-start.3 = (f32[2,256,256]{2,1,0:T(8,128)S(1)}, f32[2,256,256]{2,1,0:T(8,128)S(1)}, u32[]{:S(2)}, u32[]{:S(2)}) collective-permute-start(f32[2,256,256]{2,1,0:T(8,128)S(1)} %collective-permute-done.1.ahead_ref), channel_id=1, source_target_pairs={{0,32},{1,33},{2,34},{3,35},{4,36},{5,37},{6,38},{7,39},{8,40},{9,... | collective-permute-start | bytes 1572872 | tf_op jit(solution)/shard_map/ppermute | solution.py:173
  37.6 1.0 copy-start
  41.7 25.2 %all-to-all-start = ((f32[4,3,2,64,256]{4,3,2,1,0:T(8,128)}), f32[4,3,2,64,256]{4,3,2,1,0:T(8,128)S(1)}, u32[]{:S(2)}, u32[]{:S(2)}) async-start(f32[4,3,2,64,256]{4,3,2,1,0:T(8,128)} %shard_map.37), calls=%async_computation | async-start | bytes 3145728 | tf_op jit(solution)/shard_map/all_to_all | solution.py:208
  46.5 6.8 %collective-permute-start.4 = (f32[16,256]{1,0:T(8,128)S(1)}, f32[16,256]{1,0:T(8,128)S(1)}, u32[]{:S(2)}, u32[]{:S(2)}) collective-permute-start(f32[16,256]{1,0:T(8,128)S(1)} %bitcast.21), channel_id=1, source_target_pairs={{0,496},{1,497},{2,498},{3,499},{4,500},{5,501},{6,502},{7,503},{8... | collective-permute-start | bytes 49160 | tf_op jit(solution)/shard_map/ppermute | solution.py:190
  53.3 10.1 %collective-permute-start.5 = (f32[3,16,256]{2,1,0:T(8,128)S(1)}, f32[3,16,256]{2,1,0:T(8,128)S(1)}, u32[]{:S(2)}, u32[]{:S(2)}) collective-permute-start(f32[3,16,256]{2,1,0:T(8,128)S(1)} %pad_maximum_fusion.refs_0_), channel_id=1, source_target_pairs={{0,4},{4,0},{8,12},{12,8},{1,5},{5,1},{9,13},{13,9},{2,6},{6,2},{1... | collective-permute-start | bytes 147464 | tf_op jit(solution)/shard_map/ppermute | solution.py:194
  55.8 7.6 %collective-permute-start.6 = (f32[3,16,256]{2,1,0:T(8,128)S(1)}, f32[3,16,256]{2,1,0:T(8,128)S(1)}, u32[]{:S(2)}, u32[]{:S(2)}) collective-permute-start(f32[3,16,256]{2,1,0:T(8,128)S(1)} %pad_maximum_fusion.refs_0_), channel_id=1, source_target_pairs={{0,8},{4,12},{8,0},{12,4},{1,9},{5,13},{9,1},{13,5},{2,10},{6,14},... | collective-permute-start | bytes 147464 | tf_op jit(solution)/shard_map/ppermute | solution.py:194
  58.3 7.8 %collective-permute-start.7 = (f32[3,16,256]{2,1,0:T(8,128)S(1)}, f32[3,16,256]{2,1,0:T(8,128)S(1)}, u32[]{:S(2)}, u32[]{:S(2)}) collective-permute-start(f32[3,16,256]{2,1,0:T(8,128)S(1)} %pad_maximum_fusion.refs_0_), channel_id=1, source_target_pairs={{0,12},{4,8},{8,4},{12,0},{1,13},{5,9},{9,5},{13,1},{2,14},{6,10},... | collective-permute-start | bytes 147464 | tf_op jit(solution)/shard_map/ppermute | solution.py:194
  67.7 21.2 %all-to-all-start.2 = ((f32[8,3,16,256]{3,2,1,0:T(8,128)}), f32[8,3,16,256]{3,2,1,0:T(8,128)S(1)}, u32[]{:S(2)}, u32[]{:S(2)}) async-start(f32[8,3,16,256]{3,2,1,0:T(8,128)} %shard_map.39), calls=%async_computation.2 | async-start | bytes 786432 | tf_op jit(solution)/shard_map/all_to_all | solution.py:212
  72.3 10.4 %collective-permute-start.8 = (f32[4,3,16,256]{3,2,1,0:T(8,128)S(1)}, f32[4,3,16,256]{3,2,1,0:T(8,128)S(1)}, u32[]{:S(2)}, u32[]{:S(2)}) collective-permute-start(f32[4,3,16,256]{3,2,1,0:T(8,128)S(1)} %shard_map.38.refs_0_), channel_id=1, source_target_pairs={{0,1},{1,0},{2,3},{3,2},{4,5},{5,4},{6,7},{7,6},{8,9},{9,8},{10,11... | collective-permute-start | bytes 589832 | tf_op jit(solution)/shard_map/ppermute | solution.py:194
  74.9 9.9 %collective-permute-start.9 = (f32[4,3,16,256]{3,2,1,0:T(8,128)S(1)}, f32[4,3,16,256]{3,2,1,0:T(8,128)S(1)}, u32[]{:S(2)}, u32[]{:S(2)}) collective-permute-start(f32[4,3,16,256]{3,2,1,0:T(8,128)S(1)} %shard_map.38.refs_0_), channel_id=1, source_target_pairs={{0,2},{1,3},{2,0},{3,1},{4,6},{5,7},{6,4},{7,5},{8,10},{9,11},{10,... | collective-permute-start | bytes 589832 | tf_op jit(solution)/shard_map/ppermute | solution.py:194
  79.6 9.3 %collective-permute-start.10 = (f32[4,3,16,256]{3,2,1,0:T(8,128)S(1)}, f32[4,3,16,256]{3,2,1,0:T(8,128)S(1)}, u32[]{:S(2)}, u32[]{:S(2)}) collective-permute-start(f32[4,3,16,256]{3,2,1,0:T(8,128)S(1)} %shard_map.38.refs_0_), channel_id=1, source_target_pairs={{0,3},{1,2},{2,1},{3,0},{4,7},{5,6},{6,5},{7,4},{8,11},{9,10},{10,... | collective-permute-start | bytes 589832 | tf_op jit(solution)/shard_map/ppermute | solution.py:194
  90.1 11.1 %collective-permute-start.11 = (f32[3,8,256]{2,1,0:T(8,128)S(1)}, f32[3,8,256]{2,1,0:T(8,128)S(1)}, u32[]{:S(2)}, u32[]{:S(2)}) collective-permute-start(f32[3,8,256]{2,1,0:T(8,128)S(1)} %get-tuple-element.15), channel_id=1, source_target_pairs={{0,449},{1,457},{2,465},{3,473},{4,451},{5,459},{6,467},{7,475},{8... | collective-permute-start | bytes 73736 | tf_op jit(solution)/shard_map/ppermute | solution.py:228
  99.2 11.7 %collective-permute-start.12 = (f32[3,8,256]{2,1,0:T(8,128)S(1)}, f32[3,8,256]{2,1,0:T(8,128)S(1)}, u32[]{:S(2)}, u32[]{:S(2)}) collective-permute-start(f32[3,8,256]{2,1,0:T(8,128)S(1)} %get-tuple-element.16), channel_id=1, source_target_pairs={{0,448},{1,456},{2,464},{3,472},{4,450},{5,458},{6,466},{7,474},{8... | collective-permute-start | bytes 73736 | tf_op jit(solution)/shard_map/ppermute | solution.py:228

commit v5 on v4

--- a/solution.py
+++ b/solution.py
@@ -36,47 +36,51 @@
 
 
 def codes_of(codes, tile):
-    return codes[pl.ds(jnp.clip(tile, 0, codes.shape[0] - 1), 1), :].astype(F32)
-
-
-def down(values):
-    size = values.shape[1]
-    return jnp.broadcast_to(values, (size, size)).T
+    return codes[pl.ds(jnp.clip(tile, 0, codes.shape[0] - 1), 1), :]
+
+
+def columns_of(codes, tiles):
+    total = codes_of(codes, tiles[0])
+    for k, tile in enumerate(tiles[1:], 1):
+        total = total + (codes_of(codes, tile) << (2 * k))
+    size = codes.shape[1]
+    return jnp.broadcast_to(total, (size, size)).T
 
 
 def masked(tile, total, gap):
-    return jnp.where(((total == 3.0) | (total == 5.0)) & (gap > 3), tile, 0.0)
-
-
-def product_kernel(factor, place, left_ref, home_ref, ahead_ref, beside0_ref, beside1_ref, codes, out):
+    return jnp.where(((total == 3) | (total == 5)) & (gap > 3), tile, 0.0)
+
+
+def product_kernel(factor, place, left_ref, ahead_ref, beside0_ref, beside1_ref, codes, home_ref, out):
     row, col, core = place[0], place[1], place[3]
     slots, size = left_ref.shape[0], left_ref.shape[1]
     rows_count = codes.shape[0] // slots
     block = size // out.shape[0]
     col_codes = codes_of(codes, col)
+    tile_rows = [slot * rows_count + row - 2 for slot in range(slots)]
+    keys = [(slot, e) for e in (4, 3, 2) for slot in range(slots)]
+    columns = columns_of(codes, [tile_rows[slot] + e for slot, e in keys])
     gap = lax.broadcasted_iota(jnp.int32, (size, size), 1) - lax.broadcasted_iota(jnp.int32, (size, size), 0)
-    for slot in range(slots):
+    lefts = [left_ref[jnp.where(row < 2, 0, slot)] for slot in range(slots)]
+    left_halves = [halves(left) for left in lefts]
+    for k, (slot, e) in enumerate(keys):
+        tile_row = tile_rows[slot]
         other = slots - 1 - slot
-        tile_row = slot * rows_count + row - 2
-        left = left_ref[jnp.where(row < 2, 0, slot)]
-        left_halves = halves(left)
+        if e == 4:
+            tile = ahead_ref[jnp.where(row >= rows_count - 2, other, slot)]
+        elif e == 3:
+            after = beside1_ref[jnp.where(row >= rows_count - 1, other, slot)]
+            tile = jnp.where(core == 0, beside0_ref[slot], after)
+        else:
+            tile = home_ref[slot]
+        total = ((columns >> (2 * k)) & 3) + col_codes
+        right = halves(masked(tile, total, gap + (col - tile_row - e) * size))
         live = (tile_row >= 0) & (col > tile_row + TOP)
         scale = jnp.where(live, factor, 0.0).astype(F32)
-        for number in range(WIN):
-            e = TOP - number
-            if e == 4:
-                tile = ahead_ref[jnp.where(row >= rows_count - 2, other, slot)]
-            elif e == 3:
-                after = beside1_ref[jnp.where(row >= rows_count - 1, other, slot)]
-                tile = jnp.where(core == 0, beside0_ref[slot], after)
-            else:
-                tile = home_ref[slot]
-            total = down(codes_of(codes, tile_row + e)) + col_codes
-            right = halves(masked(tile, total, gap + (col - tile_row - e) * size))
-            own = jnp.where((tile_row >= 0) & (col == tile_row + e), 1.0, 0.0).astype(F32)
-            full = scale * times(left_halves, right) + own * left
-            for x in range(out.shape[0]):
-                out[x, number, slot] = full[x * block:(x + 1) * block]
+        own = jnp.where((tile_row >= 0) & (col == tile_row + e), 1.0, 0.0).astype(F32)
+        full = scale * times(left_halves[slot], right) + own * lefts[slot]
+        for x in range(out.shape[0]):
+            out[x, TOP - e, slot] = full[x * block:(x + 1) * block]
 
 
 def add_kernel(got, out):
@@ -92,19 +96,19 @@
                 out[slot * deep + z, number] = total[z * piece:(z + 1) * piece]
 
 
-def pack_kernel(wide, place, codes, *refs):
-    bits, out, columns = refs[:-2], refs[-2], refs[-1]
+def pack_kernel(wide, place, codes, bits0, bits1, bits2, out, columns):
     row, half, x, zl = place[0], place[2], place[4], place[5]
     part, size = out.shape[2:]
     first = row + half * (codes.shape[0] // 2)
-    for k, (at, beyond) in enumerate(((0, 1), (0, 2), (1, 1))):
-        columns[...] = down(codes_of(codes, first + at))
-        lanes = codes_of(codes, first + at + beyond)
-        for i, ref in enumerate(bits):
-            start = pl.multiple_of(((zl ^ i) * wide + x) * part, part)
-            total = columns[pl.ds(start, part), :] + lanes
-            steps = lax.broadcasted_iota(jnp.int32, (part, size), 1) - lax.broadcasted_iota(jnp.int32, (part, size), 0)
-            out[i, k] = masked(ref[k], total, steps - start + beyond * size)
+    columns[...] = columns_of(codes, [first, first + 1])
+    steps = lax.broadcasted_iota(jnp.int32, (part, size), 1) - lax.broadcasted_iota(jnp.int32, (part, size), 0)
+    for i in range(out.shape[0]):
+        start = pl.multiple_of(((zl ^ i) * wide + x) * part, part)
+        down = columns[pl.ds(start, part), :]
+        for k, (at, beyond) in enumerate(((0, 1), (0, 2), (1, 1))):
+            piece = bits0[k] if i == 0 else bits1[k] if i == 1 else bits2[i - 2, k]
+            total = ((down >> (2 * at)) & 3) + codes_of(codes, first + at + beyond)
+            out[i, k] = masked(piece, total, steps - start + beyond * size)
 
 
 def finish_kernel(factor, place, got, *refs):
@@ -133,6 +137,12 @@
         out_b[w] = rows[w, pl.ds(pl.multiple_of((1 - half) * piece, piece), piece), :]
 
 
+def order_kernel(place, back0, back1, out):
+    swap = (place[1] + place[6]) % 2 == 1
+    out[:, 0] = jnp.where(swap, back1[...], back0[...])
+    out[:, 1] = jnp.where(swap, back0[...], back1[...])
+
+
 def call(kernel, in_count, outs, scratch, flops, *args):
     spec = pl.BlockSpec(memory_space=pltpu.VMEM)
     moved = sum(math.prod(a.shape) * 4 for a in args) + sum(math.prod(s) * 4 for s in outs)
@@ -159,7 +169,8 @@
     row = lax.axis_index("y") * sizes[1] + core
     half = lax.axis_index("zh")
     col = lax.axis_index(AXES[2:])
-    place = jnp.stack([row, col, half, core, lax.axis_index("x"), lax.axis_index("zl")]).astype(jnp.int32)
+    late = (row >= rows_count - 2).astype(jnp.int32)
+    place = jnp.stack([row, col, half, core, lax.axis_index("x"), lax.axis_index("zl"), late]).astype(jnp.int32)
     home = inside[:, 0, 0, 0]
     out_tiles = outer[:, 0, 0, 0]
 
@@ -170,6 +181,7 @@
     left = row_shift(out_tiles, 1)
     ahead = row_shift(home, -1)
     beside0 = lax.ppermute(home, "core", [(1, 0)])
+    left, ahead = lax.optimization_barrier((left, ahead))
     beside1 = lax.ppermute(ahead, "core", [(0, 1)])
 
     codes = sequence.reshape(tile_count, size)
@@ -188,26 +200,27 @@
         return r // sizes[1], r % sizes[1], zh, zl, x
 
     next1 = lax.ppermute(near1, AXES, pairs_of(sizes, previous_row))
-    bits = jnp.stack([near1, near2, next1])
-
-    def partners(v, axis, n):
-        return [v] + [lax.ppermute(v, axis, [(i, i ^ j) for i in range(n)]) for j in range(1, n)]
-
-    (pack,) = call(
-        functools.partial(pack_kernel, sizes[4]),
-        1, [(sizes[3], 3, part, size)], [pltpu.VMEM((size, size), F32)], 10**6,
-        place, codes, *partners(bits, "zl", sizes[3]),
-    )
+
+    def partner(v, axis, n, j):
+        return lax.ppermute(v, axis, [(i, i ^ j) for i in range(n)])
 
     wide = (sizes[4], WIN, slots, size // sizes[4], size)
     (parts,) = call(
         functools.partial(product_kernel, factor),
         1, [wide], [], WIN * slots * 6 * size**3,
-        place, left, home, ahead, beside0, beside1, codes,
-    )
+        place, left, ahead, beside0, beside1, codes, home,
+    )
+    bits0 = jnp.stack([near1, near2, next1])
+    bits1 = partner(bits0, "zl", sizes[3], 1)
+    bits2 = partner(jnp.stack([bits0, bits1]), "zl", sizes[3], 2)
+    (pack,) = call(
+        functools.partial(pack_kernel, sizes[4]),
+        1, [(sizes[3], 3, part, size)], [pltpu.VMEM((size, size), jnp.int32)], 10**6,
+        place, codes, bits0, bits1, bits2,
+    )
+    packs = [pack] + [partner(pack, "x", sizes[4], j) for j in range(1, sizes[4])]
     parts = lax.all_to_all(parts, "x", 0, 0)
-    parts, pack = lax.optimization_barrier((parts, pack))
-    packs = partners(pack, "x", sizes[4])
+    parts, _ = lax.optimization_barrier((parts, pack))
     (ready,) = call(add_kernel, 0, [(slots * sizes[3], WIN, part, size)], [], 10**6, parts)
     got = lax.all_to_all(ready, ("zh", "zl"), 0, 0)
     piece = part // slots
@@ -226,10 +239,8 @@
         return target
 
     back = [lax.ppermute(sent[flip], AXES, pairs_of(sizes, sent_to(flip))) for flip in range(2)]
-    swap = (col % 2 == 1) ^ (row >= rows_count - 2)
-    low = jnp.where(swap, back[1], back[0])
-    high = jnp.where(swap, back[0], back[1])
-    return jnp.stack([low, high], 1)[:, :, None]
+    (result,) = call(order_kernel, 1, [(WIN, slots, piece, size)], [], 10**4, place, *back)
+    return result[:, :, None]
 
 
 def solution(mesh):

time: 112 us -> 112 us (level)
  the two profiles are of different devices: /device:TPU:6 before, /device:TPU:4 now
where the time goes in v5:
time: 112 us; the launch traced here: 111 us
  starting transfers between devices  66.1 us (59%)
  waiting for transfers between devices  36.1 us (32%)
  Pallas kernels  6.88 us (6%)
  local copies, waits for them, and re-layouts  1.9 us (2%)
    ppermute x5, starting transfers between devices, partner(): return lax.ppermute(v, axis, [(i, i ^ j) for i in range(n)])  15.9 us
    ppermute x5, waiting for transfers between devices, partner(): return lax.ppermute(v, axis, [(i, i ^ j) for i in range(n)])  14 us
    all_to_all x1, starting transfers between devices, on_device(): spread = lax.all_to_all(spread, AXES[2:], 0, 0)  13.4 us
    ppermute x2, starting transfers between devices, on_device(): lax.ppermute(sent[flip], AXES, pairs_of(sizes, sent_to(flip)))  13 us
    all_to_all x1, waiting for transfers between devices, on_device(): spread = lax.all_to_all(spread, AXES[2:], 0, 0)  10 us
    ppermute x2, waiting for transfers between devices, on_device(): lax.ppermute(sent[flip], AXES, pairs_of(sizes, sent_to(flip)))  9.99 us
    ppermute x2, starting transfers between devices, row_shift(): return lax.ppermute(v, 'y', [(i, (i + by) % n) for i in range(n)])  7.3 us
    pallas_call x5, Pallas kernels, call(): pl.pallas_call(kernel, out_shape=[jax.ShapeDtypeStruct(s, F32) for s in o...  6.88 us
  transfers between devices with their start and end apart: 15, of which 8 were waited for; matrix products, arithmetic and copies ran while one was open for 1% of the time, Pallas kernels for 3%

profile of v5, /device:TPU:4, one launch (start us, length us, event | category | flops | bytes accessed | tf_op | source)
XLA Modules:
  0.0 111.2 jit_solution(15723123592102998822)
XLA Ops:
  0.0 1.3 %collective-permute-start.2 = (f32[2,256,256]{2,1,0:T(8,128)}, f32[2,256,256]{2,1,0:T(8,128)S(1)}, u32[]{:S(2)}, u32[]{:S(2)}) collective-permute-start(f32[2,256,256]{2,1,0:T(8,128)} %bitcast.18), channel_id=1, source_target_pairs={{32,0},{33,1},{34,2},{35,3},{36,4},{37,5},{38,6},{39,7},{40,8},{41... | collective-permute-start | bytes 1572872 | tf_op jit(solution)/shard_map/ppermute | solution.py:183
  1.3 3.5 %collective-permute-start = (f32[2,256,256]{2,1,0:T(8,128)}, f32[2,256,256]{2,1,0:T(8,128)S(1)}, u32[]{:S(2)}, u32[]{:S(2)}) collective-permute-start(f32[2,256,256]{2,1,0:T(8,128)} %bitcast.25), channel_id=1, source_target_pairs={{0,64},{64,128},{128,192},{192,256},{256,320},{320,384},{384,448},... | collective-permute-start | bytes 1572872 | tf_op jit(solution)/shard_map/ppermute | solution.py:179
  4.8 3.8 %collective-permute-start.1 = (f32[2,256,256]{2,1,0:T(8,128)}, f32[2,256,256]{2,1,0:T(8,128)S(1)}, u32[]{:S(2)}, u32[]{:S(2)}) collective-permute-start(f32[2,256,256]{2,1,0:T(8,128)} %bitcast.19), channel_id=1, source_target_pairs={{0,448},{64,0},{128,64},{192,128},{256,192},{320,256},{384,320},{4... | collective-permute-start | bytes 1572872 | tf_op jit(solution)/shard_map/ppermute | solution.py:179
  8.6 0.0 collective-permute-done.2.beside0_ref
  8.6 13.4 %all-to-all-start.1 = ((f32[32,16,256]{2,1,0:T(8,128)}), f32[32,16,256]{2,1,0:T(8,128)S(1)}, u32[]{:S(2)}, u32[]{:S(2)}) async-start(f32[32,16,256]{2,1,0:T(8,128)} %bitcast.20), calls=%async_computation.1 | async-start | bytes 1048576 | tf_op jit(solution)/shard_map/all_to_all | solution.py:190
  22.1 0.0 collective-permute-done.left_ref
  22.1 0.0 collective-permute-done.1.ahead_ref
  22.1 2.3 %collective-permute-start.3 = (f32[2,256,256]{2,1,0:T(8,128)S(1)}, f32[2,256,256]{2,1,0:T(8,128)S(1)}, u32[]{:S(2)}, u32[]{:S(2)}) collective-permute-start(f32[2,256,256]{2,1,0:T(8,128)S(1)} %collective-permute-done.1.ahead_ref), channel_id=1, source_target_pairs={{0,32},{1,33},{2,34},{3,35},{4,36},{5,37},{6,38},{7,39},{8,40},{9,... | collective-permute-start | bytes 1572872 | tf_op jit(solution)/shard_map/ppermute | solution.py:185
  24.4 0.8 reshape.3.codes
  25.2 0.1 stack.52.place
  25.2 0.6 collective-permute-done.3.beside1_ref
  25.8 0.0 copy-start
  25.8 1.0 copy-done
  26.9 3.0 %shard_map.37 = f32[4,3,2,64,256]{4,3,2,1,0:T(8,128)} custom-call(s32[7]{0:T(128)S(1)} %stack.52.place, f32[2,256,256]{2,1,0:T(8,128)S(1)} %collective-permute-done.left_ref, f32[2,256,256]{2,1,0:T(8,128)S(1)} %collective-permute-done.1.ahead_ref, f32[2,256,256]{2,1,0:T(8,128)S(1)} %collective-permute-done.2.beside0_ref, ...), custom_call_target="tpu_custom_call" | custom-call | flops 603979776 | bytes 4227100 | tf_op jit(solution)/shard_map/pallas_call | solution.py:149
  29.9 10.0 %all-to-all-done.1 = f32[32,16,256]{2,1,0:T(8,128)S(1)} async-done(((f32[32,16,256]{2,1,0:T(8,128)}), f32[32,16,256]{2,1,0:T(8,128)S(1)}, u32[]{:S(2)}, u32[]{:S(2)}) %all-to-all-start.1) | async-done | bytes 524320 | tf_op jit(solution)/shard_map/all_to_all | solution.py:190
  39.9 4.8 %all-to-all-start = ((f32[4,3,2,64,256]{4,3,2,1,0:T(8,128)}), f32[4,3,2,64,256]{4,3,2,1,0:T(8,128)S(1)}, u32[]{:S(2)}, u32[]{:S(2)}) async-start(f32[4,3,2,64,256]{4,3,2,1,0:T(8,128)} %shard_map.37), calls=%async_computation | async-start | bytes 3145728 | tf_op jit(solution)/shard_map/all_to_all | solution.py:222
  44.7 3.1 %collective-permute-start.4 = (f32[16,256]{1,0:T(8,128)S(1)}, f32[16,256]{1,0:T(8,128)S(1)}, u32[]{:S(2)}, u32[]{:S(2)}) collective-permute-start(f32[16,256]{1,0:T(8,128)S(1)} %bitcast.23), channel_id=1, source_target_pairs={{0,496},{1,497},{2,498},{3,499},{4,500},{5,501},{6,502},{7,503},{8... | collective-permute-start | bytes 49160 | tf_op jit(solution)/shard_map/ppermute | solution.py:202
  47.9 1.4 %collective-permute-done.4 = f32[16,256]{1,0:T(8,128)S(1)} collective-permute-done((f32[16,256]{1,0:T(8,128)S(1)}, f32[16,256]{1,0:T(8,128)S(1)}, u32[]{:S(2)}, u32[]{:S(2)}) %collective-permute-start.4) | collective-permute-done | bytes 16416 | tf_op jit(solution)/shard_map/ppermute | solution.py:202
  49.3 2.6 %collective-permute-start.5 = (f32[3,16,256]{2,1,0:T(8,128)S(1)}, f32[3,16,256]{2,1,0:T(8,128)S(1)}, u32[]{:S(2)}, u32[]{:S(2)}) collective-permute-start(f32[3,16,256]{2,1,0:T(8,128)S(1)} %get-tuple-element.22.bits0), channel_id=1, source_target_pairs={{0,4},{4,0},{8,12},{12,8},{1,5},{5,1},{9,13},{13,9},{2,6},{6,2},{1... | collective-permute-start | bytes 147464 | tf_op jit(solution)/shard_map/ppermute | solution.py:205
  51.9 3.4 %collective-permute-done.5.bits1 = f32[3,16,256]{2,1,0:T(8,128)S(1)} collective-permute-done((f32[3,16,256]{2,1,0:T(8,128)S(1)}, f32[3,16,256]{2,1,0:T(8,128)S(1)}, u32[]{:S(2)}, u32[]{:S(2)}) %collective-permute-start.5) | collective-permute-done | bytes 49184 | tf_op jit(solution)/shard_map/ppermute | solution.py:205
  55.3 4.1 %collective-permute-start.6 = (f32[2,3,16,256]{3,2,1,0:T(8,128)S(1)}, f32[2,3,16,256]{3,2,1,0:T(8,128)S(1)}, u32[]{:S(2)}, u32[]{:S(2)}) collective-permute-start(f32[2,3,16,256]{3,2,1,0:T(8,128)S(1)} %pad_maximum_fusion), channel_id=1, source_target_pairs={{0,8},{4,12},{8,0},{12,4},{1,9},{5,13},{9,1},{13,5},{2,10},{6,14},... | collective-permute-start | bytes 294920 | tf_op jit(solution)/shard_map/ppermute | solution.py:205
  59.4 4.6 %collective-permute-done.6.bits2 = f32[2,3,16,256]{3,2,1,0:T(8,128)S(1)} collective-permute-done((f32[2,3,16,256]{3,2,1,0:T(8,128)S(1)}, f32[2,3,16,256]{3,2,1,0:T(8,128)S(1)}, u32[]{:S(2)}, u32[]{:S(2)}) %collective-permute-start.6) | collective-permute-done | bytes 98336 | tf_op jit(solution)/shard_map/ppermute | solution.py:205
  64.0 0.7 shard_map.38.refs_0_
  64.7 0.0 all-to-all-done.got
  64.7 0.8 shard_map.39
  65.5 5.1 %all-to-all-start.2 = ((f32[8,3,16,256]{3,2,1,0:T(8,128)}), f32[8,3,16,256]{3,2,1,0:T(8,128)S(1)}, u32[]{:S(2)}, u32[]{:S(2)}) async-start(f32[8,3,16,256]{3,2,1,0:T(8,128)} %shard_map.39), calls=%async_computation.2 | async-start | bytes 786432 | tf_op jit(solution)/shard_map/all_to_all | solution.py:225
  70.6 3.1 %collective-permute-start.7 = (f32[4,3,16,256]{3,2,1,0:T(8,128)S(1)}, f32[4,3,16,256]{3,2,1,0:T(8,128)S(1)}, u32[]{:S(2)}, u32[]{:S(2)}) collective-permute-start(f32[4,3,16,256]{3,2,1,0:T(8,128)S(1)} %shard_map.38.refs_0_), channel_id=1, source_target_pairs={{0,1},{1,0},{2,3},{3,2},{4,5},{5,4},{6,7},{7,6},{8,9},{9,8},{10,11... | collective-permute-start | bytes 589832 | tf_op jit(solution)/shard_map/ppermute | solution.py:205
  73.7 2.8 %collective-permute-start.8 = (f32[4,3,16,256]{3,2,1,0:T(8,128)S(1)}, f32[4,3,16,256]{3,2,1,0:T(8,128)S(1)}, u32[]{:S(2)}, u32[]{:S(2)}) collective-permute-start(f32[4,3,16,256]{3,2,1,0:T(8,128)S(1)} %shard_map.38.refs_0_), channel_id=1, source_target_pairs={{0,2},{1,3},{2,0},{3,1},{4,6},{5,7},{6,4},{7,5},{8,10},{9,11},{10,... | collective-permute-start | bytes 589832 | tf_op jit(solution)/shard_map/ppermute | solution.py:205
  76.5 3.4 %collective-permute-start.9 = (f32[4,3,16,256]{3,2,1,0:T(8,128)S(1)}, f32[4,3,16,256]{3,2,1,0:T(8,128)S(1)}, u32[]{:S(2)}, u32[]{:S(2)}) collective-permute-start(f32[4,3,16,256]{3,2,1,0:T(8,128)S(1)} %shard_map.38.refs_0_), channel_id=1, source_target_pairs={{0,3},{1,2},{2,1},{3,0},{4,7},{5,6},{6,5},{7,4},{8,11},{9,10},{10,... | collective-permute-start | bytes 589832 | tf_op jit(solution)/shard_map/ppermute | solution.py:205
  79.9 0.0 collective-permute-done.7.refs_1_
  79.9 3.0 %collective-permute-done.8.refs_2_ = f32[4,3,16,256]{3,2,1,0:T(8,128)S(1)} collective-permute-done((f32[4,3,16,256]{3,2,1,0:T(8,128)S(1)}, f32[4,3,16,256]{3,2,1,0:T(8,128)S(1)}, u32[]{:S(2)}, u32[]{:S(2)}) %collective-permute-start.8) | collective-permute-done | bytes 196640 | tf_op jit(solution)/shard_map/ppermute | solution.py:205
  82.8 3.1 %collective-permute-done.9.refs_3_ = f32[4,3,16,256]{3,2,1,0:T(8,128)S(1)} collective-permute-done((f32[4,3,16,256]{3,2,1,0:T(8,128)S(1)}, f32[4,3,16,256]{3,2,1,0:T(8,128)S(1)}, u32[]{:S(2)}, u32[]{:S(2)}) %collective-permute-start.9) | collective-permute-done | bytes 196640 | tf_op jit(solution)/shard_map/ppermute | solution.py:205
  85.9 0.0 all-to-all-done.2.got
  85.9 1.2 %shard_map.40 = (f32[3,8,256]{2,1,0:T(8,128)S(1)}, f32[3,8,256]{2,1,0:T(8,128)S(1)}) custom-call(s32[7]{0:T(128)S(1)} %stack.52.place, f32[8,3,16,256]{3,2,1,0:T(8,128)S(1)} %all-to-all-done.2.got, f32[4,3,16,256]{3,2,1,0:T(8,128)S(1)} %shard_map.38.refs_0_, f32[4,3,16,256]{3,2,1,0:T(8,128)S(1)} %collective-permute-done.7.refs_1_, ...), custom_call_target="tpu_custom_call" | custom-call | flops 18874368 | bytes 1228828 | tf_op jit(solution)/shard_map/pallas_call | solution.py:149
  87.1 10.9 %collective-permute-start.10 = (f32[3,8,256]{2,1,0:T(8,128)S(1)}, f32[3,8,256]{2,1,0:T(8,128)S(1)}, u32[]{:S(2)}, u32[]{:S(2)}) collective-permute-start(f32[3,8,256]{2,1,0:T(8,128)S(1)} %get-tuple-element.17), channel_id=1, source_target_pairs={{0,448},{1,456},{2,464},{3,472},{4,450},{5,458},{6,466},{7,474},{8... | collective-permute-start | bytes 73736 | tf_op jit(solution)/shard_map/ppermute | solution.py:241
  98.0 2.0 %collective-permute-start.11 = (f32[3,8,256]{2,1,0:T(8,128)S(1)}, f32[3,8,256]{2,1,0:T(8,128)S(1)}, u32[]{:S(2)}, u32[]{:S(2)}) collective-permute-start(f32[3,8,256]{2,1,0:T(8,128)S(1)} %get-tuple-element.18), channel_id=1, source_target_pairs={{0,449},{1,457},{2,465},{3,473},{4,451},{5,459},{6,467},{7,475},{8... | collective-permute-start | bytes 73736 | tf_op jit(solution)/shard_map/ppermute | solution.py:241
  100.0 0.0 collective-permute-done.10.back0
  100.1 10.0 %collective-permute-done.11.back1 = f32[3,8,256]{2,1,0:T(8,128)S(1)} collective-permute-done((f32[3,8,256]{2,1,0:T(8,128)S(1)}, f32[3,8,256]{2,1,0:T(8,128)S(1)}, u32[]{:S(2)}, u32[]{:S(2)}) %collective-permute-start.11) | collective-permute-done | bytes 24608 | tf_op jit(solution)/shard_map/ppermute | solution.py:241
  110.0 1.2 %shard_map.41 = f32[3,2,8,256]{3,2,1,0:T(8,128)} custom-call(s32[7]{0:T(128)S(1)} %stack.52.place, f32[3,8,256]{2,1,0:T(8,128)S(1)} %collective-permute-done.10.back0, f32[3,8,256]{2,1,0:T(8,128)S(1)} %collective-permute-done.11.back1), custom_call_target="tpu_custom_call" | custom-call | flops 10000 | bytes 98332 | tf_op jit(solution)/shard_map/pallas_call | solution.py:149
  (3 shorter events, 0.0 us)
Async XLA Ops:
  0.0 8.6 %collective-permute-start.2 = (f32[2,256,256]{2,1,0:T(8,128)}, f32[2,256,256]{2,1,0:T(8,128)S(1)}, u32[]{:S(2)}, u32[]{:S(2)}) collective-permute-start(f32[2,256,256]{2,1,0:T(8,128)} %bitcast.18), channel_id=1, source_target_pairs={{32,0},{33,1},{34,2},{35,3},{36,4},{37,5},{38,6},{39,7},{40,8},{41... | collective-permute-start | bytes 1572872 | tf_op jit(solution)/shard_map/ppermute | solution.py:183
  1.3 20.8 %collective-permute-start = (f32[2,256,256]{2,1,0:T(8,128)}, f32[2,256,256]{2,1,0:T(8,128)S(1)}, u32[]{:S(2)}, u32[]{:S(2)}) collective-permute-start(f32[2,256,256]{2,1,0:T(8,128)} %bitcast.25), channel_id=1, source_target_pairs={{0,64},{64,128},{128,192},{192,256},{256,320},{320,384},{384,448},... | collective-permute-start | bytes 1572872 | tf_op jit(solution)/shard_map/ppermute | solution.py:179
  4.8 17.3 %collective-permute-start.1 = (f32[2,256,256]{2,1,0:T(8,128)}, f32[2,256,256]{2,1,0:T(8,128)S(1)}, u32[]{:S(2)}, u32[]{:S(2)}) collective-permute-start(f32[2,256,256]{2,1,0:T(8,128)} %bitcast.19), channel_id=1, source_target_pairs={{0,448},{64,0},{128,64},{192,128},{256,192},{320,256},{384,320},{4... | collective-permute-start | bytes 1572872 | tf_op jit(solution)/shard_map/ppermute | solution.py:179
  8.6 31.3 %all-to-all-start.1 = ((f32[32,16,256]{2,1,0:T(8,128)}), f32[32,16,256]{2,1,0:T(8,128)S(1)}, u32[]{:S(2)}, u32[]{:S(2)}) async-start(f32[32,16,256]{2,1,0:T(8,128)} %bitcast.20), calls=%async_computation.1 | async-start | bytes 1048576 | tf_op jit(solution)/shard_map/all_to_all | solution.py:190
  22.1 3.7 %collective-permute-start.3 = (f32[2,256,256]{2,1,0:T(8,128)S(1)}, f32[2,256,256]{2,1,0:T(8,128)S(1)}, u32[]{:S(2)}, u32[]{:S(2)}) collective-permute-start(f32[2,256,256]{2,1,0:T(8,128)S(1)} %collective-permute-done.1.ahead_ref), channel_id=1, source_target_pairs={{0,32},{1,33},{2,34},{3,35},{4,36},{5,37},{6,38},{7,39},{8,40},{9,... | collective-permute-start | bytes 1572872 | tf_op jit(solution)/shard_map/ppermute | solution.py:185
  25.8 1.0 copy-start
  39.9 24.7 %all-to-all-start = ((f32[4,3,2,64,256]{4,3,2,1,0:T(8,128)}), f32[4,3,2,64,256]{4,3,2,1,0:T(8,128)S(1)}, u32[]{:S(2)}, u32[]{:S(2)}) async-start(f32[4,3,2,64,256]{4,3,2,1,0:T(8,128)} %shard_map.37), calls=%async_computation | async-start | bytes 3145728 | tf_op jit(solution)/shard_map/all_to_all | solution.py:222
  44.7 4.5 %collective-permute-start.4 = (f32[16,256]{1,0:T(8,128)S(1)}, f32[16,256]{1,0:T(8,128)S(1)}, u32[]{:S(2)}, u32[]{:S(2)}) collective-permute-start(f32[16,256]{1,0:T(8,128)S(1)} %bitcast.23), channel_id=1, source_target_pairs={{0,496},{1,497},{2,498},{3,499},{4,500},{5,501},{6,502},{7,503},{8... | collective-permute-start | bytes 49160 | tf_op jit(solution)/shard_map/ppermute | solution.py:202
  49.3 6.0 %collective-permute-start.5 = (f32[3,16,256]{2,1,0:T(8,128)S(1)}, f32[3,16,256]{2,1,0:T(8,128)S(1)}, u32[]{:S(2)}, u32[]{:S(2)}) collective-permute-start(f32[3,16,256]{2,1,0:T(8,128)S(1)} %get-tuple-element.22.bits0), channel_id=1, source_target_pairs={{0,4},{4,0},{8,12},{12,8},{1,5},{5,1},{9,13},{13,9},{2,6},{6,2},{1... | collective-permute-start | bytes 147464 | tf_op jit(solution)/shard_map/ppermute | solution.py:205
  55.3 8.7 %collective-permute-start.6 = (f32[2,3,16,256]{3,2,1,0:T(8,128)S(1)}, f32[2,3,16,256]{3,2,1,0:T(8,128)S(1)}, u32[]{:S(2)}, u32[]{:S(2)}) collective-permute-start(f32[2,3,16,256]{3,2,1,0:T(8,128)S(1)} %pad_maximum_fusion), channel_id=1, source_target_pairs={{0,8},{4,12},{8,0},{12,4},{1,9},{5,13},{9,1},{13,5},{2,10},{6,14},... | collective-permute-start | bytes 294920 | tf_op jit(solution)/shard_map/ppermute | solution.py:205
  65.5 20.4 %all-to-all-start.2 = ((f32[8,3,16,256]{3,2,1,0:T(8,128)}), f32[8,3,16,256]{3,2,1,0:T(8,128)S(1)}, u32[]{:S(2)}, u32[]{:S(2)}) async-start(f32[8,3,16,256]{3,2,1,0:T(8,128)} %shard_map.39), calls=%async_computation.2 | async-start | bytes 786432 | tf_op jit(solution)/shard_map/all_to_all | solution.py:225
  70.6 9.2 %collective-permute-start.7 = (f32[4,3,16,256]{3,2,1,0:T(8,128)S(1)}, f32[4,3,16,256]{3,2,1,0:T(8,128)S(1)}, u32[]{:S(2)}, u32[]{:S(2)}) collective-permute-start(f32[4,3,16,256]{3,2,1,0:T(8,128)S(1)} %shard_map.38.refs_0_), channel_id=1, source_target_pairs={{0,1},{1,0},{2,3},{3,2},{4,5},{5,4},{6,7},{7,6},{8,9},{9,8},{10,11... | collective-permute-start | bytes 589832 | tf_op jit(solution)/shard_map/ppermute | solution.py:205
  73.7 9.1 %collective-permute-start.8 = (f32[4,3,16,256]{3,2,1,0:T(8,128)S(1)}, f32[4,3,16,256]{3,2,1,0:T(8,128)S(1)}, u32[]{:S(2)}, u32[]{:S(2)}) collective-permute-start(f32[4,3,16,256]{3,2,1,0:T(8,128)S(1)} %shard_map.38.refs_0_), channel_id=1, source_target_pairs={{0,2},{1,3},{2,0},{3,1},{4,6},{5,7},{6,4},{7,5},{8,10},{9,11},{10,... | collective-permute-start | bytes 589832 | tf_op jit(solution)/shard_map/ppermute | solution.py:205
  76.5 9.4 %collective-permute-start.9 = (f32[4,3,16,256]{3,2,1,0:T(8,128)S(1)}, f32[4,3,16,256]{3,2,1,0:T(8,128)S(1)}, u32[]{:S(2)}, u32[]{:S(2)}) collective-permute-start(f32[4,3,16,256]{3,2,1,0:T(8,128)S(1)} %shard_map.38.refs_0_), channel_id=1, source_target_pairs={{0,3},{1,2},{2,1},{3,0},{4,7},{5,6},{6,5},{7,4},{8,11},{9,10},{10,... | collective-permute-start | bytes 589832 | tf_op jit(solution)/shard_map/ppermute | solution.py:205
  87.1 13.0 %collective-permute-start.10 = (f32[3,8,256]{2,1,0:T(8,128)S(1)}, f32[3,8,256]{2,1,0:T(8,128)S(1)}, u32[]{:S(2)}, u32[]{:S(2)}) collective-permute-start(f32[3,8,256]{2,1,0:T(8,128)S(1)} %get-tuple-element.17), channel_id=1, source_target_pairs={{0,448},{1,456},{2,464},{3,472},{4,450},{5,458},{6,466},{7,474},{8... | collective-permute-start | bytes 73736 | tf_op jit(solution)/shard_map/ppermute | solution.py:241
  98.0 12.0 %collective-permute-start.11 = (f32[3,8,256]{2,1,0:T(8,128)S(1)}, f32[3,8,256]{2,1,0:T(8,128)S(1)}, u32[]{:S(2)}, u32[]{:S(2)}) collective-permute-start(f32[3,8,256]{2,1,0:T(8,128)S(1)} %get-tuple-element.18), channel_id=1, source_target_pairs={{0,449},{1,457},{2,465},{3,473},{4,451},{5,459},{6,467},{7,475},{8... | collective-permute-start | bytes 73736 | tf_op jit(solution)/shard_map/ppermute | solution.py:241

commit v6 on v5

--- a/solution.py
+++ b/solution.py
@@ -39,24 +39,25 @@
     return codes[pl.ds(jnp.clip(tile, 0, codes.shape[0] - 1), 1), :]
 
 
+def partners_of(code):
+    return jnp.where(code == 0, 8, jnp.where(code == 1, 4, jnp.where(code == 2, 10, 5)))
+
+
 def columns_of(codes, tiles):
-    total = codes_of(codes, tiles[0])
+    total = partners_of(codes_of(codes, tiles[0]))
     for k, tile in enumerate(tiles[1:], 1):
-        total = total + (codes_of(codes, tile) << (2 * k))
+        total = total + (partners_of(codes_of(codes, tile)) << (4 * k))
     size = codes.shape[1]
     return jnp.broadcast_to(total, (size, size)).T
-
-
-def masked(tile, total, gap):
-    return jnp.where(((total == 3) | (total == 5)) & (gap > 3), tile, 0.0)
 
 
 def product_kernel(factor, place, left_ref, ahead_ref, beside0_ref, beside1_ref, codes, home_ref, out):
     row, col, core = place[0], place[1], place[3]
     slots, size = left_ref.shape[0], left_ref.shape[1]
     rows_count = codes.shape[0] // slots
-    block = size // out.shape[0]
-    col_codes = codes_of(codes, col)
+    block = out.shape[2]
+    deep = size // block
+    col_bits = 1 << codes_of(codes, col)
     tile_rows = [slot * rows_count + row - 2 for slot in range(slots)]
     keys = [(slot, e) for e in (4, 3, 2) for slot in range(slots)]
     columns = columns_of(codes, [tile_rows[slot] + e for slot, e in keys])
@@ -66,34 +67,22 @@
     for k, (slot, e) in enumerate(keys):
         tile_row = tile_rows[slot]
         other = slots - 1 - slot
+        allowed = (columns & (col_bits << (4 * k))) != 0
         if e == 4:
             tile = ahead_ref[jnp.where(row >= rows_count - 2, other, slot)]
+            allowed = allowed & (gap > 3 - (col - tile_row - e) * size)
         elif e == 3:
             after = beside1_ref[jnp.where(row >= rows_count - 1, other, slot)]
             tile = jnp.where(core == 0, beside0_ref[slot], after)
         else:
             tile = home_ref[slot]
-        total = ((columns >> (2 * k)) & 3) + col_codes
-        right = halves(masked(tile, total, gap + (col - tile_row - e) * size))
+        right = halves(jnp.where(allowed, tile, 0.0))
         live = (tile_row >= 0) & (col > tile_row + TOP)
         scale = jnp.where(live, factor, 0.0).astype(F32)
         own = jnp.where((tile_row >= 0) & (col == tile_row + e), 1.0, 0.0).astype(F32)
         full = scale * times(left_halves[slot], right) + own * lefts[slot]
-        for x in range(out.shape[0]):
-            out[x, TOP - e, slot] = full[x * block:(x + 1) * block]
-
-
-def add_kernel(got, out):
-    slots, rows = got.shape[2:4]
-    deep = out.shape[0] // slots
-    piece = rows // deep
-    for number in range(WIN):
-        for slot in range(slots):
-            total = got[0, number, slot]
-            for k in range(1, got.shape[0]):
-                total = total + got[k, number, slot]
-            for z in range(deep):
-                out[slot * deep + z, number] = total[z * piece:(z + 1) * piece]
+        for q in range(deep):
+            out[slot * deep + q, TOP - e] = full[q * block:(q + 1) * block]
 
 
 def pack_kernel(wide, place, codes, bits0, bits1, bits2, out, columns):
@@ -107,8 +96,9 @@
         down = columns[pl.ds(start, part), :]
         for k, (at, beyond) in enumerate(((0, 1), (0, 2), (1, 1))):
             piece = bits0[k] if i == 0 else bits1[k] if i == 1 else bits2[i - 2, k]
-            total = ((down >> (2 * at)) & 3) + codes_of(codes, first + at + beyond)
-            out[i, k] = masked(piece, total, steps - start + beyond * size)
+            allowed = (down & (1 << (codes_of(codes, first + at + beyond) + 4 * at))) != 0
+            far = steps > 3 + start - beyond * size
+            out[i, k] = jnp.where(allowed & far, piece, 0.0)
 
 
 def finish_kernel(factor, place, got, *refs):
@@ -204,10 +194,9 @@
     def partner(v, axis, n, j):
         return lax.ppermute(v, axis, [(i, i ^ j) for i in range(n)])
 
-    wide = (sizes[4], WIN, slots, size // sizes[4], size)
     (parts,) = call(
         functools.partial(product_kernel, factor),
-        1, [wide], [], WIN * slots * 6 * size**3,
+        1, [(cols_count, WIN, part, size)], [], WIN * slots * 6 * size**3,
         place, left, ahead, beside0, beside1, codes, home,
     )
     bits0 = jnp.stack([near1, near2, next1])
@@ -219,10 +208,7 @@
         place, codes, bits0, bits1, bits2,
     )
     packs = [pack] + [partner(pack, "x", sizes[4], j) for j in range(1, sizes[4])]
-    parts = lax.all_to_all(parts, "x", 0, 0)
-    parts, _ = lax.optimization_barrier((parts, pack))
-    (ready,) = call(add_kernel, 0, [(slots * sizes[3], WIN, part, size)], [], 10**6, parts)
-    got = lax.all_to_all(ready, ("zh", "zl"), 0, 0)
+    got = lax.all_to_all(parts, AXES[2:], 0, 0)
     piece = part // slots
     sent = call(
         functools.partial(finish_kernel, factor),
@@ -234,7 +220,7 @@
         def target(y, c, zh, zl, x):
             r = (y * sizes[1] + c - 2) % rows_count
             pick = zh if flip == 0 else 1 - zh
-            n = 2 * (x * sizes[3] + zl) + pick
+            n = 2 * (zl * sizes[4] + x) + pick
             return r // sizes[1], r % sizes[1], n // (sizes[3] * sizes[4]), n // sizes[4] % sizes[3], n % sizes[4]
         return target
 

time: 112 us -> 127 us (1.13)
  the two profiles are of different devices: /device:TPU:4 before, /device:TPU:28 now
where the time goes in v6:
time: 127 us; the launch traced here: 126 us
  waiting for transfers between devices  67.2 us (53%)
  starting transfers between devices  50.7 us (40%)
  Pallas kernels  5.89 us (5%)
  local copies, waits for them, and re-layouts  1.91 us (2%)
    ppermute x5, waiting for transfers between devices, partner(): return lax.ppermute(v, axis, [(i, i ^ j) for i in range(n)])  42.3 us
    ppermute x5, starting transfers between devices, partner(): return lax.ppermute(v, axis, [(i, i ^ j) for i in range(n)])  16.1 us
    all_to_all x1, starting transfers between devices, on_device(): spread = lax.all_to_all(spread, AXES[2:], 0, 0)  13.4 us
    ppermute x2, waiting for transfers between devices, on_device(): lax.ppermute(sent[flip], AXES, pairs_of(sizes, sent_to(flip)))  12.4 us
    all_to_all x1, waiting for transfers between devices, on_device(): spread = lax.all_to_all(spread, AXES[2:], 0, 0)  7.91 us
    ppermute x2, starting transfers between devices, row_shift(): return lax.ppermute(v, 'y', [(i, (i + by) % n) for i in range(n)])  6.62 us
    pallas_call x4, Pallas kernels, call(): pl.pallas_call(kernel, out_shape=[jax.ShapeDtypeStruct(s, F32) for s in o...  5.89 us
    all_to_all x1, starting transfers between devices, on_device(): got = lax.all_to_all(parts, AXES[2:], 0, 0)  5.57 us
  transfers between devices with their start and end apart: 14, of which 10 were waited for; matrix products, arithmetic and copies ran while one was open for 1% of the time, Pallas kernels for 3%

profile of v6, /device:TPU:28, one launch (start us, length us, event | category | flops | bytes accessed | tf_op | source)
XLA Modules:
  0.0 125.9 jit_solution(12189029507821975610)
XLA Ops:
  0.0 1.3 %collective-permute-start.2 = (f32[2,256,256]{2,1,0:T(8,128)}, f32[2,256,256]{2,1,0:T(8,128)S(1)}, u32[]{:S(2)}, u32[]{:S(2)}) collective-permute-start(f32[2,256,256]{2,1,0:T(8,128)} %bitcast.18), channel_id=1, source_target_pairs={{32,0},{33,1},{34,2},{35,3},{36,4},{37,5},{38,6},{39,7},{40,8},{41... | collective-permute-start | bytes 1572872 | tf_op jit(solution)/shard_map/ppermute | solution.py:173
  1.3 4.7 %collective-permute-start = (f32[2,256,256]{2,1,0:T(8,128)}, f32[2,256,256]{2,1,0:T(8,128)S(1)}, u32[]{:S(2)}, u32[]{:S(2)}) collective-permute-start(f32[2,256,256]{2,1,0:T(8,128)} %bitcast.25), channel_id=1, source_target_pairs={{0,64},{64,128},{128,192},{192,256},{256,320},{320,384},{384,448},... | collective-permute-start | bytes 1572872 | tf_op jit(solution)/shard_map/ppermute | solution.py:169
  6.0 1.9 %collective-permute-start.1 = (f32[2,256,256]{2,1,0:T(8,128)}, f32[2,256,256]{2,1,0:T(8,128)S(1)}, u32[]{:S(2)}, u32[]{:S(2)}) collective-permute-start(f32[2,256,256]{2,1,0:T(8,128)} %bitcast.19), channel_id=1, source_target_pairs={{0,448},{64,0},{128,64},{192,128},{256,192},{320,256},{384,320},{4... | collective-permute-start | bytes 1572872 | tf_op jit(solution)/shard_map/ppermute | solution.py:169
  7.9 0.0 collective-permute-done.2.beside0_ref
  7.9 13.4 %all-to-all-start.1 = ((f32[32,16,256]{2,1,0:T(8,128)}), f32[32,16,256]{2,1,0:T(8,128)S(1)}, u32[]{:S(2)}, u32[]{:S(2)}) async-start(f32[32,16,256]{2,1,0:T(8,128)} %bitcast.20), calls=%async_computation.1 | async-start | bytes 1048576 | tf_op jit(solution)/shard_map/all_to_all | solution.py:180
  21.4 0.0 collective-permute-done.left_ref
  21.4 2.6 %collective-permute-done.1.ahead_ref = f32[2,256,256]{2,1,0:T(8,128)S(1)} collective-permute-done((f32[2,256,256]{2,1,0:T(8,128)}, f32[2,256,256]{2,1,0:T(8,128)S(1)}, u32[]{:S(2)}, u32[]{:S(2)}) %collective-permute-start.1) | collective-permute-done | bytes 524320 | tf_op jit(solution)/shard_map/ppermute | solution.py:169
  24.0 1.9 %collective-permute-start.3 = (f32[2,256,256]{2,1,0:T(8,128)S(1)}, f32[2,256,256]{2,1,0:T(8,128)S(1)}, u32[]{:S(2)}, u32[]{:S(2)}) collective-permute-start(f32[2,256,256]{2,1,0:T(8,128)S(1)} %collective-permute-done.1.ahead_ref), channel_id=1, source_target_pairs={{0,32},{1,33},{2,34},{3,35},{4,36},{5,37},{6,38},{7,39},{8,40},{9,... | collective-permute-start | bytes 1572872 | tf_op jit(solution)/shard_map/ppermute | solution.py:175
  26.0 0.8 reshape.3.codes
  26.8 0.1 stack.52.place
  26.9 0.6 collective-permute-done.3.beside1_ref
  27.5 0.0 copy-start
  27.5 1.0 copy-done
  28.5 2.9 %shard_map.37 = f32[32,3,16,256]{3,2,1,0:T(8,128)} custom-call(s32[7]{0:T(128)S(1)} %stack.52.place, f32[2,256,256]{2,1,0:T(8,128)S(1)} %collective-permute-done.left_ref, f32[2,256,256]{2,1,0:T(8,128)S(1)} %collective-permute-done.1.ahead_ref, f32[2,256,256]{2,1,0:T(8,128)S(1)} %collective-permute-done.2.beside0_ref, ...), custom_call_target="tpu_custom_call" | custom-call | flops 603979776 | bytes 4227100 | tf_op jit(solution)/shard_map/pallas_call | solution.py:139
  31.4 7.9 %all-to-all-done.1 = f32[32,16,256]{2,1,0:T(8,128)S(1)} async-done(((f32[32,16,256]{2,1,0:T(8,128)}), f32[32,16,256]{2,1,0:T(8,128)S(1)}, u32[]{:S(2)}, u32[]{:S(2)}) %all-to-all-start.1) | async-done | bytes 524320 | tf_op jit(solution)/shard_map/all_to_all | solution.py:180
  39.3 5.6 %all-to-all-start = ((f32[32,3,16,256]{3,2,1,0:T(8,128)}), f32[32,3,16,256]{3,2,1,0:T(8,128)S(1)}, u32[]{:S(2)}, u32[]{:S(2)}) async-start(f32[32,3,16,256]{3,2,1,0:T(8,128)} %shard_map.37), calls=%async_computation | async-start | bytes 3145728 | tf_op jit(solution)/shard_map/all_to_all | solution.py:211
  44.9 1.9 %collective-permute-start.4 = (f32[16,256]{1,0:T(8,128)S(1)}, f32[16,256]{1,0:T(8,128)S(1)}, u32[]{:S(2)}, u32[]{:S(2)}) collective-permute-start(f32[16,256]{1,0:T(8,128)S(1)} %bitcast.23), channel_id=1, source_target_pairs={{0,496},{1,497},{2,498},{3,499},{4,500},{5,501},{6,502},{7,503},{8... | collective-permute-start | bytes 49160 | tf_op jit(solution)/shard_map/ppermute | solution.py:192
  46.8 1.4 %collective-permute-done.4 = f32[16,256]{1,0:T(8,128)S(1)} collective-permute-done((f32[16,256]{1,0:T(8,128)S(1)}, f32[16,256]{1,0:T(8,128)S(1)}, u32[]{:S(2)}, u32[]{:S(2)}) %collective-permute-start.4) | collective-permute-done | bytes 16416 | tf_op jit(solution)/shard_map/ppermute | solution.py:192
  48.2 3.4 %collective-permute-start.5 = (f32[3,16,256]{2,1,0:T(8,128)S(1)}, f32[3,16,256]{2,1,0:T(8,128)S(1)}, u32[]{:S(2)}, u32[]{:S(2)}) collective-permute-start(f32[3,16,256]{2,1,0:T(8,128)S(1)} %get-tuple-element.20.bits0), channel_id=1, source_target_pairs={{0,4},{4,0},{8,12},{12,8},{1,5},{5,1},{9,13},{13,9},{2,6},{6,2},{1... | collective-permute-start | bytes 147464 | tf_op jit(solution)/shard_map/ppermute | solution.py:195
  51.6 30.2 %collective-permute-done.5.bits1 = f32[3,16,256]{2,1,0:T(8,128)S(1)} collective-permute-done((f32[3,16,256]{2,1,0:T(8,128)S(1)}, f32[3,16,256]{2,1,0:T(8,128)S(1)}, u32[]{:S(2)}, u32[]{:S(2)}) %collective-permute-start.5) | collective-permute-done | bytes 49184 | tf_op jit(solution)/shard_map/ppermute | solution.py:195
  81.8 3.5 %collective-permute-start.6 = (f32[2,3,16,256]{3,2,1,0:T(8,128)S(1)}, f32[2,3,16,256]{3,2,1,0:T(8,128)S(1)}, u32[]{:S(2)}, u32[]{:S(2)}) collective-permute-start(f32[2,3,16,256]{3,2,1,0:T(8,128)S(1)} %pad_maximum_fusion), channel_id=1, source_target_pairs={{0,8},{4,12},{8,0},{12,4},{1,9},{5,13},{9,1},{13,5},{2,10},{6,14},... | collective-permute-start | bytes 294920 | tf_op jit(solution)/shard_map/ppermute | solution.py:195
  85.3 4.8 %collective-permute-done.6.bits2 = f32[2,3,16,256]{3,2,1,0:T(8,128)S(1)} collective-permute-done((f32[2,3,16,256]{3,2,1,0:T(8,128)S(1)}, f32[2,3,16,256]{3,2,1,0:T(8,128)S(1)}, u32[]{:S(2)}, u32[]{:S(2)}) %collective-permute-start.6) | collective-permute-done | bytes 98336 | tf_op jit(solution)/shard_map/ppermute | solution.py:195
  90.1 0.7 shard_map.38.refs_0_
  90.8 3.1 %collective-permute-start.7 = (f32[4,3,16,256]{3,2,1,0:T(8,128)S(1)}, f32[4,3,16,256]{3,2,1,0:T(8,128)S(1)}, u32[]{:S(2)}, u32[]{:S(2)}) collective-permute-start(f32[4,3,16,256]{3,2,1,0:T(8,128)S(1)} %shard_map.38.refs_0_), channel_id=1, source_target_pairs={{0,1},{1,0},{2,3},{3,2},{4,5},{5,4},{6,7},{7,6},{8,9},{9,8},{10,11... | collective-permute-start | bytes 589832 | tf_op jit(solution)/shard_map/ppermute | solution.py:195
  93.9 3.0 %collective-permute-start.8 = (f32[4,3,16,256]{3,2,1,0:T(8,128)S(1)}, f32[4,3,16,256]{3,2,1,0:T(8,128)S(1)}, u32[]{:S(2)}, u32[]{:S(2)}) collective-permute-start(f32[4,3,16,256]{3,2,1,0:T(8,128)S(1)} %shard_map.38.refs_0_), channel_id=1, source_target_pairs={{0,2},{1,3},{2,0},{3,1},{4,6},{5,7},{6,4},{7,5},{8,10},{9,11},{10,... | collective-permute-start | bytes 589832 | tf_op jit(solution)/shard_map/ppermute | solution.py:195
  96.9 3.1 %collective-permute-start.9 = (f32[4,3,16,256]{3,2,1,0:T(8,128)S(1)}, f32[4,3,16,256]{3,2,1,0:T(8,128)S(1)}, u32[]{:S(2)}, u32[]{:S(2)}) collective-permute-start(f32[4,3,16,256]{3,2,1,0:T(8,128)S(1)} %shard_map.38.refs_0_), channel_id=1, source_target_pairs={{0,3},{1,2},{2,1},{3,0},{4,7},{5,6},{6,5},{7,4},{8,11},{9,10},{10,... | collective-permute-start | bytes 589832 | tf_op jit(solution)/shard_map/ppermute | solution.py:195
  100.0 0.0 collective-permute-done.7.refs_1_
  100.0 3.2 %collective-permute-done.8.refs_2_ = f32[4,3,16,256]{3,2,1,0:T(8,128)S(1)} collective-permute-done((f32[4,3,16,256]{3,2,1,0:T(8,128)S(1)}, f32[4,3,16,256]{3,2,1,0:T(8,128)S(1)}, u32[]{:S(2)}, u32[]{:S(2)}) %collective-permute-start.8) | collective-permute-done | bytes 196640 | tf_op jit(solution)/shard_map/ppermute | solution.py:195
  103.2 4.1 %collective-permute-done.9.refs_3_ = f32[4,3,16,256]{3,2,1,0:T(8,128)S(1)} collective-permute-done((f32[4,3,16,256]{3,2,1,0:T(8,128)S(1)}, f32[4,3,16,256]{3,2,1,0:T(8,128)S(1)}, u32[]{:S(2)}, u32[]{:S(2)}) %collective-permute-start.9) | collective-permute-done | bytes 196640 | tf_op jit(solution)/shard_map/ppermute | solution.py:195
  107.3 0.0 all-to-all-done.got
  107.3 1.2 shard_map.39
  108.5 1.9 %collective-permute-start.10 = (f32[3,8,256]{2,1,0:T(8,128)S(1)}, f32[3,8,256]{2,1,0:T(8,128)S(1)}, u32[]{:S(2)}, u32[]{:S(2)}) collective-permute-start(f32[3,8,256]{2,1,0:T(8,128)S(1)} %get-tuple-element.15), channel_id=1, source_target_pairs={{0,448},{1,450},{2,452},{3,454},{4,456},{5,458},{6,460},{7,462},{8... | collective-permute-start | bytes 73736 | tf_op jit(solution)/shard_map/ppermute | solution.py:227
  110.4 1.9 %collective-permute-start.11 = (f32[3,8,256]{2,1,0:T(8,128)S(1)}, f32[3,8,256]{2,1,0:T(8,128)S(1)}, u32[]{:S(2)}, u32[]{:S(2)}) collective-permute-start(f32[3,8,256]{2,1,0:T(8,128)S(1)} %get-tuple-element.16), channel_id=1, source_target_pairs={{0,449},{1,451},{2,453},{3,455},{4,457},{5,459},{6,461},{7,463},{8... | collective-permute-start | bytes 73736 | tf_op jit(solution)/shard_map/ppermute | solution.py:227
  112.3 4.0 %collective-permute-done.10.back0 = f32[3,8,256]{2,1,0:T(8,128)S(1)} collective-permute-done((f32[3,8,256]{2,1,0:T(8,128)S(1)}, f32[3,8,256]{2,1,0:T(8,128)S(1)}, u32[]{:S(2)}, u32[]{:S(2)}) %collective-permute-start.10) | collective-permute-done | bytes 24608 | tf_op jit(solution)/shard_map/ppermute | solution.py:227
  116.3 8.4 %collective-permute-done.11.back1 = f32[3,8,256]{2,1,0:T(8,128)S(1)} collective-permute-done((f32[3,8,256]{2,1,0:T(8,128)S(1)}, f32[3,8,256]{2,1,0:T(8,128)S(1)}, u32[]{:S(2)}, u32[]{:S(2)}) %collective-permute-start.11) | collective-permute-done | bytes 24608 | tf_op jit(solution)/shard_map/ppermute | solution.py:227
  124.7 1.2 shard_map.40
  (3 shorter events, 0.0 us)
Async XLA Ops:
  0.0 7.9 %collective-permute-start.2 = (f32[2,256,256]{2,1,0:T(8,128)}, f32[2,256,256]{2,1,0:T(8,128)S(1)}, u32[]{:S(2)}, u32[]{:S(2)}) collective-permute-start(f32[2,256,256]{2,1,0:T(8,128)} %bitcast.18), channel_id=1, source_target_pairs={{32,0},{33,1},{34,2},{35,3},{36,4},{37,5},{38,6},{39,7},{40,8},{41... | collective-permute-start | bytes 1572872 | tf_op jit(solution)/shard_map/ppermute | solution.py:173
  1.3 20.1 %collective-permute-start = (f32[2,256,256]{2,1,0:T(8,128)}, f32[2,256,256]{2,1,0:T(8,128)S(1)}, u32[]{:S(2)}, u32[]{:S(2)}) collective-permute-start(f32[2,256,256]{2,1,0:T(8,128)} %bitcast.25), channel_id=1, source_target_pairs={{0,64},{64,128},{128,192},{192,256},{256,320},{320,384},{384,448},... | collective-permute-start | bytes 1572872 | tf_op jit(solution)/shard_map/ppermute | solution.py:169
  6.0 18.0 %collective-permute-start.1 = (f32[2,256,256]{2,1,0:T(8,128)}, f32[2,256,256]{2,1,0:T(8,128)S(1)}, u32[]{:S(2)}, u32[]{:S(2)}) collective-permute-start(f32[2,256,256]{2,1,0:T(8,128)} %bitcast.19), channel_id=1, source_target_pairs={{0,448},{64,0},{128,64},{192,128},{256,192},{320,256},{384,320},{4... | collective-permute-start | bytes 1572872 | tf_op jit(solution)/shard_map/ppermute | solution.py:169
  7.9 31.3 %all-to-all-start.1 = ((f32[32,16,256]{2,1,0:T(8,128)}), f32[32,16,256]{2,1,0:T(8,128)S(1)}, u32[]{:S(2)}, u32[]{:S(2)}) async-start(f32[32,16,256]{2,1,0:T(8,128)} %bitcast.20), calls=%async_computation.1 | async-start | bytes 1048576 | tf_op jit(solution)/shard_map/all_to_all | solution.py:180
  24.0 3.4 %collective-permute-start.3 = (f32[2,256,256]{2,1,0:T(8,128)S(1)}, f32[2,256,256]{2,1,0:T(8,128)S(1)}, u32[]{:S(2)}, u32[]{:S(2)}) collective-permute-start(f32[2,256,256]{2,1,0:T(8,128)S(1)} %collective-permute-done.1.ahead_ref), channel_id=1, source_target_pairs={{0,32},{1,33},{2,34},{3,35},{4,36},{5,37},{6,38},{7,39},{8,40},{9,... | collective-permute-start | bytes 1572872 | tf_op jit(solution)/shard_map/ppermute | solution.py:175
  27.5 1.0 copy-start
  39.3 68.0 %all-to-all-start = ((f32[32,3,16,256]{3,2,1,0:T(8,128)}), f32[32,3,16,256]{3,2,1,0:T(8,128)S(1)}, u32[]{:S(2)}, u32[]{:S(2)}) async-start(f32[32,3,16,256]{3,2,1,0:T(8,128)} %shard_map.37), calls=%async_computation | async-start | bytes 3145728 | tf_op jit(solution)/shard_map/all_to_all | solution.py:211
  44.9 3.4 %collective-permute-start.4 = (f32[16,256]{1,0:T(8,128)S(1)}, f32[16,256]{1,0:T(8,128)S(1)}, u32[]{:S(2)}, u32[]{:S(2)}) collective-permute-start(f32[16,256]{1,0:T(8,128)S(1)} %bitcast.23), channel_id=1, source_target_pairs={{0,496},{1,497},{2,498},{3,499},{4,500},{5,501},{6,502},{7,503},{8... | collective-permute-start | bytes 49160 | tf_op jit(solution)/shard_map/ppermute | solution.py:192
  48.2 33.6 %collective-permute-start.5 = (f32[3,16,256]{2,1,0:T(8,128)S(1)}, f32[3,16,256]{2,1,0:T(8,128)S(1)}, u32[]{:S(2)}, u32[]{:S(2)}) collective-permute-start(f32[3,16,256]{2,1,0:T(8,128)S(1)} %get-tuple-element.20.bits0), channel_id=1, source_target_pairs={{0,4},{4,0},{8,12},{12,8},{1,5},{5,1},{9,13},{13,9},{2,6},{6,2},{1... | collective-permute-start | bytes 147464 | tf_op jit(solution)/shard_map/ppermute | solution.py:195
  81.8 8.3 %collective-permute-start.6 = (f32[2,3,16,256]{3,2,1,0:T(8,128)S(1)}, f32[2,3,16,256]{3,2,1,0:T(8,128)S(1)}, u32[]{:S(2)}, u32[]{:S(2)}) collective-permute-start(f32[2,3,16,256]{3,2,1,0:T(8,128)S(1)} %pad_maximum_fusion), channel_id=1, source_target_pairs={{0,8},{4,12},{8,0},{12,4},{1,9},{5,13},{9,1},{13,5},{2,10},{6,14},... | collective-permute-start | bytes 294920 | tf_op jit(solution)/shard_map/ppermute | solution.py:195
  90.8 9.2 %collective-permute-start.7 = (f32[4,3,16,256]{3,2,1,0:T(8,128)S(1)}, f32[4,3,16,256]{3,2,1,0:T(8,128)S(1)}, u32[]{:S(2)}, u32[]{:S(2)}) collective-permute-start(f32[4,3,16,256]{3,2,1,0:T(8,128)S(1)} %shard_map.38.refs_0_), channel_id=1, source_target_pairs={{0,1},{1,0},{2,3},{3,2},{4,5},{5,4},{6,7},{7,6},{8,9},{9,8},{10,11... | collective-permute-start | bytes 589832 | tf_op jit(solution)/shard_map/ppermute | solution.py:195
  93.9 9.3 %collective-permute-start.8 = (f32[4,3,16,256]{3,2,1,0:T(8,128)S(1)}, f32[4,3,16,256]{3,2,1,0:T(8,128)S(1)}, u32[]{:S(2)}, u32[]{:S(2)}) collective-permute-start(f32[4,3,16,256]{3,2,1,0:T(8,128)S(1)} %shard_map.38.refs_0_), channel_id=1, source_target_pairs={{0,2},{1,3},{2,0},{3,1},{4,6},{5,7},{6,4},{7,5},{8,10},{9,11},{10,... | collective-permute-start | bytes 589832 | tf_op jit(solution)/shard_map/ppermute | solution.py:195
  96.9 10.4 %collective-permute-start.9 = (f32[4,3,16,256]{3,2,1,0:T(8,128)S(1)}, f32[4,3,16,256]{3,2,1,0:T(8,128)S(1)}, u32[]{:S(2)}, u32[]{:S(2)}) collective-permute-start(f32[4,3,16,256]{3,2,1,0:T(8,128)S(1)} %shard_map.38.refs_0_), channel_id=1, source_target_pairs={{0,3},{1,2},{2,1},{3,0},{4,7},{5,6},{6,5},{7,4},{8,11},{9,10},{10,... | collective-permute-start | bytes 589832 | tf_op jit(solution)/shard_map/ppermute | solution.py:195
  108.5 7.8 %collective-permute-start.10 = (f32[3,8,256]{2,1,0:T(8,128)S(1)}, f32[3,8,256]{2,1,0:T(8,128)S(1)}, u32[]{:S(2)}, u32[]{:S(2)}) collective-permute-start(f32[3,8,256]{2,1,0:T(8,128)S(1)} %get-tuple-element.15), channel_id=1, source_target_pairs={{0,448},{1,450},{2,452},{3,454},{4,456},{5,458},{6,460},{7,462},{8... | collective-permute-start | bytes 73736 | tf_op jit(solution)/shard_map/ppermute | solution.py:227
  110.4 14.3 %collective-permute-start.11 = (f32[3,8,256]{2,1,0:T(8,128)S(1)}, f32[3,8,256]{2,1,0:T(8,128)S(1)}, u32[]{:S(2)}, u32[]{:S(2)}) collective-permute-start(f32[3,8,256]{2,1,0:T(8,128)S(1)} %get-tuple-element.16), channel_id=1, source_target_pairs={{0,449},{1,451},{2,453},{3,455},{4,457},{5,459},{6,461},{7,463},{8... | collective-permute-start | bytes 73736 | tf_op jit(solution)/shard_map/ppermute | solution.py:227

commit v7 on v5

--- a/solution.py
+++ b/solution.py
@@ -39,16 +39,16 @@
     return codes[pl.ds(jnp.clip(tile, 0, codes.shape[0] - 1), 1), :]
 
 
+def partners_of(code):
+    return jnp.where(code == 0, 8, jnp.where(code == 1, 4, jnp.where(code == 2, 10, 5)))
+
+
 def columns_of(codes, tiles):
-    total = codes_of(codes, tiles[0])
+    total = partners_of(codes_of(codes, tiles[0]))
     for k, tile in enumerate(tiles[1:], 1):
-        total = total + (codes_of(codes, tile) << (2 * k))
+        total = total + (partners_of(codes_of(codes, tile)) << (4 * k))
     size = codes.shape[1]
     return jnp.broadcast_to(total, (size, size)).T
-
-
-def masked(tile, total, gap):
-    return jnp.where(((total == 3) | (total == 5)) & (gap > 3), tile, 0.0)
 
 
 def product_kernel(factor, place, left_ref, ahead_ref, beside0_ref, beside1_ref, codes, home_ref, out):
@@ -56,7 +56,7 @@
     slots, size = left_ref.shape[0], left_ref.shape[1]
     rows_count = codes.shape[0] // slots
     block = size // out.shape[0]
-    col_codes = codes_of(codes, col)
+    col_bits = 1 << codes_of(codes, col)
     tile_rows = [slot * rows_count + row - 2 for slot in range(slots)]
     keys = [(slot, e) for e in (4, 3, 2) for slot in range(slots)]
     columns = columns_of(codes, [tile_rows[slot] + e for slot, e in keys])
@@ -66,15 +66,16 @@
     for k, (slot, e) in enumerate(keys):
         tile_row = tile_rows[slot]
         other = slots - 1 - slot
+        allowed = (columns & (col_bits << (4 * k))) != 0
         if e == 4:
             tile = ahead_ref[jnp.where(row >= rows_count - 2, other, slot)]
+            allowed = allowed & (gap > 3 - (col - tile_row - e) * size)
         elif e == 3:
             after = beside1_ref[jnp.where(row >= rows_count - 1, other, slot)]
             tile = jnp.where(core == 0, beside0_ref[slot], after)
         else:
             tile = home_ref[slot]
-        total = ((columns >> (2 * k)) & 3) + col_codes
-        right = halves(masked(tile, total, gap + (col - tile_row - e) * size))
+        right = halves(jnp.where(allowed, tile, 0.0))
         live = (tile_row >= 0) & (col > tile_row + TOP)
         scale = jnp.where(live, factor, 0.0).astype(F32)
         own = jnp.where((tile_row >= 0) & (col == tile_row + e), 1.0, 0.0).astype(F32)
@@ -96,30 +97,30 @@
                 out[slot * deep + z, number] = total[z * piece:(z + 1) * piece]
 
 
-def pack_kernel(wide, place, codes, bits0, bits1, bits2, out, columns):
-    row, half, x, zl = place[0], place[2], place[4], place[5]
-    part, size = out.shape[2:]
+def pack_kernel(place, codes, gathered, next1, out, columns):
+    row, half, zl = place[0], place[2], place[5]
+    count, part, size = gathered.shape[0], gathered.shape[2], out.shape[2]
     first = row + half * (codes.shape[0] // 2)
     columns[...] = columns_of(codes, [first, first + 1])
     steps = lax.broadcasted_iota(jnp.int32, (part, size), 1) - lax.broadcasted_iota(jnp.int32, (part, size), 0)
-    for i in range(out.shape[0]):
-        start = pl.multiple_of(((zl ^ i) * wide + x) * part, part)
+    for i in range(count):
+        start = pl.multiple_of((zl * count + i) * part, part)
         down = columns[pl.ds(start, part), :]
         for k, (at, beyond) in enumerate(((0, 1), (0, 2), (1, 1))):
-            piece = bits0[k] if i == 0 else bits1[k] if i == 1 else bits2[i - 2, k]
-            total = ((down >> (2 * at)) & 3) + codes_of(codes, first + at + beyond)
-            out[i, k] = masked(piece, total, steps - start + beyond * size)
+            piece = gathered[i, k] if k < 2 else next1[i]
+            allowed = (down & (1 << (codes_of(codes, first + at + beyond) + 4 * at))) != 0
+            far = steps > 3 + start - beyond * size
+            out[k, i * part:(i + 1) * part] = jnp.where(allowed & far, piece, 0.0)
 
 
 def finish_kernel(factor, place, got, *refs):
     packs, out_a, out_b, whole, rows = refs[:-4], refs[-4], refs[-3], refs[-2], refs[-1]
-    half, x, zl = place[2], place[4], place[5]
-    deep, _, part, _ = packs[0].shape
+    half, zl = place[2], place[5]
+    rows_each = packs[0].shape[1]
     for j, pack in enumerate(packs):
-        for i in range(deep):
-            start = pl.multiple_of(((zl ^ i) * len(packs) + (x ^ j)) * part, part)
-            for k in range(3):
-                whole[k, pl.ds(start, part), :] = pack[i, k]
+        start = pl.multiple_of((zl ^ j) * rows_each, rows_each)
+        for k in range(3):
+            whole[k, pl.ds(start, rows_each), :] = pack[k]
     sums = []
     for w in range(WIN):
         total = got[0, w]
@@ -186,8 +187,7 @@
 
     codes = sequence.reshape(tile_count, size)
 
-    spread, beside0 = lax.optimization_barrier((home.reshape(cols_count, part, size), beside0))
-    spread = lax.all_to_all(spread, AXES[2:], 0, 0)
+    spread = lax.all_to_all(home.reshape(cols_count, part, size), AXES[2:], 0, 0)
     first = jnp.minimum(row + half * rows_count + 1, cols_count - 1)
     second = jnp.minimum(row + half * rows_count + 2, cols_count - 1)
     near1 = lax.dynamic_index_in_dim(spread, first, 0, False)
@@ -199,7 +199,8 @@
         r = (r - 1) % rows_count
         return r // sizes[1], r % sizes[1], zh, zl, x
 
-    next1 = lax.ppermute(near1, AXES, pairs_of(sizes, previous_row))
+    near = jnp.stack([near1, near2])
+    gathered = lax.all_to_all(jnp.broadcast_to(near, (sizes[4],) + near.shape), "x", 0, 0)
 
     def partner(v, axis, n, j):
         return lax.ppermute(v, axis, [(i, i ^ j) for i in range(n)])
@@ -210,18 +211,17 @@
         1, [wide], [], WIN * slots * 6 * size**3,
         place, left, ahead, beside0, beside1, codes, home,
     )
-    bits0 = jnp.stack([near1, near2, next1])
-    bits1 = partner(bits0, "zl", sizes[3], 1)
-    bits2 = partner(jnp.stack([bits0, bits1]), "zl", sizes[3], 2)
+    parts, gathered = lax.optimization_barrier((parts, gathered))
+    next1 = lax.ppermute(gathered[:, 0], AXES, pairs_of(sizes, previous_row))
     (pack,) = call(
-        functools.partial(pack_kernel, sizes[4]),
-        1, [(sizes[3], 3, part, size)], [pltpu.VMEM((size, size), jnp.int32)], 10**6,
-        place, codes, bits0, bits1, bits2,
-    )
-    packs = [pack] + [partner(pack, "x", sizes[4], j) for j in range(1, sizes[4])]
+        pack_kernel, 1, [(3, sizes[4] * part, size)], [pltpu.VMEM((size, size), jnp.int32)], 10**6,
+        place, codes, gathered, next1,
+    )
+    packs = [pack] + [partner(pack, "zl", sizes[3], j) for j in range(1, sizes[3])]
     parts = lax.all_to_all(parts, "x", 0, 0)
     parts, _ = lax.optimization_barrier((parts, pack))
     (ready,) = call(add_kernel, 0, [(slots * sizes[3], WIN, part, size)], [], 10**6, parts)
+    ready, *packs = lax.optimization_barrier((ready, *packs))
     got = lax.all_to_all(ready, ("zh", "zl"), 0, 0)
     piece = part // slots
     sent = call(

time: 112 us -> 118 us (1.054)
  the two profiles are of different devices: /device:TPU:4 before, /device:TPU:28 now
where the time goes in v7:
time: 118 us; the launch traced here: 117 us
  starting transfers between devices  53.3 us (45%)
  waiting for transfers between devices  35.6 us (30%)
  blocking collectives  21.5 us (18%)
  Pallas kernels  5.95 us (5%)
    all_to_all x1, blocking collectives, on_device(): got = lax.all_to_all(ready, ('zh', 'zl'), 0, 0)  21.5 us
    all_to_all x1, starting transfers between devices, on_device(): lax.all_to_all(home.reshape(cols_count, part, size), AXES[2:], 0, 0)  13.6 us
    ppermute x2, waiting for transfers between devices, row_shift(): return lax.ppermute(v, 'y', [(i, (i + by) % n) for i in range(n)])  12.9 us
    ppermute x3, waiting for transfers between devices, partner(): return lax.ppermute(v, axis, [(i, i ^ j) for i in range(n)])  11.7 us
    ppermute x3, starting transfers between devices, partner(): return lax.ppermute(v, axis, [(i, i ^ j) for i in range(n)])  10.1 us
    ppermute x2, waiting for transfers between devices, on_device(): lax.ppermute(sent[flip], AXES, pairs_of(sizes, sent_to(flip)))  8.6 us
    ppermute x2, starting transfers between devices, on_device(): lax.ppermute(sent[flip], AXES, pairs_of(sizes, sent_to(flip)))  7.46 us
    ppermute x2, starting transfers between devices, row_shift(): return lax.ppermute(v, 'y', [(i, (i + by) % n) for i in range(n)])  6.62 us
  transfers between devices with their start and end apart: 13, of which 8 were waited for; matrix products, arithmetic and copies ran while one was open for 1% of the time, Pallas kernels for 3%

profile of v7, /device:TPU:28, one launch (start us, length us, event | category | flops | bytes accessed | tf_op | source)
XLA Modules:
  0.0 117.3 jit_solution(6673279103946186387)
XLA Ops:
  0.0 0.0 copy-start
  0.0 0.0 copy-start.1
  0.0 13.6 %all-to-all-start = ((f32[32,16,256]{2,1,0:T(8,128)}), f32[32,16,256]{2,1,0:T(8,128)S(1)}, u32[]{:S(2)}, u32[]{:S(2)}) async-start(f32[32,16,256]{2,1,0:T(8,128)} %bitcast.15), calls=%async_computation | async-start | bytes 1048576 | tf_op jit(solution)/shard_map/all_to_all | solution.py:190
  13.6 4.7 %collective-permute-start = (f32[2,256,256]{2,1,0:T(8,128)}, f32[2,256,256]{2,1,0:T(8,128)S(1)}, u32[]{:S(2)}, u32[]{:S(2)}) collective-permute-start(f32[2,256,256]{2,1,0:T(8,128)} %bitcast.19), channel_id=1, source_target_pairs={{0,64},{64,128},{128,192},{192,256},{256,320},{320,384},{384,448},... | collective-permute-start | bytes 1572872 | tf_op jit(solution)/shard_map/ppermute | solution.py:180
  18.3 1.9 %collective-permute-start.1 = (f32[2,256,256]{2,1,0:T(8,128)}, f32[2,256,256]{2,1,0:T(8,128)S(1)}, u32[]{:S(2)}, u32[]{:S(2)}) collective-permute-start(f32[2,256,256]{2,1,0:T(8,128)} %bitcast.16), channel_id=1, source_target_pairs={{0,448},{64,0},{128,64},{192,128},{256,192},{320,256},{384,320},{4... | collective-permute-start | bytes 1572872 | tf_op jit(solution)/shard_map/ppermute | solution.py:180
  20.2 1.3 %collective-permute-start.2 = (f32[2,256,256]{2,1,0:T(8,128)}, f32[2,256,256]{2,1,0:T(8,128)S(1)}, u32[]{:S(2)}, u32[]{:S(2)}) collective-permute-start(f32[2,256,256]{2,1,0:T(8,128)} %bitcast.17), channel_id=1, source_target_pairs={{32,0},{33,1},{34,2},{35,3},{36,4},{37,5},{38,6},{39,7},{40,8},{41... | collective-permute-start | bytes 1572872 | tf_op jit(solution)/shard_map/ppermute | solution.py:184
  21.5 7.7 %collective-permute-done.left_ref = f32[2,256,256]{2,1,0:T(8,128)S(1)} collective-permute-done((f32[2,256,256]{2,1,0:T(8,128)}, f32[2,256,256]{2,1,0:T(8,128)S(1)}, u32[]{:S(2)}, u32[]{:S(2)}) %collective-permute-start) | collective-permute-done | bytes 524320 | tf_op jit(solution)/shard_map/ppermute | solution.py:180
  29.2 5.2 %collective-permute-done.1.ahead_ref = f32[2,256,256]{2,1,0:T(8,128)S(1)} collective-permute-done((f32[2,256,256]{2,1,0:T(8,128)}, f32[2,256,256]{2,1,0:T(8,128)S(1)}, u32[]{:S(2)}, u32[]{:S(2)}) %collective-permute-start.1) | collective-permute-done | bytes 524320 | tf_op jit(solution)/shard_map/ppermute | solution.py:180
  34.4 1.3 %collective-permute-start.3 = (f32[2,256,256]{2,1,0:T(8,128)S(1)}, f32[2,256,256]{2,1,0:T(8,128)S(1)}, u32[]{:S(2)}, u32[]{:S(2)}) collective-permute-start(f32[2,256,256]{2,1,0:T(8,128)S(1)} %collective-permute-done.1.ahead_ref), channel_id=1, source_target_pairs={{0,32},{1,33},{2,34},{3,35},{4,36},{5,37},{6,38},{7,39},{8,40},{9,... | collective-permute-start | bytes 1572872 | tf_op jit(solution)/shard_map/ppermute | solution.py:186
  35.8 0.0 all-to-all-done
  35.8 0.7 broadcast_in_dim.6
  36.5 4.8 %all-to-all-start.1 = ((f32[4,2,16,256]{3,2,1,0:T(8,128)}), f32[4,2,16,256]{3,2,1,0:T(8,128)S(1)}, u32[]{:S(2)}, u32[]{:S(2)}) async-start(f32[4,2,16,256]{3,2,1,0:T(8,128)} %broadcast_in_dim.6), calls=%async_computation.1 | async-start | bytes 262144 | tf_op jit(solution)/shard_map/all_to_all | solution.py:203
  41.3 0.0 copy-done.1
  41.3 0.1 stack.40.place
  41.4 0.0 collective-permute-done.2.beside0_ref
  41.4 0.0 collective-permute-done.3.beside1_ref
  41.4 0.0 copy-done
  41.4 2.9 %shard_map.37 = f32[4,3,2,64,256]{4,3,2,1,0:T(8,128)} custom-call(s32[7]{0:T(128)S(1)} %stack.40.place, f32[2,256,256]{2,1,0:T(8,128)S(1)} %collective-permute-done.left_ref, f32[2,256,256]{2,1,0:T(8,128)S(1)} %collective-permute-done.1.ahead_ref, f32[2,256,256]{2,1,0:T(8,128)S(1)} %collective-permute-done.2.beside0_ref, ...), custom_call_target="tpu_custom_call" | custom-call | flops 603979776 | bytes 4227100 | tf_op jit(solution)/shard_map/pallas_call | solution.py:150
  44.2 0.3 all-to-all-done.1.gathered
  44.5 6.2 %all-to-all-start.2 = ((f32[4,3,2,64,256]{4,3,2,1,0:T(8,128)}), f32[4,3,2,64,256]{4,3,2,1,0:T(8,128)S(1)}, u32[]{:S(2)}, u32[]{:S(2)}) async-start(f32[4,3,2,64,256]{4,3,2,1,0:T(8,128)} %shard_map.37), calls=%async_computation.2 | async-start | bytes 3145728 | tf_op jit(solution)/shard_map/all_to_all | solution.py:221
  50.8 1.9 %collective-permute-start.4 = (f32[4,16,256]{2,1,0:T(8,128)S(1)}, f32[4,16,256]{2,1,0:T(8,128)S(1)}, u32[]{:S(2)}, u32[]{:S(2)}) collective-permute-start(f32[4,16,256]{2,1,0:T(8,128)S(1)} %slice_bitcast_fusion), channel_id=1, source_target_pairs={{0,496},{1,497},{2,498},{3,499},{4,500},{5,501},{6,502},{7,503},{8... | collective-permute-start | bytes 196616 | tf_op jit(solution)/shard_map/ppermute | solution.py:215
  52.7 1.9 %collective-permute-done.4.next1 = f32[4,16,256]{2,1,0:T(8,128)S(1)} collective-permute-done((f32[4,16,256]{2,1,0:T(8,128)S(1)}, f32[4,16,256]{2,1,0:T(8,128)S(1)}, u32[]{:S(2)}, u32[]{:S(2)}) %collective-permute-start.4) | collective-permute-done | bytes 65568 | tf_op jit(solution)/shard_map/ppermute | solution.py:215
  54.6 0.7 shard_map.38.refs_0_
  55.3 3.4 %collective-permute-start.5 = (f32[3,64,256]{2,1,0:T(8,128)S(1)}, f32[3,64,256]{2,1,0:T(8,128)S(1)}, u32[]{:S(2)}, u32[]{:S(2)}) collective-permute-start(f32[3,64,256]{2,1,0:T(8,128)S(1)} %shard_map.38.refs_0_), channel_id=1, source_target_pairs={{0,4},{4,0},{8,12},{12,8},{1,5},{5,1},{9,13},{13,9},{2,6},{6,2},{1... | collective-permute-start | bytes 589832 | tf_op jit(solution)/shard_map/ppermute | solution.py:206
  58.6 4.3 %collective-permute-start.6 = (f32[3,64,256]{2,1,0:T(8,128)S(1)}, f32[3,64,256]{2,1,0:T(8,128)S(1)}, u32[]{:S(2)}, u32[]{:S(2)}) collective-permute-start(f32[3,64,256]{2,1,0:T(8,128)S(1)} %shard_map.38.refs_0_), channel_id=1, source_target_pairs={{0,8},{4,12},{8,0},{12,4},{1,9},{5,13},{9,1},{13,5},{2,10},{6,14},... | collective-permute-start | bytes 589832 | tf_op jit(solution)/shard_map/ppermute | solution.py:206
  62.9 2.5 %collective-permute-start.7 = (f32[3,64,256]{2,1,0:T(8,128)S(1)}, f32[3,64,256]{2,1,0:T(8,128)S(1)}, u32[]{:S(2)}, u32[]{:S(2)}) collective-permute-start(f32[3,64,256]{2,1,0:T(8,128)S(1)} %shard_map.38.refs_0_), channel_id=1, source_target_pairs={{0,12},{4,8},{8,4},{12,0},{1,13},{5,9},{9,5},{13,1},{2,14},{6,10},... | collective-permute-start | bytes 589832 | tf_op jit(solution)/shard_map/ppermute | solution.py:206
  65.4 0.2 all-to-all-done.2.got
  65.6 0.1 shard_map.39
  65.6 0.0 collective-permute-done.5.refs_1_
  65.7 11.7 %collective-permute-done.6.refs_2_ = f32[3,64,256]{2,1,0:T(8,128)S(1)} collective-permute-done((f32[3,64,256]{2,1,0:T(8,128)S(1)}, f32[3,64,256]{2,1,0:T(8,128)S(1)}, u32[]{:S(2)}, u32[]{:S(2)}) %collective-permute-start.6) | collective-permute-done | bytes 196640 | tf_op jit(solution)/shard_map/ppermute | solution.py:206
  77.4 0.0 collective-permute-done.7.refs_3_
  77.4 21.5 %all_to_all.20.got = f32[8,3,16,256]{3,2,1,0:T(8,128)S(1)} all-to-all(f32[8,3,16,256]{3,2,1,0:T(8,128)S(1)} %shard_map.39), channel_id=1, replica_groups=mesh['y'=8,'core'=2,'zh'=2,'zl'=4,'x'=4] {'zh','zl'}, dimensions={0} | all-to-all | bytes 786432 | tf_op jit(solution)/shard_map/all_to_all | solution.py:225
  98.9 1.2 %shard_map.40 = (f32[3,8,256]{2,1,0:T(8,128)S(1)}, f32[3,8,256]{2,1,0:T(8,128)S(1)}) custom-call(s32[7]{0:T(128)S(1)} %stack.40.place, f32[8,3,16,256]{3,2,1,0:T(8,128)S(1)} %all_to_all.20.got, f32[3,64,256]{2,1,0:T(8,128)S(1)} %shard_map.38.refs_0_, f32[3,64,256]{2,1,0:T(8,128)S(1)} %collective-permute-done.5.refs_1_, ...), custom_call_target="tpu_custom_call" | custom-call | flops 18874368 | bytes 1228828 | tf_op jit(solution)/shard_map/pallas_call | solution.py:150
  100.0 2.8 %collective-permute-start.8 = (f32[3,8,256]{2,1,0:T(8,128)S(1)}, f32[3,8,256]{2,1,0:T(8,128)S(1)}, u32[]{:S(2)}, u32[]{:S(2)}) collective-permute-start(f32[3,8,256]{2,1,0:T(8,128)S(1)} %get-tuple-element.27), channel_id=1, source_target_pairs={{0,448},{1,456},{2,464},{3,472},{4,450},{5,458},{6,466},{7,474},{8... | collective-permute-start | bytes 73736 | tf_op jit(solution)/shard_map/ppermute | solution.py:241
  102.9 4.6 %collective-permute-start.9 = (f32[3,8,256]{2,1,0:T(8,128)S(1)}, f32[3,8,256]{2,1,0:T(8,128)S(1)}, u32[]{:S(2)}, u32[]{:S(2)}) collective-permute-start(f32[3,8,256]{2,1,0:T(8,128)S(1)} %get-tuple-element.28), channel_id=1, source_target_pairs={{0,449},{1,457},{2,465},{3,473},{4,451},{5,459},{6,467},{7,475},{8... | collective-permute-start | bytes 73736 | tf_op jit(solution)/shard_map/ppermute | solution.py:241
  107.5 2.8 %collective-permute-done.8.back0 = f32[3,8,256]{2,1,0:T(8,128)S(1)} collective-permute-done((f32[3,8,256]{2,1,0:T(8,128)S(1)}, f32[3,8,256]{2,1,0:T(8,128)S(1)}, u32[]{:S(2)}, u32[]{:S(2)}) %collective-permute-start.8) | collective-permute-done | bytes 24608 | tf_op jit(solution)/shard_map/ppermute | solution.py:241
  110.3 5.8 %collective-permute-done.9.back1 = f32[3,8,256]{2,1,0:T(8,128)S(1)} collective-permute-done((f32[3,8,256]{2,1,0:T(8,128)S(1)}, f32[3,8,256]{2,1,0:T(8,128)S(1)}, u32[]{:S(2)}, u32[]{:S(2)}) %collective-permute-start.9) | collective-permute-done | bytes 24608 | tf_op jit(solution)/shard_map/ppermute | solution.py:241
  116.1 1.2 %shard_map.41 = f32[3,2,8,256]{3,2,1,0:T(8,128)} custom-call(s32[7]{0:T(128)S(1)} %stack.40.place, f32[3,8,256]{2,1,0:T(8,128)S(1)} %collective-permute-done.8.back0, f32[3,8,256]{2,1,0:T(8,128)S(1)} %collective-permute-done.9.back1), custom_call_target="tpu_custom_call" | custom-call | flops 10000 | bytes 98332 | tf_op jit(solution)/shard_map/pallas_call | solution.py:150
  (4 shorter events, 0.0 us)
Async XLA Ops:
  0.0 41.4 %copy-start = (f32[2,1,1,1,256,256]{5,4,3,2,1,0:T(8,128)S(1)}, f32[2,1,1,1,256,256]{5,4,3,2,1,0:T(8,128)}, u32[]{:S(2)}) copy-start(f32[2,1,1,1,256,256]{5,4,3,2,1,0:T(8,128)} %param.3) | copy-start | bytes 1572868
  0.0 41.3 %copy-start.1 = (s32[8192]{0:T(1024)S(1)}, s32[8192]{0:T(1024)}, u32[]{:S(2)}) copy-start(s32[8192]{0:T(1024)} %param.5) | copy-start | bytes 98308
  0.0 35.8 %all-to-all-start = ((f32[32,16,256]{2,1,0:T(8,128)}), f32[32,16,256]{2,1,0:T(8,128)S(1)}, u32[]{:S(2)}, u32[]{:S(2)}) async-start(f32[32,16,256]{2,1,0:T(8,128)} %bitcast.15), calls=%async_computation | async-start | bytes 1048576 | tf_op jit(solution)/shard_map/all_to_all | solution.py:190
  13.6 15.6 %collective-permute-start = (f32[2,256,256]{2,1,0:T(8,128)}, f32[2,256,256]{2,1,0:T(8,128)S(1)}, u32[]{:S(2)}, u32[]{:S(2)}) collective-permute-start(f32[2,256,256]{2,1,0:T(8,128)} %bitcast.19), channel_id=1, source_target_pairs={{0,64},{64,128},{128,192},{192,256},{256,320},{320,384},{384,448},... | collective-permute-start | bytes 1572872 | tf_op jit(solution)/shard_map/ppermute | solution.py:180
  18.3 16.1 %collective-permute-start.1 = (f32[2,256,256]{2,1,0:T(8,128)}, f32[2,256,256]{2,1,0:T(8,128)S(1)}, u32[]{:S(2)}, u32[]{:S(2)}) collective-permute-start(f32[2,256,256]{2,1,0:T(8,128)} %bitcast.16), channel_id=1, source_target_pairs={{0,448},{64,0},{128,64},{192,128},{256,192},{320,256},{384,320},{4... | collective-permute-start | bytes 1572872 | tf_op jit(solution)/shard_map/ppermute | solution.py:180
  20.2 21.2 %collective-permute-start.2 = (f32[2,256,256]{2,1,0:T(8,128)}, f32[2,256,256]{2,1,0:T(8,128)S(1)}, u32[]{:S(2)}, u32[]{:S(2)}) collective-permute-start(f32[2,256,256]{2,1,0:T(8,128)} %bitcast.17), channel_id=1, source_target_pairs={{32,0},{33,1},{34,2},{35,3},{36,4},{37,5},{38,6},{39,7},{40,8},{41... | collective-permute-start | bytes 1572872 | tf_op jit(solution)/shard_map/ppermute | solution.py:184
  34.4 6.9 %collective-permute-start.3 = (f32[2,256,256]{2,1,0:T(8,128)S(1)}, f32[2,256,256]{2,1,0:T(8,128)S(1)}, u32[]{:S(2)}, u32[]{:S(2)}) collective-permute-start(f32[2,256,256]{2,1,0:T(8,128)S(1)} %collective-permute-done.1.ahead_ref), channel_id=1, source_target_pairs={{0,32},{1,33},{2,34},{3,35},{4,36},{5,37},{6,38},{7,39},{8,40},{9,... | collective-permute-start | bytes 1572872 | tf_op jit(solution)/shard_map/ppermute | solution.py:186
  36.5 8.1 %all-to-all-start.1 = ((f32[4,2,16,256]{3,2,1,0:T(8,128)}), f32[4,2,16,256]{3,2,1,0:T(8,128)S(1)}, u32[]{:S(2)}, u32[]{:S(2)}) async-start(f32[4,2,16,256]{3,2,1,0:T(8,128)} %broadcast_in_dim.6), calls=%async_computation.1 | async-start | bytes 262144 | tf_op jit(solution)/shard_map/all_to_all | solution.py:203
  44.5 21.0 %all-to-all-start.2 = ((f32[4,3,2,64,256]{4,3,2,1,0:T(8,128)}), f32[4,3,2,64,256]{4,3,2,1,0:T(8,128)S(1)}, u32[]{:S(2)}, u32[]{:S(2)}) async-start(f32[4,3,2,64,256]{4,3,2,1,0:T(8,128)} %shard_map.37), calls=%async_computation.2 | async-start | bytes 3145728 | tf_op jit(solution)/shard_map/all_to_all | solution.py:221
  50.8 3.8 %collective-permute-start.4 = (f32[4,16,256]{2,1,0:T(8,128)S(1)}, f32[4,16,256]{2,1,0:T(8,128)S(1)}, u32[]{:S(2)}, u32[]{:S(2)}) collective-permute-start(f32[4,16,256]{2,1,0:T(8,128)S(1)} %slice_bitcast_fusion), channel_id=1, source_target_pairs={{0,496},{1,497},{2,498},{3,499},{4,500},{5,501},{6,502},{7,503},{8... | collective-permute-start | bytes 196616 | tf_op jit(solution)/shard_map/ppermute | solution.py:215
  55.3 10.4 %collective-permute-start.5 = (f32[3,64,256]{2,1,0:T(8,128)S(1)}, f32[3,64,256]{2,1,0:T(8,128)S(1)}, u32[]{:S(2)}, u32[]{:S(2)}) collective-permute-start(f32[3,64,256]{2,1,0:T(8,128)S(1)} %shard_map.38.refs_0_), channel_id=1, source_target_pairs={{0,4},{4,0},{8,12},{12,8},{1,5},{5,1},{9,13},{13,9},{2,6},{6,2},{1... | collective-permute-start | bytes 589832 | tf_op jit(solution)/shard_map/ppermute | solution.py:206
  58.6 18.7 %collective-permute-start.6 = (f32[3,64,256]{2,1,0:T(8,128)S(1)}, f32[3,64,256]{2,1,0:T(8,128)S(1)}, u32[]{:S(2)}, u32[]{:S(2)}) collective-permute-start(f32[3,64,256]{2,1,0:T(8,128)S(1)} %shard_map.38.refs_0_), channel_id=1, source_target_pairs={{0,8},{4,12},{8,0},{12,4},{1,9},{5,13},{9,1},{13,5},{2,10},{6,14},... | collective-permute-start | bytes 589832 | tf_op jit(solution)/shard_map/ppermute | solution.py:206
  62.9 14.5 %collective-permute-start.7 = (f32[3,64,256]{2,1,0:T(8,128)S(1)}, f32[3,64,256]{2,1,0:T(8,128)S(1)}, u32[]{:S(2)}, u32[]{:S(2)}) collective-permute-start(f32[3,64,256]{2,1,0:T(8,128)S(1)} %shard_map.38.refs_0_), channel_id=1, source_target_pairs={{0,12},{4,8},{8,4},{12,0},{1,13},{5,9},{9,5},{13,1},{2,14},{6,10},... | collective-permute-start | bytes 589832 | tf_op jit(solution)/shard_map/ppermute | solution.py:206
  100.0 10.2 %collective-permute-start.8 = (f32[3,8,256]{2,1,0:T(8,128)S(1)}, f32[3,8,256]{2,1,0:T(8,128)S(1)}, u32[]{:S(2)}, u32[]{:S(2)}) collective-permute-start(f32[3,8,256]{2,1,0:T(8,128)S(1)} %get-tuple-element.27), channel_id=1, source_target_pairs={{0,448},{1,456},{2,464},{3,472},{4,450},{5,458},{6,466},{7,474},{8... | collective-permute-start | bytes 73736 | tf_op jit(solution)/shard_map/ppermute | solution.py:241
  102.9 13.2 %collective-permute-start.9 = (f32[3,8,256]{2,1,0:T(8,128)S(1)}, f32[3,8,256]{2,1,0:T(8,128)S(1)}, u32[]{:S(2)}, u32[]{:S(2)}) collective-permute-start(f32[3,8,256]{2,1,0:T(8,128)S(1)} %get-tuple-element.28), channel_id=1, source_target_pairs={{0,449},{1,457},{2,465},{3,473},{4,451},{5,459},{6,467},{7,475},{8... | collective-permute-start | bytes 73736 | tf_op jit(solution)/shard_map/ppermute | solution.py:241

commit v8 on v7

--- a/solution.py
+++ b/solution.py
@@ -97,30 +97,36 @@
                 out[slot * deep + z, number] = total[z * piece:(z + 1) * piece]
 
 
-def pack_kernel(place, codes, gathered, next1, out, columns):
-    row, half, zl = place[0], place[2], place[5]
-    count, part, size = gathered.shape[0], gathered.shape[2], out.shape[2]
+def pack_kernel(wide, place, codes, gathered, next1, out, columns):
+    row, half, x = place[0], place[2], place[4]
+    count, part, size = gathered.shape[0], gathered.shape[2], out.shape[3]
     first = row + half * (codes.shape[0] // 2)
     columns[...] = columns_of(codes, [first, first + 1])
     steps = lax.broadcasted_iota(jnp.int32, (part, size), 1) - lax.broadcasted_iota(jnp.int32, (part, size), 0)
     for i in range(count):
-        start = pl.multiple_of((zl * count + i) * part, part)
+        start = pl.multiple_of((i * wide + x) * part, part)
         down = columns[pl.ds(start, part), :]
         for k, (at, beyond) in enumerate(((0, 1), (0, 2), (1, 1))):
             piece = gathered[i, k] if k < 2 else next1[i]
             allowed = (down & (1 << (codes_of(codes, first + at + beyond) + 4 * at))) != 0
             far = steps > 3 + start - beyond * size
-            out[k, i * part:(i + 1) * part] = jnp.where(allowed & far, piece, 0.0)
-
-
-def finish_kernel(factor, place, got, *refs):
-    packs, out_a, out_b, whole, rows = refs[:-4], refs[-4], refs[-3], refs[-2], refs[-1]
-    half, zl = place[2], place[5]
-    rows_each = packs[0].shape[1]
-    for j, pack in enumerate(packs):
-        start = pl.multiple_of((zl ^ j) * rows_each, rows_each)
-        for k in range(3):
-            whole[k, pl.ds(start, rows_each), :] = pack[k]
+            out[k, i] = jnp.where(allowed & far, piece, 0.0)
+
+
+def assemble_kernel(place, *refs):
+    packs, high, low, whole = refs[:-3], refs[-3], refs[-2], refs[-1]
+    x = place[4]
+    _, deep, part, _ = packs[0].shape
+    for k in range(3):
+        for j, pack in enumerate(packs):
+            for i in range(deep):
+                start = pl.multiple_of((i * len(packs) + (x ^ j)) * part, part)
+                whole[k, pl.ds(start, part), :] = pack[k, i]
+        high[k], low[k] = halves(whole[k])
+
+
+def finish_kernel(factor, place, got, high, low, out_a, out_b, rows):
+    half = place[2]
     sums = []
     for w in range(WIN):
         total = got[0, w]
@@ -129,8 +135,8 @@
         sums.append(total)
     w4 = sums[0]
     w4_halves = halves(w4)
-    w3 = sums[1] + factor * times(w4_halves, halves(whole[2]))
-    w2 = sums[2] + factor * (times(w4_halves, halves(whole[1])) + times(halves(w3), halves(whole[0])))
+    w3 = sums[1] + factor * times(w4_halves, (high[2], low[2]))
+    w2 = sums[2] + factor * (times(w4_halves, (high[1], low[1])) + times(halves(w3), (high[0], low[0])))
     piece = out_a.shape[1]
     for w, value in enumerate((w4, w3, w2)):
         rows[w] = value
@@ -144,12 +150,12 @@
     out[:, 1] = jnp.where(swap, back0[...], back1[...])
 
 
-def call(kernel, in_count, outs, scratch, flops, *args):
+def call(kernel, in_count, outs, scratch, flops, *args, kind=F32):
     spec = pl.BlockSpec(memory_space=pltpu.VMEM)
     moved = sum(math.prod(a.shape) * 4 for a in args) + sum(math.prod(s) * 4 for s in outs)
     return pl.pallas_call(
         kernel,
-        out_shape=[jax.ShapeDtypeStruct(s, F32) for s in outs],
+        out_shape=[jax.ShapeDtypeStruct(s, kind) for s in outs],
         in_specs=[pl.BlockSpec(memory_space=pltpu.SMEM)] * in_count + [spec] * (len(args) - in_count),
         out_specs=[spec] * len(outs),
         scratch_shapes=scratch,
@@ -200,7 +206,7 @@
         return r // sizes[1], r % sizes[1], zh, zl, x
 
     near = jnp.stack([near1, near2])
-    gathered = lax.all_to_all(jnp.broadcast_to(near, (sizes[4],) + near.shape), "x", 0, 0)
+    gathered = lax.all_to_all(jnp.broadcast_to(near, (sizes[3],) + near.shape), "zl", 0, 0)
 
     def partner(v, axis, n, j):
         return lax.ppermute(v, axis, [(i, i ^ j) for i in range(n)])
@@ -214,20 +220,24 @@
     parts, gathered = lax.optimization_barrier((parts, gathered))
     next1 = lax.ppermute(gathered[:, 0], AXES, pairs_of(sizes, previous_row))
     (pack,) = call(
-        pack_kernel, 1, [(3, sizes[4] * part, size)], [pltpu.VMEM((size, size), jnp.int32)], 10**6,
+        functools.partial(pack_kernel, sizes[4]),
+        1, [(3, sizes[3], part, size)], [pltpu.VMEM((size, size), jnp.int32)], 10**6,
         place, codes, gathered, next1,
     )
-    packs = [pack] + [partner(pack, "zl", sizes[3], j) for j in range(1, sizes[3])]
+    packs = {j: partner(pack, "x", sizes[4], j) for j in (2, 1, 3)}
+    high, low = call(
+        assemble_kernel, 1, [(3, size, size)] * 2, [pltpu.VMEM((3, size, size), F32)], 2 * 10**10,
+        place, pack, *(packs[j] for j in range(1, sizes[4])), kind=jnp.bfloat16,
+    )
     parts = lax.all_to_all(parts, "x", 0, 0)
     parts, _ = lax.optimization_barrier((parts, pack))
     (ready,) = call(add_kernel, 0, [(slots * sizes[3], WIN, part, size)], [], 10**6, parts)
-    ready, *packs = lax.optimization_barrier((ready, *packs))
     got = lax.all_to_all(ready, ("zh", "zl"), 0, 0)
     piece = part // slots
     sent = call(
         functools.partial(finish_kernel, factor),
-        1, [(WIN, piece, size)] * 2, [pltpu.VMEM((3, size, size), F32), pltpu.VMEM((WIN, part, size), F32)],
-        3 * 6 * part * size**2, place, got, *packs,
+        1, [(WIN, piece, size)] * 2, [pltpu.VMEM((WIN, part, size), F32)],
+        3 * 6 * part * size**2, place, got, high, low,
     )
 
     def sent_to(flip):

time: 118 us -> 109 us (0.924)
  the two profiles are of different devices: /device:TPU:28 before, /device:TPU:4 now
where the time goes in v8:
time: 109 us; the launch traced here: 108 us
  starting transfers between devices  65.8 us (60%)
  waiting for transfers between devices  34.3 us (31%)
  Pallas kernels  7.39 us (7%)
    all_to_all x1, starting transfers between devices, on_device(): lax.all_to_all(home.reshape(cols_count, part, size), AXES[2:], 0, 0)  13.6 us
    ppermute x2, starting transfers between devices, on_device(): lax.ppermute(sent[flip], AXES, pairs_of(sizes, sent_to(flip)))  12.7 us
    all_to_all x1, waiting for transfers between devices, on_device(): got = lax.all_to_all(ready, ('zh', 'zl'), 0, 0)  10.6 us
    ppermute x2, waiting for transfers between devices, row_shift(): return lax.ppermute(v, 'y', [(i, (i + by) % n) for i in range(n)])  9.81 us
    ppermute x3, starting transfers between devices, partner(): return lax.ppermute(v, axis, [(i, i ^ j) for i in range(n)])  9.21 us
    ppermute x2, waiting for transfers between devices, on_device(): lax.ppermute(sent[flip], AXES, pairs_of(sizes, sent_to(flip)))  7.88 us
    pallas_call x6, Pallas kernels, call(): pl.pallas_call(kernel, out_shape=[jax.ShapeDtypeStruct(s, kind) for s in...  7.39 us
    ppermute x2, starting transfers between devices, row_shift(): return lax.ppermute(v, 'y', [(i, (i + by) % n) for i in range(n)])  7.3 us
  transfers between devices with their start and end apart: 14, of which 8 were waited for; matrix products, arithmetic and copies ran while one was open for 1% of the time, Pallas kernels for 5%

profile of v8, /device:TPU:4, one launch (start us, length us, event | category | flops | bytes accessed | tf_op | source)
XLA Modules:
  0.0 108.5 jit_solution(4206068229263926190)
XLA Ops:
  0.0 0.0 copy-start
  0.0 0.0 copy-start.1
  0.0 13.6 %all-to-all-start = ((f32[32,16,256]{2,1,0:T(8,128)}), f32[32,16,256]{2,1,0:T(8,128)S(1)}, u32[]{:S(2)}, u32[]{:S(2)}) async-start(f32[32,16,256]{2,1,0:T(8,128)} %bitcast.15), calls=%async_computation | async-start | bytes 1048576 | tf_op jit(solution)/shard_map/all_to_all | solution.py:196
  13.6 3.5 %collective-permute-start = (f32[2,256,256]{2,1,0:T(8,128)}, f32[2,256,256]{2,1,0:T(8,128)S(1)}, u32[]{:S(2)}, u32[]{:S(2)}) collective-permute-start(f32[2,256,256]{2,1,0:T(8,128)} %bitcast.19), channel_id=1, source_target_pairs={{0,64},{64,128},{128,192},{192,256},{256,320},{320,384},{384,448},... | collective-permute-start | bytes 1572872 | tf_op jit(solution)/shard_map/ppermute | solution.py:186
  17.1 3.8 %collective-permute-start.1 = (f32[2,256,256]{2,1,0:T(8,128)}, f32[2,256,256]{2,1,0:T(8,128)S(1)}, u32[]{:S(2)}, u32[]{:S(2)}) collective-permute-start(f32[2,256,256]{2,1,0:T(8,128)} %bitcast.16), channel_id=1, source_target_pairs={{0,448},{64,0},{128,64},{192,128},{256,192},{320,256},{384,320},{4... | collective-permute-start | bytes 1572872 | tf_op jit(solution)/shard_map/ppermute | solution.py:186
  20.9 1.3 %collective-permute-start.2 = (f32[2,256,256]{2,1,0:T(8,128)}, f32[2,256,256]{2,1,0:T(8,128)S(1)}, u32[]{:S(2)}, u32[]{:S(2)}) collective-permute-start(f32[2,256,256]{2,1,0:T(8,128)} %bitcast.17), channel_id=1, source_target_pairs={{32,0},{33,1},{34,2},{35,3},{36,4},{37,5},{38,6},{39,7},{40,8},{41... | collective-permute-start | bytes 1572872 | tf_op jit(solution)/shard_map/ppermute | solution.py:190
  22.2 8.3 %collective-permute-done.left_ref = f32[2,256,256]{2,1,0:T(8,128)S(1)} collective-permute-done((f32[2,256,256]{2,1,0:T(8,128)}, f32[2,256,256]{2,1,0:T(8,128)S(1)}, u32[]{:S(2)}, u32[]{:S(2)}) %collective-permute-start) | collective-permute-done | bytes 524320 | tf_op jit(solution)/shard_map/ppermute | solution.py:186
  30.5 1.5 %collective-permute-done.1.ahead_ref = f32[2,256,256]{2,1,0:T(8,128)S(1)} collective-permute-done((f32[2,256,256]{2,1,0:T(8,128)}, f32[2,256,256]{2,1,0:T(8,128)S(1)}, u32[]{:S(2)}, u32[]{:S(2)}) %collective-permute-start.1) | collective-permute-done | bytes 524320 | tf_op jit(solution)/shard_map/ppermute | solution.py:186
  32.0 1.3 %collective-permute-start.3 = (f32[2,256,256]{2,1,0:T(8,128)S(1)}, f32[2,256,256]{2,1,0:T(8,128)S(1)}, u32[]{:S(2)}, u32[]{:S(2)}) collective-permute-start(f32[2,256,256]{2,1,0:T(8,128)S(1)} %collective-permute-done.1.ahead_ref), channel_id=1, source_target_pairs={{0,32},{1,33},{2,34},{3,35},{4,36},{5,37},{6,38},{7,39},{8,40},{9,... | collective-permute-start | bytes 1572872 | tf_op jit(solution)/shard_map/ppermute | solution.py:192
  33.3 0.0 all-to-all-done
  33.4 0.7 broadcast_in_dim.6
  34.1 4.5 %all-to-all-start.1 = ((f32[4,2,16,256]{3,2,1,0:T(8,128)}), f32[4,2,16,256]{3,2,1,0:T(8,128)S(1)}, u32[]{:S(2)}, u32[]{:S(2)}) async-start(f32[4,2,16,256]{3,2,1,0:T(8,128)} %broadcast_in_dim.6), calls=%async_computation.1 | async-start | bytes 262144 | tf_op jit(solution)/shard_map/all_to_all | solution.py:209
  38.6 0.0 copy-done.1
  38.6 0.1 stack.40.place
  38.7 0.0 collective-permute-done.2.beside0_ref
  38.7 0.0 collective-permute-done.3.beside1_ref
  38.7 0.0 copy-done
  38.7 2.8 %shard_map.37 = f32[4,3,2,64,256]{4,3,2,1,0:T(8,128)} custom-call(s32[7]{0:T(128)S(1)} %stack.40.place, f32[2,256,256]{2,1,0:T(8,128)S(1)} %collective-permute-done.left_ref, f32[2,256,256]{2,1,0:T(8,128)S(1)} %collective-permute-done.1.ahead_ref, f32[2,256,256]{2,1,0:T(8,128)S(1)} %collective-permute-done.2.beside0_ref, ...), custom_call_target="tpu_custom_call" | custom-call | flops 603979776 | bytes 4227100 | tf_op jit(solution)/shard_map/pallas_call | solution.py:156
  41.6 3.0 %all-to-all-done.1.gathered = f32[4,2,16,256]{3,2,1,0:T(8,128)S(1)} async-done(((f32[4,2,16,256]{3,2,1,0:T(8,128)}), f32[4,2,16,256]{3,2,1,0:T(8,128)S(1)}, u32[]{:S(2)}, u32[]{:S(2)}) %all-to-all-start.1) | async-done | bytes 131104 | tf_op jit(solution)/shard_map/all_to_all | solution.py:209
  44.5 4.8 %all-to-all-start.2 = ((f32[4,3,2,64,256]{4,3,2,1,0:T(8,128)}), f32[4,3,2,64,256]{4,3,2,1,0:T(8,128)S(1)}, u32[]{:S(2)}, u32[]{:S(2)}) async-start(f32[4,3,2,64,256]{4,3,2,1,0:T(8,128)} %shard_map.37), calls=%async_computation.2 | async-start | bytes 3145728 | tf_op jit(solution)/shard_map/all_to_all | solution.py:232
  49.3 5.1 %collective-permute-start.4 = (f32[4,16,256]{2,1,0:T(8,128)S(1)}, f32[4,16,256]{2,1,0:T(8,128)S(1)}, u32[]{:S(2)}, u32[]{:S(2)}) collective-permute-start(f32[4,16,256]{2,1,0:T(8,128)S(1)} %slice_bitcast_fusion), channel_id=1, source_target_pairs={{0,496},{1,497},{2,498},{3,499},{4,500},{5,501},{6,502},{7,503},{8... | collective-permute-start | bytes 196616 | tf_op jit(solution)/shard_map/ppermute | solution.py:221
  54.4 1.9 %collective-permute-done.4.next1 = f32[4,16,256]{2,1,0:T(8,128)S(1)} collective-permute-done((f32[4,16,256]{2,1,0:T(8,128)S(1)}, f32[4,16,256]{2,1,0:T(8,128)S(1)}, u32[]{:S(2)}, u32[]{:S(2)}) %collective-permute-start.4) | collective-permute-done | bytes 65568 | tf_op jit(solution)/shard_map/ppermute | solution.py:221
  56.3 0.7 shard_map.38.refs_0_
  57.0 3.1 %collective-permute-start.5 = (f32[3,4,16,256]{3,2,1,0:T(8,128)S(1)}, f32[3,4,16,256]{3,2,1,0:T(8,128)S(1)}, u32[]{:S(2)}, u32[]{:S(2)}) collective-permute-start(f32[3,4,16,256]{3,2,1,0:T(8,128)S(1)} %shard_map.38.refs_0_), channel_id=1, source_target_pairs={{0,1},{1,0},{2,3},{3,2},{4,5},{5,4},{6,7},{7,6},{8,9},{9,8},{10,11... | collective-permute-start | bytes 589832 | tf_op jit(solution)/shard_map/ppermute | solution.py:212
  60.1 2.8 %collective-permute-start.6 = (f32[3,4,16,256]{3,2,1,0:T(8,128)S(1)}, f32[3,4,16,256]{3,2,1,0:T(8,128)S(1)}, u32[]{:S(2)}, u32[]{:S(2)}) collective-permute-start(f32[3,4,16,256]{3,2,1,0:T(8,128)S(1)} %shard_map.38.refs_0_), channel_id=1, source_target_pairs={{0,2},{1,3},{2,0},{3,1},{4,6},{5,7},{6,4},{7,5},{8,10},{9,11},{10,... | collective-permute-start | bytes 589832 | tf_op jit(solution)/shard_map/ppermute | solution.py:212
  62.8 3.4 %collective-permute-start.7 = (f32[3,4,16,256]{3,2,1,0:T(8,128)S(1)}, f32[3,4,16,256]{3,2,1,0:T(8,128)S(1)}, u32[]{:S(2)}, u32[]{:S(2)}) collective-permute-start(f32[3,4,16,256]{3,2,1,0:T(8,128)S(1)} %shard_map.38.refs_0_), channel_id=1, source_target_pairs={{0,3},{1,2},{2,1},{3,0},{4,7},{5,6},{6,5},{7,4},{8,11},{9,10},{10,... | collective-permute-start | bytes 589832 | tf_op jit(solution)/shard_map/ppermute | solution.py:212
  66.2 0.6 all-to-all-done.2.got
  66.9 0.8 shard_map.39
  67.7 6.0 %all-to-all-start.3 = ((f32[8,3,16,256]{3,2,1,0:T(8,128)}), f32[8,3,16,256]{3,2,1,0:T(8,128)S(1)}, u32[]{:S(2)}, u32[]{:S(2)}) async-start(f32[8,3,16,256]{3,2,1,0:T(8,128)} %shard_map.39), calls=%async_computation.3 | async-start | bytes 786432 | tf_op jit(solution)/shard_map/all_to_all | solution.py:235
  73.7 0.0 collective-permute-done.5.refs_1_
  73.7 0.0 collective-permute-done.6.refs_2_
  73.7 0.5 collective-permute-done.7.refs_3_
  74.2 0.8 shard_map.40
  75.0 10.6 %all-to-all-done.3.got = f32[8,3,16,256]{3,2,1,0:T(8,128)S(1)} async-done(((f32[8,3,16,256]{3,2,1,0:T(8,128)}), f32[8,3,16,256]{3,2,1,0:T(8,128)S(1)}, u32[]{:S(2)}, u32[]{:S(2)}) %all-to-all-start.3) | async-done | bytes 393248 | tf_op jit(solution)/shard_map/all_to_all | solution.py:235
  85.5 1.1 %shard_map.41 = (f32[3,8,256]{2,1,0:T(8,128)S(1)}, f32[3,8,256]{2,1,0:T(8,128)S(1)}) custom-call(s32[7]{0:T(128)S(1)} %stack.40.place, f32[8,3,16,256]{3,2,1,0:T(8,128)S(1)} %all-to-all-done.3.got, bf16[3,256,256]{2,1,0:T(8,128)(2,1)S(1)} %get-tuple-element.19.high, bf16[3,256,256]{2,1,0:T(8,128)(2,1)S(1)} %get-tuple-element.20.low), custom_call_target="tpu_custom_call" | custom-call | flops 18874368 | bytes 2015260 | tf_op jit(solution)/shard_map/pallas_call | solution.py:156
  86.7 8.6 %collective-permute-start.8 = (f32[3,8,256]{2,1,0:T(8,128)S(1)}, f32[3,8,256]{2,1,0:T(8,128)S(1)}, u32[]{:S(2)}, u32[]{:S(2)}) collective-permute-start(f32[3,8,256]{2,1,0:T(8,128)S(1)} %get-tuple-element.21), channel_id=1, source_target_pairs={{0,448},{1,456},{2,464},{3,472},{4,450},{5,458},{6,466},{7,474},{8... | collective-permute-start | bytes 73736 | tf_op jit(solution)/shard_map/ppermute | solution.py:251
  95.3 4.1 %collective-permute-start.9 = (f32[3,8,256]{2,1,0:T(8,128)S(1)}, f32[3,8,256]{2,1,0:T(8,128)S(1)}, u32[]{:S(2)}, u32[]{:S(2)}) collective-permute-start(f32[3,8,256]{2,1,0:T(8,128)S(1)} %get-tuple-element.22), channel_id=1, source_target_pairs={{0,449},{1,457},{2,465},{3,473},{4,451},{5,459},{6,467},{7,475},{8... | collective-permute-start | bytes 73736 | tf_op jit(solution)/shard_map/ppermute | solution.py:251
  99.4 0.0 collective-permute-done.8.back0
  99.4 7.9 %collective-permute-done.9.back1 = f32[3,8,256]{2,1,0:T(8,128)S(1)} collective-permute-done((f32[3,8,256]{2,1,0:T(8,128)S(1)}, f32[3,8,256]{2,1,0:T(8,128)S(1)}, u32[]{:S(2)}, u32[]{:S(2)}) %collective-permute-start.9) | collective-permute-done | bytes 24608 | tf_op jit(solution)/shard_map/ppermute | solution.py:251
  107.3 1.2 %shard_map.42 = f32[3,2,8,256]{3,2,1,0:T(8,128)} custom-call(s32[7]{0:T(128)S(1)} %stack.40.place, f32[3,8,256]{2,1,0:T(8,128)S(1)} %collective-permute-done.8.back0, f32[3,8,256]{2,1,0:T(8,128)S(1)} %collective-permute-done.9.back1), custom_call_target="tpu_custom_call" | custom-call | flops 10000 | bytes 98332 | tf_op jit(solution)/shard_map/pallas_call | solution.py:156
  (4 shorter events, 0.0 us)
Async XLA Ops:
  0.0 38.7 %copy-start = (f32[2,1,1,1,256,256]{5,4,3,2,1,0:T(8,128)S(1)}, f32[2,1,1,1,256,256]{5,4,3,2,1,0:T(8,128)}, u32[]{:S(2)}) copy-start(f32[2,1,1,1,256,256]{5,4,3,2,1,0:T(8,128)} %param.3) | copy-start | bytes 1572868
  0.0 38.6 %copy-start.1 = (s32[8192]{0:T(1024)S(1)}, s32[8192]{0:T(1024)}, u32[]{:S(2)}) copy-start(s32[8192]{0:T(1024)} %param.5) | copy-start | bytes 98308
  0.0 33.3 %all-to-all-start = ((f32[32,16,256]{2,1,0:T(8,128)}), f32[32,16,256]{2,1,0:T(8,128)S(1)}, u32[]{:S(2)}, u32[]{:S(2)}) async-start(f32[32,16,256]{2,1,0:T(8,128)} %bitcast.15), calls=%async_computation | async-start | bytes 1048576 | tf_op jit(solution)/shard_map/all_to_all | solution.py:196
  13.6 16.9 %collective-permute-start = (f32[2,256,256]{2,1,0:T(8,128)}, f32[2,256,256]{2,1,0:T(8,128)S(1)}, u32[]{:S(2)}, u32[]{:S(2)}) collective-permute-start(f32[2,256,256]{2,1,0:T(8,128)} %bitcast.19), channel_id=1, source_target_pairs={{0,64},{64,128},{128,192},{192,256},{256,320},{320,384},{384,448},... | collective-permute-start | bytes 1572872 | tf_op jit(solution)/shard_map/ppermute | solution.py:186
  17.1 14.9 %collective-permute-start.1 = (f32[2,256,256]{2,1,0:T(8,128)}, f32[2,256,256]{2,1,0:T(8,128)S(1)}, u32[]{:S(2)}, u32[]{:S(2)}) collective-permute-start(f32[2,256,256]{2,1,0:T(8,128)} %bitcast.16), channel_id=1, source_target_pairs={{0,448},{64,0},{128,64},{192,128},{256,192},{320,256},{384,320},{4... | collective-permute-start | bytes 1572872 | tf_op jit(solution)/shard_map/ppermute | solution.py:186
  20.9 17.8 %collective-permute-start.2 = (f32[2,256,256]{2,1,0:T(8,128)}, f32[2,256,256]{2,1,0:T(8,128)S(1)}, u32[]{:S(2)}, u32[]{:S(2)}) collective-permute-start(f32[2,256,256]{2,1,0:T(8,128)} %bitcast.17), channel_id=1, source_target_pairs={{32,0},{33,1},{34,2},{35,3},{36,4},{37,5},{38,6},{39,7},{40,8},{41... | collective-permute-start | bytes 1572872 | tf_op jit(solution)/shard_map/ppermute | solution.py:190
  32.0 6.7 %collective-permute-start.3 = (f32[2,256,256]{2,1,0:T(8,128)S(1)}, f32[2,256,256]{2,1,0:T(8,128)S(1)}, u32[]{:S(2)}, u32[]{:S(2)}) collective-permute-start(f32[2,256,256]{2,1,0:T(8,128)S(1)} %collective-permute-done.1.ahead_ref), channel_id=1, source_target_pairs={{0,32},{1,33},{2,34},{3,35},{4,36},{5,37},{6,38},{7,39},{8,40},{9,... | collective-permute-start | bytes 1572872 | tf_op jit(solution)/shard_map/ppermute | solution.py:192
  34.1 10.5 %all-to-all-start.1 = ((f32[4,2,16,256]{3,2,1,0:T(8,128)}), f32[4,2,16,256]{3,2,1,0:T(8,128)S(1)}, u32[]{:S(2)}, u32[]{:S(2)}) async-start(f32[4,2,16,256]{3,2,1,0:T(8,128)} %broadcast_in_dim.6), calls=%async_computation.1 | async-start | bytes 262144 | tf_op jit(solution)/shard_map/all_to_all | solution.py:209
  44.5 22.3 %all-to-all-start.2 = ((f32[4,3,2,64,256]{4,3,2,1,0:T(8,128)}), f32[4,3,2,64,256]{4,3,2,1,0:T(8,128)S(1)}, u32[]{:S(2)}, u32[]{:S(2)}) async-start(f32[4,3,2,64,256]{4,3,2,1,0:T(8,128)} %shard_map.37), calls=%async_computation.2 | async-start | bytes 3145728 | tf_op jit(solution)/shard_map/all_to_all | solution.py:232
  49.3 7.0 %collective-permute-start.4 = (f32[4,16,256]{2,1,0:T(8,128)S(1)}, f32[4,16,256]{2,1,0:T(8,128)S(1)}, u32[]{:S(2)}, u32[]{:S(2)}) collective-permute-start(f32[4,16,256]{2,1,0:T(8,128)S(1)} %slice_bitcast_fusion), channel_id=1, source_target_pairs={{0,496},{1,497},{2,498},{3,499},{4,500},{5,501},{6,502},{7,503},{8... | collective-permute-start | bytes 196616 | tf_op jit(solution)/shard_map/ppermute | solution.py:221
  57.0 16.7 %collective-permute-start.5 = (f32[3,4,16,256]{3,2,1,0:T(8,128)S(1)}, f32[3,4,16,256]{3,2,1,0:T(8,128)S(1)}, u32[]{:S(2)}, u32[]{:S(2)}) collective-permute-start(f32[3,4,16,256]{3,2,1,0:T(8,128)S(1)} %shard_map.38.refs_0_), channel_id=1, source_target_pairs={{0,1},{1,0},{2,3},{3,2},{4,5},{5,4},{6,7},{7,6},{8,9},{9,8},{10,11... | collective-permute-start | bytes 589832 | tf_op jit(solution)/shard_map/ppermute | solution.py:212
  60.1 13.6 %collective-permute-start.6 = (f32[3,4,16,256]{3,2,1,0:T(8,128)S(1)}, f32[3,4,16,256]{3,2,1,0:T(8,128)S(1)}, u32[]{:S(2)}, u32[]{:S(2)}) collective-permute-start(f32[3,4,16,256]{3,2,1,0:T(8,128)S(1)} %shard_map.38.refs_0_), channel_id=1, source_target_pairs={{0,2},{1,3},{2,0},{3,1},{4,6},{5,7},{6,4},{7,5},{8,10},{9,11},{10,... | collective-permute-start | bytes 589832 | tf_op jit(solution)/shard_map/ppermute | solution.py:212
  62.8 11.3 %collective-permute-start.7 = (f32[3,4,16,256]{3,2,1,0:T(8,128)S(1)}, f32[3,4,16,256]{3,2,1,0:T(8,128)S(1)}, u32[]{:S(2)}, u32[]{:S(2)}) collective-permute-start(f32[3,4,16,256]{3,2,1,0:T(8,128)S(1)} %shard_map.38.refs_0_), channel_id=1, source_target_pairs={{0,3},{1,2},{2,1},{3,0},{4,7},{5,6},{6,5},{7,4},{8,11},{9,10},{10,... | collective-permute-start | bytes 589832 | tf_op jit(solution)/shard_map/ppermute | solution.py:212
  67.7 17.9 %all-to-all-start.3 = ((f32[8,3,16,256]{3,2,1,0:T(8,128)}), f32[8,3,16,256]{3,2,1,0:T(8,128)S(1)}, u32[]{:S(2)}, u32[]{:S(2)}) async-start(f32[8,3,16,256]{3,2,1,0:T(8,128)} %shard_map.39), calls=%async_computation.3 | async-start | bytes 786432 | tf_op jit(solution)/shard_map/all_to_all | solution.py:235
  86.7 12.8 %collective-permute-start.8 = (f32[3,8,256]{2,1,0:T(8,128)S(1)}, f32[3,8,256]{2,1,0:T(8,128)S(1)}, u32[]{:S(2)}, u32[]{:S(2)}) collective-permute-start(f32[3,8,256]{2,1,0:T(8,128)S(1)} %get-tuple-element.21), channel_id=1, source_target_pairs={{0,448},{1,456},{2,464},{3,472},{4,450},{5,458},{6,466},{7,474},{8... | collective-permute-start | bytes 73736 | tf_op jit(solution)/shard_map/ppermute | solution.py:251
  95.3 12.0 %collective-permute-start.9 = (f32[3,8,256]{2,1,0:T(8,128)S(1)}, f32[3,8,256]{2,1,0:T(8,128)S(1)}, u32[]{:S(2)}, u32[]{:S(2)}) collective-permute-start(f32[3,8,256]{2,1,0:T(8,128)S(1)} %get-tuple-element.22), channel_id=1, source_target_pairs={{0,449},{1,457},{2,465},{3,473},{4,451},{5,459},{6,467},{7,475},{8... | collective-permute-start | bytes 73736 | tf_op jit(solution)/shard_map/ppermute | solution.py:251

commit v9 on v8

--- a/solution.py
+++ b/solution.py
@@ -51,8 +51,8 @@
     return jnp.broadcast_to(total, (size, size)).T
 
 
-def product_kernel(factor, place, left_ref, ahead_ref, beside0_ref, beside1_ref, codes, home_ref, out):
-    row, col, core = place[0], place[1], place[3]
+def product_kernel(factor, place, left_ref, ahead_ref, beside_ref, codes, home_ref, out):
+    row, col = place[0], place[1]
     slots, size = left_ref.shape[0], left_ref.shape[1]
     rows_count = codes.shape[0] // slots
     block = size // out.shape[0]
@@ -71,8 +71,7 @@
             tile = ahead_ref[jnp.where(row >= rows_count - 2, other, slot)]
             allowed = allowed & (gap > 3 - (col - tile_row - e) * size)
         elif e == 3:
-            after = beside1_ref[jnp.where(row >= rows_count - 1, other, slot)]
-            tile = jnp.where(core == 0, beside0_ref[slot], after)
+            tile = beside_ref[jnp.where(row >= rows_count - 1, other, slot)]
         else:
             tile = home_ref[slot]
         right = halves(jnp.where(allowed, tile, 0.0))
@@ -113,12 +112,12 @@
             out[k, i] = jnp.where(allowed & far, piece, 0.0)
 
 
-def assemble_kernel(place, *refs):
+def assemble_kernel(order, place, *refs):
     packs, high, low, whole = refs[:-3], refs[-3], refs[-2], refs[-1]
     x = place[4]
     _, deep, part, _ = packs[0].shape
     for k in range(3):
-        for j, pack in enumerate(packs):
+        for j, pack in zip(order, packs):
             for i in range(deep):
                 start = pl.multiple_of((i * len(packs) + (x ^ j)) * part, part)
                 whole[k, pl.ds(start, part), :] = pack[k, i]
@@ -186,10 +185,8 @@
         return lax.ppermute(v, "y", [(i, (i + by) % n) for i in range(n)])
 
     left = row_shift(out_tiles, 1)
+    beside = lax.ppermute(home, AXES[:2], [(i, (i - 1) % rows_count) for i in range(rows_count)])
     ahead = row_shift(home, -1)
-    beside0 = lax.ppermute(home, "core", [(1, 0)])
-    left, ahead = lax.optimization_barrier((left, ahead))
-    beside1 = lax.ppermute(ahead, "core", [(0, 1)])
 
     codes = sequence.reshape(tile_count, size)
 
@@ -215,7 +212,7 @@
     (parts,) = call(
         functools.partial(product_kernel, factor),
         1, [wide], [], WIN * slots * 6 * size**3,
-        place, left, ahead, beside0, beside1, codes, home,
+        place, left, ahead, beside, codes, home,
     )
     parts, gathered = lax.optimization_barrier((parts, gathered))
     next1 = lax.ppermute(gathered[:, 0], AXES, pairs_of(sizes, previous_row))
@@ -224,10 +221,11 @@
         1, [(3, sizes[3], part, size)], [pltpu.VMEM((size, size), jnp.int32)], 10**6,
         place, codes, gathered, next1,
     )
-    packs = {j: partner(pack, "x", sizes[4], j) for j in (2, 1, 3)}
+    order = (0, 1, 3, 2)
+    packs = [pack] + [partner(pack, "x", sizes[4], j) for j in order[1:]]
     high, low = call(
-        assemble_kernel, 1, [(3, size, size)] * 2, [pltpu.VMEM((3, size, size), F32)], 2 * 10**10,
-        place, pack, *(packs[j] for j in range(1, sizes[4])), kind=jnp.bfloat16,
+        functools.partial(assemble_kernel, order), 1, [(3, size, size)] * 2, [pltpu.VMEM((3, size, size), F32)], 2 * 10**10,
+        place, *packs, kind=jnp.bfloat16,
     )
     parts = lax.all_to_all(parts, "x", 0, 0)
     parts, _ = lax.optimization_barrier((parts, pack))

time: 109 us -> 105 us (0.963)
  starting transfers between devices: 65.8 us -> 62 us
    all_to_all x1, waiting for transfers between devices: 0.01 us -> 8.88 us  [on_device(): lax.all_to_all(home.reshape(cols_count, part, size), AXES[2:], 0, 0)]
    ppermute x2, waiting for transfers between devices: 9.81 us -> 2.72 us  [row_shift(): return lax.ppermute(v, 'y', [(i, (i + by) % n) for i in range(n)])]
    all_to_all x1, waiting for transfers between devices: 2.96 us -> 0.18 us  [on_device(): lax.all_to_all(jnp.broadcast_to(near, (sizes[3],) + near.shape), 'zl', 0, 0)]
    ppermute x2, starting transfers between devices: 12.7 us -> 10.4 us  [on_device(): lax.ppermute(sent[flip], AXES, pairs_of(sizes, sent_to(flip)))]
    ppermute x2 -> x1, starting transfers between devices: 2.6 us -> 0.8 us  [on_device(): lax.ppermute(home, AXES[:2], [(i, (i - 1) % rows_count) for i in range(ro...]
    all_to_all x1, waiting for transfers between devices: 10.6 us -> 12 us  [on_device(): got = lax.all_to_all(ready, ('zh', 'zl'), 0, 0)]
    all_to_all x1, starting transfers between devices: 4.54 us -> 3.32 us  [on_device(): lax.all_to_all(jnp.broadcast_to(near, (sizes[3],) + near.shape), 'zl', 0, 0)]
    ppermute x3, starting transfers between devices: 9.21 us -> 10.4 us  [partner(): return lax.ppermute(v, axis, [(i, i ^ j) for i in range(n)])]
  transfers between devices with their start and end apart: 14 -> 13, of which waited for: 8 -> 6; matrix products, arithmetic and copies ran while one was open for 1% -> 1% of each run, Pallas kernels for 5% -> 5%
where the time goes in v9:
time: 105 us
  starting transfers between devices  62 us (59%)
  waiting for transfers between devices  34.3 us (33%)
  Pallas kernels  7.4 us (7%)
    all_to_all x1, starting transfers between devices, on_device(): lax.all_to_all(home.reshape(cols_count, part, size), AXES[2:], 0, 0)  13.6 us
    all_to_all x1, waiting for transfers between devices, on_device(): got = lax.all_to_all(ready, ('zh', 'zl'), 0, 0)  12 us
    ppermute x3, starting transfers between devices, partner(): return lax.ppermute(v, axis, [(i, i ^ j) for i in range(n)])  10.4 us
    ppermute x2, starting transfers between devices, on_device(): lax.ppermute(sent[flip], AXES, pairs_of(sizes, sent_to(flip)))  10.4 us
    all_to_all x1, waiting for transfers between devices, on_device(): lax.all_to_all(home.reshape(cols_count, part, size), AXES[2:], 0, 0)  8.88 us
    ppermute x2, waiting for transfers between devices, on_device(): lax.ppermute(sent[flip], AXES, pairs_of(sizes, sent_to(flip)))  8.58 us
    pallas_call x6, Pallas kernels, call(): pl.pallas_call(kernel, out_shape=[jax.ShapeDtypeStruct(s, kind) for s in...  7.4 us
    ppermute x2, starting transfers between devices, row_shift(): return lax.ppermute(v, 'y', [(i, (i + by) % n) for i in range(n)])  7.12 us
  transfers between devices with their start and end apart: 13, of which 6 were waited for; matrix products, arithmetic and copies ran while one was open for 1% of the time, Pallas kernels for 5%

profile of v9, /device:TPU:4, one launch (start us, length us, event | category | flops | bytes accessed | tf_op | source)
XLA Modules:
  0.0 104.6 jit_solution(4920908198276362024)
XLA Ops:
  0.0 0.0 copy-start
  0.0 0.0 copy-start.1
  0.0 13.6 %all-to-all-start = ((f32[32,16,256]{2,1,0:T(8,128)}), f32[32,16,256]{2,1,0:T(8,128)S(1)}, u32[]{:S(2)}, u32[]{:S(2)}) async-start(f32[32,16,256]{2,1,0:T(8,128)} %bitcast.15), calls=%async_computation | async-start | bytes 1048576 | tf_op jit(solution)/shard_map/all_to_all | solution.py:193
  13.6 3.5 %collective-permute-start = (f32[2,256,256]{2,1,0:T(8,128)}, f32[2,256,256]{2,1,0:T(8,128)S(1)}, u32[]{:S(2)}, u32[]{:S(2)}) collective-permute-start(f32[2,256,256]{2,1,0:T(8,128)} %bitcast.19), channel_id=1, source_target_pairs={{0,64},{64,128},{128,192},{192,256},{256,320},{320,384},{384,448},... | collective-permute-start | bytes 1572872 | tf_op jit(solution)/shard_map/ppermute | solution.py:185
  17.1 0.8 collective-permute-start.2
  17.9 3.6 %collective-permute-start.1 = (f32[2,256,256]{2,1,0:T(8,128)}, f32[2,256,256]{2,1,0:T(8,128)S(1)}, u32[]{:S(2)}, u32[]{:S(2)}) collective-permute-start(f32[2,256,256]{2,1,0:T(8,128)} %bitcast.17), channel_id=1, source_target_pairs={{0,448},{64,0},{128,64},{192,128},{256,192},{320,256},{384,320},{4... | collective-permute-start | bytes 1572872 | tf_op jit(solution)/shard_map/ppermute | solution.py:185
  21.5 8.9 %all-to-all-done = f32[32,16,256]{2,1,0:T(8,128)S(1)} async-done(((f32[32,16,256]{2,1,0:T(8,128)}), f32[32,16,256]{2,1,0:T(8,128)S(1)}, u32[]{:S(2)}, u32[]{:S(2)}) %all-to-all-start) | async-done | bytes 524320 | tf_op jit(solution)/shard_map/all_to_all | solution.py:193
  30.4 0.7 broadcast_in_dim.6
  31.1 3.3 %all-to-all-start.1 = ((f32[4,2,16,256]{3,2,1,0:T(8,128)}), f32[4,2,16,256]{3,2,1,0:T(8,128)S(1)}, u32[]{:S(2)}, u32[]{:S(2)}) async-start(f32[4,2,16,256]{3,2,1,0:T(8,128)} %broadcast_in_dim.6), calls=%async_computation.1 | async-start | bytes 262144 | tf_op jit(solution)/shard_map/all_to_all | solution.py:206
  34.4 0.0 copy-done.1
  34.5 0.1 stack.40.place
  34.6 0.0 collective-permute-done.left_ref
  34.6 0.0 collective-permute-done.2.beside_ref
  34.6 2.7 %collective-permute-done.1.ahead_ref = f32[2,256,256]{2,1,0:T(8,128)S(1)} collective-permute-done((f32[2,256,256]{2,1,0:T(8,128)}, f32[2,256,256]{2,1,0:T(8,128)S(1)}, u32[]{:S(2)}, u32[]{:S(2)}) %collective-permute-start.1) | collective-permute-done | bytes 524320 | tf_op jit(solution)/shard_map/ppermute | solution.py:185
  37.3 0.0 copy-done
  37.3 2.8 %shard_map.37 = f32[4,3,2,64,256]{4,3,2,1,0:T(8,128)} custom-call(s32[7]{0:T(128)S(1)} %stack.40.place, f32[2,256,256]{2,1,0:T(8,128)S(1)} %collective-permute-done.left_ref, f32[2,256,256]{2,1,0:T(8,128)S(1)} %collective-permute-done.1.ahead_ref, f32[2,256,256]{2,1,0:T(8,128)S(1)} %collective-permute-done.2.beside_ref, s32[32,256]{1,0:T(8,128)S(1)} %reshape.3.codes, ...), custom_call_target="tpu_custom_call" | custom-call | flops 603979776 | bytes 3702812 | tf_op jit(solution)/shard_map/pallas_call | solution.py:155
  40.1 0.2 all-to-all-done.1.gathered
  40.3 4.8 %all-to-all-start.2 = ((f32[4,3,2,64,256]{4,3,2,1,0:T(8,128)}), f32[4,3,2,64,256]{4,3,2,1,0:T(8,128)S(1)}, u32[]{:S(2)}, u32[]{:S(2)}) async-start(f32[4,3,2,64,256]{4,3,2,1,0:T(8,128)} %shard_map.37), calls=%async_computation.2 | async-start | bytes 3145728 | tf_op jit(solution)/shard_map/all_to_all | solution.py:230
  45.1 5.1 %collective-permute-start.3 = (f32[4,16,256]{2,1,0:T(8,128)S(1)}, f32[4,16,256]{2,1,0:T(8,128)S(1)}, u32[]{:S(2)}, u32[]{:S(2)}) collective-permute-start(f32[4,16,256]{2,1,0:T(8,128)S(1)} %slice_bitcast_fusion), channel_id=1, source_target_pairs={{0,496},{1,497},{2,498},{3,499},{4,500},{5,501},{6,502},{7,503},{8... | collective-permute-start | bytes 196616 | tf_op jit(solution)/shard_map/ppermute | solution.py:218
  50.2 1.9 %collective-permute-done.3.next1 = f32[4,16,256]{2,1,0:T(8,128)S(1)} collective-permute-done((f32[4,16,256]{2,1,0:T(8,128)S(1)}, f32[4,16,256]{2,1,0:T(8,128)S(1)}, u32[]{:S(2)}, u32[]{:S(2)}) %collective-permute-start.3) | collective-permute-done | bytes 65568 | tf_op jit(solution)/shard_map/ppermute | solution.py:218
  52.1 0.7 shard_map.38.refs_0_
  52.8 2.2 %collective-permute-start.6 = (f32[3,4,16,256]{3,2,1,0:T(8,128)S(1)}, f32[3,4,16,256]{3,2,1,0:T(8,128)S(1)}, u32[]{:S(2)}, u32[]{:S(2)}) collective-permute-start(f32[3,4,16,256]{3,2,1,0:T(8,128)S(1)} %shard_map.38.refs_0_), channel_id=1, source_target_pairs={{0,2},{1,3},{2,0},{3,1},{4,6},{5,7},{6,4},{7,5},{8,10},{9,11},{10,... | collective-permute-start | bytes 589832 | tf_op jit(solution)/shard_map/ppermute | solution.py:209
  55.0 4.2 %collective-permute-start.5 = (f32[3,4,16,256]{3,2,1,0:T(8,128)S(1)}, f32[3,4,16,256]{3,2,1,0:T(8,128)S(1)}, u32[]{:S(2)}, u32[]{:S(2)}) collective-permute-start(f32[3,4,16,256]{3,2,1,0:T(8,128)S(1)} %shard_map.38.refs_0_), channel_id=1, source_target_pairs={{0,3},{1,2},{2,1},{3,0},{4,7},{5,6},{6,5},{7,4},{8,11},{9,10},{10,... | collective-permute-start | bytes 589832 | tf_op jit(solution)/shard_map/ppermute | solution.py:209
  59.3 4.0 %collective-permute-start.4 = (f32[3,4,16,256]{3,2,1,0:T(8,128)S(1)}, f32[3,4,16,256]{3,2,1,0:T(8,128)S(1)}, u32[]{:S(2)}, u32[]{:S(2)}) collective-permute-start(f32[3,4,16,256]{3,2,1,0:T(8,128)S(1)} %shard_map.38.refs_0_), channel_id=1, source_target_pairs={{0,1},{1,0},{2,3},{3,2},{4,5},{5,4},{6,7},{7,6},{8,9},{9,8},{10,11... | collective-permute-start | bytes 589832 | tf_op jit(solution)/shard_map/ppermute | solution.py:209
  63.2 0.0 all-to-all-done.2.got
  63.3 0.8 shard_map.39
  64.1 6.5 %all-to-all-start.3 = ((f32[8,3,16,256]{3,2,1,0:T(8,128)}), f32[8,3,16,256]{3,2,1,0:T(8,128)S(1)}, u32[]{:S(2)}, u32[]{:S(2)}) async-start(f32[8,3,16,256]{3,2,1,0:T(8,128)} %shard_map.39), calls=%async_computation.3 | async-start | bytes 786432 | tf_op jit(solution)/shard_map/all_to_all | solution.py:233
  70.6 0.0 collective-permute-done.6.refs_3_
  70.6 0.0 collective-permute-done.5.refs_2_
  70.6 0.0 collective-permute-done.4.refs_1_
  70.6 0.8 shard_map.40
  71.4 12.0 %all-to-all-done.3.got = f32[8,3,16,256]{3,2,1,0:T(8,128)S(1)} async-done(((f32[8,3,16,256]{3,2,1,0:T(8,128)}), f32[8,3,16,256]{3,2,1,0:T(8,128)S(1)}, u32[]{:S(2)}, u32[]{:S(2)}) %all-to-all-start.3) | async-done | bytes 393248 | tf_op jit(solution)/shard_map/all_to_all | solution.py:233
  83.4 1.1 %shard_map.41 = (f32[3,8,256]{2,1,0:T(8,128)S(1)}, f32[3,8,256]{2,1,0:T(8,128)S(1)}) custom-call(s32[7]{0:T(128)S(1)} %stack.40.place, f32[8,3,16,256]{3,2,1,0:T(8,128)S(1)} %all-to-all-done.3.got, bf16[3,256,256]{2,1,0:T(8,128)(2,1)S(1)} %get-tuple-element.15.high, bf16[3,256,256]{2,1,0:T(8,128)(2,1)S(1)} %get-tuple-element.16.low), custom_call_target="tpu_custom_call" | custom-call | flops 18874368 | bytes 2015260 | tf_op jit(solution)/shard_map/pallas_call | solution.py:155
  84.5 6.9 %collective-permute-start.7 = (f32[3,8,256]{2,1,0:T(8,128)S(1)}, f32[3,8,256]{2,1,0:T(8,128)S(1)}, u32[]{:S(2)}, u32[]{:S(2)}) collective-permute-start(f32[3,8,256]{2,1,0:T(8,128)S(1)} %get-tuple-element.17), channel_id=1, source_target_pairs={{0,448},{1,456},{2,464},{3,472},{4,450},{5,458},{6,466},{7,474},{8... | collective-permute-start | bytes 73736 | tf_op jit(solution)/shard_map/ppermute | solution.py:249
  91.4 3.4 %collective-permute-start.8 = (f32[3,8,256]{2,1,0:T(8,128)S(1)}, f32[3,8,256]{2,1,0:T(8,128)S(1)}, u32[]{:S(2)}, u32[]{:S(2)}) collective-permute-start(f32[3,8,256]{2,1,0:T(8,128)S(1)} %get-tuple-element.18), channel_id=1, source_target_pairs={{0,449},{1,457},{2,465},{3,473},{4,451},{5,459},{6,467},{7,475},{8... | collective-permute-start | bytes 73736 | tf_op jit(solution)/shard_map/ppermute | solution.py:249
  94.9 0.0 collective-permute-done.7.back0
  94.9 8.6 %collective-permute-done.8.back1 = f32[3,8,256]{2,1,0:T(8,128)S(1)} collective-permute-done((f32[3,8,256]{2,1,0:T(8,128)S(1)}, f32[3,8,256]{2,1,0:T(8,128)S(1)}, u32[]{:S(2)}, u32[]{:S(2)}) %collective-permute-start.8) | collective-permute-done | bytes 24608 | tf_op jit(solution)/shard_map/ppermute | solution.py:249
  103.5 1.2 %shard_map.42 = f32[3,2,8,256]{3,2,1,0:T(8,128)} custom-call(s32[7]{0:T(128)S(1)} %stack.40.place, f32[3,8,256]{2,1,0:T(8,128)S(1)} %collective-permute-done.7.back0, f32[3,8,256]{2,1,0:T(8,128)S(1)} %collective-permute-done.8.back1), custom_call_target="tpu_custom_call" | custom-call | flops 10000 | bytes 98332 | tf_op jit(solution)/shard_map/pallas_call | solution.py:155
  (4 shorter events, 0.0 us)
Async XLA Ops:
  0.0 37.3 %copy-start = (f32[2,1,1,1,256,256]{5,4,3,2,1,0:T(8,128)S(1)}, f32[2,1,1,1,256,256]{5,4,3,2,1,0:T(8,128)}, u32[]{:S(2)}) copy-start(f32[2,1,1,1,256,256]{5,4,3,2,1,0:T(8,128)} %param.3) | copy-start | bytes 1572868
  0.0 34.4 %copy-start.1 = (s32[8192]{0:T(1024)S(1)}, s32[8192]{0:T(1024)}, u32[]{:S(2)}) copy-start(s32[8192]{0:T(1024)} %param.5) | copy-start | bytes 98308
  0.0 30.4 %all-to-all-start = ((f32[32,16,256]{2,1,0:T(8,128)}), f32[32,16,256]{2,1,0:T(8,128)S(1)}, u32[]{:S(2)}, u32[]{:S(2)}) async-start(f32[32,16,256]{2,1,0:T(8,128)} %bitcast.15), calls=%async_computation | async-start | bytes 1048576 | tf_op jit(solution)/shard_map/all_to_all | solution.py:193
  13.6 21.0 %collective-permute-start = (f32[2,256,256]{2,1,0:T(8,128)}, f32[2,256,256]{2,1,0:T(8,128)S(1)}, u32[]{:S(2)}, u32[]{:S(2)}) collective-permute-start(f32[2,256,256]{2,1,0:T(8,128)} %bitcast.19), channel_id=1, source_target_pairs={{0,64},{64,128},{128,192},{192,256},{256,320},{320,384},{384,448},... | collective-permute-start | bytes 1572872 | tf_op jit(solution)/shard_map/ppermute | solution.py:185
  17.1 17.5 %collective-permute-start.2 = (f32[2,256,256]{2,1,0:T(8,128)}, f32[2,256,256]{2,1,0:T(8,128)S(1)}, u32[]{:S(2)}, u32[]{:S(2)}) collective-permute-start(f32[2,256,256]{2,1,0:T(8,128)} %bitcast.16), channel_id=1, source_target_pairs={{0,480},{32,0},{64,32},{96,64},{128,96},{160,128},{192,160},{224,1... | collective-permute-start | bytes 1572872 | tf_op jit(solution)/shard_map/ppermute | solution.py:188
  17.9 19.4 %collective-permute-start.1 = (f32[2,256,256]{2,1,0:T(8,128)}, f32[2,256,256]{2,1,0:T(8,128)S(1)}, u32[]{:S(2)}, u32[]{:S(2)}) collective-permute-start(f32[2,256,256]{2,1,0:T(8,128)} %bitcast.17), channel_id=1, source_target_pairs={{0,448},{64,0},{128,64},{192,128},{256,192},{320,256},{384,320},{4... | collective-permute-start | bytes 1572872 | tf_op jit(solution)/shard_map/ppermute | solution.py:185
  31.1 9.2 %all-to-all-start.1 = ((f32[4,2,16,256]{3,2,1,0:T(8,128)}), f32[4,2,16,256]{3,2,1,0:T(8,128)S(1)}, u32[]{:S(2)}, u32[]{:S(2)}) async-start(f32[4,2,16,256]{3,2,1,0:T(8,128)} %broadcast_in_dim.6), calls=%async_computation.1 | async-start | bytes 262144 | tf_op jit(solution)/shard_map/all_to_all | solution.py:206
  40.3 22.9 %all-to-all-start.2 = ((f32[4,3,2,64,256]{4,3,2,1,0:T(8,128)}), f32[4,3,2,64,256]{4,3,2,1,0:T(8,128)S(1)}, u32[]{:S(2)}, u32[]{:S(2)}) async-start(f32[4,3,2,64,256]{4,3,2,1,0:T(8,128)} %shard_map.37), calls=%async_computation.2 | async-start | bytes 3145728 | tf_op jit(solution)/shard_map/all_to_all | solution.py:230
  45.1 7.0 %collective-permute-start.3 = (f32[4,16,256]{2,1,0:T(8,128)S(1)}, f32[4,16,256]{2,1,0:T(8,128)S(1)}, u32[]{:S(2)}, u32[]{:S(2)}) collective-permute-start(f32[4,16,256]{2,1,0:T(8,128)S(1)} %slice_bitcast_fusion), channel_id=1, source_target_pairs={{0,496},{1,497},{2,498},{3,499},{4,500},{5,501},{6,502},{7,503},{8... | collective-permute-start | bytes 196616 | tf_op jit(solution)/shard_map/ppermute | solution.py:218
  52.8 17.8 %collective-permute-start.6 = (f32[3,4,16,256]{3,2,1,0:T(8,128)S(1)}, f32[3,4,16,256]{3,2,1,0:T(8,128)S(1)}, u32[]{:S(2)}, u32[]{:S(2)}) collective-permute-start(f32[3,4,16,256]{3,2,1,0:T(8,128)S(1)} %shard_map.38.refs_0_), channel_id=1, source_target_pairs={{0,2},{1,3},{2,0},{3,1},{4,6},{5,7},{6,4},{7,5},{8,10},{9,11},{10,... | collective-permute-start | bytes 589832 | tf_op jit(solution)/shard_map/ppermute | solution.py:209
  55.0 15.6 %collective-permute-start.5 = (f32[3,4,16,256]{3,2,1,0:T(8,128)S(1)}, f32[3,4,16,256]{3,2,1,0:T(8,128)S(1)}, u32[]{:S(2)}, u32[]{:S(2)}) collective-permute-start(f32[3,4,16,256]{3,2,1,0:T(8,128)S(1)} %shard_map.38.refs_0_), channel_id=1, source_target_pairs={{0,3},{1,2},{2,1},{3,0},{4,7},{5,6},{6,5},{7,4},{8,11},{9,10},{10,... | collective-permute-start | bytes 589832 | tf_op jit(solution)/shard_map/ppermute | solution.py:209
  59.3 11.3 %collective-permute-start.4 = (f32[3,4,16,256]{3,2,1,0:T(8,128)S(1)}, f32[3,4,16,256]{3,2,1,0:T(8,128)S(1)}, u32[]{:S(2)}, u32[]{:S(2)}) collective-permute-start(f32[3,4,16,256]{3,2,1,0:T(8,128)S(1)} %shard_map.38.refs_0_), channel_id=1, source_target_pairs={{0,1},{1,0},{2,3},{3,2},{4,5},{5,4},{6,7},{7,6},{8,9},{9,8},{10,11... | collective-permute-start | bytes 589832 | tf_op jit(solution)/shard_map/ppermute | solution.py:209
  64.1 19.3 %all-to-all-start.3 = ((f32[8,3,16,256]{3,2,1,0:T(8,128)}), f32[8,3,16,256]{3,2,1,0:T(8,128)S(1)}, u32[]{:S(2)}, u32[]{:S(2)}) async-start(f32[8,3,16,256]{3,2,1,0:T(8,128)} %shard_map.39), calls=%async_computation.3 | async-start | bytes 786432 | tf_op jit(solution)/shard_map/all_to_all | solution.py:233
  84.5 10.4 %collective-permute-start.7 = (f32[3,8,256]{2,1,0:T(8,128)S(1)}, f32[3,8,256]{2,1,0:T(8,128)S(1)}, u32[]{:S(2)}, u32[]{:S(2)}) collective-permute-start(f32[3,8,256]{2,1,0:T(8,128)S(1)} %get-tuple-element.17), channel_id=1, source_target_pairs={{0,448},{1,456},{2,464},{3,472},{4,450},{5,458},{6,466},{7,474},{8... | collective-permute-start | bytes 73736 | tf_op jit(solution)/shard_map/ppermute | solution.py:249
  91.4 12.0 %collective-permute-start.8 = (f32[3,8,256]{2,1,0:T(8,128)S(1)}, f32[3,8,256]{2,1,0:T(8,128)S(1)}, u32[]{:S(2)}, u32[]{:S(2)}) collective-permute-start(f32[3,8,256]{2,1,0:T(8,128)S(1)} %get-tuple-element.18), channel_id=1, source_target_pairs={{0,449},{1,457},{2,465},{3,473},{4,451},{5,459},{6,467},{7,475},{8... | collective-permute-start | bytes 73736 | tf_op jit(solution)/shard_map/ppermute | solution.py:249

commit v10 on v9

--- a/solution.py
+++ b/solution.py
@@ -51,15 +51,24 @@
     return jnp.broadcast_to(total, (size, size)).T
 
 
-def product_kernel(factor, place, left_ref, ahead_ref, beside_ref, codes, home_ref, out):
+def columns_kernel(slots, place, codes, for_products, for_pack):
+    row, half = place[0], place[2]
+    rows_count = codes.shape[0] // slots
+    for_products[...] = columns_of(codes, [slot * rows_count + row - 2 + e for e in (4, 3, 2) for slot in range(slots)])
+    first = row + half * rows_count
+    for_pack[...] = columns_of(codes, [first, first + 1])
+
+
+def product_kernel(factor, place, left_ref, ahead_ref, beside_ref, codes, columns_ref, home_ref, out):
     row, col = place[0], place[1]
     slots, size = left_ref.shape[0], left_ref.shape[1]
     rows_count = codes.shape[0] // slots
-    block = size // out.shape[0]
+    piece = size // codes.shape[0]
+    chunks = size // out.shape[0] // piece
     col_bits = 1 << codes_of(codes, col)
     tile_rows = [slot * rows_count + row - 2 for slot in range(slots)]
     keys = [(slot, e) for e in (4, 3, 2) for slot in range(slots)]
-    columns = columns_of(codes, [tile_rows[slot] + e for slot, e in keys])
+    columns = columns_ref[...]
     gap = lax.broadcasted_iota(jnp.int32, (size, size), 1) - lax.broadcasted_iota(jnp.int32, (size, size), 0)
     lefts = [left_ref[jnp.where(row < 2, 0, slot)] for slot in range(slots)]
     left_halves = [halves(left) for left in lefts]
@@ -80,7 +89,9 @@
         own = jnp.where((tile_row >= 0) & (col == tile_row + e), 1.0, 0.0).astype(F32)
         full = scale * times(left_halves[slot], right) + own * lefts[slot]
         for x in range(out.shape[0]):
-            out[x, TOP - e, slot] = full[x * block:(x + 1) * block]
+            for chunk in range(chunks):
+                start = (chunk % slots) * (size // slots) + (chunk // slots * out.shape[0] + x) * piece
+                out[x, TOP - e, slot, chunk * piece:(chunk + 1) * piece] = full[start:start + piece]
 
 
 def add_kernel(got, out):
@@ -96,11 +107,10 @@
                 out[slot * deep + z, number] = total[z * piece:(z + 1) * piece]
 
 
-def pack_kernel(wide, place, codes, gathered, next1, out, columns):
+def pack_kernel(wide, place, codes, columns, gathered, next1, out):
     row, half, x = place[0], place[2], place[4]
     count, part, size = gathered.shape[0], gathered.shape[2], out.shape[3]
     first = row + half * (codes.shape[0] // 2)
-    columns[...] = columns_of(codes, [first, first + 1])
     steps = lax.broadcasted_iota(jnp.int32, (part, size), 1) - lax.broadcasted_iota(jnp.int32, (part, size), 0)
     for i in range(count):
         start = pl.multiple_of((i * wide + x) * part, part)
@@ -144,7 +154,7 @@
 
 
 def order_kernel(place, back0, back1, out):
-    swap = (place[1] + place[6]) % 2 == 1
+    swap = (place[2] + place[6]) % 2 == 1
     out[:, 0] = jnp.where(swap, back1[...], back0[...])
     out[:, 1] = jnp.where(swap, back0[...], back1[...])
 
@@ -189,8 +199,12 @@
     ahead = row_shift(home, -1)
 
     codes = sequence.reshape(tile_count, size)
+    columns, pack_columns = call(
+        functools.partial(columns_kernel, slots), 1, [(size, size)] * 2, [], 10**6, place, codes, kind=jnp.int32
+    )
 
     spread = lax.all_to_all(home.reshape(cols_count, part, size), AXES[2:], 0, 0)
+    spread, columns, pack_columns = lax.optimization_barrier((spread, columns, pack_columns))
     first = jnp.minimum(row + half * rows_count + 1, cols_count - 1)
     second = jnp.minimum(row + half * rows_count + 2, cols_count - 1)
     near1 = lax.dynamic_index_in_dim(spread, first, 0, False)
@@ -212,14 +226,13 @@
     (parts,) = call(
         functools.partial(product_kernel, factor),
         1, [wide], [], WIN * slots * 6 * size**3,
-        place, left, ahead, beside, codes, home,
+        place, left, ahead, beside, codes, columns, home,
     )
     parts, gathered = lax.optimization_barrier((parts, gathered))
     next1 = lax.ppermute(gathered[:, 0], AXES, pairs_of(sizes, previous_row))
     (pack,) = call(
         functools.partial(pack_kernel, sizes[4]),
-        1, [(3, sizes[3], part, size)], [pltpu.VMEM((size, size), jnp.int32)], 10**6,
-        place, codes, gathered, next1,
+        1, [(3, sizes[3], part, size)], [], 10**6, place, codes, pack_columns, gathered, next1,
     )
     order = (0, 1, 3, 2)
     packs = [pack] + [partner(pack, "x", sizes[4], j) for j in order[1:]]
@@ -240,10 +253,7 @@
 
     def sent_to(flip):
         def target(y, c, zh, zl, x):
-            r = (y * sizes[1] + c - 2) % rows_count
-            pick = zh if flip == 0 else 1 - zh
-            n = 2 * (x * sizes[3] + zl) + pick
-            return r // sizes[1], r % sizes[1], n // (sizes[3] * sizes[4]), n // sizes[4] % sizes[3], n % sizes[4]
+            return (y - 1) % sizes[0], c, zh ^ flip, zl, x
         return target
 
     back = [lax.ppermute(sent[flip], AXES, pairs_of(sizes, sent_to(flip))) for flip in range(2)]

time: 105 us -> 104 us (level)
  the two profiles are of different devices: /device:TPU:4 before, /device:TPU:6 now
where the time goes in v10:
time: 104 us; the launch traced here: 102 us
  starting transfers between devices  58.5 us (56%)
  waiting for transfers between devices  34.1 us (33%)
  Pallas kernels  7.94 us (8%)
  local copies, waits for them, and re-layouts  1.54 us (1%)
    all_to_all x1, starting transfers between devices, on_device(): lax.all_to_all(home.reshape(cols_count, part, size), AXES[2:], 0, 0)  13.5 us
    all_to_all x1, waiting for transfers between devices, on_device(): got = lax.all_to_all(ready, ('zh', 'zl'), 0, 0)  11.8 us
    ppermute x3, starting transfers between devices, partner(): return lax.ppermute(v, axis, [(i, i ^ j) for i in range(n)])  9.27 us
    ppermute x2, starting transfers between devices, on_device(): lax.ppermute(sent[flip], AXES, pairs_of(sizes, sent_to(flip)))  9 us
    ppermute x2, waiting for transfers between devices, on_device(): lax.ppermute(sent[flip], AXES, pairs_of(sizes, sent_to(flip)))  8.59 us
    pallas_call x7, Pallas kernels, call(): pl.pallas_call(kernel, out_shape=[jax.ShapeDtypeStruct(s, kind) for s in...  7.94 us
    all_to_all x1, waiting for transfers between devices, on_device(): lax.all_to_all(home.reshape(cols_count, part, size), AXES[2:], 0, 0)  7.31 us
    ppermute x2, starting transfers between devices, row_shift(): return lax.ppermute(v, 'y', [(i, (i + by) % n) for i in range(n)])  7.12 us
  transfers between devices with their start and end apart: 13, of which 7 were waited for; matrix products, arithmetic and copies ran while one was open for 2% of the time, Pallas kernels for 6%

profile of v10, /device:TPU:6, one launch (start us, length us, event | category | flops | bytes accessed | tf_op | source)
XLA Modules:
  0.0 102.2 jit_solution(1813202077339747194)
XLA Ops:
  0.0 0.0 copy-start
  0.0 13.5 %all-to-all-start = ((f32[32,16,256]{2,1,0:T(8,128)}), f32[32,16,256]{2,1,0:T(8,128)S(1)}, u32[]{:S(2)}, u32[]{:S(2)}) async-start(f32[32,16,256]{2,1,0:T(8,128)} %bitcast.15), calls=%async_computation | async-start | bytes 1048576 | tf_op jit(solution)/shard_map/all_to_all | solution.py:206
  13.6 3.5 %collective-permute-start = (f32[2,256,256]{2,1,0:T(8,128)}, f32[2,256,256]{2,1,0:T(8,128)S(1)}, u32[]{:S(2)}, u32[]{:S(2)}) collective-permute-start(f32[2,256,256]{2,1,0:T(8,128)} %bitcast.19), channel_id=1, source_target_pairs={{0,64},{64,128},{128,192},{192,256},{256,320},{320,384},{384,448},... | collective-permute-start | bytes 1572872 | tf_op jit(solution)/shard_map/ppermute | solution.py:195
  17.0 0.8 collective-permute-start.2
  17.8 3.6 %collective-permute-start.1 = (f32[2,256,256]{2,1,0:T(8,128)}, f32[2,256,256]{2,1,0:T(8,128)S(1)}, u32[]{:S(2)}, u32[]{:S(2)}) collective-permute-start(f32[2,256,256]{2,1,0:T(8,128)} %bitcast.17), channel_id=1, source_target_pairs={{0,448},{64,0},{128,64},{192,128},{256,192},{320,256},{384,320},{4... | collective-permute-start | bytes 1572872 | tf_op jit(solution)/shard_map/ppermute | solution.py:195
  21.5 0.8 reshape.3.codes
  22.3 0.1 stack.40.place
  22.4 0.7 shard_map.37
  23.1 7.3 %all-to-all-done = f32[32,16,256]{2,1,0:T(8,128)S(1)} async-done(((f32[32,16,256]{2,1,0:T(8,128)}), f32[32,16,256]{2,1,0:T(8,128)S(1)}, u32[]{:S(2)}, u32[]{:S(2)}) %all-to-all-start) | async-done | bytes 524320 | tf_op jit(solution)/shard_map/all_to_all | solution.py:206
  30.4 0.7 broadcast_in_dim.6
  31.1 3.3 %all-to-all-start.1 = ((f32[4,2,16,256]{3,2,1,0:T(8,128)}), f32[4,2,16,256]{3,2,1,0:T(8,128)S(1)}, u32[]{:S(2)}, u32[]{:S(2)}) async-start(f32[4,2,16,256]{3,2,1,0:T(8,128)} %broadcast_in_dim.6), calls=%async_computation.1 | async-start | bytes 262144 | tf_op jit(solution)/shard_map/all_to_all | solution.py:220
  34.4 0.0 collective-permute-done.left_ref
  34.4 0.0 collective-permute-done.2.beside_ref
  34.4 2.8 %collective-permute-done.1.ahead_ref = f32[2,256,256]{2,1,0:T(8,128)S(1)} collective-permute-done((f32[2,256,256]{2,1,0:T(8,128)}, f32[2,256,256]{2,1,0:T(8,128)S(1)}, u32[]{:S(2)}, u32[]{:S(2)}) %collective-permute-start.1) | collective-permute-done | bytes 524320 | tf_op jit(solution)/shard_map/ppermute | solution.py:195
  37.2 0.0 copy-done
  37.2 2.8 %shard_map.38 = f32[4,3,2,64,256]{4,3,2,1,0:T(8,128)} custom-call(s32[7]{0:T(128)S(1)} %stack.40.place, f32[2,256,256]{2,1,0:T(8,128)S(1)} %collective-permute-done.left_ref, f32[2,256,256]{2,1,0:T(8,128)S(1)} %collective-permute-done.1.ahead_ref, f32[2,256,256]{2,1,0:T(8,128)S(1)} %collective-permute-done.2.beside_ref, s32[32,256]{1,0:T(8,128)S(1)} %reshape.3.codes, ...), custom_call_target="tpu_custom_call" | custom-call | flops 603979776 | bytes 3964956 | tf_op jit(solution)/shard_map/pallas_call | solution.py:165
  40.0 0.2 all-to-all-done.1.gathered
  40.3 4.8 %all-to-all-start.2 = ((f32[4,3,2,64,256]{4,3,2,1,0:T(8,128)}), f32[4,3,2,64,256]{4,3,2,1,0:T(8,128)S(1)}, u32[]{:S(2)}, u32[]{:S(2)}) async-start(f32[4,3,2,64,256]{4,3,2,1,0:T(8,128)} %shard_map.38), calls=%async_computation.2 | async-start | bytes 3145728 | tf_op jit(solution)/shard_map/all_to_all | solution.py:243
  45.1 5.1 %collective-permute-start.3 = (f32[4,16,256]{2,1,0:T(8,128)S(1)}, f32[4,16,256]{2,1,0:T(8,128)S(1)}, u32[]{:S(2)}, u32[]{:S(2)}) collective-permute-start(f32[4,16,256]{2,1,0:T(8,128)S(1)} %slice_bitcast_fusion), channel_id=1, source_target_pairs={{0,496},{1,497},{2,498},{3,499},{4,500},{5,501},{6,502},{7,503},{8... | collective-permute-start | bytes 196616 | tf_op jit(solution)/shard_map/ppermute | solution.py:232
  50.1 1.9 %collective-permute-done.3.next1 = f32[4,16,256]{2,1,0:T(8,128)S(1)} collective-permute-done((f32[4,16,256]{2,1,0:T(8,128)S(1)}, f32[4,16,256]{2,1,0:T(8,128)S(1)}, u32[]{:S(2)}, u32[]{:S(2)}) %collective-permute-start.3) | collective-permute-done | bytes 65568 | tf_op jit(solution)/shard_map/ppermute | solution.py:232
  52.0 0.6 shard_map.39.refs_0_
  52.6 3.4 %collective-permute-start.6 = (f32[3,4,16,256]{3,2,1,0:T(8,128)S(1)}, f32[3,4,16,256]{3,2,1,0:T(8,128)S(1)}, u32[]{:S(2)}, u32[]{:S(2)}) collective-permute-start(f32[3,4,16,256]{3,2,1,0:T(8,128)S(1)} %shard_map.39.refs_0_), channel_id=1, source_target_pairs={{0,2},{1,3},{2,0},{3,1},{4,6},{5,7},{6,4},{7,5},{8,10},{9,11},{10,... | collective-permute-start | bytes 589832 | tf_op jit(solution)/shard_map/ppermute | solution.py:223
  56.0 4.0 %collective-permute-start.5 = (f32[3,4,16,256]{3,2,1,0:T(8,128)S(1)}, f32[3,4,16,256]{3,2,1,0:T(8,128)S(1)}, u32[]{:S(2)}, u32[]{:S(2)}) collective-permute-start(f32[3,4,16,256]{3,2,1,0:T(8,128)S(1)} %shard_map.39.refs_0_), channel_id=1, source_target_pairs={{0,3},{1,2},{2,1},{3,0},{4,7},{5,6},{6,5},{7,4},{8,11},{9,10},{10,... | collective-permute-start | bytes 589832 | tf_op jit(solution)/shard_map/ppermute | solution.py:223
  60.0 1.9 %collective-permute-start.4 = (f32[3,4,16,256]{3,2,1,0:T(8,128)S(1)}, f32[3,4,16,256]{3,2,1,0:T(8,128)S(1)}, u32[]{:S(2)}, u32[]{:S(2)}) collective-permute-start(f32[3,4,16,256]{3,2,1,0:T(8,128)S(1)} %shard_map.39.refs_0_), channel_id=1, source_target_pairs={{0,1},{1,0},{2,3},{3,2},{4,5},{5,4},{6,7},{7,6},{8,9},{9,8},{10,11... | collective-permute-start | bytes 589832 | tf_op jit(solution)/shard_map/ppermute | solution.py:223
  61.9 1.4 %all-to-all-done.2.got = f32[4,3,2,64,256]{4,3,2,1,0:T(8,128)S(1)} async-done(((f32[4,3,2,64,256]{4,3,2,1,0:T(8,128)}), f32[4,3,2,64,256]{4,3,2,1,0:T(8,128)S(1)}, u32[]{:S(2)}, u32[]{:S(2)}) %all-to-all-start.2) | async-done | bytes 1572896 | tf_op jit(solution)/shard_map/all_to_all | solution.py:243
  63.3 0.8 shard_map.40
  64.1 5.6 %all-to-all-start.3 = ((f32[8,3,16,256]{3,2,1,0:T(8,128)}), f32[8,3,16,256]{3,2,1,0:T(8,128)S(1)}, u32[]{:S(2)}, u32[]{:S(2)}) async-start(f32[8,3,16,256]{3,2,1,0:T(8,128)} %shard_map.40), calls=%async_computation.3 | async-start | bytes 786432 | tf_op jit(solution)/shard_map/all_to_all | solution.py:246
  69.7 0.0 collective-permute-done.6.refs_3_
  69.7 0.0 collective-permute-done.5.refs_2_
  69.7 0.0 collective-permute-done.4.refs_1_
  69.7 0.8 shard_map.41
  70.5 11.8 %all-to-all-done.3.got = f32[8,3,16,256]{3,2,1,0:T(8,128)S(1)} async-done(((f32[8,3,16,256]{3,2,1,0:T(8,128)}), f32[8,3,16,256]{3,2,1,0:T(8,128)S(1)}, u32[]{:S(2)}, u32[]{:S(2)}) %all-to-all-start.3) | async-done | bytes 393248 | tf_op jit(solution)/shard_map/all_to_all | solution.py:246
  82.3 1.1 %shard_map.42 = (f32[3,8,256]{2,1,0:T(8,128)S(1)}, f32[3,8,256]{2,1,0:T(8,128)S(1)}) custom-call(s32[7]{0:T(128)S(1)} %stack.40.place, f32[8,3,16,256]{3,2,1,0:T(8,128)S(1)} %all-to-all-done.3.got, bf16[3,256,256]{2,1,0:T(8,128)(2,1)S(1)} %get-tuple-element.25.high, bf16[3,256,256]{2,1,0:T(8,128)(2,1)S(1)} %get-tuple-element.26.low), custom_call_target="tpu_custom_call" | custom-call | flops 18874368 | bytes 2015260 | tf_op jit(solution)/shard_map/pallas_call | solution.py:165
  83.4 7.1 %collective-permute-start.7 = (f32[3,8,256]{2,1,0:T(8,128)S(1)}, f32[3,8,256]{2,1,0:T(8,128)S(1)}, u32[]{:S(2)}, u32[]{:S(2)}) collective-permute-start(f32[3,8,256]{2,1,0:T(8,128)S(1)} %get-tuple-element.27), channel_id=1, source_target_pairs={{0,448},{1,449},{2,450},{3,451},{4,452},{5,453},{6,454},{7,455},{8... | collective-permute-start | bytes 73736 | tf_op jit(solution)/shard_map/ppermute | solution.py:259
  90.5 1.9 %collective-permute-start.8 = (f32[3,8,256]{2,1,0:T(8,128)S(1)}, f32[3,8,256]{2,1,0:T(8,128)S(1)}, u32[]{:S(2)}, u32[]{:S(2)}) collective-permute-start(f32[3,8,256]{2,1,0:T(8,128)S(1)} %get-tuple-element.28), channel_id=1, source_target_pairs={{0,464},{1,465},{2,466},{3,467},{4,468},{5,469},{6,470},{7,471},{8... | collective-permute-start | bytes 73736 | tf_op jit(solution)/shard_map/ppermute | solution.py:259
  92.5 0.0 collective-permute-done.7.back0
  92.5 8.6 %collective-permute-done.8.back1 = f32[3,8,256]{2,1,0:T(8,128)S(1)} collective-permute-done((f32[3,8,256]{2,1,0:T(8,128)S(1)}, f32[3,8,256]{2,1,0:T(8,128)S(1)}, u32[]{:S(2)}, u32[]{:S(2)}) %collective-permute-start.8) | collective-permute-done | bytes 24608 | tf_op jit(solution)/shard_map/ppermute | solution.py:259
  101.1 1.2 %shard_map.43 = f32[3,2,8,256]{3,2,1,0:T(8,128)} custom-call(s32[7]{0:T(128)S(1)} %stack.40.place, f32[3,8,256]{2,1,0:T(8,128)S(1)} %collective-permute-done.7.back0, f32[3,8,256]{2,1,0:T(8,128)S(1)} %collective-permute-done.8.back1), custom_call_target="tpu_custom_call" | custom-call | flops 10000 | bytes 98332 | tf_op jit(solution)/shard_map/pallas_call | solution.py:165
  (3 shorter events, 0.0 us)
Async XLA Ops:
  0.0 37.2 %copy-start = (f32[2,1,1,1,256,256]{5,4,3,2,1,0:T(8,128)S(1)}, f32[2,1,1,1,256,256]{5,4,3,2,1,0:T(8,128)}, u32[]{:S(2)}) copy-start(f32[2,1,1,1,256,256]{5,4,3,2,1,0:T(8,128)} %param.3) | copy-start | bytes 1572868
  0.0 30.4 %all-to-all-start = ((f32[32,16,256]{2,1,0:T(8,128)}), f32[32,16,256]{2,1,0:T(8,128)S(1)}, u32[]{:S(2)}, u32[]{:S(2)}) async-start(f32[32,16,256]{2,1,0:T(8,128)} %bitcast.15), calls=%async_computation | async-start | bytes 1048576 | tf_op jit(solution)/shard_map/all_to_all | solution.py:206
  13.6 20.8 %collective-permute-start = (f32[2,256,256]{2,1,0:T(8,128)}, f32[2,256,256]{2,1,0:T(8,128)S(1)}, u32[]{:S(2)}, u32[]{:S(2)}) collective-permute-start(f32[2,256,256]{2,1,0:T(8,128)} %bitcast.19), channel_id=1, source_target_pairs={{0,64},{64,128},{128,192},{192,256},{256,320},{320,384},{384,448},... | collective-permute-start | bytes 1572872 | tf_op jit(solution)/shard_map/ppermute | solution.py:195
  17.0 17.4 %collective-permute-start.2 = (f32[2,256,256]{2,1,0:T(8,128)}, f32[2,256,256]{2,1,0:T(8,128)S(1)}, u32[]{:S(2)}, u32[]{:S(2)}) collective-permute-start(f32[2,256,256]{2,1,0:T(8,128)} %bitcast.16), channel_id=1, source_target_pairs={{0,480},{32,0},{64,32},{96,64},{128,96},{160,128},{192,160},{224,1... | collective-permute-start | bytes 1572872 | tf_op jit(solution)/shard_map/ppermute | solution.py:198
  17.8 19.4 %collective-permute-start.1 = (f32[2,256,256]{2,1,0:T(8,128)}, f32[2,256,256]{2,1,0:T(8,128)S(1)}, u32[]{:S(2)}, u32[]{:S(2)}) collective-permute-start(f32[2,256,256]{2,1,0:T(8,128)} %bitcast.17), channel_id=1, source_target_pairs={{0,448},{64,0},{128,64},{192,128},{256,192},{320,256},{384,320},{4... | collective-permute-start | bytes 1572872 | tf_op jit(solution)/shard_map/ppermute | solution.py:195
  31.1 9.2 %all-to-all-start.1 = ((f32[4,2,16,256]{3,2,1,0:T(8,128)}), f32[4,2,16,256]{3,2,1,0:T(8,128)S(1)}, u32[]{:S(2)}, u32[]{:S(2)}) async-start(f32[4,2,16,256]{3,2,1,0:T(8,128)} %broadcast_in_dim.6), calls=%async_computation.1 | async-start | bytes 262144 | tf_op jit(solution)/shard_map/all_to_all | solution.py:220
  40.3 23.0 %all-to-all-start.2 = ((f32[4,3,2,64,256]{4,3,2,1,0:T(8,128)}), f32[4,3,2,64,256]{4,3,2,1,0:T(8,128)S(1)}, u32[]{:S(2)}, u32[]{:S(2)}) async-start(f32[4,3,2,64,256]{4,3,2,1,0:T(8,128)} %shard_map.38), calls=%async_computation.2 | async-start | bytes 3145728 | tf_op jit(solution)/shard_map/all_to_all | solution.py:243
  45.1 6.9 %collective-permute-start.3 = (f32[4,16,256]{2,1,0:T(8,128)S(1)}, f32[4,16,256]{2,1,0:T(8,128)S(1)}, u32[]{:S(2)}, u32[]{:S(2)}) collective-permute-start(f32[4,16,256]{2,1,0:T(8,128)S(1)} %slice_bitcast_fusion), channel_id=1, source_target_pairs={{0,496},{1,497},{2,498},{3,499},{4,500},{5,501},{6,502},{7,503},{8... | collective-permute-start | bytes 196616 | tf_op jit(solution)/shard_map/ppermute | solution.py:232
  52.6 17.1 %collective-permute-start.6 = (f32[3,4,16,256]{3,2,1,0:T(8,128)S(1)}, f32[3,4,16,256]{3,2,1,0:T(8,128)S(1)}, u32[]{:S(2)}, u32[]{:S(2)}) collective-permute-start(f32[3,4,16,256]{3,2,1,0:T(8,128)S(1)} %shard_map.39.refs_0_), channel_id=1, source_target_pairs={{0,2},{1,3},{2,0},{3,1},{4,6},{5,7},{6,4},{7,5},{8,10},{9,11},{10,... | collective-permute-start | bytes 589832 | tf_op jit(solution)/shard_map/ppermute | solution.py:223
  56.0 13.7 %collective-permute-start.5 = (f32[3,4,16,256]{3,2,1,0:T(8,128)S(1)}, f32[3,4,16,256]{3,2,1,0:T(8,128)S(1)}, u32[]{:S(2)}, u32[]{:S(2)}) collective-permute-start(f32[3,4,16,256]{3,2,1,0:T(8,128)S(1)} %shard_map.39.refs_0_), channel_id=1, source_target_pairs={{0,3},{1,2},{2,1},{3,0},{4,7},{5,6},{6,5},{7,4},{8,11},{9,10},{10,... | collective-permute-start | bytes 589832 | tf_op jit(solution)/shard_map/ppermute | solution.py:223
  60.0 9.8 %collective-permute-start.4 = (f32[3,4,16,256]{3,2,1,0:T(8,128)S(1)}, f32[3,4,16,256]{3,2,1,0:T(8,128)S(1)}, u32[]{:S(2)}, u32[]{:S(2)}) collective-permute-start(f32[3,4,16,256]{3,2,1,0:T(8,128)S(1)} %shard_map.39.refs_0_), channel_id=1, source_target_pairs={{0,1},{1,0},{2,3},{3,2},{4,5},{5,4},{6,7},{7,6},{8,9},{9,8},{10,11... | collective-permute-start | bytes 589832 | tf_op jit(solution)/shard_map/ppermute | solution.py:223
  64.1 18.2 %all-to-all-start.3 = ((f32[8,3,16,256]{3,2,1,0:T(8,128)}), f32[8,3,16,256]{3,2,1,0:T(8,128)S(1)}, u32[]{:S(2)}, u32[]{:S(2)}) async-start(f32[8,3,16,256]{3,2,1,0:T(8,128)} %shard_map.40), calls=%async_computation.3 | async-start | bytes 786432 | tf_op jit(solution)/shard_map/all_to_all | solution.py:246
  83.4 9.0 %collective-permute-start.7 = (f32[3,8,256]{2,1,0:T(8,128)S(1)}, f32[3,8,256]{2,1,0:T(8,128)S(1)}, u32[]{:S(2)}, u32[]{:S(2)}) collective-permute-start(f32[3,8,256]{2,1,0:T(8,128)S(1)} %get-tuple-element.27), channel_id=1, source_target_pairs={{0,448},{1,449},{2,450},{3,451},{4,452},{5,453},{6,454},{7,455},{8... | collective-permute-start | bytes 73736 | tf_op jit(solution)/shard_map/ppermute | solution.py:259
  90.5 10.5 %collective-permute-start.8 = (f32[3,8,256]{2,1,0:T(8,128)S(1)}, f32[3,8,256]{2,1,0:T(8,128)S(1)}, u32[]{:S(2)}, u32[]{:S(2)}) collective-permute-start(f32[3,8,256]{2,1,0:T(8,128)S(1)} %get-tuple-element.28), channel_id=1, source_target_pairs={{0,464},{1,465},{2,466},{3,467},{4,468},{5,469},{6,470},{7,471},{8... | collective-permute-start | bytes 73736 | tf_op jit(solution)/shard_map/ppermute | solution.py:259

commit v11 on v10

--- a/solution.py
+++ b/solution.py
@@ -59,7 +59,7 @@
     for_pack[...] = columns_of(codes, [first, first + 1])
 
 
-def product_kernel(factor, place, left_ref, ahead_ref, beside_ref, codes, columns_ref, home_ref, out):
+def product_kernel(factor, place, left_ref, ahead_ref, beside_ref, codes, columns_ref, home_ref, sent, out, sems):
     row, col = place[0], place[1]
     slots, size = left_ref.shape[0], left_ref.shape[1]
     rows_count = codes.shape[0] // slots
@@ -72,6 +72,7 @@
     gap = lax.broadcasted_iota(jnp.int32, (size, size), 1) - lax.broadcasted_iota(jnp.int32, (size, size), 0)
     lefts = [left_ref[jnp.where(row < 2, 0, slot)] for slot in range(slots)]
     left_halves = [halves(left) for left in lefts]
+    copies = []
     for k, (slot, e) in enumerate(keys):
         tile_row = tile_rows[slot]
         other = slots - 1 - slot
@@ -92,6 +93,10 @@
             for chunk in range(chunks):
                 start = (chunk % slots) * (size // slots) + (chunk // slots * out.shape[0] + x) * piece
                 out[x, TOP - e, slot, chunk * piece:(chunk + 1) * piece] = full[start:start + piece]
+        copies.append(pltpu.make_async_copy(out.at[:, TOP - e, slot], sent.at[:, TOP - e, slot], sems.at[k]))
+        copies[-1].start()
+    for copy in copies:
+        copy.wait()
 
 
 def add_kernel(got, out):
@@ -153,20 +158,20 @@
         out_b[w] = rows[w, pl.ds(pl.multiple_of((1 - half) * piece, piece), piece), :]
 
 
-def order_kernel(place, back0, back1, out):
+def order_kernel(place, back1, back0, out):
     swap = (place[2] + place[6]) % 2 == 1
     out[:, 0] = jnp.where(swap, back1[...], back0[...])
     out[:, 1] = jnp.where(swap, back0[...], back1[...])
 
 
-def call(kernel, in_count, outs, scratch, flops, *args, kind=F32):
+def call(kernel, in_count, outs, scratch, flops, *args, kind=F32, space=pltpu.VMEM):
     spec = pl.BlockSpec(memory_space=pltpu.VMEM)
     moved = sum(math.prod(a.shape) * 4 for a in args) + sum(math.prod(s) * 4 for s in outs)
     return pl.pallas_call(
         kernel,
         out_shape=[jax.ShapeDtypeStruct(s, kind) for s in outs],
         in_specs=[pl.BlockSpec(memory_space=pltpu.SMEM)] * in_count + [spec] * (len(args) - in_count),
-        out_specs=[spec] * len(outs),
+        out_specs=[pl.BlockSpec(memory_space=space)] * len(outs),
         scratch_shapes=scratch,
         cost_estimate=pl.CostEstimate(flops=flops, bytes_accessed=moved, transcendentals=0),
         compiler_params=pltpu.CompilerParams(vmem_limit_bytes=24 * 1024 * 1024),
@@ -225,8 +230,8 @@
     wide = (sizes[4], WIN, slots, size // sizes[4], size)
     (parts,) = call(
         functools.partial(product_kernel, factor),
-        1, [wide], [], WIN * slots * 6 * size**3,
-        place, left, ahead, beside, codes, columns, home,
+        1, [wide], [pltpu.VMEM(wide, F32), pltpu.SemaphoreType.DMA((WIN * slots,))], WIN * slots * 6 * size**3,
+        place, left, ahead, beside, codes, columns, home, space=pl.ANY,
     )
     parts, gathered = lax.optimization_barrier((parts, gathered))
     next1 = lax.ppermute(gathered[:, 0], AXES, pairs_of(sizes, previous_row))
@@ -257,7 +262,7 @@
         return target
 
     back = [lax.ppermute(sent[flip], AXES, pairs_of(sizes, sent_to(flip))) for flip in range(2)]
-    (result,) = call(order_kernel, 1, [(WIN, slots, piece, size)], [], 10**4, place, *back)
+    (result,) = call(order_kernel, 1, [(WIN, slots, piece, size)], [], 10**4, place, *back[::-1])
     return result[:, :, None]
 
 

time: 104 us -> 102 us (0.981)
  the two profiles are of different devices: /device:TPU:6 before, /device:TPU:24 now
where the time goes in v11:
time: 102 us; the launch traced here: 101 us
  starting transfers between devices  52.2 us (51%)
  waiting for transfers between devices  39.6 us (39%)
  Pallas kernels  7.65 us (8%)
  local copies, waits for them, and re-layouts  1.54 us (2%)
    all_to_all x1, starting transfers between devices, on_device(): lax.all_to_all(home.reshape(cols_count, part, size), AXES[2:], 0, 0)  13.3 us
    all_to_all x1, waiting for transfers between devices, on_device(): got = lax.all_to_all(ready, ('zh', 'zl'), 0, 0)  11.1 us
    ppermute x3, starting transfers between devices, partner(): return lax.ppermute(v, axis, [(i, i ^ j) for i in range(n)])  10.4 us
    all_to_all x1, waiting for transfers between devices, on_device(): lax.all_to_all(home.reshape(cols_count, part, size), AXES[2:], 0, 0)  9.45 us
    all_to_all x1, starting transfers between devices, on_device(): got = lax.all_to_all(ready, ('zh', 'zl'), 0, 0)  8.42 us
    ppermute x2, waiting for transfers between devices, on_device(): lax.ppermute(sent[flip], AXES, pairs_of(sizes, sent_to(flip)))  7.88 us
    pallas_call x7, Pallas kernels, call(): pl.pallas_call(kernel, out_shape=[jax.ShapeDtypeStruct(s, kind) for s in...  7.65 us
    ppermute x2, starting transfers between devices, row_shift(): return lax.ppermute(v, 'y', [(i, (i + by) % n) for i in range(n)])  6.62 us
  transfers between devices with their start and end apart: 13, of which 6 were waited for; matrix products, arithmetic and copies ran while one was open for 2% of the time, Pallas kernels for 5%

profile of v11, /device:TPU:24, one launch (start us, length us, event | category | flops | bytes accessed | tf_op | source)
XLA Modules:
  0.0 101.2 jit_solution(5411769574195100093)
XLA Ops:
  0.0 0.0 copy-start
  0.0 13.3 %all-to-all-start = ((f32[32,16,256]{2,1,0:T(8,128)}), f32[32,16,256]{2,1,0:T(8,128)S(1)}, u32[]{:S(2)}, u32[]{:S(2)}) async-start(f32[32,16,256]{2,1,0:T(8,128)} %bitcast.15), calls=%async_computation | async-start | bytes 1048576 | tf_op jit(solution)/shard_map/all_to_all | solution.py:211
  13.3 4.7 %collective-permute-start = (f32[2,256,256]{2,1,0:T(8,128)}, f32[2,256,256]{2,1,0:T(8,128)S(1)}, u32[]{:S(2)}, u32[]{:S(2)}) collective-permute-start(f32[2,256,256]{2,1,0:T(8,128)} %bitcast.19), channel_id=1, source_target_pairs={{0,64},{64,128},{128,192},{192,256},{256,320},{320,384},{384,448},... | collective-permute-start | bytes 1572872 | tf_op jit(solution)/shard_map/ppermute | solution.py:200
  18.0 0.0 collective-permute-start.2
  18.0 1.9 %collective-permute-start.1 = (f32[2,256,256]{2,1,0:T(8,128)}, f32[2,256,256]{2,1,0:T(8,128)S(1)}, u32[]{:S(2)}, u32[]{:S(2)}) collective-permute-start(f32[2,256,256]{2,1,0:T(8,128)} %bitcast.17), channel_id=1, source_target_pairs={{0,448},{64,0},{128,64},{192,128},{256,192},{320,256},{384,320},{4... | collective-permute-start | bytes 1572872 | tf_op jit(solution)/shard_map/ppermute | solution.py:200
  20.0 0.8 reshape.3.codes
  20.8 0.1 stack.40.place
  20.9 0.7 shard_map.37
  21.6 9.5 %all-to-all-done = f32[32,16,256]{2,1,0:T(8,128)S(1)} async-done(((f32[32,16,256]{2,1,0:T(8,128)}), f32[32,16,256]{2,1,0:T(8,128)S(1)}, u32[]{:S(2)}, u32[]{:S(2)}) %all-to-all-start) | async-done | bytes 524320 | tf_op jit(solution)/shard_map/all_to_all | solution.py:211
  31.0 0.7 broadcast_in_dim.6
  31.7 3.3 %all-to-all-start.1 = ((f32[4,2,16,256]{3,2,1,0:T(8,128)}), f32[4,2,16,256]{3,2,1,0:T(8,128)S(1)}, u32[]{:S(2)}, u32[]{:S(2)}) async-start(f32[4,2,16,256]{3,2,1,0:T(8,128)} %broadcast_in_dim.6), calls=%async_computation.1 | async-start | bytes 262144 | tf_op jit(solution)/shard_map/all_to_all | solution.py:225
  35.0 0.0 collective-permute-done.left_ref
  35.0 0.0 collective-permute-done.2.beside_ref
  35.0 3.7 %collective-permute-done.1.ahead_ref = f32[2,256,256]{2,1,0:T(8,128)S(1)} collective-permute-done((f32[2,256,256]{2,1,0:T(8,128)}, f32[2,256,256]{2,1,0:T(8,128)S(1)}, u32[]{:S(2)}, u32[]{:S(2)}) %collective-permute-start.1) | collective-permute-done | bytes 524320 | tf_op jit(solution)/shard_map/ppermute | solution.py:200
  38.7 0.0 copy-done
  38.7 2.5 %shard_map.38 = f32[4,3,2,64,256]{4,3,2,1,0:T(8,128)} custom-call(s32[7]{0:T(128)S(1)} %stack.40.place, f32[2,256,256]{2,1,0:T(8,128)S(1)} %collective-permute-done.left_ref, f32[2,256,256]{2,1,0:T(8,128)S(1)} %collective-permute-done.1.ahead_ref, f32[2,256,256]{2,1,0:T(8,128)S(1)} %collective-permute-done.2.beside_ref, s32[32,256]{1,0:T(8,128)S(1)} %reshape.3.codes, ...), custom_call_target="tpu_custom_call" | custom-call | flops 603979776 | bytes 3964956 | tf_op jit(solution)/shard_map/pallas_call | solution.py:170
  41.2 0.0 all-to-all-done.1.gathered
  41.3 4.3 %all-to-all-start.2 = ((f32[4,3,2,64,256]{4,3,2,1,0:T(8,128)}), f32[4,3,2,64,256]{4,3,2,1,0:T(8,128)S(1)}, u32[]{:S(2)}, u32[]{:S(2)}) async-start(f32[4,3,2,64,256]{4,3,2,1,0:T(8,128)} %shard_map.38), calls=%async_computation.2 | async-start | bytes 3145728 | tf_op jit(solution)/shard_map/all_to_all | solution.py:248
  45.6 1.9 %collective-permute-start.3 = (f32[4,16,256]{2,1,0:T(8,128)S(1)}, f32[4,16,256]{2,1,0:T(8,128)S(1)}, u32[]{:S(2)}, u32[]{:S(2)}) collective-permute-start(f32[4,16,256]{2,1,0:T(8,128)S(1)} %slice_bitcast_fusion), channel_id=1, source_target_pairs={{0,496},{1,497},{2,498},{3,499},{4,500},{5,501},{6,502},{7,503},{8... | collective-permute-start | bytes 196616 | tf_op jit(solution)/shard_map/ppermute | solution.py:237
  47.5 1.9 %collective-permute-done.3.next1 = f32[4,16,256]{2,1,0:T(8,128)S(1)} collective-permute-done((f32[4,16,256]{2,1,0:T(8,128)S(1)}, f32[4,16,256]{2,1,0:T(8,128)S(1)}, u32[]{:S(2)}, u32[]{:S(2)}) %collective-permute-start.3) | collective-permute-done | bytes 65568 | tf_op jit(solution)/shard_map/ppermute | solution.py:237
  49.4 0.6 shard_map.39.refs_0_
  50.0 5.4 %collective-permute-start.6 = (f32[3,4,16,256]{3,2,1,0:T(8,128)S(1)}, f32[3,4,16,256]{3,2,1,0:T(8,128)S(1)}, u32[]{:S(2)}, u32[]{:S(2)}) collective-permute-start(f32[3,4,16,256]{3,2,1,0:T(8,128)S(1)} %shard_map.39.refs_0_), channel_id=1, source_target_pairs={{0,2},{1,3},{2,0},{3,1},{4,6},{5,7},{6,4},{7,5},{8,10},{9,11},{10,... | collective-permute-start | bytes 589832 | tf_op jit(solution)/shard_map/ppermute | solution.py:228
  55.4 3.1 %collective-permute-start.5 = (f32[3,4,16,256]{3,2,1,0:T(8,128)S(1)}, f32[3,4,16,256]{3,2,1,0:T(8,128)S(1)}, u32[]{:S(2)}, u32[]{:S(2)}) collective-permute-start(f32[3,4,16,256]{3,2,1,0:T(8,128)S(1)} %shard_map.39.refs_0_), channel_id=1, source_target_pairs={{0,3},{1,2},{2,1},{3,0},{4,7},{5,6},{6,5},{7,4},{8,11},{9,10},{10,... | collective-permute-start | bytes 589832 | tf_op jit(solution)/shard_map/ppermute | solution.py:228
  58.5 1.9 %collective-permute-start.4 = (f32[3,4,16,256]{3,2,1,0:T(8,128)S(1)}, f32[3,4,16,256]{3,2,1,0:T(8,128)S(1)}, u32[]{:S(2)}, u32[]{:S(2)}) collective-permute-start(f32[3,4,16,256]{3,2,1,0:T(8,128)S(1)} %shard_map.39.refs_0_), channel_id=1, source_target_pairs={{0,1},{1,0},{2,3},{3,2},{4,5},{5,4},{6,7},{7,6},{8,9},{9,8},{10,11... | collective-permute-start | bytes 589832 | tf_op jit(solution)/shard_map/ppermute | solution.py:228
  60.4 5.6 %all-to-all-done.2.got = f32[4,3,2,64,256]{4,3,2,1,0:T(8,128)S(1)} async-done(((f32[4,3,2,64,256]{4,3,2,1,0:T(8,128)}), f32[4,3,2,64,256]{4,3,2,1,0:T(8,128)S(1)}, u32[]{:S(2)}, u32[]{:S(2)}) %all-to-all-start.2) | async-done | bytes 1572896 | tf_op jit(solution)/shard_map/all_to_all | solution.py:248
  66.0 0.8 shard_map.40
  66.8 8.4 %all-to-all-start.3 = ((f32[8,3,16,256]{3,2,1,0:T(8,128)}), f32[8,3,16,256]{3,2,1,0:T(8,128)S(1)}, u32[]{:S(2)}, u32[]{:S(2)}) async-start(f32[8,3,16,256]{3,2,1,0:T(8,128)} %shard_map.40), calls=%async_computation.3 | async-start | bytes 786432 | tf_op jit(solution)/shard_map/all_to_all | solution.py:251
  75.3 0.0 collective-permute-done.6.refs_3_
  75.3 0.0 collective-permute-done.5.refs_2_
  75.3 0.0 collective-permute-done.4.refs_1_
  75.3 0.8 shard_map.41
  76.1 11.1 %all-to-all-done.3.got = f32[8,3,16,256]{3,2,1,0:T(8,128)S(1)} async-done(((f32[8,3,16,256]{3,2,1,0:T(8,128)}), f32[8,3,16,256]{3,2,1,0:T(8,128)S(1)}, u32[]{:S(2)}, u32[]{:S(2)}) %all-to-all-start.3) | async-done | bytes 393248 | tf_op jit(solution)/shard_map/all_to_all | solution.py:251
  87.2 1.1 %shard_map.42 = (f32[3,8,256]{2,1,0:T(8,128)S(1)}, f32[3,8,256]{2,1,0:T(8,128)S(1)}) custom-call(s32[7]{0:T(128)S(1)} %stack.40.place, f32[8,3,16,256]{3,2,1,0:T(8,128)S(1)} %all-to-all-done.3.got, bf16[3,256,256]{2,1,0:T(8,128)(2,1)S(1)} %get-tuple-element.25.high, bf16[3,256,256]{2,1,0:T(8,128)(2,1)S(1)} %get-tuple-element.26.low), custom_call_target="tpu_custom_call" | custom-call | flops 18874368 | bytes 2015260 | tf_op jit(solution)/shard_map/pallas_call | solution.py:170
  88.3 1.9 %collective-permute-start.7 = (f32[3,8,256]{2,1,0:T(8,128)S(1)}, f32[3,8,256]{2,1,0:T(8,128)S(1)}, u32[]{:S(2)}, u32[]{:S(2)}) collective-permute-start(f32[3,8,256]{2,1,0:T(8,128)S(1)} %get-tuple-element.27), channel_id=1, source_target_pairs={{0,464},{1,465},{2,466},{3,467},{4,468},{5,469},{6,470},{7,471},{8... | collective-permute-start | bytes 73736 | tf_op jit(solution)/shard_map/ppermute | solution.py:264
  90.2 1.9 %collective-permute-start.8 = (f32[3,8,256]{2,1,0:T(8,128)S(1)}, f32[3,8,256]{2,1,0:T(8,128)S(1)}, u32[]{:S(2)}, u32[]{:S(2)}) collective-permute-start(f32[3,8,256]{2,1,0:T(8,128)S(1)} %get-tuple-element.28), channel_id=1, source_target_pairs={{0,448},{1,449},{2,450},{3,451},{4,452},{5,453},{6,454},{7,455},{8... | collective-permute-start | bytes 73736 | tf_op jit(solution)/shard_map/ppermute | solution.py:264
  92.1 7.9 %collective-permute-done.7.back1 = f32[3,8,256]{2,1,0:T(8,128)S(1)} collective-permute-done((f32[3,8,256]{2,1,0:T(8,128)S(1)}, f32[3,8,256]{2,1,0:T(8,128)S(1)}, u32[]{:S(2)}, u32[]{:S(2)}) %collective-permute-start.7) | collective-permute-done | bytes 24608 | tf_op jit(solution)/shard_map/ppermute | solution.py:264
  100.0 0.0 collective-permute-done.8.back0
  100.0 1.2 %shard_map.43 = f32[3,2,8,256]{3,2,1,0:T(8,128)} custom-call(s32[7]{0:T(128)S(1)} %stack.40.place, f32[3,8,256]{2,1,0:T(8,128)S(1)} %collective-permute-done.7.back1, f32[3,8,256]{2,1,0:T(8,128)S(1)} %collective-permute-done.8.back0), custom_call_target="tpu_custom_call" | custom-call | flops 10000 | bytes 98332 | tf_op jit(solution)/shard_map/pallas_call | solution.py:170
  (3 shorter events, 0.0 us)
Async XLA Ops:
  0.0 38.7 %copy-start = (f32[2,1,1,1,256,256]{5,4,3,2,1,0:T(8,128)S(1)}, f32[2,1,1,1,256,256]{5,4,3,2,1,0:T(8,128)}, u32[]{:S(2)}) copy-start(f32[2,1,1,1,256,256]{5,4,3,2,1,0:T(8,128)} %param.3) | copy-start | bytes 1572868
  0.0 31.0 %all-to-all-start = ((f32[32,16,256]{2,1,0:T(8,128)}), f32[32,16,256]{2,1,0:T(8,128)S(1)}, u32[]{:S(2)}, u32[]{:S(2)}) async-start(f32[32,16,256]{2,1,0:T(8,128)} %bitcast.15), calls=%async_computation | async-start | bytes 1048576 | tf_op jit(solution)/shard_map/all_to_all | solution.py:211
  13.3 21.7 %collective-permute-start = (f32[2,256,256]{2,1,0:T(8,128)}, f32[2,256,256]{2,1,0:T(8,128)S(1)}, u32[]{:S(2)}, u32[]{:S(2)}) collective-permute-start(f32[2,256,256]{2,1,0:T(8,128)} %bitcast.19), channel_id=1, source_target_pairs={{0,64},{64,128},{128,192},{192,256},{256,320},{320,384},{384,448},... | collective-permute-start | bytes 1572872 | tf_op jit(solution)/shard_map/ppermute | solution.py:200
  18.0 17.0 %collective-permute-start.2 = (f32[2,256,256]{2,1,0:T(8,128)}, f32[2,256,256]{2,1,0:T(8,128)S(1)}, u32[]{:S(2)}, u32[]{:S(2)}) collective-permute-start(f32[2,256,256]{2,1,0:T(8,128)} %bitcast.16), channel_id=1, source_target_pairs={{0,480},{32,0},{64,32},{96,64},{128,96},{160,128},{192,160},{224,1... | collective-permute-start | bytes 1572872 | tf_op jit(solution)/shard_map/ppermute | solution.py:203
  18.0 20.7 %collective-permute-start.1 = (f32[2,256,256]{2,1,0:T(8,128)}, f32[2,256,256]{2,1,0:T(8,128)S(1)}, u32[]{:S(2)}, u32[]{:S(2)}) collective-permute-start(f32[2,256,256]{2,1,0:T(8,128)} %bitcast.17), channel_id=1, source_target_pairs={{0,448},{64,0},{128,64},{192,128},{256,192},{320,256},{384,320},{4... | collective-permute-start | bytes 1572872 | tf_op jit(solution)/shard_map/ppermute | solution.py:200
  31.7 9.6 %all-to-all-start.1 = ((f32[4,2,16,256]{3,2,1,0:T(8,128)}), f32[4,2,16,256]{3,2,1,0:T(8,128)S(1)}, u32[]{:S(2)}, u32[]{:S(2)}) async-start(f32[4,2,16,256]{3,2,1,0:T(8,128)} %broadcast_in_dim.6), calls=%async_computation.1 | async-start | bytes 262144 | tf_op jit(solution)/shard_map/all_to_all | solution.py:225
  41.3 24.8 %all-to-all-start.2 = ((f32[4,3,2,64,256]{4,3,2,1,0:T(8,128)}), f32[4,3,2,64,256]{4,3,2,1,0:T(8,128)S(1)}, u32[]{:S(2)}, u32[]{:S(2)}) async-start(f32[4,3,2,64,256]{4,3,2,1,0:T(8,128)} %shard_map.38), calls=%async_computation.2 | async-start | bytes 3145728 | tf_op jit(solution)/shard_map/all_to_all | solution.py:248
  45.6 3.8 %collective-permute-start.3 = (f32[4,16,256]{2,1,0:T(8,128)S(1)}, f32[4,16,256]{2,1,0:T(8,128)S(1)}, u32[]{:S(2)}, u32[]{:S(2)}) collective-permute-start(f32[4,16,256]{2,1,0:T(8,128)S(1)} %slice_bitcast_fusion), channel_id=1, source_target_pairs={{0,496},{1,497},{2,498},{3,499},{4,500},{5,501},{6,502},{7,503},{8... | collective-permute-start | bytes 196616 | tf_op jit(solution)/shard_map/ppermute | solution.py:237
  50.0 25.3 %collective-permute-start.6 = (f32[3,4,16,256]{3,2,1,0:T(8,128)S(1)}, f32[3,4,16,256]{3,2,1,0:T(8,128)S(1)}, u32[]{:S(2)}, u32[]{:S(2)}) collective-permute-start(f32[3,4,16,256]{3,2,1,0:T(8,128)S(1)} %shard_map.39.refs_0_), channel_id=1, source_target_pairs={{0,2},{1,3},{2,0},{3,1},{4,6},{5,7},{6,4},{7,5},{8,10},{9,11},{10,... | collective-permute-start | bytes 589832 | tf_op jit(solution)/shard_map/ppermute | solution.py:228
  55.4 19.9 %collective-permute-start.5 = (f32[3,4,16,256]{3,2,1,0:T(8,128)S(1)}, f32[3,4,16,256]{3,2,1,0:T(8,128)S(1)}, u32[]{:S(2)}, u32[]{:S(2)}) collective-permute-start(f32[3,4,16,256]{3,2,1,0:T(8,128)S(1)} %shard_map.39.refs_0_), channel_id=1, source_target_pairs={{0,3},{1,2},{2,1},{3,0},{4,7},{5,6},{6,5},{7,4},{8,11},{9,10},{10,... | collective-permute-start | bytes 589832 | tf_op jit(solution)/shard_map/ppermute | solution.py:228
  58.5 16.8 %collective-permute-start.4 = (f32[3,4,16,256]{3,2,1,0:T(8,128)S(1)}, f32[3,4,16,256]{3,2,1,0:T(8,128)S(1)}, u32[]{:S(2)}, u32[]{:S(2)}) collective-permute-start(f32[3,4,16,256]{3,2,1,0:T(8,128)S(1)} %shard_map.39.refs_0_), channel_id=1, source_target_pairs={{0,1},{1,0},{2,3},{3,2},{4,5},{5,4},{6,7},{7,6},{8,9},{9,8},{10,11... | collective-permute-start | bytes 589832 | tf_op jit(solution)/shard_map/ppermute | solution.py:228
  66.8 20.3 %all-to-all-start.3 = ((f32[8,3,16,256]{3,2,1,0:T(8,128)}), f32[8,3,16,256]{3,2,1,0:T(8,128)S(1)}, u32[]{:S(2)}, u32[]{:S(2)}) async-start(f32[8,3,16,256]{3,2,1,0:T(8,128)} %shard_map.40), calls=%async_computation.3 | async-start | bytes 786432 | tf_op jit(solution)/shard_map/all_to_all | solution.py:251
  88.3 11.7 %collective-permute-start.7 = (f32[3,8,256]{2,1,0:T(8,128)S(1)}, f32[3,8,256]{2,1,0:T(8,128)S(1)}, u32[]{:S(2)}, u32[]{:S(2)}) collective-permute-start(f32[3,8,256]{2,1,0:T(8,128)S(1)} %get-tuple-element.27), channel_id=1, source_target_pairs={{0,464},{1,465},{2,466},{3,467},{4,468},{5,469},{6,470},{7,471},{8... | collective-permute-start | bytes 73736 | tf_op jit(solution)/shard_map/ppermute | solution.py:264
  90.2 9.8 %collective-permute-start.8 = (f32[3,8,256]{2,1,0:T(8,128)S(1)}, f32[3,8,256]{2,1,0:T(8,128)S(1)}, u32[]{:S(2)}, u32[]{:S(2)}) collective-permute-start(f32[3,8,256]{2,1,0:T(8,128)S(1)} %get-tuple-element.28), channel_id=1, source_target_pairs={{0,448},{1,449},{2,450},{3,451},{4,452},{5,453},{6,454},{7,455},{8... | collective-permute-start | bytes 73736 | tf_op jit(solution)/shard_map/ppermute | solution.py:264

commit v12 on v11

--- a/solution.py
+++ b/solution.py
@@ -239,7 +239,7 @@
         functools.partial(pack_kernel, sizes[4]),
         1, [(3, sizes[3], part, size)], [], 10**6, place, codes, pack_columns, gathered, next1,
     )
-    order = (0, 1, 3, 2)
+    order = (0, 2, 3, 1)
     packs = [pack] + [partner(pack, "x", sizes[4], j) for j in order[1:]]
     high, low = call(
         functools.partial(assemble_kernel, order), 1, [(3, size, size)] * 2, [pltpu.VMEM((3, size, size), F32)], 2 * 10**10,

time: 102 us -> 102 us (level)
  no operation moved by 1% of the time
where the time goes in v12:
time: 102 us; the launch traced here: 101 us
  starting transfers between devices  51.6 us (51%)
  waiting for transfers between devices  40.2 us (39%)
  Pallas kernels  7.65 us (8%)
  local copies, waits for them, and re-layouts  1.54 us (2%)
    all_to_all x1, starting transfers between devices, on_device(): lax.all_to_all(home.reshape(cols_count, part, size), AXES[2:], 0, 0)  13.3 us
    all_to_all x1, waiting for transfers between devices, on_device(): got = lax.all_to_all(ready, ('zh', 'zl'), 0, 0)  11.1 us
    ppermute x3, starting transfers between devices, partner(): return lax.ppermute(v, axis, [(i, i ^ j) for i in range(n)])  10.4 us
    all_to_all x1, waiting for transfers between devices, on_device(): lax.all_to_all(home.reshape(cols_count, part, size), AXES[2:], 0, 0)  9.45 us
    ppermute x2, waiting for transfers between devices, on_device(): lax.ppermute(sent[flip], AXES, pairs_of(sizes, sent_to(flip)))  7.88 us
    all_to_all x1, starting transfers between devices, on_device(): got = lax.all_to_all(ready, ('zh', 'zl'), 0, 0)  7.82 us
    pallas_call x7, Pallas kernels, call(): pl.pallas_call(kernel, out_shape=[jax.ShapeDtypeStruct(s, kind) for s in...  7.65 us
    ppermute x2, starting transfers between devices, row_shift(): return lax.ppermute(v, 'y', [(i, (i + by) % n) for i in range(n)])  6.62 us
  transfers between devices with their start and end apart: 13, of which 6 were waited for; matrix products, arithmetic and copies ran while one was open for 2% of the time, Pallas kernels for 5%

profile of v12, /device:TPU:24, one launch (start us, length us, event | category | flops | bytes accessed | tf_op | source)
XLA Modules:
  0.0 101.2 jit_solution(17824913055982518987)
XLA Ops:
  0.0 0.0 copy-start
  0.0 13.3 %all-to-all-start = ((f32[32,16,256]{2,1,0:T(8,128)}), f32[32,16,256]{2,1,0:T(8,128)S(1)}, u32[]{:S(2)}, u32[]{:S(2)}) async-start(f32[32,16,256]{2,1,0:T(8,128)} %bitcast.15), calls=%async_computation | async-start | bytes 1048576 | tf_op jit(solution)/shard_map/all_to_all | solution.py:211
  13.3 4.7 %collective-permute-start = (f32[2,256,256]{2,1,0:T(8,128)}, f32[2,256,256]{2,1,0:T(8,128)S(1)}, u32[]{:S(2)}, u32[]{:S(2)}) collective-permute-start(f32[2,256,256]{2,1,0:T(8,128)} %bitcast.19), channel_id=1, source_target_pairs={{0,64},{64,128},{128,192},{192,256},{256,320},{320,384},{384,448},... | collective-permute-start | bytes 1572872 | tf_op jit(solution)/shard_map/ppermute | solution.py:200
  18.0 0.0 collective-permute-start.2
  18.0 1.9 %collective-permute-start.1 = (f32[2,256,256]{2,1,0:T(8,128)}, f32[2,256,256]{2,1,0:T(8,128)S(1)}, u32[]{:S(2)}, u32[]{:S(2)}) collective-permute-start(f32[2,256,256]{2,1,0:T(8,128)} %bitcast.17), channel_id=1, source_target_pairs={{0,448},{64,0},{128,64},{192,128},{256,192},{320,256},{384,320},{4... | collective-permute-start | bytes 1572872 | tf_op jit(solution)/shard_map/ppermute | solution.py:200
  20.0 0.8 reshape.3.codes
  20.8 0.1 stack.40.place
  20.9 0.7 shard_map.37
  21.6 9.5 %all-to-all-done = f32[32,16,256]{2,1,0:T(8,128)S(1)} async-done(((f32[32,16,256]{2,1,0:T(8,128)}), f32[32,16,256]{2,1,0:T(8,128)S(1)}, u32[]{:S(2)}, u32[]{:S(2)}) %all-to-all-start) | async-done | bytes 524320 | tf_op jit(solution)/shard_map/all_to_all | solution.py:211
  31.0 0.7 broadcast_in_dim.6
  31.7 3.3 %all-to-all-start.1 = ((f32[4,2,16,256]{3,2,1,0:T(8,128)}), f32[4,2,16,256]{3,2,1,0:T(8,128)S(1)}, u32[]{:S(2)}, u32[]{:S(2)}) async-start(f32[4,2,16,256]{3,2,1,0:T(8,128)} %broadcast_in_dim.6), calls=%async_computation.1 | async-start | bytes 262144 | tf_op jit(solution)/shard_map/all_to_all | solution.py:225
  35.0 0.0 collective-permute-done.left_ref
  35.0 0.0 collective-permute-done.2.beside_ref
  35.0 3.7 %collective-permute-done.1.ahead_ref = f32[2,256,256]{2,1,0:T(8,128)S(1)} collective-permute-done((f32[2,256,256]{2,1,0:T(8,128)}, f32[2,256,256]{2,1,0:T(8,128)S(1)}, u32[]{:S(2)}, u32[]{:S(2)}) %collective-permute-start.1) | collective-permute-done | bytes 524320 | tf_op jit(solution)/shard_map/ppermute | solution.py:200
  38.7 0.0 copy-done
  38.7 2.5 %shard_map.38 = f32[4,3,2,64,256]{4,3,2,1,0:T(8,128)} custom-call(s32[7]{0:T(128)S(1)} %stack.40.place, f32[2,256,256]{2,1,0:T(8,128)S(1)} %collective-permute-done.left_ref, f32[2,256,256]{2,1,0:T(8,128)S(1)} %collective-permute-done.1.ahead_ref, f32[2,256,256]{2,1,0:T(8,128)S(1)} %collective-permute-done.2.beside_ref, s32[32,256]{1,0:T(8,128)S(1)} %reshape.3.codes, ...), custom_call_target="tpu_custom_call" | custom-call | flops 603979776 | bytes 3964956 | tf_op jit(solution)/shard_map/pallas_call | solution.py:170
  41.2 0.0 all-to-all-done.1.gathered
  41.3 4.3 %all-to-all-start.2 = ((f32[4,3,2,64,256]{4,3,2,1,0:T(8,128)}), f32[4,3,2,64,256]{4,3,2,1,0:T(8,128)S(1)}, u32[]{:S(2)}, u32[]{:S(2)}) async-start(f32[4,3,2,64,256]{4,3,2,1,0:T(8,128)} %shard_map.38), calls=%async_computation.2 | async-start | bytes 3145728 | tf_op jit(solution)/shard_map/all_to_all | solution.py:248
  45.6 1.9 %collective-permute-start.3 = (f32[4,16,256]{2,1,0:T(8,128)S(1)}, f32[4,16,256]{2,1,0:T(8,128)S(1)}, u32[]{:S(2)}, u32[]{:S(2)}) collective-permute-start(f32[4,16,256]{2,1,0:T(8,128)S(1)} %slice_bitcast_fusion), channel_id=1, source_target_pairs={{0,496},{1,497},{2,498},{3,499},{4,500},{5,501},{6,502},{7,503},{8... | collective-permute-start | bytes 196616 | tf_op jit(solution)/shard_map/ppermute | solution.py:237
  47.5 1.9 %collective-permute-done.3.next1 = f32[4,16,256]{2,1,0:T(8,128)S(1)} collective-permute-done((f32[4,16,256]{2,1,0:T(8,128)S(1)}, f32[4,16,256]{2,1,0:T(8,128)S(1)}, u32[]{:S(2)}, u32[]{:S(2)}) %collective-permute-start.3) | collective-permute-done | bytes 65568 | tf_op jit(solution)/shard_map/ppermute | solution.py:237
  49.4 0.6 shard_map.39.refs_0_
  50.0 3.9 %collective-permute-start.6 = (f32[3,4,16,256]{3,2,1,0:T(8,128)S(1)}, f32[3,4,16,256]{3,2,1,0:T(8,128)S(1)}, u32[]{:S(2)}, u32[]{:S(2)}) collective-permute-start(f32[3,4,16,256]{3,2,1,0:T(8,128)S(1)} %shard_map.39.refs_0_), channel_id=1, source_target_pairs={{0,1},{1,0},{2,3},{3,2},{4,5},{5,4},{6,7},{7,6},{8,9},{9,8},{10,11... | collective-permute-start | bytes 589832 | tf_op jit(solution)/shard_map/ppermute | solution.py:228
  53.9 4.0 %collective-permute-start.5 = (f32[3,4,16,256]{3,2,1,0:T(8,128)S(1)}, f32[3,4,16,256]{3,2,1,0:T(8,128)S(1)}, u32[]{:S(2)}, u32[]{:S(2)}) collective-permute-start(f32[3,4,16,256]{3,2,1,0:T(8,128)S(1)} %shard_map.39.refs_0_), channel_id=1, source_target_pairs={{0,3},{1,2},{2,1},{3,0},{4,7},{5,6},{6,5},{7,4},{8,11},{9,10},{10,... | collective-permute-start | bytes 589832 | tf_op jit(solution)/shard_map/ppermute | solution.py:228
  57.9 2.5 %collective-permute-start.4 = (f32[3,4,16,256]{3,2,1,0:T(8,128)S(1)}, f32[3,4,16,256]{3,2,1,0:T(8,128)S(1)}, u32[]{:S(2)}, u32[]{:S(2)}) collective-permute-start(f32[3,4,16,256]{3,2,1,0:T(8,128)S(1)} %shard_map.39.refs_0_), channel_id=1, source_target_pairs={{0,2},{1,3},{2,0},{3,1},{4,6},{5,7},{6,4},{7,5},{8,10},{9,11},{10,... | collective-permute-start | bytes 589832 | tf_op jit(solution)/shard_map/ppermute | solution.py:228
  60.4 6.2 %all-to-all-done.2.got = f32[4,3,2,64,256]{4,3,2,1,0:T(8,128)S(1)} async-done(((f32[4,3,2,64,256]{4,3,2,1,0:T(8,128)}), f32[4,3,2,64,256]{4,3,2,1,0:T(8,128)S(1)}, u32[]{:S(2)}, u32[]{:S(2)}) %all-to-all-start.2) | async-done | bytes 1572896 | tf_op jit(solution)/shard_map/all_to_all | solution.py:248
  66.6 0.8 shard_map.40
  67.5 7.8 %all-to-all-start.3 = ((f32[8,3,16,256]{3,2,1,0:T(8,128)}), f32[8,3,16,256]{3,2,1,0:T(8,128)S(1)}, u32[]{:S(2)}, u32[]{:S(2)}) async-start(f32[8,3,16,256]{3,2,1,0:T(8,128)} %shard_map.40), calls=%async_computation.3 | async-start | bytes 786432 | tf_op jit(solution)/shard_map/all_to_all | solution.py:251
  75.3 0.0 collective-permute-done.6.refs_3_
  75.3 0.0 collective-permute-done.5.refs_2_
  75.3 0.0 collective-permute-done.4.refs_1_
  75.3 0.8 shard_map.41
  76.1 11.1 %all-to-all-done.3.got = f32[8,3,16,256]{3,2,1,0:T(8,128)S(1)} async-done(((f32[8,3,16,256]{3,2,1,0:T(8,128)}), f32[8,3,16,256]{3,2,1,0:T(8,128)S(1)}, u32[]{:S(2)}, u32[]{:S(2)}) %all-to-all-start.3) | async-done | bytes 393248 | tf_op jit(solution)/shard_map/all_to_all | solution.py:251
  87.2 1.1 %shard_map.42 = (f32[3,8,256]{2,1,0:T(8,128)S(1)}, f32[3,8,256]{2,1,0:T(8,128)S(1)}) custom-call(s32[7]{0:T(128)S(1)} %stack.40.place, f32[8,3,16,256]{3,2,1,0:T(8,128)S(1)} %all-to-all-done.3.got, bf16[3,256,256]{2,1,0:T(8,128)(2,1)S(1)} %get-tuple-element.25.high, bf16[3,256,256]{2,1,0:T(8,128)(2,1)S(1)} %get-tuple-element.26.low), custom_call_target="tpu_custom_call" | custom-call | flops 18874368 | bytes 2015260 | tf_op jit(solution)/shard_map/pallas_call | solution.py:170
  88.3 1.9 %collective-permute-start.7 = (f32[3,8,256]{2,1,0:T(8,128)S(1)}, f32[3,8,256]{2,1,0:T(8,128)S(1)}, u32[]{:S(2)}, u32[]{:S(2)}) collective-permute-start(f32[3,8,256]{2,1,0:T(8,128)S(1)} %get-tuple-element.27), channel_id=1, source_target_pairs={{0,464},{1,465},{2,466},{3,467},{4,468},{5,469},{6,470},{7,471},{8... | collective-permute-start | bytes 73736 | tf_op jit(solution)/shard_map/ppermute | solution.py:264
  90.2 1.9 %collective-permute-start.8 = (f32[3,8,256]{2,1,0:T(8,128)S(1)}, f32[3,8,256]{2,1,0:T(8,128)S(1)}, u32[]{:S(2)}, u32[]{:S(2)}) collective-permute-start(f32[3,8,256]{2,1,0:T(8,128)S(1)} %get-tuple-element.28), channel_id=1, source_target_pairs={{0,448},{1,449},{2,450},{3,451},{4,452},{5,453},{6,454},{7,455},{8... | collective-permute-start | bytes 73736 | tf_op jit(solution)/shard_map/ppermute | solution.py:264
  92.1 7.9 %collective-permute-done.7.back1 = f32[3,8,256]{2,1,0:T(8,128)S(1)} collective-permute-done((f32[3,8,256]{2,1,0:T(8,128)S(1)}, f32[3,8,256]{2,1,0:T(8,128)S(1)}, u32[]{:S(2)}, u32[]{:S(2)}) %collective-permute-start.7) | collective-permute-done | bytes 24608 | tf_op jit(solution)/shard_map/ppermute | solution.py:264
  100.0 0.0 collective-permute-done.8.back0
  100.0 1.2 %shard_map.43 = f32[3,2,8,256]{3,2,1,0:T(8,128)} custom-call(s32[7]{0:T(128)S(1)} %stack.40.place, f32[3,8,256]{2,1,0:T(8,128)S(1)} %collective-permute-done.7.back1, f32[3,8,256]{2,1,0:T(8,128)S(1)} %collective-permute-done.8.back0), custom_call_target="tpu_custom_call" | custom-call | flops 10000 | bytes 98332 | tf_op jit(solution)/shard_map/pallas_call | solution.py:170
  (3 shorter events, 0.0 us)
Async XLA Ops:
  0.0 38.7 %copy-start = (f32[2,1,1,1,256,256]{5,4,3,2,1,0:T(8,128)S(1)}, f32[2,1,1,1,256,256]{5,4,3,2,1,0:T(8,128)}, u32[]{:S(2)}) copy-start(f32[2,1,1,1,256,256]{5,4,3,2,1,0:T(8,128)} %param.3) | copy-start | bytes 1572868
  0.0 31.0 %all-to-all-start = ((f32[32,16,256]{2,1,0:T(8,128)}), f32[32,16,256]{2,1,0:T(8,128)S(1)}, u32[]{:S(2)}, u32[]{:S(2)}) async-start(f32[32,16,256]{2,1,0:T(8,128)} %bitcast.15), calls=%async_computation | async-start | bytes 1048576 | tf_op jit(solution)/shard_map/all_to_all | solution.py:211
  13.3 21.7 %collective-permute-start = (f32[2,256,256]{2,1,0:T(8,128)}, f32[2,256,256]{2,1,0:T(8,128)S(1)}, u32[]{:S(2)}, u32[]{:S(2)}) collective-permute-start(f32[2,256,256]{2,1,0:T(8,128)} %bitcast.19), channel_id=1, source_target_pairs={{0,64},{64,128},{128,192},{192,256},{256,320},{320,384},{384,448},... | collective-permute-start | bytes 1572872 | tf_op jit(solution)/shard_map/ppermute | solution.py:200
  18.0 17.0 %collective-permute-start.2 = (f32[2,256,256]{2,1,0:T(8,128)}, f32[2,256,256]{2,1,0:T(8,128)S(1)}, u32[]{:S(2)}, u32[]{:S(2)}) collective-permute-start(f32[2,256,256]{2,1,0:T(8,128)} %bitcast.16), channel_id=1, source_target_pairs={{0,480},{32,0},{64,32},{96,64},{128,96},{160,128},{192,160},{224,1... | collective-permute-start | bytes 1572872 | tf_op jit(solution)/shard_map/ppermute | solution.py:203
  18.0 20.7 %collective-permute-start.1 = (f32[2,256,256]{2,1,0:T(8,128)}, f32[2,256,256]{2,1,0:T(8,128)S(1)}, u32[]{:S(2)}, u32[]{:S(2)}) collective-permute-start(f32[2,256,256]{2,1,0:T(8,128)} %bitcast.17), channel_id=1, source_target_pairs={{0,448},{64,0},{128,64},{192,128},{256,192},{320,256},{384,320},{4... | collective-permute-start | bytes 1572872 | tf_op jit(solution)/shard_map/ppermute | solution.py:200
  31.7 9.6 %all-to-all-start.1 = ((f32[4,2,16,256]{3,2,1,0:T(8,128)}), f32[4,2,16,256]{3,2,1,0:T(8,128)S(1)}, u32[]{:S(2)}, u32[]{:S(2)}) async-start(f32[4,2,16,256]{3,2,1,0:T(8,128)} %broadcast_in_dim.6), calls=%async_computation.1 | async-start | bytes 262144 | tf_op jit(solution)/shard_map/all_to_all | solution.py:225
  41.3 25.4 %all-to-all-start.2 = ((f32[4,3,2,64,256]{4,3,2,1,0:T(8,128)}), f32[4,3,2,64,256]{4,3,2,1,0:T(8,128)S(1)}, u32[]{:S(2)}, u32[]{:S(2)}) async-start(f32[4,3,2,64,256]{4,3,2,1,0:T(8,128)} %shard_map.38), calls=%async_computation.2 | async-start | bytes 3145728 | tf_op jit(solution)/shard_map/all_to_all | solution.py:248
  45.6 3.8 %collective-permute-start.3 = (f32[4,16,256]{2,1,0:T(8,128)S(1)}, f32[4,16,256]{2,1,0:T(8,128)S(1)}, u32[]{:S(2)}, u32[]{:S(2)}) collective-permute-start(f32[4,16,256]{2,1,0:T(8,128)S(1)} %slice_bitcast_fusion), channel_id=1, source_target_pairs={{0,496},{1,497},{2,498},{3,499},{4,500},{5,501},{6,502},{7,503},{8... | collective-permute-start | bytes 196616 | tf_op jit(solution)/shard_map/ppermute | solution.py:237
  50.0 25.3 %collective-permute-start.6 = (f32[3,4,16,256]{3,2,1,0:T(8,128)S(1)}, f32[3,4,16,256]{3,2,1,0:T(8,128)S(1)}, u32[]{:S(2)}, u32[]{:S(2)}) collective-permute-start(f32[3,4,16,256]{3,2,1,0:T(8,128)S(1)} %shard_map.39.refs_0_), channel_id=1, source_target_pairs={{0,1},{1,0},{2,3},{3,2},{4,5},{5,4},{6,7},{7,6},{8,9},{9,8},{10,11... | collective-permute-start | bytes 589832 | tf_op jit(solution)/shard_map/ppermute | solution.py:228
  53.9 21.4 %collective-permute-start.5 = (f32[3,4,16,256]{3,2,1,0:T(8,128)S(1)}, f32[3,4,16,256]{3,2,1,0:T(8,128)S(1)}, u32[]{:S(2)}, u32[]{:S(2)}) collective-permute-start(f32[3,4,16,256]{3,2,1,0:T(8,128)S(1)} %shard_map.39.refs_0_), channel_id=1, source_target_pairs={{0,3},{1,2},{2,1},{3,0},{4,7},{5,6},{6,5},{7,4},{8,11},{9,10},{10,... | collective-permute-start | bytes 589832 | tf_op jit(solution)/shard_map/ppermute | solution.py:228
  57.9 17.4 %collective-permute-start.4 = (f32[3,4,16,256]{3,2,1,0:T(8,128)S(1)}, f32[3,4,16,256]{3,2,1,0:T(8,128)S(1)}, u32[]{:S(2)}, u32[]{:S(2)}) collective-permute-start(f32[3,4,16,256]{3,2,1,0:T(8,128)S(1)} %shard_map.39.refs_0_), channel_id=1, source_target_pairs={{0,2},{1,3},{2,0},{3,1},{4,6},{5,7},{6,4},{7,5},{8,10},{9,11},{10,... | collective-permute-start | bytes 589832 | tf_op jit(solution)/shard_map/ppermute | solution.py:228
  67.5 19.7 %all-to-all-start.3 = ((f32[8,3,16,256]{3,2,1,0:T(8,128)}), f32[8,3,16,256]{3,2,1,0:T(8,128)S(1)}, u32[]{:S(2)}, u32[]{:S(2)}) async-start(f32[8,3,16,256]{3,2,1,0:T(8,128)} %shard_map.40), calls=%async_computation.3 | async-start | bytes 786432 | tf_op jit(solution)/shard_map/all_to_all | solution.py:251
  88.3 11.7 %collective-permute-start.7 = (f32[3,8,256]{2,1,0:T(8,128)S(1)}, f32[3,8,256]{2,1,0:T(8,128)S(1)}, u32[]{:S(2)}, u32[]{:S(2)}) collective-permute-start(f32[3,8,256]{2,1,0:T(8,128)S(1)} %get-tuple-element.27), channel_id=1, source_target_pairs={{0,464},{1,465},{2,466},{3,467},{4,468},{5,469},{6,470},{7,471},{8... | collective-permute-start | bytes 73736 | tf_op jit(solution)/shard_map/ppermute | solution.py:264
  90.2 9.8 %collective-permute-start.8 = (f32[3,8,256]{2,1,0:T(8,128)S(1)}, f32[3,8,256]{2,1,0:T(8,128)S(1)}, u32[]{:S(2)}, u32[]{:S(2)}) collective-permute-start(f32[3,8,256]{2,1,0:T(8,128)S(1)} %get-tuple-element.28), channel_id=1, source_target_pairs={{0,448},{1,449},{2,450},{3,451},{4,452},{5,453},{6,454},{7,455},{8... | collective-permute-start | bytes 73736 | tf_op jit(solution)/shard_map/ppermute | solution.py:264

commit v13 on v12

--- a/solution.py
+++ b/solution.py
@@ -227,6 +227,7 @@
     def partner(v, axis, n, j):
         return lax.ppermute(v, axis, [(i, i ^ j) for i in range(n)])
 
+    ahead, beside, gathered = lax.optimization_barrier((ahead, beside, gathered))
     wide = (sizes[4], WIN, slots, size // sizes[4], size)
     (parts,) = call(
         functools.partial(product_kernel, factor),

time: 102 us -> 101 us (level)
  the two profiles are of different devices: /device:TPU:24 before, /device:TPU:6 now
where the time goes in v13:
time: 101 us; the launch traced here: 98.8 us
  starting transfers between devices  56.4 us (56%)
  waiting for transfers between devices  33.1 us (33%)
  Pallas kernels  7.65 us (8%)
  local copies, waits for them, and re-layouts  1.53 us (2%)
    all_to_all x1, starting transfers between devices, on_device(): lax.all_to_all(home.reshape(cols_count, part, size), AXES[2:], 0, 0)  13.5 us
    ppermute x3, starting transfers between devices, partner(): return lax.ppermute(v, axis, [(i, i ^ j) for i in range(n)])  9.82 us
    ppermute x2, starting transfers between devices, on_device(): lax.ppermute(sent[flip], AXES, pairs_of(sizes, sent_to(flip)))  9.32 us
    all_to_all x1, waiting for transfers between devices, on_device(): got = lax.all_to_all(ready, ('zh', 'zl'), 0, 0)  9.27 us
    pallas_call x7, Pallas kernels, call(): pl.pallas_call(kernel, out_shape=[jax.ShapeDtypeStruct(s, kind) for s in...  7.65 us
    all_to_all x1, waiting for transfers between devices, on_device(): lax.all_to_all(home.reshape(cols_count, part, size), AXES[2:], 0, 0)  7.03 us
    all_to_all x1, waiting for transfers between devices, on_device(): lax.all_to_all(jnp.broadcast_to(near, (sizes[3],) + near.shape), 'zl', 0, 0)  5.87 us
    ppermute x2, starting transfers between devices, row_shift(): return lax.ppermute(v, 'y', [(i, (i + by) % n) for i in range(n)])  5.83 us
  transfers between devices with their start and end apart: 13, of which 8 were waited for; matrix products, arithmetic and copies ran while one was open for 2% of the time, Pallas kernels for 3%

profile of v13, /device:TPU:6, one launch (start us, length us, event | category | flops | bytes accessed | tf_op | source)
XLA Modules:
  0.0 98.8 jit_solution(12107649929347942285)
XLA Ops:
  0.0 0.0 copy-start
  0.0 13.5 %all-to-all-start = ((f32[32,16,256]{2,1,0:T(8,128)}), f32[32,16,256]{2,1,0:T(8,128)S(1)}, u32[]{:S(2)}, u32[]{:S(2)}) async-start(f32[32,16,256]{2,1,0:T(8,128)} %bitcast.15), calls=%async_computation | async-start | bytes 1048576 | tf_op jit(solution)/shard_map/all_to_all | solution.py:211
  13.6 2.4 %collective-permute-start.2 = (f32[2,256,256]{2,1,0:T(8,128)}, f32[2,256,256]{2,1,0:T(8,128)S(1)}, u32[]{:S(2)}, u32[]{:S(2)}) collective-permute-start(f32[2,256,256]{2,1,0:T(8,128)} %bitcast.16), channel_id=1, source_target_pairs={{0,480},{32,0},{64,32},{96,64},{128,96},{160,128},{192,160},{224,1... | collective-permute-start | bytes 1572872 | tf_op jit(solution)/shard_map/ppermute | solution.py:203
  15.9 3.2 %collective-permute-start.1 = (f32[2,256,256]{2,1,0:T(8,128)}, f32[2,256,256]{2,1,0:T(8,128)S(1)}, u32[]{:S(2)}, u32[]{:S(2)}) collective-permute-start(f32[2,256,256]{2,1,0:T(8,128)} %bitcast.17), channel_id=1, source_target_pairs={{0,448},{64,0},{128,64},{192,128},{256,192},{320,256},{384,320},{4... | collective-permute-start | bytes 1572872 | tf_op jit(solution)/shard_map/ppermute | solution.py:200
  19.2 2.6 %collective-permute-start = (f32[2,256,256]{2,1,0:T(8,128)}, f32[2,256,256]{2,1,0:T(8,128)S(1)}, u32[]{:S(2)}, u32[]{:S(2)}) collective-permute-start(f32[2,256,256]{2,1,0:T(8,128)} %bitcast.19), channel_id=1, source_target_pairs={{0,64},{64,128},{128,192},{192,256},{256,320},{320,384},{384,448},... | collective-permute-start | bytes 1572872 | tf_op jit(solution)/shard_map/ppermute | solution.py:200
  21.8 0.8 reshape.3.codes
  22.6 0.1 stack.40.place
  22.6 0.7 shard_map.37
  23.4 7.0 %all-to-all-done = f32[32,16,256]{2,1,0:T(8,128)S(1)} async-done(((f32[32,16,256]{2,1,0:T(8,128)}), f32[32,16,256]{2,1,0:T(8,128)S(1)}, u32[]{:S(2)}, u32[]{:S(2)}) %all-to-all-start) | async-done | bytes 524320 | tf_op jit(solution)/shard_map/all_to_all | solution.py:211
  30.4 0.7 broadcast_in_dim.6
  31.0 3.3 %all-to-all-start.1 = ((f32[4,2,16,256]{3,2,1,0:T(8,128)}), f32[4,2,16,256]{3,2,1,0:T(8,128)S(1)}, u32[]{:S(2)}, u32[]{:S(2)}) async-start(f32[4,2,16,256]{3,2,1,0:T(8,128)} %broadcast_in_dim.6), calls=%async_computation.1 | async-start | bytes 262144 | tf_op jit(solution)/shard_map/all_to_all | solution.py:225
  34.4 0.0 collective-permute-done.2.beside_ref
  34.4 0.0 collective-permute-done.1.ahead_ref
  34.4 5.9 %all-to-all-done.1.gathered = f32[4,2,16,256]{3,2,1,0:T(8,128)S(1)} async-done(((f32[4,2,16,256]{3,2,1,0:T(8,128)}), f32[4,2,16,256]{3,2,1,0:T(8,128)S(1)}, u32[]{:S(2)}, u32[]{:S(2)}) %all-to-all-start.1) | async-done | bytes 131104 | tf_op jit(solution)/shard_map/all_to_all | solution.py:225
  40.3 0.0 collective-permute-done.left_ref
  40.3 0.0 copy-done
  40.3 2.5 %shard_map.38 = f32[4,3,2,64,256]{4,3,2,1,0:T(8,128)} custom-call(s32[7]{0:T(128)S(1)} %stack.40.place, f32[2,256,256]{2,1,0:T(8,128)S(1)} %collective-permute-done.left_ref, f32[2,256,256]{2,1,0:T(8,128)S(1)} %collective-permute-done.1.ahead_ref, f32[2,256,256]{2,1,0:T(8,128)S(1)} %collective-permute-done.2.beside_ref, s32[32,256]{1,0:T(8,128)S(1)} %reshape.3.codes, ...), custom_call_target="tpu_custom_call" | custom-call | flops 603979776 | bytes 3964956 | tf_op jit(solution)/shard_map/pallas_call | solution.py:170
  42.8 4.8 %all-to-all-start.2 = ((f32[4,3,2,64,256]{4,3,2,1,0:T(8,128)}), f32[4,3,2,64,256]{4,3,2,1,0:T(8,128)S(1)}, u32[]{:S(2)}, u32[]{:S(2)}) async-start(f32[4,3,2,64,256]{4,3,2,1,0:T(8,128)} %shard_map.38), calls=%async_computation.2 | async-start | bytes 3145728 | tf_op jit(solution)/shard_map/all_to_all | solution.py:249
  47.6 2.9 %collective-permute-start.3 = (f32[4,16,256]{2,1,0:T(8,128)S(1)}, f32[4,16,256]{2,1,0:T(8,128)S(1)}, u32[]{:S(2)}, u32[]{:S(2)}) collective-permute-start(f32[4,16,256]{2,1,0:T(8,128)S(1)} %slice_bitcast_fusion), channel_id=1, source_target_pairs={{0,496},{1,497},{2,498},{3,499},{4,500},{5,501},{6,502},{7,503},{8... | collective-permute-start | bytes 196616 | tf_op jit(solution)/shard_map/ppermute | solution.py:238
  50.5 1.9 %collective-permute-done.3.next1 = f32[4,16,256]{2,1,0:T(8,128)S(1)} collective-permute-done((f32[4,16,256]{2,1,0:T(8,128)S(1)}, f32[4,16,256]{2,1,0:T(8,128)S(1)}, u32[]{:S(2)}, u32[]{:S(2)}) %collective-permute-start.3) | collective-permute-done | bytes 65568 | tf_op jit(solution)/shard_map/ppermute | solution.py:238
  52.3 0.6 shard_map.39.refs_0_
  52.9 2.8 %collective-permute-start.6 = (f32[3,4,16,256]{3,2,1,0:T(8,128)S(1)}, f32[3,4,16,256]{3,2,1,0:T(8,128)S(1)}, u32[]{:S(2)}, u32[]{:S(2)}) collective-permute-start(f32[3,4,16,256]{3,2,1,0:T(8,128)S(1)} %shard_map.39.refs_0_), channel_id=1, source_target_pairs={{0,1},{1,0},{2,3},{3,2},{4,5},{5,4},{6,7},{7,6},{8,9},{9,8},{10,11... | collective-permute-start | bytes 589832 | tf_op jit(solution)/shard_map/ppermute | solution.py:228
  55.7 3.1 %collective-permute-start.5 = (f32[3,4,16,256]{3,2,1,0:T(8,128)S(1)}, f32[3,4,16,256]{3,2,1,0:T(8,128)S(1)}, u32[]{:S(2)}, u32[]{:S(2)}) collective-permute-start(f32[3,4,16,256]{3,2,1,0:T(8,128)S(1)} %shard_map.39.refs_0_), channel_id=1, source_target_pairs={{0,3},{1,2},{2,1},{3,0},{4,7},{5,6},{6,5},{7,4},{8,11},{9,10},{10,... | collective-permute-start | bytes 589832 | tf_op jit(solution)/shard_map/ppermute | solution.py:228
  58.8 4.0 %collective-permute-start.4 = (f32[3,4,16,256]{3,2,1,0:T(8,128)S(1)}, f32[3,4,16,256]{3,2,1,0:T(8,128)S(1)}, u32[]{:S(2)}, u32[]{:S(2)}) collective-permute-start(f32[3,4,16,256]{3,2,1,0:T(8,128)S(1)} %shard_map.39.refs_0_), channel_id=1, source_target_pairs={{0,2},{1,3},{2,0},{3,1},{4,6},{5,7},{6,4},{7,5},{8,10},{9,11},{10,... | collective-permute-start | bytes 589832 | tf_op jit(solution)/shard_map/ppermute | solution.py:228
  62.8 3.4 %all-to-all-done.2.got = f32[4,3,2,64,256]{4,3,2,1,0:T(8,128)S(1)} async-done(((f32[4,3,2,64,256]{4,3,2,1,0:T(8,128)}), f32[4,3,2,64,256]{4,3,2,1,0:T(8,128)S(1)}, u32[]{:S(2)}, u32[]{:S(2)}) %all-to-all-start.2) | async-done | bytes 1572896 | tf_op jit(solution)/shard_map/all_to_all | solution.py:249
  66.2 0.8 shard_map.40
  67.0 4.5 %all-to-all-start.3 = ((f32[8,3,16,256]{3,2,1,0:T(8,128)}), f32[8,3,16,256]{3,2,1,0:T(8,128)S(1)}, u32[]{:S(2)}, u32[]{:S(2)}) async-start(f32[8,3,16,256]{3,2,1,0:T(8,128)} %shard_map.40), calls=%async_computation.3 | async-start | bytes 786432 | tf_op jit(solution)/shard_map/all_to_all | solution.py:252
  71.5 0.0 collective-permute-done.6.refs_3_
  71.5 1.8 %collective-permute-done.5.refs_2_ = f32[3,4,16,256]{3,2,1,0:T(8,128)S(1)} collective-permute-done((f32[3,4,16,256]{3,2,1,0:T(8,128)S(1)}, f32[3,4,16,256]{3,2,1,0:T(8,128)S(1)}, u32[]{:S(2)}, u32[]{:S(2)}) %collective-permute-start.5) | collective-permute-done | bytes 196640 | tf_op jit(solution)/shard_map/ppermute | solution.py:228
  73.4 0.0 collective-permute-done.4.refs_1_
  73.4 0.8 shard_map.41
  74.2 9.3 %all-to-all-done.3.got = f32[8,3,16,256]{3,2,1,0:T(8,128)S(1)} async-done(((f32[8,3,16,256]{3,2,1,0:T(8,128)}), f32[8,3,16,256]{3,2,1,0:T(8,128)S(1)}, u32[]{:S(2)}, u32[]{:S(2)}) %all-to-all-start.3) | async-done | bytes 393248 | tf_op jit(solution)/shard_map/all_to_all | solution.py:252
  83.4 1.1 %shard_map.42 = (f32[3,8,256]{2,1,0:T(8,128)S(1)}, f32[3,8,256]{2,1,0:T(8,128)S(1)}) custom-call(s32[7]{0:T(128)S(1)} %stack.40.place, f32[8,3,16,256]{3,2,1,0:T(8,128)S(1)} %all-to-all-done.3.got, bf16[3,256,256]{2,1,0:T(8,128)(2,1)S(1)} %get-tuple-element.31.high, bf16[3,256,256]{2,1,0:T(8,128)(2,1)S(1)} %get-tuple-element.32.low), custom_call_target="tpu_custom_call" | custom-call | flops 18874368 | bytes 2015260 | tf_op jit(solution)/shard_map/pallas_call | solution.py:170
  84.5 7.4 %collective-permute-start.7 = (f32[3,8,256]{2,1,0:T(8,128)S(1)}, f32[3,8,256]{2,1,0:T(8,128)S(1)}, u32[]{:S(2)}, u32[]{:S(2)}) collective-permute-start(f32[3,8,256]{2,1,0:T(8,128)S(1)} %get-tuple-element.33), channel_id=1, source_target_pairs={{0,464},{1,465},{2,466},{3,467},{4,468},{5,469},{6,470},{7,471},{8... | collective-permute-start | bytes 73736 | tf_op jit(solution)/shard_map/ppermute | solution.py:265
  91.9 1.9 %collective-permute-start.8 = (f32[3,8,256]{2,1,0:T(8,128)S(1)}, f32[3,8,256]{2,1,0:T(8,128)S(1)}, u32[]{:S(2)}, u32[]{:S(2)}) collective-permute-start(f32[3,8,256]{2,1,0:T(8,128)S(1)} %get-tuple-element.34), channel_id=1, source_target_pairs={{0,448},{1,449},{2,450},{3,451},{4,452},{5,453},{6,454},{7,455},{8... | collective-permute-start | bytes 73736 | tf_op jit(solution)/shard_map/ppermute | solution.py:265
  93.9 1.2 %collective-permute-done.7.back1 = f32[3,8,256]{2,1,0:T(8,128)S(1)} collective-permute-done((f32[3,8,256]{2,1,0:T(8,128)S(1)}, f32[3,8,256]{2,1,0:T(8,128)S(1)}, u32[]{:S(2)}, u32[]{:S(2)}) %collective-permute-start.7) | collective-permute-done | bytes 24608 | tf_op jit(solution)/shard_map/ppermute | solution.py:265
  95.1 2.6 %collective-permute-done.8.back0 = f32[3,8,256]{2,1,0:T(8,128)S(1)} collective-permute-done((f32[3,8,256]{2,1,0:T(8,128)S(1)}, f32[3,8,256]{2,1,0:T(8,128)S(1)}, u32[]{:S(2)}, u32[]{:S(2)}) %collective-permute-start.8) | collective-permute-done | bytes 24608 | tf_op jit(solution)/shard_map/ppermute | solution.py:265
  97.7 1.2 %shard_map.43 = f32[3,2,8,256]{3,2,1,0:T(8,128)} custom-call(s32[7]{0:T(128)S(1)} %stack.40.place, f32[3,8,256]{2,1,0:T(8,128)S(1)} %collective-permute-done.7.back1, f32[3,8,256]{2,1,0:T(8,128)S(1)} %collective-permute-done.8.back0), custom_call_target="tpu_custom_call" | custom-call | flops 10000 | bytes 98332 | tf_op jit(solution)/shard_map/pallas_call | solution.py:170
  (3 shorter events, 0.0 us)
Async XLA Ops:
  0.0 40.3 %copy-start = (f32[2,1,1,1,256,256]{5,4,3,2,1,0:T(8,128)S(1)}, f32[2,1,1,1,256,256]{5,4,3,2,1,0:T(8,128)}, u32[]{:S(2)}) copy-start(f32[2,1,1,1,256,256]{5,4,3,2,1,0:T(8,128)} %param.3) | copy-start | bytes 1572868
  0.0 30.4 %all-to-all-start = ((f32[32,16,256]{2,1,0:T(8,128)}), f32[32,16,256]{2,1,0:T(8,128)S(1)}, u32[]{:S(2)}, u32[]{:S(2)}) async-start(f32[32,16,256]{2,1,0:T(8,128)} %bitcast.15), calls=%async_computation | async-start | bytes 1048576 | tf_op jit(solution)/shard_map/all_to_all | solution.py:211
  13.6 20.8 %collective-permute-start.2 = (f32[2,256,256]{2,1,0:T(8,128)}, f32[2,256,256]{2,1,0:T(8,128)S(1)}, u32[]{:S(2)}, u32[]{:S(2)}) collective-permute-start(f32[2,256,256]{2,1,0:T(8,128)} %bitcast.16), channel_id=1, source_target_pairs={{0,480},{32,0},{64,32},{96,64},{128,96},{160,128},{192,160},{224,1... | collective-permute-start | bytes 1572872 | tf_op jit(solution)/shard_map/ppermute | solution.py:203
  15.9 18.5 %collective-permute-start.1 = (f32[2,256,256]{2,1,0:T(8,128)}, f32[2,256,256]{2,1,0:T(8,128)S(1)}, u32[]{:S(2)}, u32[]{:S(2)}) collective-permute-start(f32[2,256,256]{2,1,0:T(8,128)} %bitcast.17), channel_id=1, source_target_pairs={{0,448},{64,0},{128,64},{192,128},{256,192},{320,256},{384,320},{4... | collective-permute-start | bytes 1572872 | tf_op jit(solution)/shard_map/ppermute | solution.py:200
  19.2 21.1 %collective-permute-start = (f32[2,256,256]{2,1,0:T(8,128)}, f32[2,256,256]{2,1,0:T(8,128)S(1)}, u32[]{:S(2)}, u32[]{:S(2)}) collective-permute-start(f32[2,256,256]{2,1,0:T(8,128)} %bitcast.19), channel_id=1, source_target_pairs={{0,64},{64,128},{128,192},{192,256},{256,320},{320,384},{384,448},... | collective-permute-start | bytes 1572872 | tf_op jit(solution)/shard_map/ppermute | solution.py:200
  31.0 9.2 %all-to-all-start.1 = ((f32[4,2,16,256]{3,2,1,0:T(8,128)}), f32[4,2,16,256]{3,2,1,0:T(8,128)S(1)}, u32[]{:S(2)}, u32[]{:S(2)}) async-start(f32[4,2,16,256]{3,2,1,0:T(8,128)} %broadcast_in_dim.6), calls=%async_computation.1 | async-start | bytes 262144 | tf_op jit(solution)/shard_map/all_to_all | solution.py:225
  42.8 23.4 %all-to-all-start.2 = ((f32[4,3,2,64,256]{4,3,2,1,0:T(8,128)}), f32[4,3,2,64,256]{4,3,2,1,0:T(8,128)S(1)}, u32[]{:S(2)}, u32[]{:S(2)}) async-start(f32[4,3,2,64,256]{4,3,2,1,0:T(8,128)} %shard_map.38), calls=%async_computation.2 | async-start | bytes 3145728 | tf_op jit(solution)/shard_map/all_to_all | solution.py:249
  47.6 4.7 %collective-permute-start.3 = (f32[4,16,256]{2,1,0:T(8,128)S(1)}, f32[4,16,256]{2,1,0:T(8,128)S(1)}, u32[]{:S(2)}, u32[]{:S(2)}) collective-permute-start(f32[4,16,256]{2,1,0:T(8,128)S(1)} %slice_bitcast_fusion), channel_id=1, source_target_pairs={{0,496},{1,497},{2,498},{3,499},{4,500},{5,501},{6,502},{7,503},{8... | collective-permute-start | bytes 196616 | tf_op jit(solution)/shard_map/ppermute | solution.py:238
  52.9 18.6 %collective-permute-start.6 = (f32[3,4,16,256]{3,2,1,0:T(8,128)S(1)}, f32[3,4,16,256]{3,2,1,0:T(8,128)S(1)}, u32[]{:S(2)}, u32[]{:S(2)}) collective-permute-start(f32[3,4,16,256]{3,2,1,0:T(8,128)S(1)} %shard_map.39.refs_0_), channel_id=1, source_target_pairs={{0,1},{1,0},{2,3},{3,2},{4,5},{5,4},{6,7},{7,6},{8,9},{9,8},{10,11... | collective-permute-start | bytes 589832 | tf_op jit(solution)/shard_map/ppermute | solution.py:228
  55.7 17.7 %collective-permute-start.5 = (f32[3,4,16,256]{3,2,1,0:T(8,128)S(1)}, f32[3,4,16,256]{3,2,1,0:T(8,128)S(1)}, u32[]{:S(2)}, u32[]{:S(2)}) collective-permute-start(f32[3,4,16,256]{3,2,1,0:T(8,128)S(1)} %shard_map.39.refs_0_), channel_id=1, source_target_pairs={{0,3},{1,2},{2,1},{3,0},{4,7},{5,6},{6,5},{7,4},{8,11},{9,10},{10,... | collective-permute-start | bytes 589832 | tf_op jit(solution)/shard_map/ppermute | solution.py:228
  58.8 14.6 %collective-permute-start.4 = (f32[3,4,16,256]{3,2,1,0:T(8,128)S(1)}, f32[3,4,16,256]{3,2,1,0:T(8,128)S(1)}, u32[]{:S(2)}, u32[]{:S(2)}) collective-permute-start(f32[3,4,16,256]{3,2,1,0:T(8,128)S(1)} %shard_map.39.refs_0_), channel_id=1, source_target_pairs={{0,2},{1,3},{2,0},{3,1},{4,6},{5,7},{6,4},{7,5},{8,10},{9,11},{10,... | collective-permute-start | bytes 589832 | tf_op jit(solution)/shard_map/ppermute | solution.py:228
  67.0 16.4 %all-to-all-start.3 = ((f32[8,3,16,256]{3,2,1,0:T(8,128)}), f32[8,3,16,256]{3,2,1,0:T(8,128)S(1)}, u32[]{:S(2)}, u32[]{:S(2)}) async-start(f32[8,3,16,256]{3,2,1,0:T(8,128)} %shard_map.40), calls=%async_computation.3 | async-start | bytes 786432 | tf_op jit(solution)/shard_map/all_to_all | solution.py:252
  84.5 10.5 %collective-permute-start.7 = (f32[3,8,256]{2,1,0:T(8,128)S(1)}, f32[3,8,256]{2,1,0:T(8,128)S(1)}, u32[]{:S(2)}, u32[]{:S(2)}) collective-permute-start(f32[3,8,256]{2,1,0:T(8,128)S(1)} %get-tuple-element.33), channel_id=1, source_target_pairs={{0,464},{1,465},{2,466},{3,467},{4,468},{5,469},{6,470},{7,471},{8... | collective-permute-start | bytes 73736 | tf_op jit(solution)/shard_map/ppermute | solution.py:265
  91.9 5.7 %collective-permute-start.8 = (f32[3,8,256]{2,1,0:T(8,128)S(1)}, f32[3,8,256]{2,1,0:T(8,128)S(1)}, u32[]{:S(2)}, u32[]{:S(2)}) collective-permute-start(f32[3,8,256]{2,1,0:T(8,128)S(1)} %get-tuple-element.34), channel_id=1, source_target_pairs={{0,448},{1,449},{2,450},{3,451},{4,452},{5,453},{6,454},{7,455},{8... | collective-permute-start | bytes 73736 | tf_op jit(solution)/shard_map/ppermute | solution.py:265

commit v14 on v13

--- a/solution.py
+++ b/solution.py
@@ -240,14 +240,14 @@
         functools.partial(pack_kernel, sizes[4]),
         1, [(3, sizes[3], part, size)], [], 10**6, place, codes, pack_columns, gathered, next1,
     )
+    parts = lax.all_to_all(parts, "x", 0, 0)
+    parts, later = lax.optimization_barrier((parts, pack))
     order = (0, 2, 3, 1)
-    packs = [pack] + [partner(pack, "x", sizes[4], j) for j in order[1:]]
+    packs = [pack] + [partner(later if j == 2 else pack, "x", sizes[4], j) for j in order[1:]]
     high, low = call(
         functools.partial(assemble_kernel, order), 1, [(3, size, size)] * 2, [pltpu.VMEM((3, size, size), F32)], 2 * 10**10,
         place, *packs, kind=jnp.bfloat16,
     )
-    parts = lax.all_to_all(parts, "x", 0, 0)
-    parts, _ = lax.optimization_barrier((parts, pack))
     (ready,) = call(add_kernel, 0, [(slots * sizes[3], WIN, part, size)], [], 10**6, parts)
     got = lax.all_to_all(ready, ("zh", "zl"), 0, 0)
     piece = part // slots

time: 101 us -> 101 us (level); the launches traced: 98.8 us -> 99.9 us
  waiting for transfers between devices: 33.1 us -> 36.1 us
  starting transfers between devices: 56.4 us -> 54.4 us
    all_to_all x1, waiting for transfers between devices: 3.43 us -> 7.13 us  [on_device(): parts = lax.all_to_all(parts, 'x', 0, 0)]
    ppermute x2, starting transfers between devices: 9.32 us -> 7.39 us  [on_device(): lax.ppermute(sent[flip], AXES, pairs_of(sizes, sent_to(flip)))]
    ppermute x3, waiting for transfers between devices: 1.84 us -> 0.01 us  [partner(): return lax.ppermute(v, axis, [(i, i ^ j) for i in range(n)])]
    all_to_all x1, waiting for transfers between devices: 9.27 us -> 11.1 us  [on_device(): got = lax.all_to_all(ready, ('zh', 'zl'), 0, 0)]
  transfers between devices with their start and end apart: 13 -> 13, of which waited for: 8 -> 6; matrix products, arithmetic and copies ran while one was open for 2% -> 2% of each run, Pallas kernels for 3% -> 3%
where the time goes in v14:
time: 101 us; the launch traced here: 99.9 us
  starting transfers between devices  54.4 us (54%)
  waiting for transfers between devices  36.1 us (36%)
  Pallas kernels  7.65 us (8%)
  local copies, waits for them, and re-layouts  1.53 us (2%)
    all_to_all x1, starting transfers between devices, on_device(): lax.all_to_all(home.reshape(cols_count, part, size), AXES[2:], 0, 0)  13.5 us
    all_to_all x1, waiting for transfers between devices, on_device(): got = lax.all_to_all(ready, ('zh', 'zl'), 0, 0)  11.1 us
    ppermute x3, starting transfers between devices, partner(): return lax.ppermute(v, axis, [(i, i ^ j) for i in range(n)])  9.8 us
    pallas_call x7, Pallas kernels, call(): pl.pallas_call(kernel, out_shape=[jax.ShapeDtypeStruct(s, kind) for s in...  7.65 us
    ppermute x2, starting transfers between devices, on_device(): lax.ppermute(sent[flip], AXES, pairs_of(sizes, sent_to(flip)))  7.39 us
    all_to_all x1, waiting for transfers between devices, on_device(): parts = lax.all_to_all(parts, 'x', 0, 0)  7.13 us
    all_to_all x1, waiting for transfers between devices, on_device(): lax.all_to_all(home.reshape(cols_count, part, size), AXES[2:], 0, 0)  7.03 us
    all_to_all x1, waiting for transfers between devices, on_device(): lax.all_to_all(jnp.broadcast_to(near, (sizes[3],) + near.shape), 'zl', 0, 0)  5.87 us
  transfers between devices with their start and end apart: 13, of which 6 were waited for; matrix products, arithmetic and copies ran while one was open for 2% of the time, Pallas kernels for 3%

profile of v14, /device:TPU:6, one launch (start us, length us, event | category | flops | bytes accessed | tf_op | source)
XLA Modules:
  0.0 99.9 jit_solution(2615146180652618422)
XLA Ops:
  0.0 0.0 copy-start
  0.0 13.5 %all-to-all-start = ((f32[32,16,256]{2,1,0:T(8,128)}), f32[32,16,256]{2,1,0:T(8,128)S(1)}, u32[]{:S(2)}, u32[]{:S(2)}) async-start(f32[32,16,256]{2,1,0:T(8,128)} %bitcast.15), calls=%async_computation | async-start | bytes 1048576 | tf_op jit(solution)/shard_map/all_to_all | solution.py:211
  13.6 2.4 %collective-permute-start.2 = (f32[2,256,256]{2,1,0:T(8,128)}, f32[2,256,256]{2,1,0:T(8,128)S(1)}, u32[]{:S(2)}, u32[]{:S(2)}) collective-permute-start(f32[2,256,256]{2,1,0:T(8,128)} %bitcast.16), channel_id=1, source_target_pairs={{0,480},{32,0},{64,32},{96,64},{128,96},{160,128},{192,160},{224,1... | collective-permute-start | bytes 1572872 | tf_op jit(solution)/shard_map/ppermute | solution.py:203
  15.9 3.2 %collective-permute-start.1 = (f32[2,256,256]{2,1,0:T(8,128)}, f32[2,256,256]{2,1,0:T(8,128)S(1)}, u32[]{:S(2)}, u32[]{:S(2)}) collective-permute-start(f32[2,256,256]{2,1,0:T(8,128)} %bitcast.17), channel_id=1, source_target_pairs={{0,448},{64,0},{128,64},{192,128},{256,192},{320,256},{384,320},{4... | collective-permute-start | bytes 1572872 | tf_op jit(solution)/shard_map/ppermute | solution.py:200
  19.2 2.6 %collective-permute-start = (f32[2,256,256]{2,1,0:T(8,128)}, f32[2,256,256]{2,1,0:T(8,128)S(1)}, u32[]{:S(2)}, u32[]{:S(2)}) collective-permute-start(f32[2,256,256]{2,1,0:T(8,128)} %bitcast.19), channel_id=1, source_target_pairs={{0,64},{64,128},{128,192},{192,256},{256,320},{320,384},{384,448},... | collective-permute-start | bytes 1572872 | tf_op jit(solution)/shard_map/ppermute | solution.py:200
  21.8 0.8 reshape.3.codes
  22.6 0.1 stack.40.place
  22.6 0.7 shard_map.37
  23.4 7.0 %all-to-all-done = f32[32,16,256]{2,1,0:T(8,128)S(1)} async-done(((f32[32,16,256]{2,1,0:T(8,128)}), f32[32,16,256]{2,1,0:T(8,128)S(1)}, u32[]{:S(2)}, u32[]{:S(2)}) %all-to-all-start) | async-done | bytes 524320 | tf_op jit(solution)/shard_map/all_to_all | solution.py:211
  30.4 0.7 broadcast_in_dim.6
  31.0 3.3 %all-to-all-start.1 = ((f32[4,2,16,256]{3,2,1,0:T(8,128)}), f32[4,2,16,256]{3,2,1,0:T(8,128)S(1)}, u32[]{:S(2)}, u32[]{:S(2)}) async-start(f32[4,2,16,256]{3,2,1,0:T(8,128)} %broadcast_in_dim.6), calls=%async_computation.1 | async-start | bytes 262144 | tf_op jit(solution)/shard_map/all_to_all | solution.py:225
  34.4 0.0 collective-permute-done.2.beside_ref
  34.4 0.0 collective-permute-done.1.ahead_ref
  34.4 5.9 %all-to-all-done.1.gathered = f32[4,2,16,256]{3,2,1,0:T(8,128)S(1)} async-done(((f32[4,2,16,256]{3,2,1,0:T(8,128)}), f32[4,2,16,256]{3,2,1,0:T(8,128)S(1)}, u32[]{:S(2)}, u32[]{:S(2)}) %all-to-all-start.1) | async-done | bytes 131104 | tf_op jit(solution)/shard_map/all_to_all | solution.py:225
  40.3 0.0 collective-permute-done.left_ref
  40.3 0.0 copy-done
  40.3 2.5 %shard_map.38 = f32[4,3,2,64,256]{4,3,2,1,0:T(8,128)} custom-call(s32[7]{0:T(128)S(1)} %stack.40.place, f32[2,256,256]{2,1,0:T(8,128)S(1)} %collective-permute-done.left_ref, f32[2,256,256]{2,1,0:T(8,128)S(1)} %collective-permute-done.1.ahead_ref, f32[2,256,256]{2,1,0:T(8,128)S(1)} %collective-permute-done.2.beside_ref, s32[32,256]{1,0:T(8,128)S(1)} %reshape.3.codes, ...), custom_call_target="tpu_custom_call" | custom-call | flops 603979776 | bytes 3964956 | tf_op jit(solution)/shard_map/pallas_call | solution.py:170
  42.8 4.8 %all-to-all-start.2 = ((f32[4,3,2,64,256]{4,3,2,1,0:T(8,128)}), f32[4,3,2,64,256]{4,3,2,1,0:T(8,128)S(1)}, u32[]{:S(2)}, u32[]{:S(2)}) async-start(f32[4,3,2,64,256]{4,3,2,1,0:T(8,128)} %shard_map.38), calls=%async_computation.2 | async-start | bytes 3145728 | tf_op jit(solution)/shard_map/all_to_all | solution.py:243
  47.6 2.9 %collective-permute-start.3 = (f32[4,16,256]{2,1,0:T(8,128)S(1)}, f32[4,16,256]{2,1,0:T(8,128)S(1)}, u32[]{:S(2)}, u32[]{:S(2)}) collective-permute-start(f32[4,16,256]{2,1,0:T(8,128)S(1)} %slice_bitcast_fusion), channel_id=1, source_target_pairs={{0,496},{1,497},{2,498},{3,499},{4,500},{5,501},{6,502},{7,503},{8... | collective-permute-start | bytes 196616 | tf_op jit(solution)/shard_map/ppermute | solution.py:238
  50.5 1.9 %collective-permute-done.3.next1 = f32[4,16,256]{2,1,0:T(8,128)S(1)} collective-permute-done((f32[4,16,256]{2,1,0:T(8,128)S(1)}, f32[4,16,256]{2,1,0:T(8,128)S(1)}, u32[]{:S(2)}, u32[]{:S(2)}) %collective-permute-start.3) | collective-permute-done | bytes 65568 | tf_op jit(solution)/shard_map/ppermute | solution.py:238
  52.3 0.6 shard_map.39.refs_0_
  52.9 2.8 %collective-permute-start.6 = (f32[3,4,16,256]{3,2,1,0:T(8,128)S(1)}, f32[3,4,16,256]{3,2,1,0:T(8,128)S(1)}, u32[]{:S(2)}, u32[]{:S(2)}) collective-permute-start(f32[3,4,16,256]{3,2,1,0:T(8,128)S(1)} %shard_map.39.refs_0_), channel_id=1, source_target_pairs={{0,1},{1,0},{2,3},{3,2},{4,5},{5,4},{6,7},{7,6},{8,9},{9,8},{10,11... | collective-permute-start | bytes 589832 | tf_op jit(solution)/shard_map/ppermute | solution.py:228
  55.7 3.1 %collective-permute-start.5 = (f32[3,4,16,256]{3,2,1,0:T(8,128)S(1)}, f32[3,4,16,256]{3,2,1,0:T(8,128)S(1)}, u32[]{:S(2)}, u32[]{:S(2)}) collective-permute-start(f32[3,4,16,256]{3,2,1,0:T(8,128)S(1)} %shard_map.39.refs_0_), channel_id=1, source_target_pairs={{0,3},{1,2},{2,1},{3,0},{4,7},{5,6},{6,5},{7,4},{8,11},{9,10},{10,... | collective-permute-start | bytes 589832 | tf_op jit(solution)/shard_map/ppermute | solution.py:228
  58.8 7.1 %all-to-all-done.2.got = f32[4,3,2,64,256]{4,3,2,1,0:T(8,128)S(1)} async-done(((f32[4,3,2,64,256]{4,3,2,1,0:T(8,128)}), f32[4,3,2,64,256]{4,3,2,1,0:T(8,128)S(1)}, u32[]{:S(2)}, u32[]{:S(2)}) %all-to-all-start.2) | async-done | bytes 1572896 | tf_op jit(solution)/shard_map/all_to_all | solution.py:243
  65.9 4.0 %collective-permute-start.4 = (f32[3,4,16,256]{3,2,1,0:T(8,128)S(1)}, f32[3,4,16,256]{3,2,1,0:T(8,128)S(1)}, u32[]{:S(2)}, u32[]{:S(2)}) collective-permute-start(f32[3,4,16,256]{3,2,1,0:T(8,128)S(1)} %shard_map.39.refs_0_), channel_id=1, source_target_pairs={{0,2},{1,3},{2,0},{3,1},{4,6},{5,7},{6,4},{7,5},{8,10},{9,11},{10,... | collective-permute-start | bytes 589832 | tf_op jit(solution)/shard_map/ppermute | solution.py:228
  69.9 0.8 shard_map.40
  70.7 4.5 %all-to-all-start.3 = ((f32[8,3,16,256]{3,2,1,0:T(8,128)}), f32[8,3,16,256]{3,2,1,0:T(8,128)S(1)}, u32[]{:S(2)}, u32[]{:S(2)}) async-start(f32[8,3,16,256]{3,2,1,0:T(8,128)} %shard_map.40), calls=%async_computation.3 | async-start | bytes 786432 | tf_op jit(solution)/shard_map/all_to_all | solution.py:252
  75.2 0.0 collective-permute-done.6.refs_3_
  75.2 0.0 collective-permute-done.5.refs_2_
  75.2 0.0 collective-permute-done.4.refs_1_
  75.3 0.8 shard_map.41
  76.0 11.1 %all-to-all-done.3.got = f32[8,3,16,256]{3,2,1,0:T(8,128)S(1)} async-done(((f32[8,3,16,256]{3,2,1,0:T(8,128)}), f32[8,3,16,256]{3,2,1,0:T(8,128)S(1)}, u32[]{:S(2)}, u32[]{:S(2)}) %all-to-all-start.3) | async-done | bytes 393248 | tf_op jit(solution)/shard_map/all_to_all | solution.py:252
  87.1 1.1 %shard_map.42 = (f32[3,8,256]{2,1,0:T(8,128)S(1)}, f32[3,8,256]{2,1,0:T(8,128)S(1)}) custom-call(s32[7]{0:T(128)S(1)} %stack.40.place, f32[8,3,16,256]{3,2,1,0:T(8,128)S(1)} %all-to-all-done.3.got, bf16[3,256,256]{2,1,0:T(8,128)(2,1)S(1)} %get-tuple-element.33.high, bf16[3,256,256]{2,1,0:T(8,128)(2,1)S(1)} %get-tuple-element.34.low), custom_call_target="tpu_custom_call" | custom-call | flops 18874368 | bytes 2015260 | tf_op jit(solution)/shard_map/pallas_call | solution.py:170
  88.2 3.9 %collective-permute-start.7 = (f32[3,8,256]{2,1,0:T(8,128)S(1)}, f32[3,8,256]{2,1,0:T(8,128)S(1)}, u32[]{:S(2)}, u32[]{:S(2)}) collective-permute-start(f32[3,8,256]{2,1,0:T(8,128)S(1)} %get-tuple-element.35), channel_id=1, source_target_pairs={{0,464},{1,465},{2,466},{3,467},{4,468},{5,469},{6,470},{7,471},{8... | collective-permute-start | bytes 73736 | tf_op jit(solution)/shard_map/ppermute | solution.py:265
  92.2 3.5 %collective-permute-start.8 = (f32[3,8,256]{2,1,0:T(8,128)S(1)}, f32[3,8,256]{2,1,0:T(8,128)S(1)}, u32[]{:S(2)}, u32[]{:S(2)}) collective-permute-start(f32[3,8,256]{2,1,0:T(8,128)S(1)} %get-tuple-element.36), channel_id=1, source_target_pairs={{0,448},{1,449},{2,450},{3,451},{4,452},{5,453},{6,454},{7,455},{8... | collective-permute-start | bytes 73736 | tf_op jit(solution)/shard_map/ppermute | solution.py:265
  95.6 3.1 %collective-permute-done.7.back1 = f32[3,8,256]{2,1,0:T(8,128)S(1)} collective-permute-done((f32[3,8,256]{2,1,0:T(8,128)S(1)}, f32[3,8,256]{2,1,0:T(8,128)S(1)}, u32[]{:S(2)}, u32[]{:S(2)}) %collective-permute-start.7) | collective-permute-done | bytes 24608 | tf_op jit(solution)/shard_map/ppermute | solution.py:265
  98.8 0.0 collective-permute-done.8.back0
  98.8 1.2 %shard_map.43 = f32[3,2,8,256]{3,2,1,0:T(8,128)} custom-call(s32[7]{0:T(128)S(1)} %stack.40.place, f32[3,8,256]{2,1,0:T(8,128)S(1)} %collective-permute-done.7.back1, f32[3,8,256]{2,1,0:T(8,128)S(1)} %collective-permute-done.8.back0), custom_call_target="tpu_custom_call" | custom-call | flops 10000 | bytes 98332 | tf_op jit(solution)/shard_map/pallas_call | solution.py:170
  (3 shorter events, 0.0 us)
Async XLA Ops:
  0.0 40.3 %copy-start = (f32[2,1,1,1,256,256]{5,4,3,2,1,0:T(8,128)S(1)}, f32[2,1,1,1,256,256]{5,4,3,2,1,0:T(8,128)}, u32[]{:S(2)}) copy-start(f32[2,1,1,1,256,256]{5,4,3,2,1,0:T(8,128)} %param.3) | copy-start | bytes 1572868
  0.0 30.4 %all-to-all-start = ((f32[32,16,256]{2,1,0:T(8,128)}), f32[32,16,256]{2,1,0:T(8,128)S(1)}, u32[]{:S(2)}, u32[]{:S(2)}) async-start(f32[32,16,256]{2,1,0:T(8,128)} %bitcast.15), calls=%async_computation | async-start | bytes 1048576 | tf_op jit(solution)/shard_map/all_to_all | solution.py:211
  13.6 20.8 %collective-permute-start.2 = (f32[2,256,256]{2,1,0:T(8,128)}, f32[2,256,256]{2,1,0:T(8,128)S(1)}, u32[]{:S(2)}, u32[]{:S(2)}) collective-permute-start(f32[2,256,256]{2,1,0:T(8,128)} %bitcast.16), channel_id=1, source_target_pairs={{0,480},{32,0},{64,32},{96,64},{128,96},{160,128},{192,160},{224,1... | collective-permute-start | bytes 1572872 | tf_op jit(solution)/shard_map/ppermute | solution.py:203
  15.9 18.5 %collective-permute-start.1 = (f32[2,256,256]{2,1,0:T(8,128)}, f32[2,256,256]{2,1,0:T(8,128)S(1)}, u32[]{:S(2)}, u32[]{:S(2)}) collective-permute-start(f32[2,256,256]{2,1,0:T(8,128)} %bitcast.17), channel_id=1, source_target_pairs={{0,448},{64,0},{128,64},{192,128},{256,192},{320,256},{384,320},{4... | collective-permute-start | bytes 1572872 | tf_op jit(solution)/shard_map/ppermute | solution.py:200
  19.2 21.1 %collective-permute-start = (f32[2,256,256]{2,1,0:T(8,128)}, f32[2,256,256]{2,1,0:T(8,128)S(1)}, u32[]{:S(2)}, u32[]{:S(2)}) collective-permute-start(f32[2,256,256]{2,1,0:T(8,128)} %bitcast.19), channel_id=1, source_target_pairs={{0,64},{64,128},{128,192},{192,256},{256,320},{320,384},{384,448},... | collective-permute-start | bytes 1572872 | tf_op jit(solution)/shard_map/ppermute | solution.py:200
  31.0 9.2 %all-to-all-start.1 = ((f32[4,2,16,256]{3,2,1,0:T(8,128)}), f32[4,2,16,256]{3,2,1,0:T(8,128)S(1)}, u32[]{:S(2)}, u32[]{:S(2)}) async-start(f32[4,2,16,256]{3,2,1,0:T(8,128)} %broadcast_in_dim.6), calls=%async_computation.1 | async-start | bytes 262144 | tf_op jit(solution)/shard_map/all_to_all | solution.py:225
  42.8 23.1 %all-to-all-start.2 = ((f32[4,3,2,64,256]{4,3,2,1,0:T(8,128)}), f32[4,3,2,64,256]{4,3,2,1,0:T(8,128)S(1)}, u32[]{:S(2)}, u32[]{:S(2)}) async-start(f32[4,3,2,64,256]{4,3,2,1,0:T(8,128)} %shard_map.38), calls=%async_computation.2 | async-start | bytes 3145728 | tf_op jit(solution)/shard_map/all_to_all | solution.py:243
  47.6 4.7 %collective-permute-start.3 = (f32[4,16,256]{2,1,0:T(8,128)S(1)}, f32[4,16,256]{2,1,0:T(8,128)S(1)}, u32[]{:S(2)}, u32[]{:S(2)}) collective-permute-start(f32[4,16,256]{2,1,0:T(8,128)S(1)} %slice_bitcast_fusion), channel_id=1, source_target_pairs={{0,496},{1,497},{2,498},{3,499},{4,500},{5,501},{6,502},{7,503},{8... | collective-permute-start | bytes 196616 | tf_op jit(solution)/shard_map/ppermute | solution.py:238
  52.9 22.3 %collective-permute-start.6 = (f32[3,4,16,256]{3,2,1,0:T(8,128)S(1)}, f32[3,4,16,256]{3,2,1,0:T(8,128)S(1)}, u32[]{:S(2)}, u32[]{:S(2)}) collective-permute-start(f32[3,4,16,256]{3,2,1,0:T(8,128)S(1)} %shard_map.39.refs_0_), channel_id=1, source_target_pairs={{0,1},{1,0},{2,3},{3,2},{4,5},{5,4},{6,7},{7,6},{8,9},{9,8},{10,11... | collective-permute-start | bytes 589832 | tf_op jit(solution)/shard_map/ppermute | solution.py:228
  55.7 19.5 %collective-permute-start.5 = (f32[3,4,16,256]{3,2,1,0:T(8,128)S(1)}, f32[3,4,16,256]{3,2,1,0:T(8,128)S(1)}, u32[]{:S(2)}, u32[]{:S(2)}) collective-permute-start(f32[3,4,16,256]{3,2,1,0:T(8,128)S(1)} %shard_map.39.refs_0_), channel_id=1, source_target_pairs={{0,3},{1,2},{2,1},{3,0},{4,7},{5,6},{6,5},{7,4},{8,11},{9,10},{10,... | collective-permute-start | bytes 589832 | tf_op jit(solution)/shard_map/ppermute | solution.py:228
  65.9 9.3 %collective-permute-start.4 = (f32[3,4,16,256]{3,2,1,0:T(8,128)S(1)}, f32[3,4,16,256]{3,2,1,0:T(8,128)S(1)}, u32[]{:S(2)}, u32[]{:S(2)}) collective-permute-start(f32[3,4,16,256]{3,2,1,0:T(8,128)S(1)} %shard_map.39.refs_0_), channel_id=1, source_target_pairs={{0,2},{1,3},{2,0},{3,1},{4,6},{5,7},{6,4},{7,5},{8,10},{9,11},{10,... | collective-permute-start | bytes 589832 | tf_op jit(solution)/shard_map/ppermute | solution.py:228
  70.7 16.4 %all-to-all-start.3 = ((f32[8,3,16,256]{3,2,1,0:T(8,128)}), f32[8,3,16,256]{3,2,1,0:T(8,128)S(1)}, u32[]{:S(2)}, u32[]{:S(2)}) async-start(f32[8,3,16,256]{3,2,1,0:T(8,128)} %shard_map.40), calls=%async_computation.3 | async-start | bytes 786432 | tf_op jit(solution)/shard_map/all_to_all | solution.py:252
  88.2 10.5 %collective-permute-start.7 = (f32[3,8,256]{2,1,0:T(8,128)S(1)}, f32[3,8,256]{2,1,0:T(8,128)S(1)}, u32[]{:S(2)}, u32[]{:S(2)}) collective-permute-start(f32[3,8,256]{2,1,0:T(8,128)S(1)} %get-tuple-element.35), channel_id=1, source_target_pairs={{0,464},{1,465},{2,466},{3,467},{4,468},{5,469},{6,470},{7,471},{8... | collective-permute-start | bytes 73736 | tf_op jit(solution)/shard_map/ppermute | solution.py:265
  92.2 6.6 %collective-permute-start.8 = (f32[3,8,256]{2,1,0:T(8,128)S(1)}, f32[3,8,256]{2,1,0:T(8,128)S(1)}, u32[]{:S(2)}, u32[]{:S(2)}) collective-permute-start(f32[3,8,256]{2,1,0:T(8,128)S(1)} %get-tuple-element.36), channel_id=1, source_target_pairs={{0,448},{1,449},{2,450},{3,451},{4,452},{5,453},{6,454},{7,455},{8... | collective-permute-start | bytes 73736 | tf_op jit(solution)/shard_map/ppermute | solution.py:265

commit v15 on v13

--- a/solution.py
+++ b/solution.py
@@ -32,7 +32,9 @@
 def times(a, b):
     dims = (((1,), (1,)), ((), ()))
     dot = functools.partial(lax.dot_general, dimension_numbers=dims, preferred_element_type=F32)
-    return dot(a[0], b[0]) + (dot(a[0], b[1]) + dot(a[1], b[0]))
+    rows = a[0].shape[0]
+    both = dot(jnp.concatenate([a[0], a[1]], axis=0), b[0])
+    return both[:rows] + (dot(a[0], b[1]) + both[rows:])
 
 
 def codes_of(codes, tile):

time: 101 us -> 101 us (level)
  no operation moved by 1% of the time
where the time goes in v15:
time: 101 us; the launch traced here: 98.6 us
  starting transfers between devices  56.4 us (56%)
  waiting for transfers between devices  33.1 us (33%)
  Pallas kernels  7.44 us (7%)
  local copies, waits for them, and re-layouts  1.53 us (2%)
    all_to_all x1, starting transfers between devices, on_device(): lax.all_to_all(home.reshape(cols_count, part, size), AXES[2:], 0, 0)  13.5 us
    ppermute x3, starting transfers between devices, partner(): return lax.ppermute(v, axis, [(i, i ^ j) for i in range(n)])  9.82 us
    ppermute x2, starting transfers between devices, on_device(): lax.ppermute(sent[flip], AXES, pairs_of(sizes, sent_to(flip)))  9.32 us
    all_to_all x1, waiting for transfers between devices, on_device(): got = lax.all_to_all(ready, ('zh', 'zl'), 0, 0)  9.27 us
    pallas_call x7, Pallas kernels, call(): pl.pallas_call(kernel, out_shape=[jax.ShapeDtypeStruct(s, kind) for s in...  7.44 us
    all_to_all x1, waiting for transfers between devices, on_device(): lax.all_to_all(home.reshape(cols_count, part, size), AXES[2:], 0, 0)  7.03 us
    all_to_all x1, waiting for transfers between devices, on_device(): lax.all_to_all(jnp.broadcast_to(near, (sizes[3],) + near.shape), 'zl', 0, 0)  5.87 us
    ppermute x2, starting transfers between devices, row_shift(): return lax.ppermute(v, 'y', [(i, (i + by) % n) for i in range(n)])  5.83 us
  transfers between devices with their start and end apart: 13, of which 8 were waited for; matrix products, arithmetic and copies ran while one was open for 2% of the time, Pallas kernels for 3%

profile of v15, /device:TPU:6, one launch (start us, length us, event | category | flops | bytes accessed | tf_op | source)
XLA Modules:
  0.0 98.6 jit_solution(4196006365423799789)
XLA Ops:
  0.0 0.0 copy-start
  0.0 13.5 %all-to-all-start = ((f32[32,16,256]{2,1,0:T(8,128)}), f32[32,16,256]{2,1,0:T(8,128)S(1)}, u32[]{:S(2)}, u32[]{:S(2)}) async-start(f32[32,16,256]{2,1,0:T(8,128)} %bitcast.15), calls=%async_computation | async-start | bytes 1048576 | tf_op jit(solution)/shard_map/all_to_all | solution.py:213
  13.6 2.4 %collective-permute-start.2 = (f32[2,256,256]{2,1,0:T(8,128)}, f32[2,256,256]{2,1,0:T(8,128)S(1)}, u32[]{:S(2)}, u32[]{:S(2)}) collective-permute-start(f32[2,256,256]{2,1,0:T(8,128)} %bitcast.16), channel_id=1, source_target_pairs={{0,480},{32,0},{64,32},{96,64},{128,96},{160,128},{192,160},{224,1... | collective-permute-start | bytes 1572872 | tf_op jit(solution)/shard_map/ppermute | solution.py:205
  15.9 3.2 %collective-permute-start.1 = (f32[2,256,256]{2,1,0:T(8,128)}, f32[2,256,256]{2,1,0:T(8,128)S(1)}, u32[]{:S(2)}, u32[]{:S(2)}) collective-permute-start(f32[2,256,256]{2,1,0:T(8,128)} %bitcast.17), channel_id=1, source_target_pairs={{0,448},{64,0},{128,64},{192,128},{256,192},{320,256},{384,320},{4... | collective-permute-start | bytes 1572872 | tf_op jit(solution)/shard_map/ppermute | solution.py:202
  19.2 2.6 %collective-permute-start = (f32[2,256,256]{2,1,0:T(8,128)}, f32[2,256,256]{2,1,0:T(8,128)S(1)}, u32[]{:S(2)}, u32[]{:S(2)}) collective-permute-start(f32[2,256,256]{2,1,0:T(8,128)} %bitcast.19), channel_id=1, source_target_pairs={{0,64},{64,128},{128,192},{192,256},{256,320},{320,384},{384,448},... | collective-permute-start | bytes 1572872 | tf_op jit(solution)/shard_map/ppermute | solution.py:202
  21.8 0.8 reshape.3.codes
  22.6 0.1 stack.40.place
  22.6 0.7 shard_map.37
  23.4 7.0 %all-to-all-done = f32[32,16,256]{2,1,0:T(8,128)S(1)} async-done(((f32[32,16,256]{2,1,0:T(8,128)}), f32[32,16,256]{2,1,0:T(8,128)S(1)}, u32[]{:S(2)}, u32[]{:S(2)}) %all-to-all-start) | async-done | bytes 524320 | tf_op jit(solution)/shard_map/all_to_all | solution.py:213
  30.4 0.7 broadcast_in_dim.6
  31.0 3.3 %all-to-all-start.1 = ((f32[4,2,16,256]{3,2,1,0:T(8,128)}), f32[4,2,16,256]{3,2,1,0:T(8,128)S(1)}, u32[]{:S(2)}, u32[]{:S(2)}) async-start(f32[4,2,16,256]{3,2,1,0:T(8,128)} %broadcast_in_dim.6), calls=%async_computation.1 | async-start | bytes 262144 | tf_op jit(solution)/shard_map/all_to_all | solution.py:227
  34.4 0.0 collective-permute-done.2.beside_ref
  34.4 0.0 collective-permute-done.1.ahead_ref
  34.4 5.9 %all-to-all-done.1.gathered = f32[4,2,16,256]{3,2,1,0:T(8,128)S(1)} async-done(((f32[4,2,16,256]{3,2,1,0:T(8,128)}), f32[4,2,16,256]{3,2,1,0:T(8,128)S(1)}, u32[]{:S(2)}, u32[]{:S(2)}) %all-to-all-start.1) | async-done | bytes 131104 | tf_op jit(solution)/shard_map/all_to_all | solution.py:227
  40.3 0.0 collective-permute-done.left_ref
  40.3 0.0 copy-done
  40.3 2.4 %shard_map.38 = f32[4,3,2,64,256]{4,3,2,1,0:T(8,128)} custom-call(s32[7]{0:T(128)S(1)} %stack.40.place, f32[2,256,256]{2,1,0:T(8,128)S(1)} %collective-permute-done.left_ref, f32[2,256,256]{2,1,0:T(8,128)S(1)} %collective-permute-done.1.ahead_ref, f32[2,256,256]{2,1,0:T(8,128)S(1)} %collective-permute-done.2.beside_ref, s32[32,256]{1,0:T(8,128)S(1)} %reshape.3.codes, ...), custom_call_target="tpu_custom_call" | custom-call | flops 603979776 | bytes 3964956 | tf_op jit(solution)/shard_map/pallas_call | solution.py:172
  42.7 4.8 %all-to-all-start.2 = ((f32[4,3,2,64,256]{4,3,2,1,0:T(8,128)}), f32[4,3,2,64,256]{4,3,2,1,0:T(8,128)S(1)}, u32[]{:S(2)}, u32[]{:S(2)}) async-start(f32[4,3,2,64,256]{4,3,2,1,0:T(8,128)} %shard_map.38), calls=%async_computation.2 | async-start | bytes 3145728 | tf_op jit(solution)/shard_map/all_to_all | solution.py:251
  47.5 2.9 %collective-permute-start.3 = (f32[4,16,256]{2,1,0:T(8,128)S(1)}, f32[4,16,256]{2,1,0:T(8,128)S(1)}, u32[]{:S(2)}, u32[]{:S(2)}) collective-permute-start(f32[4,16,256]{2,1,0:T(8,128)S(1)} %slice_bitcast_fusion), channel_id=1, source_target_pairs={{0,496},{1,497},{2,498},{3,499},{4,500},{5,501},{6,502},{7,503},{8... | collective-permute-start | bytes 196616 | tf_op jit(solution)/shard_map/ppermute | solution.py:240
  50.4 1.9 %collective-permute-done.3.next1 = f32[4,16,256]{2,1,0:T(8,128)S(1)} collective-permute-done((f32[4,16,256]{2,1,0:T(8,128)S(1)}, f32[4,16,256]{2,1,0:T(8,128)S(1)}, u32[]{:S(2)}, u32[]{:S(2)}) %collective-permute-start.3) | collective-permute-done | bytes 65568 | tf_op jit(solution)/shard_map/ppermute | solution.py:240
  52.3 0.6 shard_map.39.refs_0_
  52.9 2.8 %collective-permute-start.6 = (f32[3,4,16,256]{3,2,1,0:T(8,128)S(1)}, f32[3,4,16,256]{3,2,1,0:T(8,128)S(1)}, u32[]{:S(2)}, u32[]{:S(2)}) collective-permute-start(f32[3,4,16,256]{3,2,1,0:T(8,128)S(1)} %shard_map.39.refs_0_), channel_id=1, source_target_pairs={{0,1},{1,0},{2,3},{3,2},{4,5},{5,4},{6,7},{7,6},{8,9},{9,8},{10,11... | collective-permute-start | bytes 589832 | tf_op jit(solution)/shard_map/ppermute | solution.py:230
  55.6 3.1 %collective-permute-start.5 = (f32[3,4,16,256]{3,2,1,0:T(8,128)S(1)}, f32[3,4,16,256]{3,2,1,0:T(8,128)S(1)}, u32[]{:S(2)}, u32[]{:S(2)}) collective-permute-start(f32[3,4,16,256]{3,2,1,0:T(8,128)S(1)} %shard_map.39.refs_0_), channel_id=1, source_target_pairs={{0,3},{1,2},{2,1},{3,0},{4,7},{5,6},{6,5},{7,4},{8,11},{9,10},{10,... | collective-permute-start | bytes 589832 | tf_op jit(solution)/shard_map/ppermute | solution.py:230
  58.7 4.0 %collective-permute-start.4 = (f32[3,4,16,256]{3,2,1,0:T(8,128)S(1)}, f32[3,4,16,256]{3,2,1,0:T(8,128)S(1)}, u32[]{:S(2)}, u32[]{:S(2)}) collective-permute-start(f32[3,4,16,256]{3,2,1,0:T(8,128)S(1)} %shard_map.39.refs_0_), channel_id=1, source_target_pairs={{0,2},{1,3},{2,0},{3,1},{4,6},{5,7},{6,4},{7,5},{8,10},{9,11},{10,... | collective-permute-start | bytes 589832 | tf_op jit(solution)/shard_map/ppermute | solution.py:230
  62.7 3.4 %all-to-all-done.2.got = f32[4,3,2,64,256]{4,3,2,1,0:T(8,128)S(1)} async-done(((f32[4,3,2,64,256]{4,3,2,1,0:T(8,128)}), f32[4,3,2,64,256]{4,3,2,1,0:T(8,128)S(1)}, u32[]{:S(2)}, u32[]{:S(2)}) %all-to-all-start.2) | async-done | bytes 1572896 | tf_op jit(solution)/shard_map/all_to_all | solution.py:251
  66.1 0.8 shard_map.40
  66.9 4.5 %all-to-all-start.3 = ((f32[8,3,16,256]{3,2,1,0:T(8,128)}), f32[8,3,16,256]{3,2,1,0:T(8,128)S(1)}, u32[]{:S(2)}, u32[]{:S(2)}) async-start(f32[8,3,16,256]{3,2,1,0:T(8,128)} %shard_map.40), calls=%async_computation.3 | async-start | bytes 786432 | tf_op jit(solution)/shard_map/all_to_all | solution.py:254
  71.5 0.0 collective-permute-done.6.refs_3_
  71.5 1.8 %collective-permute-done.5.refs_2_ = f32[3,4,16,256]{3,2,1,0:T(8,128)S(1)} collective-permute-done((f32[3,4,16,256]{3,2,1,0:T(8,128)S(1)}, f32[3,4,16,256]{3,2,1,0:T(8,128)S(1)}, u32[]{:S(2)}, u32[]{:S(2)}) %collective-permute-start.5) | collective-permute-done | bytes 196640 | tf_op jit(solution)/shard_map/ppermute | solution.py:230
  73.3 0.0 collective-permute-done.4.refs_1_
  73.3 0.8 shard_map.41
  74.1 9.3 %all-to-all-done.3.got = f32[8,3,16,256]{3,2,1,0:T(8,128)S(1)} async-done(((f32[8,3,16,256]{3,2,1,0:T(8,128)}), f32[8,3,16,256]{3,2,1,0:T(8,128)S(1)}, u32[]{:S(2)}, u32[]{:S(2)}) %all-to-all-start.3) | async-done | bytes 393248 | tf_op jit(solution)/shard_map/all_to_all | solution.py:254
  83.4 1.0 shard_map.42
  84.3 7.4 %collective-permute-start.7 = (f32[3,8,256]{2,1,0:T(8,128)S(1)}, f32[3,8,256]{2,1,0:T(8,128)S(1)}, u32[]{:S(2)}, u32[]{:S(2)}) collective-permute-start(f32[3,8,256]{2,1,0:T(8,128)S(1)} %get-tuple-element.33), channel_id=1, source_target_pairs={{0,464},{1,465},{2,466},{3,467},{4,468},{5,469},{6,470},{7,471},{8... | collective-permute-start | bytes 73736 | tf_op jit(solution)/shard_map/ppermute | solution.py:267
  91.7 1.9 %collective-permute-start.8 = (f32[3,8,256]{2,1,0:T(8,128)S(1)}, f32[3,8,256]{2,1,0:T(8,128)S(1)}, u32[]{:S(2)}, u32[]{:S(2)}) collective-permute-start(f32[3,8,256]{2,1,0:T(8,128)S(1)} %get-tuple-element.34), channel_id=1, source_target_pairs={{0,448},{1,449},{2,450},{3,451},{4,452},{5,453},{6,454},{7,455},{8... | collective-permute-start | bytes 73736 | tf_op jit(solution)/shard_map/ppermute | solution.py:267
  93.7 1.2 %collective-permute-done.7.back1 = f32[3,8,256]{2,1,0:T(8,128)S(1)} collective-permute-done((f32[3,8,256]{2,1,0:T(8,128)S(1)}, f32[3,8,256]{2,1,0:T(8,128)S(1)}, u32[]{:S(2)}, u32[]{:S(2)}) %collective-permute-start.7) | collective-permute-done | bytes 24608 | tf_op jit(solution)/shard_map/ppermute | solution.py:267
  94.9 2.6 %collective-permute-done.8.back0 = f32[3,8,256]{2,1,0:T(8,128)S(1)} collective-permute-done((f32[3,8,256]{2,1,0:T(8,128)S(1)}, f32[3,8,256]{2,1,0:T(8,128)S(1)}, u32[]{:S(2)}, u32[]{:S(2)}) %collective-permute-start.8) | collective-permute-done | bytes 24608 | tf_op jit(solution)/shard_map/ppermute | solution.py:267
  97.5 1.2 %shard_map.43 = f32[3,2,8,256]{3,2,1,0:T(8,128)} custom-call(s32[7]{0:T(128)S(1)} %stack.40.place, f32[3,8,256]{2,1,0:T(8,128)S(1)} %collective-permute-done.7.back1, f32[3,8,256]{2,1,0:T(8,128)S(1)} %collective-permute-done.8.back0), custom_call_target="tpu_custom_call" | custom-call | flops 10000 | bytes 98332 | tf_op jit(solution)/shard_map/pallas_call | solution.py:172
  (3 shorter events, 0.0 us)
Async XLA Ops:
  0.0 40.3 %copy-start = (f32[2,1,1,1,256,256]{5,4,3,2,1,0:T(8,128)S(1)}, f32[2,1,1,1,256,256]{5,4,3,2,1,0:T(8,128)}, u32[]{:S(2)}) copy-start(f32[2,1,1,1,256,256]{5,4,3,2,1,0:T(8,128)} %param.3) | copy-start | bytes 1572868
  0.0 30.4 %all-to-all-start = ((f32[32,16,256]{2,1,0:T(8,128)}), f32[32,16,256]{2,1,0:T(8,128)S(1)}, u32[]{:S(2)}, u32[]{:S(2)}) async-start(f32[32,16,256]{2,1,0:T(8,128)} %bitcast.15), calls=%async_computation | async-start | bytes 1048576 | tf_op jit(solution)/shard_map/all_to_all | solution.py:213
  13.6 20.8 %collective-permute-start.2 = (f32[2,256,256]{2,1,0:T(8,128)}, f32[2,256,256]{2,1,0:T(8,128)S(1)}, u32[]{:S(2)}, u32[]{:S(2)}) collective-permute-start(f32[2,256,256]{2,1,0:T(8,128)} %bitcast.16), channel_id=1, source_target_pairs={{0,480},{32,0},{64,32},{96,64},{128,96},{160,128},{192,160},{224,1... | collective-permute-start | bytes 1572872 | tf_op jit(solution)/shard_map/ppermute | solution.py:205
  15.9 18.5 %collective-permute-start.1 = (f32[2,256,256]{2,1,0:T(8,128)}, f32[2,256,256]{2,1,0:T(8,128)S(1)}, u32[]{:S(2)}, u32[]{:S(2)}) collective-permute-start(f32[2,256,256]{2,1,0:T(8,128)} %bitcast.17), channel_id=1, source_target_pairs={{0,448},{64,0},{128,64},{192,128},{256,192},{320,256},{384,320},{4... | collective-permute-start | bytes 1572872 | tf_op jit(solution)/shard_map/ppermute | solution.py:202
  19.2 21.1 %collective-permute-start = (f32[2,256,256]{2,1,0:T(8,128)}, f32[2,256,256]{2,1,0:T(8,128)S(1)}, u32[]{:S(2)}, u32[]{:S(2)}) collective-permute-start(f32[2,256,256]{2,1,0:T(8,128)} %bitcast.19), channel_id=1, source_target_pairs={{0,64},{64,128},{128,192},{192,256},{256,320},{320,384},{384,448},... | collective-permute-start | bytes 1572872 | tf_op jit(solution)/shard_map/ppermute | solution.py:202
  31.0 9.2 %all-to-all-start.1 = ((f32[4,2,16,256]{3,2,1,0:T(8,128)}), f32[4,2,16,256]{3,2,1,0:T(8,128)S(1)}, u32[]{:S(2)}, u32[]{:S(2)}) async-start(f32[4,2,16,256]{3,2,1,0:T(8,128)} %broadcast_in_dim.6), calls=%async_computation.1 | async-start | bytes 262144 | tf_op jit(solution)/shard_map/all_to_all | solution.py:227
  42.7 23.4 %all-to-all-start.2 = ((f32[4,3,2,64,256]{4,3,2,1,0:T(8,128)}), f32[4,3,2,64,256]{4,3,2,1,0:T(8,128)S(1)}, u32[]{:S(2)}, u32[]{:S(2)}) async-start(f32[4,3,2,64,256]{4,3,2,1,0:T(8,128)} %shard_map.38), calls=%async_computation.2 | async-start | bytes 3145728 | tf_op jit(solution)/shard_map/all_to_all | solution.py:251
  47.5 4.7 %collective-permute-start.3 = (f32[4,16,256]{2,1,0:T(8,128)S(1)}, f32[4,16,256]{2,1,0:T(8,128)S(1)}, u32[]{:S(2)}, u32[]{:S(2)}) collective-permute-start(f32[4,16,256]{2,1,0:T(8,128)S(1)} %slice_bitcast_fusion), channel_id=1, source_target_pairs={{0,496},{1,497},{2,498},{3,499},{4,500},{5,501},{6,502},{7,503},{8... | collective-permute-start | bytes 196616 | tf_op jit(solution)/shard_map/ppermute | solution.py:240
  52.9 18.6 %collective-permute-start.6 = (f32[3,4,16,256]{3,2,1,0:T(8,128)S(1)}, f32[3,4,16,256]{3,2,1,0:T(8,128)S(1)}, u32[]{:S(2)}, u32[]{:S(2)}) collective-permute-start(f32[3,4,16,256]{3,2,1,0:T(8,128)S(1)} %shard_map.39.refs_0_), channel_id=1, source_target_pairs={{0,1},{1,0},{2,3},{3,2},{4,5},{5,4},{6,7},{7,6},{8,9},{9,8},{10,11... | collective-permute-start | bytes 589832 | tf_op jit(solution)/shard_map/ppermute | solution.py:230
  55.6 17.7 %collective-permute-start.5 = (f32[3,4,16,256]{3,2,1,0:T(8,128)S(1)}, f32[3,4,16,256]{3,2,1,0:T(8,128)S(1)}, u32[]{:S(2)}, u32[]{:S(2)}) collective-permute-start(f32[3,4,16,256]{3,2,1,0:T(8,128)S(1)} %shard_map.39.refs_0_), channel_id=1, source_target_pairs={{0,3},{1,2},{2,1},{3,0},{4,7},{5,6},{6,5},{7,4},{8,11},{9,10},{10,... | collective-permute-start | bytes 589832 | tf_op jit(solution)/shard_map/ppermute | solution.py:230
  58.7 14.6 %collective-permute-start.4 = (f32[3,4,16,256]{3,2,1,0:T(8,128)S(1)}, f32[3,4,16,256]{3,2,1,0:T(8,128)S(1)}, u32[]{:S(2)}, u32[]{:S(2)}) collective-permute-start(f32[3,4,16,256]{3,2,1,0:T(8,128)S(1)} %shard_map.39.refs_0_), channel_id=1, source_target_pairs={{0,2},{1,3},{2,0},{3,1},{4,6},{5,7},{6,4},{7,5},{8,10},{9,11},{10,... | collective-permute-start | bytes 589832 | tf_op jit(solution)/shard_map/ppermute | solution.py:230
  66.9 16.4 %all-to-all-start.3 = ((f32[8,3,16,256]{3,2,1,0:T(8,128)}), f32[8,3,16,256]{3,2,1,0:T(8,128)S(1)}, u32[]{:S(2)}, u32[]{:S(2)}) async-start(f32[8,3,16,256]{3,2,1,0:T(8,128)} %shard_map.40), calls=%async_computation.3 | async-start | bytes 786432 | tf_op jit(solution)/shard_map/all_to_all | solution.py:254
  84.3 10.5 %collective-permute-start.7 = (f32[3,8,256]{2,1,0:T(8,128)S(1)}, f32[3,8,256]{2,1,0:T(8,128)S(1)}, u32[]{:S(2)}, u32[]{:S(2)}) collective-permute-start(f32[3,8,256]{2,1,0:T(8,128)S(1)} %get-tuple-element.33), channel_id=1, source_target_pairs={{0,464},{1,465},{2,466},{3,467},{4,468},{5,469},{6,470},{7,471},{8... | collective-permute-start | bytes 73736 | tf_op jit(solution)/shard_map/ppermute | solution.py:267
  91.7 5.7 %collective-permute-start.8 = (f32[3,8,256]{2,1,0:T(8,128)S(1)}, f32[3,8,256]{2,1,0:T(8,128)S(1)}, u32[]{:S(2)}, u32[]{:S(2)}) collective-permute-start(f32[3,8,256]{2,1,0:T(8,128)S(1)} %get-tuple-element.34), channel_id=1, source_target_pairs={{0,448},{1,449},{2,450},{3,451},{4,452},{5,453},{6,454},{7,455},{8... | collective-permute-start | bytes 73736 | tf_op jit(solution)/shard_map/ppermute | solution.py:267
